TPU v7x, 32 devices: a whole 2x2x4 slice. The times are simulated.
32 devices in a mesh: ctx: 8 (over y, x, core), tp: 4 (over z).
Axes of the slice: x: 2, y: 2, z: 4, core: 2. Of those that a mesh axis runs over, the one named last changes fastest.
Arguments:
- tokens: bfloat16 [4096, 2304], P('ctx'), may hold values from -6 to 6
- block_map: int32 [8, 2], replicated, may hold values from 0 to 15, as said below
- w_query: bfloat16 [2304, 2048], P('ctx', 'tp'), may hold values from -0.125 to 0.125
- w_key: bfloat16 [2304, 1024], P('ctx', 'tp'), may hold values from -0.125 to 0.125
- w_value: bfloat16 [2304, 1024], P('ctx', 'tp'), may hold values from -0.125 to 0.125
- w_out: bfloat16 [2048, 2304], P('tp', 'ctx'), may hold values from -0.125 to 0.125
- w_gate: bfloat16 [2304, 9216], P('ctx', 'tp'), may hold values from -0.125 to 0.125
- w_up: bfloat16 [2304, 9216], P('ctx', 'tp'), may hold values from -0.125 to 0.125
- w_down: bfloat16 [9216, 2304], P('tp', 'ctx'), may hold values from -0.0625 to 0.0625
- norm_gains: bfloat16 [4, 2304], P(None, 'ctx'), may hold values from 0.25 to 1.75
- cotangent: bfloat16 [4096, 2304], P('ctx'), may hold values from -6 to 6
Outputs:
- layer_out: bfloat16 [4096, 2304], P('ctx')
- input_grad: float32 [4096, 2304], P('ctx')
- grad_query: float32 [2304, 2048], P('ctx', 'tp')
- grad_key: float32 [2304, 1024], P('ctx', 'tp')
- grad_value: float32 [2304, 1024], P('ctx', 'tp')
- grad_out: float32 [2048, 2304], P('tp', 'ctx')
- grad_gate: float32 [2304, 9216], P('ctx', 'tp')
- grad_up: float32 [2304, 9216], P('ctx', 'tp')
- grad_down: float32 [9216, 2304], P('tp', 'ctx')
- grad_gains: float32 [4, 2304], P(None, 'ctx')
Inputs may be any that keep to these rules, and one draw needn't show every extreme that they name: Every block number appears exactly once in block_map.
All inputs are finite; a program needn't handle non-finite values.
Results may differ from a plain program's by a relative error of at most 0.025.
Values may be sent and summed in bfloat16 or wider, within the bound.
No kernel may reach another device: no remote copies, remote signals or barrier semaphores. Data moves between devices by JAX's collectives and lax.ppermute only.
A program may use at most 192 MiB of HBM per device.

v0:
```python
from functools import partial

import jax
import jax.numpy as jnp
from jax import lax
from jax.sharding import PartitionSpec as P

HD = 256
WINDOW = 4096


epsilon = 1e-06
soft_cap = 50.0
masked_score = -1e30


def rms_scale(values):
    return lax.rsqrt(jnp.mean(values * values, axis=-1, keepdims=True) + epsilon)


def norm_back(values, row_scale, gain_row, gradient):
    normed = values * row_scale
    weighted = gradient * gain_row
    gain_grad = jnp.sum(gradient * normed, axis=0)
    value_grad = row_scale * (
        weighted - normed * jnp.mean(weighted * normed, axis=-1, keepdims=True)
    )
    return (value_grad, gain_grad)


def angle_tables(positions):
    half_dim = HD // 2
    frequency = jnp.power(10000.0, -2.0 * jnp.arange(half_dim, dtype=jnp.float32) / HD)
    phases = positions.astype(jnp.float32)[:, None] * frequency[None, :]
    phases = jnp.concatenate([phases, phases], axis=-1)
    return (jnp.cos(phases), jnp.sin(phases))


def rotate(values, cosine, sine_table):
    half_dim = values.shape[-1] // 2
    turned = jnp.concatenate([-values[..., half_dim:], values[..., :half_dim]], axis=-1)
    return values * cosine + turned * sine_table


def unrotate(gradient, cosine, sine_table):
    half_dim = gradient.shape[-1] // 2
    weighted = gradient * sine_table
    turned = jnp.concatenate([weighted[..., half_dim:], -weighted[..., :half_dim]], axis=-1)
    return gradient * cosine + turned


def visible(query_index, key_index, seq_len):
    same_seq = query_index[:, None] // seq_len == key_index[None, :] // seq_len
    distance = query_index[:, None] - key_index[None, :]
    return same_seq & (distance >= 0) & (distance < WINDOW)


def capped_scores(queries, key_rows):
    raw_scores = jnp.einsum("qhd,kd->hqk", queries, key_rows, preferred_element_type=jnp.float32)
    tangent = jnp.tanh(raw_scores / soft_cap)
    return (soft_cap * tangent, tangent)


def matmul(left, right):
    return jnp.dot(left, right, preferred_element_type=jnp.float32)


def body(
    tokens, block_map, w_query, w_key, w_value, w_out, w_gate, w_up, w_down, norm_gains, cotangent
):
    ctx_count = lax.axis_size("ctx")
    tok_dev = tokens.shape[0]
    block_rows = tok_dev // 2
    seq_count = max(1, ctx_count // 16)
    seq_len = tok_dev * ctx_count // seq_count
    dealt = block_map.reshape(-1)
    offsets = jnp.arange(block_rows, dtype=jnp.int32)
    all_index = (dealt[:, None] * block_rows + offsets[None, :]).reshape(ctx_count, tok_dev)
    own_index = lax.dynamic_index_in_dim(all_index, lax.axis_index("ctx"), 0, keepdims=False)
    cosine, sine_table = angle_tables(own_index % seq_len)
    head_cos = cosine[:, None, :]
    head_sin = sine_table[:, None, :]
    gathered = (
        lax.all_gather(w_query, "ctx", axis=0, tiled=True),
        lax.all_gather(w_key, "ctx", axis=0, tiled=True),
        lax.all_gather(w_value, "ctx", axis=0, tiled=True),
        lax.all_gather(w_out, "ctx", axis=1, tiled=True),
        lax.all_gather(w_gate, "ctx", axis=0, tiled=True),
        lax.all_gather(w_up, "ctx", axis=0, tiled=True),
        lax.all_gather(w_down, "ctx", axis=1, tiled=True),
        lax.all_gather(norm_gains, "ctx", axis=1, tiled=True),
    )
    full_query, full_key, full_value, full_out, full_gate, full_up, full_down, full_gains = gathered
    gains = full_gains.astype(jnp.float32)
    inputs = tokens.astype(jnp.float32)
    in_scale = rms_scale(inputs)
    normed_in = (inputs * in_scale * gains[0]).astype(jnp.bfloat16)
    heads_dev = full_query.shape[1] // HD
    query_raw = matmul(normed_in, full_query).reshape(tok_dev, heads_dev, HD)
    key_raw = matmul(normed_in, full_key)
    value_raw = matmul(normed_in, full_value)
    queries = (rotate(query_raw, head_cos, head_sin) * HD ** (-0.5)).astype(jnp.bfloat16)
    key_rows = rotate(key_raw, cosine, sine_table).astype(jnp.bfloat16)
    kv_local = jnp.concatenate([key_rows, value_raw.astype(jnp.bfloat16)], axis=-1)
    kv_all = lax.all_gather(kv_local, "ctx", axis=0, tiled=True)
    group = 1
    while group * 2 * tok_dev <= 1024 and ctx_count % (group * 2) == 0:
        group = group * 2
    steps_count = ctx_count // group
    step_rows = group * tok_dev
    kv_steps = kv_all.reshape(steps_count, step_rows, 2 * HD)
    index_steps = all_index.reshape(steps_count, step_rows)

    def first_pass(running, block_item):
        kv_block, key_index = block_item
        allowed = visible(own_index, key_index, seq_len)[None]

        def first_compute_block(current):
            row_top, row_total = current
            capped, _ = capped_scores(queries, kv_block[:, :HD])
            capped = jnp.where(allowed, capped, masked_score)
            new_top = jnp.maximum(row_top, jnp.max(capped, axis=-1))
            weights = jnp.where(allowed, jnp.exp(capped - new_top[..., None]), 0.0)
            return (new_top, row_total * jnp.exp(row_top - new_top) + jnp.sum(weights, axis=-1))

        return (
            lax.cond(jnp.any(allowed), first_compute_block, lambda unchanged: unchanged, running),
            None,
        )

    start_top = jnp.full((heads_dev, tok_dev), masked_score, jnp.float32)
    start_total = jnp.zeros((heads_dev, tok_dev), jnp.float32)
    (row_top, row_total), _ = lax.scan(
        first_pass, (start_top, start_total), (kv_steps, index_steps)
    )
    log_total = row_top + jnp.log(row_total)

    def block_probs(kv_block, allowed):
        capped, tangent = capped_scores(queries, kv_block[:, :HD])
        capped = jnp.where(allowed, capped, masked_score)
        probs = jnp.where(allowed, jnp.exp(capped - log_total[..., None]), 0.0)
        return (probs, tangent)

    def second_pass(accumulated, block_item):
        kv_block, key_index = block_item
        allowed = visible(own_index, key_index, seq_len)[None]

        def second_compute_block(partial_sum):
            probs, _ = block_probs(kv_block, allowed)
            prob_low = probs.astype(jnp.bfloat16)
            return partial_sum + jnp.einsum(
                "hqk,kd->qhd", prob_low, kv_block[:, HD:], preferred_element_type=jnp.float32
            )

        return (
            lax.cond(
                jnp.any(allowed), second_compute_block, lambda unchanged: unchanged, accumulated
            ),
            None,
        )

    attended, _ = lax.scan(
        second_pass, jnp.zeros((tok_dev, heads_dev, HD), jnp.float32), (kv_steps, index_steps)
    )
    attn_flat = attended.astype(jnp.bfloat16).reshape(tok_dev, heads_dev * HD)
    branch = lax.psum(matmul(attn_flat, full_out).astype(jnp.bfloat16), "tp").astype(jnp.float32)
    branch_scale = rms_scale(branch)
    residual = inputs + branch * branch_scale * gains[1]
    resid_scale = rms_scale(residual)
    normed_mid = (residual * resid_scale * gains[2]).astype(jnp.bfloat16)
    gate_pre = matmul(normed_mid, full_gate)
    up_pre = matmul(normed_mid, full_up)
    active, gelu_back = jax.vjp(partial(jax.nn.gelu, approximate=True), gate_pre)
    hidden = (active * up_pre).astype(jnp.bfloat16)
    mlp_out = lax.psum(matmul(hidden, full_down).astype(jnp.bfloat16), "tp").astype(jnp.float32)
    mlp_scale = rms_scale(mlp_out)
    result = (residual + mlp_out * mlp_scale * gains[3]).astype(jnp.bfloat16)
    out_grad = cotangent.astype(jnp.float32)
    mlp_grad, gain_four = norm_back(mlp_out, mlp_scale, gains[3], out_grad)
    mlp_low = mlp_grad.astype(jnp.bfloat16)
    back_gate, back_up, back_down = (full_gate, full_up, full_down)
    hidden_grad = matmul(mlp_low, back_down.T)
    down_grad = matmul(hidden.T, mlp_low)
    gate_low = gelu_back(hidden_grad * up_pre)[0].astype(jnp.bfloat16)
    up_low = (hidden_grad * active).astype(jnp.bfloat16)
    mid_grad = lax.psum(
        (matmul(gate_low, back_gate.T) + matmul(up_low, back_up.T)).astype(jnp.bfloat16), "tp"
    ).astype(jnp.float32)
    gate_grad = matmul(normed_mid.T, gate_low)
    up_grad = matmul(normed_mid.T, up_low)
    resid_part, gain_three = norm_back(residual, resid_scale, gains[2], mid_grad)
    resid_grad = out_grad + resid_part
    branch_grad, gain_two = norm_back(branch, branch_scale, gains[1], resid_grad)
    branch_low = branch_grad.astype(jnp.bfloat16)
    attn_grad = matmul(branch_low, full_out.T)
    out_weight_grad = matmul(attn_flat.T, branch_low)
    attn_grad_low = attn_grad.astype(jnp.bfloat16).reshape(tok_dev, heads_dev, HD)
    row_dot = jnp.sum(attn_grad_low.astype(jnp.float32) * attended, axis=-1).transpose(1, 0)

    def make_back():

        def back_pass(query_grad, block_item):
            kv_block, key_index = block_item
            allowed = visible(own_index, key_index, seq_len)[None]

            def back_compute_block(running_grad):
                probs, tangent = block_probs(kv_block, allowed)
                prob_grad = jnp.einsum(
                    "qhd,kd->hqk",
                    attn_grad_low,
                    kv_block[:, HD:],
                    preferred_element_type=jnp.float32,
                )
                score_low = (
                    probs * (prob_grad - row_dot[..., None]) * (1.0 - tangent * tangent)
                ).astype(jnp.bfloat16)
                new_grad = running_grad + jnp.einsum(
                    "hqk,kd->qhd", score_low, kv_block[:, :HD], preferred_element_type=jnp.float32
                )
                prob_low = probs.astype(jnp.bfloat16)
                value_part = jnp.einsum(
                    "hqk,qhd->kd", prob_low, attn_grad_low, preferred_element_type=jnp.float32
                )
                key_part = jnp.einsum(
                    "hqk,qhd->kd", score_low, queries, preferred_element_type=jnp.float32
                )
                return (new_grad, jnp.concatenate([key_part, value_part], axis=-1))

            def skip_block(running_grad):
                return (running_grad, jnp.zeros((kv_block.shape[0], 2 * HD), jnp.float32))

            return lax.cond(jnp.any(allowed), back_compute_block, skip_block, query_grad)

        return back_pass

    start_grad = jnp.zeros((tok_dev, heads_dev, HD), jnp.float32)
    query_grad, key_terms = lax.scan(make_back(), start_grad, (kv_steps, index_steps))
    kv_grad = lax.psum_scatter(
        key_terms.reshape(ctx_count * tok_dev, 2 * HD).astype(jnp.bfloat16),
        "ctx",
        scatter_dimension=0,
        tiled=True,
    ).astype(jnp.float32)
    key_low = unrotate(kv_grad[:, :HD], cosine, sine_table).astype(jnp.bfloat16)
    value_low = kv_grad[:, HD:].astype(jnp.bfloat16)
    query_low = (
        unrotate(query_grad * HD ** (-0.5), head_cos, head_sin)
        .astype(jnp.bfloat16)
        .reshape(tok_dev, heads_dev * HD)
    )
    in_part = (
        matmul(query_low, full_query.T)
        + matmul(key_low, full_key.T)
        + matmul(value_low, full_value.T)
    )
    in_grad = lax.psum(in_part.astype(jnp.bfloat16), "tp").astype(jnp.float32)
    query_wgrad = matmul(normed_in.T, query_low)
    key_wgrad = matmul(normed_in.T, key_low)
    value_wgrad = matmul(normed_in.T, value_low)
    input_part, gain_one = norm_back(inputs, in_scale, gains[0], in_grad)
    input_grad = resid_grad + input_part
    gain_grads = jnp.stack([gain_one, gain_two, gain_three, gain_four])
    shards = (
        lax.psum_scatter(
            query_wgrad.astype(jnp.bfloat16), "ctx", scatter_dimension=0, tiled=True
        ).astype(jnp.float32),
        lax.psum_scatter(
            key_wgrad.astype(jnp.bfloat16), "ctx", scatter_dimension=0, tiled=True
        ).astype(jnp.float32),
        lax.psum_scatter(
            value_wgrad.astype(jnp.bfloat16), "ctx", scatter_dimension=0, tiled=True
        ).astype(jnp.float32),
        lax.psum_scatter(
            out_weight_grad.astype(jnp.bfloat16), "ctx", scatter_dimension=1, tiled=True
        ).astype(jnp.float32),
        lax.psum_scatter(
            gate_grad.astype(jnp.bfloat16), "ctx", scatter_dimension=0, tiled=True
        ).astype(jnp.float32),
        lax.psum_scatter(
            up_grad.astype(jnp.bfloat16), "ctx", scatter_dimension=0, tiled=True
        ).astype(jnp.float32),
        lax.psum_scatter(
            down_grad.astype(jnp.bfloat16), "ctx", scatter_dimension=1, tiled=True
        ).astype(jnp.float32),
        lax.psum_scatter(
            gain_grads.astype(jnp.bfloat16), "ctx", scatter_dimension=1, tiled=True
        ).astype(jnp.float32),
    )
    (
        query_shard,
        key_shard,
        value_shard,
        out_shard,
        gate_shard,
        up_shard,
        down_shard,
        gains_shard,
    ) = shards
    return (
        result,
        input_grad,
        query_shard,
        key_shard,
        value_shard,
        out_shard,
        gate_shard,
        up_shard,
        down_shard,
        gains_shard,
    )


def solution(mesh):
    in_specs = (
        P("ctx", None),
        P(),
        P("ctx", "tp"),
        P("ctx", "tp"),
        P("ctx", "tp"),
        P("tp", "ctx"),
        P("ctx", "tp"),
        P("ctx", "tp"),
        P("tp", "ctx"),
        P(None, "ctx"),
        P("ctx", None),
    )
    out_specs = (
        P("ctx", None),
        P("ctx", None),
        P("ctx", "tp"),
        P("ctx", "tp"),
        P("ctx", "tp"),
        P("tp", "ctx"),
        P("ctx", "tp"),
        P("ctx", "tp"),
        P("tp", "ctx"),
        P(None, "ctx"),
    )
    return jax.shard_map(body, mesh=mesh, in_specs=in_specs, out_specs=out_specs, check_vma=False)
```

profile of v0, /device:TPU:0, one launch (start us, length us, event | category | flops | bytes accessed | tf_op | source)
XLA Modules:
  0.0 1467.8 jit_solution(16556221701772705968)
XLA Ops:
  9.4 10.6 all-gather
  23.5 13.2 all-gather.10.cloned.1.call-done
  42.7 20.0 %all-gather.12.cloned.1.call-done = bf16[2304,256]{1,0:T(8,128)(2,1)} async-done(((bf16[288,256]{1,0:T(8,128)(2,1)}), bf16[2304,256]{1,0:T(8,128)(2,1)}) %all-gather.12.cloned.1.call-update) | async-done | bytes 1179664 | tf_op jit(solution)/shard_map/all_gather | solution.py:86
  66.8 26.8 %all-gather.16.cloned.1.call-done = bf16[2304,512]{1,0:T(8,128)(2,1)} async-done(((bf16[288,512]{1,0:T(8,128)(2,1)}), bf16[2304,512]{1,0:T(8,128)(2,1)}) %all-gather.16.cloned.1.call-update) | async-done | bytes 2359312 | tf_op jit(solution)/shard_map/all_gather | solution.py:84
  98.4 35.0 %all-gather.14.cloned.1.call-done = bf16[4096,512]{0,1:T(8,128)(2,1)} async-done(((bf16[512,512]{0,1:T(8,128)(2,1)}), bf16[4096,512]{0,1:T(8,128)(2,1)}) %all-gather.14.cloned.1.call-update) | async-done | bytes 4194320 | tf_op jit(solution)/shard_map/all_gather | solution.py:105
  139.9 29.0 %while.49 = (s32[]{:T(128)}, f32[2,512]{1,0:T(2,128)S(1)}, f32[2,512]{1,0:T(2,128)S(1)}, s32[512,1]{0,1:T(1,128)S(1)}, s32[512]{0:T(512)S(1)}, /*index=5*/s32[51...) while((s32[]{:T(128)}, f32[2,512]{1,0:T(2,128)S(1)}, ...), condition=%wide.region_7.8_spmd, body=%wide.region_1.7_spmd.sunk | while | flops 551050752 | bytes 13194443 | solution.py:133
  170.0 37.2 %while.50 = (s32[]{:T(128)}, f32[512,2,256]{2,0,1:T(8,128)}, s32[512,1]{0,1:T(1,128)S(1)}, s32[512]{0:T(512)S(1)}, s32[512,1]{0,1:T(1,128)S(1)}, /*index=5*/s32[...) while((s32[]{:T(128)}, f32[512,2,256]{2,0,1:T(8,128)}, ...), condition=%wide.region_12.13_spmd, body=%wide.region_8.12_spmd.sunk | while | flops 1083987456 | bytes 6853803 | solution.py:162
  217.1 93.1 %all-reduce.5.cloned.1.call-done = bf16[512,2304]{1,0:T(8,128)(2,1)} async-done(((bf16[512,2304]{1,0:T(8,128)(2,1)}), bf16[512,2304]{1,0:T(8,128)(2,1)}) %all-reduce.5.cloned.1.call-update) | async-done | bytes 2359312 | tf_op jit(solution)/shard_map/psum | solution.py:166
  318.2 56.8 %all-gather.20.cloned.1.call-done = bf16[2304,2304]{1,0:T(8,128)(2,1)} async-done(((bf16[288,2304]{1,0:T(8,128)(2,1)}), bf16[2304,2304]{1,0:T(8,128)(2,1)}) %all-gather.20.cloned.1.call-update) | async-done | bytes 10616848 | tf_op jit(solution)/shard_map/all_gather | solution.py:88
  374.9 11.6 fusion.117
  386.6 54.1 %all-gather.22.cloned.1.call-done = bf16[2304,2304]{1,0:T(8,128)(2,1)} async-done(((bf16[288,2304]{1,0:T(8,128)(2,1)}), bf16[2304,2304]{1,0:T(8,128)(2,1)}) %all-gather.22.cloned.1.call-update) | async-done | bytes 10616848 | tf_op jit(solution)/shard_map/all_gather | solution.py:89
  440.7 12.8 multiply_convert_fusion.1
  453.5 52.9 %all-gather.24.cloned.1.call-done = bf16[2304,2304]{0,1:T(8,128)(2,1)} async-done(((bf16[2304,288]{0,1:T(8,128)(2,1)}), bf16[2304,2304]{0,1:T(8,128)(2,1)}) %all-gather.24.cloned.1.call-update) | async-done | bytes 10616848 | tf_op jit(solution)/shard_map/all_gather | solution.py:90
  506.4 11.3 convolution_convert_fusion.5
  518.0 95.6 %all-reduce.7.cloned.1.call-done = bf16[512,2304]{1,0:T(8,128)(2,1)} async-done(((bf16[512,2304]{1,0:T(8,128)(2,1)}), bf16[512,2304]{1,0:T(8,128)(2,1)}) %all-reduce.7.cloned.1.call-update) | async-done | bytes 2359312 | tf_op jit(solution)/shard_map/psum | solution.py:175
  620.5 15.9 %multiply_convert_fusion = (bf16[512,2304]{1,0:T(8,128)(2,1)}, bf16[512,2304]{1,0:T(8,128)(2,1)}) fusion(f32[512,2304]{1,0:T(8,128)} %fusion.117, f32[512,2304]{1,0:T(8,128)} %get-tuple-element.815, bf16[2304,2304]{0,1:T(8,128)(2,1)} %all-gather.24.cloned.1.call-done, bf16[512,2304]{1,0:T(8,128)(2,1)S(1)} %copy-done.10, ...), kind=kOutput, calls=%fused_computation.154 | convolution fusion | flops 5473566720 | bytes 29504512 | tf_op jit(solution)/shard_map/dot_general | solution.py:65
  645.0 12.0 fusion.83
  657.1 94.8 %all-reduce.9.cloned.1.call-done = bf16[512,2304]{1,0:T(8,128)(2,1)} async-done(((bf16[512,2304]{1,0:T(8,128)(2,1)}), bf16[512,2304]{1,0:T(8,128)(2,1)}) %all-reduce.9.cloned.1.call-update) | async-done | bytes 2359312 | tf_op jit(solution)/shard_map/psum | solution.py:186
  770.1 57.7 %while.51 = (s32[]{:T(128)}, f32[512,2,256]{2,0,1:T(8,128)}, bf16[4,1024,512]{1,2,0:T(8,128)(2,1)}, s32[512,1]{0,1:T(1,128)S(1)}, s32[512]{0:T(512)S(1)}, /*inde...) while((s32[]{:T(128)}, f32[512,2,256]{2,0,1:T(8,128)}, ...), condition=%wide.region_27.28_spmd, body=%wide.region_23.27_spmd.sunk | while | flops 2708231680 | bytes 48281448 | solution.py:237
  802.1 10.4 conditional.8
  816.4 10.4 conditional.8
  834.3 48.9 %reduce-scatter.12.cloned.1.call-done = bf16[512,512]{0,1:T(8,128)(2,1)} async-done(((bf16[4096,512]{0,1:T(8,128)(2,1)}), bf16[512,512]{0,1:T(8,128)(2,1)}) %reduce-scatter.12.cloned.1.call-update) | async-done | bytes 524304 | tf_op jit(solution)/shard_map/reduce_scatter | solution.py:238
  904.0 86.5 %all-reduce.11.cloned.1.call-done = bf16[512,2304]{1,0:T(8,128)(2,1)} async-done(((bf16[512,2304]{1,0:T(8,128)(2,1)}), bf16[512,2304]{1,0:T(8,128)(2,1)}) %all-reduce.11.cloned.1.call-update) | async-done | bytes 2359312 | tf_op jit(solution)/shard_map/psum | solution.py:256
  998.1 11.3 convolution_convert_fusion
  1020.0 10.4 convolution_convert_fusion.1
  1037.6 38.0 %reduce-scatter.16.cloned.1.call-done = bf16[288,256]{1,0:T(8,128)(2,1)} async-done(((bf16[2304,256]{1,0:T(8,128)(2,1)}), bf16[288,256]{1,0:T(8,128)(2,1)}) %reduce-scatter.16.cloned.1.call-update) | async-done | bytes 147472 | tf_op jit(solution)/shard_map/reduce_scatter | solution.py:267
  1077.2 38.6 %reduce-scatter.18.cloned.1.call-done = bf16[288,256]{1,0:T(8,128)(2,1)} async-done(((bf16[2304,256]{1,0:T(8,128)(2,1)}), bf16[288,256]{1,0:T(8,128)(2,1)}) %reduce-scatter.18.cloned.1.call-update) | async-done | bytes 147472 | tf_op jit(solution)/shard_map/reduce_scatter | solution.py:270
  1124.1 29.7 %reduce-scatter.28.cloned.1.call-done = bf16[288,4]{1,0:T(8,128)(2,1)} async-done(((bf16[2304,4]{1,0:T(8,128)(2,1)}), bf16[288,4]{1,0:T(8,128)(2,1)}) %reduce-scatter.28.cloned.1.call-update) | async-done | bytes 2320
  1155.4 44.2 %reduce-scatter.14.cloned.1.call-done = bf16[288,512]{1,0:T(8,128)(2,1)} async-done(((bf16[2304,512]{1,0:T(8,128)(2,1)}), bf16[288,512]{1,0:T(8,128)(2,1)}) %reduce-scatter.14.cloned.1.call-update) | async-done | bytes 294928 | tf_op jit(solution)/shard_map/reduce_scatter | solution.py:264
  1201.4 84.3 %reduce-scatter.26.cloned.1.call-done = bf16[2304,288]{0,1:T(8,128)(2,1)} async-done(((bf16[2304,2304]{0,1:T(8,128)(2,1)}), bf16[2304,288]{0,1:T(8,128)(2,1)}) %reduce-scatter.26.cloned.1.call-update) | async-done | bytes 1327120 | tf_op jit(solution)/shard_map/reduce_scatter | solution.py:282
  1288.6 83.0 %reduce-scatter.22.cloned.1.call-done = bf16[288,2304]{1,0:T(8,128)(2,1)} async-done(((bf16[2304,2304]{1,0:T(8,128)(2,1)}), bf16[288,2304]{1,0:T(8,128)(2,1)}) %reduce-scatter.22.cloned.1.call-update) | async-done | bytes 1327120 | tf_op jit(solution)/shard_map/reduce_scatter | solution.py:276
  1374.6 83.1 %reduce-scatter.24.cloned.1.call-done = bf16[288,2304]{1,0:T(8,128)(2,1)} async-done(((bf16[2304,2304]{1,0:T(8,128)(2,1)}), bf16[288,2304]{1,0:T(8,128)(2,1)}) %reduce-scatter.24.cloned.1.call-update) | async-done | bytes 1327120 | tf_op jit(solution)/shard_map/reduce_scatter | solution.py:279
  (366 shorter events, 335.4 us)
Async XLA Ops:
  7.2 29.5 %all-gather.10.cloned.1.call-start = ((), (), s32[]{:S(2)}) async-start(), calls=%async_computation.9 | async-start | bytes 1327104 | tf_op jit(solution)/shard_map/all_gather | solution.py:85
  7.9 54.8 %all-gather.12.cloned.1.call-start = ((), (), s32[]{:S(2)}) async-start(), calls=%async_computation.10 | async-start | bytes 1327104 | tf_op jit(solution)/shard_map/all_gather | solution.py:86
  8.7 84.9 %all-gather.16.cloned.1.call-start = ((), (), s32[]{:S(2)}) async-start(), calls=%async_computation.12 | async-start | bytes 2654208 | tf_op jit(solution)/shard_map/all_gather | solution.py:84
  9.4 124.0 %all-gather.14.cloned.1.call-start = ((), (), s32[]{:S(2)}) async-start(), calls=%async_computation.11 | async-start | bytes 4718592 | tf_op jit(solution)/shard_map/all_gather | solution.py:105
  21.2 72.4 %copy-start.25 = (f32[2304]{0:T(1024)}, f32[2304]{0:T(1024)S(1)}, u32[]{:S(2)}) copy-start(f32[2304]{0:T(1024)S(1)} %get-tuple-element.719) | copy-start | bytes 27652
  23.4 70.2 %copy-start.28 = (f32[512]{0:T(512)}, f32[512]{0:T(512)S(1)}, u32[]{:S(2)}) copy-start(f32[512]{0:T(512)S(1)} %add_rsqrt_fusion.3) | copy-start | bytes 6148
  23.5 19.1 %copy-start.13 = (f32[512,128]{0,1:T(8,128)}, f32[512,128]{0,1:T(8,128)S(1)}, u32[]{:S(2)}) copy-start(f32[512,128]{0,1:T(8,128)S(1)} %broadcast_multiply_fusion.3) | copy-start | bytes 786436
  36.7 26.0 %copy-start = (bf16[512,2304]{1,0:T(8,128)(2,1)S(1)}, bf16[512,2304]{1,0:T(8,128)(2,1)}, u32[]{:S(2)}) copy-start(bf16[512,2304]{1,0:T(8,128)(2,1)} %param.23) | copy-start | bytes 7077892
  65.8 143.9 %all-gather.18.cloned.1.call-start = ((), (), s32[]{:S(2)}) async-start(), calls=%async_computation.13 | async-start | bytes 2654208 | tf_op jit(solution)/shard_map/all_gather | solution.py:87
  66.4 243.8 %all-reduce.5.cloned.1.call-start = ((), (), s32[]{:S(2)}) async-start(), calls=%async_computation.14 | async-start | bytes 4718592 | tf_op jit(solution)/shard_map/psum | solution.py:166
  97.4 42.5 %copy-start.4 = (bf16[512,2,256]{0,2,1:T(8,128)(2,1)}, bf16[512,2,256]{0,2,1:T(8,128)(2,1)S(1)}, u32[]{:S(2)}) copy-start(bf16[512,2,256]{0,2,1:T(8,128)(2,1)S(1)} %fusion.86) | copy-start | bytes 1572868
  207.2 7.1 copy-start.30
  214.4 160.6 %all-gather.20.cloned.1.call-start = ((), (), s32[]{:S(2)}) async-start(), calls=%async_computation.15 | async-start | bytes 11943936 | tf_op jit(solution)/shard_map/all_gather | solution.py:88
  215.1 225.5 %all-gather.22.cloned.1.call-start = ((), (), s32[]{:S(2)}) async-start(), calls=%async_computation.16 | async-start | bytes 11943936 | tf_op jit(solution)/shard_map/all_gather | solution.py:89
  215.9 290.5 %all-gather.24.cloned.1.call-start = ((), (), s32[]{:S(2)}) async-start(), calls=%async_computation.17 | async-start | bytes 11943936 | tf_op jit(solution)/shard_map/all_gather | solution.py:90
  216.6 396.9 %all-reduce.7.cloned.1.call-start = ((), (), s32[]{:S(2)}) async-start(), calls=%async_computation.18 | async-start | bytes 4718592 | tf_op jit(solution)/shard_map/psum | solution.py:175
  517.7 234.2 %all-reduce.9.cloned.1.call-start = ((), (), s32[]{:S(2)}) async-start(), calls=%async_computation.19 | async-start | bytes 4718592 | tf_op jit(solution)/shard_map/psum | solution.py:186
  615.9 20.5 %slice-start = ((s8[10616832]{0:T(1024)(128)(4,1)}), s8[4194304]{0:T(1024)(128)(4,1)S(1)}, s32[]{:S(2)}) async-start(s8[10616832]{0:T(1024)(128)(4,1)} %bitcast.221), calls=%async_computation.30 | async-start | bytes 8388608
  620.5 15.9 %copy-start.32 = (f32[512]{0:T(512)}, f32[512]{0:T(512)S(1)}, u32[]{:S(2)}) copy-start(f32[512]{0:T(512)S(1)} %broadcast_multiply_fusion.7) | copy-start | bytes 6148
  620.5 15.9 %slice-start.1 = ((s8[10616832]{0:T(1024)(128)(4,1)}), s8[4194304]{0:T(1024)(128)(4,1)S(1)}, s32[]{:S(2)}) async-start(s8[10616832]{0:T(1024)(128)(4,1)} %bitcast.221), calls=%async_computation.31 | async-start | bytes 8388608
  620.5 15.9 %slice-start.2 = ((s8[10616832]{0:T(1024)(128)(4,1)}), s8[2228224]{0:T(1024)(128)(4,1)S(1)}, s32[]{:S(2)}) async-start(s8[10616832]{0:T(1024)(128)(4,1)} %bitcast.221), calls=%async_computation.32 | async-start | bytes 4456448
  657.1 226.1 %reduce-scatter.12.cloned.1.call-start = ((), (), s32[]{:S(2)}) async-start(), calls=%async_computation.20 | async-start | bytes 4718592 | tf_op jit(solution)/shard_map/reduce_scatter | solution.py:238
  832.7 157.9 %all-reduce.11.cloned.1.call-start = ((), (), s32[]{:S(2)}) async-start(), calls=%async_computation.21 | async-start | bytes 4718592 | tf_op jit(solution)/shard_map/psum | solution.py:256
  894.8 140.9 %reduce-scatter.20.cloned.1.call-start = ((), (), s32[]{:S(2)}) async-start(), calls=%async_computation.25 | async-start | bytes 2654208 | tf_op jit(solution)/shard_map/reduce_scatter | solution.py:273
  899.6 176.0 %reduce-scatter.16.cloned.1.call-start = ((), (), s32[]{:S(2)}) async-start(), calls=%async_computation.23 | async-start | bytes 1327104 | tf_op jit(solution)/shard_map/reduce_scatter | solution.py:267
  901.7 214.1 %reduce-scatter.18.cloned.1.call-start = ((), (), s32[]{:S(2)}) async-start(), calls=%async_computation.24 | async-start | bytes 1327104 | tf_op jit(solution)/shard_map/reduce_scatter | solution.py:270
  903.9 91.1 %copy-start.16 = (bf16[512,2,256]{0,2,1:T(8,128)(2,1)S(1)}, bf16[512,2,256]{0,2,1:T(8,128)(2,1)}, u32[]{:S(2)}) copy-start(bf16[512,2,256]{0,2,1:T(8,128)(2,1)} %copy-done.15) | copy-start | bytes 1572868
  903.9 249.8 %reduce-scatter.28.cloned.1.call-start = ((), (), s32[]{:S(2)}) async-start(), calls=%async_computation.29 | async-start | bytes 663552
  994.9 204.6 %reduce-scatter.14.cloned.1.call-start = ((), (), s32[]{:S(2)}) async-start(), calls=%async_computation.22 | async-start | bytes 2654208 | tf_op jit(solution)/shard_map/reduce_scatter | solution.py:264
  998.0 287.7 %reduce-scatter.26.cloned.1.call-start = ((), (), s32[]{:S(2)}) async-start(), calls=%async_computation.28 | async-start | bytes 11943936 | tf_op jit(solution)/shard_map/reduce_scatter | solution.py:282
  1009.4 362.3 %reduce-scatter.22.cloned.1.call-start = ((), (), s32[]{:S(2)}) async-start(), calls=%async_computation.26 | async-start | bytes 11943936 | tf_op jit(solution)/shard_map/reduce_scatter | solution.py:276
  1019.9 437.8 %reduce-scatter.24.cloned.1.call-start = ((), (), s32[]{:S(2)}) async-start(), calls=%async_computation.27 | async-start | bytes 11943936 | tf_op jit(solution)/shard_map/reduce_scatter | solution.py:279
  (43 other events, 125.6 us)
Sparse Core Ops, SparseCore 0:
  9.9 26.7 all-gather.9
  38.6 24.0 all-gather.11
  64.6 29.0 all-gather.15
  95.9 37.4 all-gather.13
  135.1 29.0 all-gather.17
  214.5 95.6 all-reduce.4
  312.1 62.8 all-gather.19
  376.8 63.8 all-gather.21
  442.6 63.8 all-gather.23
  517.9 95.6 all-reduce.6
  657.2 94.6 all-reduce.8
  832.8 50.3 reduce-scatter.11
  894.9 95.6 all-reduce.10
  994.1 41.5 reduce-scatter.19
  1038.8 36.7 reduce-scatter.15
  1079.0 36.7 reduce-scatter.17
  1119.4 34.3 reduce-scatter.27
  1157.0 42.5 reduce-scatter.13
  1203.4 82.1 reduce-scatter.25
  1289.4 82.1 reduce-scatter.21
  1375.5 82.1 reduce-scatter.23
where the time goes:
time: 1470 us
  waiting for transfers between devices  1090 us (74%)
  matrix products  196 us (13%)
  other arithmetic  98.2 us (7%)
  local copies, waits for them, and re-layouts  47.9 us (3%)
  between operations  15.2 us (1%)
    dot_general x21, matrix products, matmul(): return jnp.dot(left, right, preferred_element_type=jnp.float32)  136 us
    psum x1, waiting for transfers between devices, body(): lax.psum(matmul(hidden, full_down).astype(jnp.bfloat16), 'tp')  95.6 us
    psum x1, waiting for transfers between devices, body(): lax.psum((matmul(gate_low, back_gate.T) + matmul(up_low, back_up.T)).asty...  94.8 us
    psum x1, waiting for transfers between devices, body(): lax.psum(matmul(attn_flat, full_out).astype(jnp.bfloat16), 'tp')  93.1 us
    psum x1, waiting for transfers between devices, body(): in_grad = lax.psum(in_part.astype(jnp.bfloat16), 'tp').astype(jnp.float32)  86.5 us
    reduce_scatter x1, waiting for transfers between devices, body(): lax.psum_scatter(down_grad.astype(jnp.bfloat16), 'ctx', scatter_dimension...  84.3 us
    reduce_scatter x1, waiting for transfers between devices, body(): lax.psum_scatter(up_grad.astype(jnp.bfloat16), 'ctx', scatter_dimension=0...  83.1 us
    reduce_scatter x1, waiting for transfers between devices, body(): lax.psum_scatter(gate_grad.astype(jnp.bfloat16), 'ctx', scatter_dimension...  83 us
  transfers between devices with their start and end apart: 21, of which 20 were waited for; matrix products, arithmetic and copies ran while one was open for 13% of the time, Pallas kernels for 0%

commit v1 on v0

v1 whole, which is shorter than its diff:
```python
from functools import partial

import jax
import jax.numpy as jnp
from jax import lax
from jax.experimental import pallas as pl
from jax.experimental.pallas import tpu as pltpu
from jax.sharding import PartitionSpec as P

HD = 256
WINDOW = 4096


epsilon = 1e-06
soft_cap = 50.0
LOG2E = 1.4426950408889634


def rms_scale(values):
    return lax.rsqrt(jnp.mean(values * values, axis=-1, keepdims=True) + epsilon)


def norm_back(values, row_scale, gain_row, gradient):
    normed = values * row_scale
    weighted = gradient * gain_row
    gain_grad = jnp.sum(gradient * normed, axis=0)
    value_grad = row_scale * (
        weighted - normed * jnp.mean(weighted * normed, axis=-1, keepdims=True)
    )
    return (value_grad, gain_grad)


def angle_tables(positions):
    half_dim = HD // 2
    frequency = jnp.power(10000.0, -2.0 * jnp.arange(half_dim, dtype=jnp.float32) / HD)
    phases = positions.astype(jnp.float32)[:, None] * frequency[None, :]
    phases = jnp.concatenate([phases, phases], axis=-1)
    return (jnp.cos(phases), jnp.sin(phases))


def rotate(values, cosine, sine_table):
    half_dim = values.shape[-1] // 2
    turned = jnp.concatenate([-values[..., half_dim:], values[..., :half_dim]], axis=-1)
    return values * cosine + turned * sine_table


def unrotate(gradient, cosine, sine_table):
    half_dim = gradient.shape[-1] // 2
    weighted = gradient * sine_table
    turned = jnp.concatenate([weighted[..., half_dim:], -weighted[..., :half_dim]], axis=-1)
    return gradient * cosine + turned


def matmul(left, right):
    return jnp.dot(left, right, preferred_element_type=jnp.float32)


def matmul_nt(left, right):
    return lax.dot_general(left, right, (((1,), (1,)), ((), ())), preferred_element_type=jnp.float32)


def tie(value, *others):
    return lax.optimization_barrier((value,) + others)[0]


def block_lists(ids_ref, first, key_blocks, own, seq_blocks, reach, list_ref):
    def look(slot, count):
        other = ids_ref[first + slot]
        gap = own - other
        whole = (gap > 0) & (gap < reach) & (own // seq_blocks == other // seq_blocks)
        list_ref[count] = slot
        return count + whole.astype(jnp.int32)

    return lax.fori_loop(0, key_blocks, look, jnp.int32(0))


def find_block(ids_ref, first, key_blocks, wanted):
    def look(slot, found):
        return jnp.where(ids_ref[first + slot] == wanted, slot, found)

    return lax.fori_loop(0, key_blocks, look, jnp.int32(-1))


def attend_kernel(
    ids_ref, own_ref, q_ref, k_ref, v_ref, o_ref, l_ref, acc_ref, sum_ref, list_ref,
    *, blk, heads, key_blocks, seq_blocks, reach
):
    chunk = pl.program_id(0)
    first = chunk * key_blocks
    q_blocks = q_ref.shape[0] // blk

    @pl.when(chunk == 0)
    def _():
        acc_ref[...] = jnp.zeros_like(acc_ref)
        sum_ref[...] = jnp.zeros_like(sum_ref)

    def tile(b, slot, mask):
        rows = pl.ds(pl.multiple_of(slot * blk, blk), blk)
        keys = k_ref[rows, :]
        vals = v_ref[rows, :]
        for h in range(heads):
            query = q_ref[b * blk : (b + 1) * blk, h * HD : (h + 1) * HD]
            capped = jnp.tanh(matmul_nt(query, keys) * (1.0 / soft_cap))
            weights = jnp.exp2(capped * (soft_cap * LOG2E))
            if mask is not None:
                weights = jnp.where(mask, weights, 0.0)
            at = (slice(b * blk, (b + 1) * blk), slice(h * HD, (h + 1) * HD))
            lanes = (slice(b * blk, (b + 1) * blk), slice(h * 128, (h + 1) * 128))
            part = weights[:, :128]
            for piece in range(1, blk // 128):
                part = part + weights[:, piece * 128 : (piece + 1) * 128]
            sum_ref[lanes] += part
            acc_ref[at] += matmul(weights.astype(jnp.bfloat16), vals)

    row_no = lax.broadcasted_iota(jnp.int32, (blk, blk), 0)
    col_no = lax.broadcasted_iota(jnp.int32, (blk, blk), 1)
    for b in range(q_blocks):
        own = own_ref[b]
        count = block_lists(ids_ref, first, key_blocks, own, seq_blocks, reach, list_ref)

        def pair(step, carry):
            tile(b, list_ref[2 * step], None)
            tile(b, list_ref[2 * step + 1], None)
            return carry

        lax.fori_loop(0, count // 2, pair, 0)

        @pl.when(count % 2 == 1)
        def _():
            tile(b, list_ref[count - 1], None)

        diagonal = find_block(ids_ref, first, key_blocks, own)

        @pl.when(diagonal >= 0)
        def _():
            tile(b, diagonal, row_no >= col_no)

        if reach < seq_blocks:
            edge = find_block(ids_ref, first, key_blocks, own - reach)

            @pl.when((edge >= 0) & (own % seq_blocks >= reach))
            def _():
                tile(b, edge, row_no < col_no)

    @pl.when(chunk == pl.num_programs(0) - 1)
    def _():
        for b in range(q_blocks):
            for h in range(heads):
                at = (slice(b * blk, (b + 1) * blk), slice(h * HD, (h + 1) * HD))
                lanes = (slice(b * blk, (b + 1) * blk), slice(h * 128, (h + 1) * 128))
                total = jnp.sum(sum_ref[lanes], axis=-1, keepdims=True)
                o_ref[at] = acc_ref[at] / total
                l_ref[lanes] = jnp.broadcast_to(total, (blk, 128))


def attend(ids, own, queries, kv_all, blk, seq_blocks):
    rows, width = queries.shape
    heads = width // HD
    total = kv_all.shape[0]
    chunk_rows = min(total, 4096)
    kernel = partial(
        attend_kernel, blk=blk, heads=heads, key_blocks=chunk_rows // blk, seq_blocks=seq_blocks,
        reach=WINDOW // blk,
    )
    whole = lambda i, *_: (0, 0)
    return pl.pallas_call(
        kernel,
        out_shape=(
            jax.ShapeDtypeStruct((rows, width), jnp.float32),
            jax.ShapeDtypeStruct((rows, heads * 128), jnp.float32),
        ),
        grid_spec=pltpu.PrefetchScalarGridSpec(
            num_scalar_prefetch=2,
            grid=(total // chunk_rows,),
            in_specs=[
                pl.BlockSpec((rows, width), whole),
                pl.BlockSpec((chunk_rows, HD), lambda i, *_: (i, 0)),
                pl.BlockSpec((chunk_rows, HD), lambda i, *_: (i, 1)),
            ],
            out_specs=[
                pl.BlockSpec((rows, width), whole),
                pl.BlockSpec((rows, heads * 128), whole),
            ],
            scratch_shapes=[
                pltpu.VMEM((rows, width), jnp.float32),
                pltpu.VMEM((rows, heads * 128), jnp.float32),
                pltpu.SMEM((chunk_rows // blk + 1,), jnp.int32),
            ],
        ),
        compiler_params=pltpu.CompilerParams(vmem_limit_bytes=40 * 2**20),
        cost_estimate=pl.CostEstimate(
            flops=4 * rows * width * total, bytes_accessed=8 * rows * width + 4 * total * HD,
            transcendentals=2 * rows * heads * total,
        ),
        name="attend",
    )(ids, own, queries, kv_all, kv_all)


def attend_back_kernel(
    ids_ref, own_ref, q_ref, do_ref, lse_ref, delta_ref, k_ref, v_ref, kt_ref, dq_ref, dkv_ref,
    dqt_ref, dk_ref, dv_ref, list_ref, *, blk, heads, key_blocks, seq_blocks, reach
):
    chunk = pl.program_id(0)
    first = chunk * key_blocks
    q_blocks = q_ref.shape[0] // blk

    @pl.when(chunk == 0)
    def _():
        dqt_ref[...] = jnp.zeros_like(dqt_ref)

    dk_ref[...] = jnp.zeros_like(dk_ref)
    dv_ref[...] = jnp.zeros_like(dv_ref)

    def tile(b, slot, mask):
        start = pl.multiple_of(slot * blk, blk)
        rows = pl.ds(start, blk)
        keys = k_ref[rows, :]
        vals = v_ref[rows, :]
        turned = kt_ref[:, rows]
        cols = slice(b * blk, (b + 1) * blk)
        dk_part = None
        for h in range(heads):
            query = q_ref[cols, h * HD : (h + 1) * HD]
            out_grad = do_ref[cols, h * HD : (h + 1) * HD]
            tangent = jnp.tanh(matmul_nt(keys, query) * (1.0 / soft_cap))
            probs = jnp.exp2(tangent * (soft_cap * LOG2E) - lse_ref[h : h + 1, cols])
            if mask is not None:
                probs = jnp.where(mask, probs, 0.0)
            prob_grad = matmul_nt(vals, out_grad)
            score = (
                probs * (prob_grad - delta_ref[h : h + 1, cols]) * (1.0 - tangent * tangent)
            ).astype(jnp.bfloat16)
            dk_new = matmul(score, query)
            dv_new = matmul(probs.astype(jnp.bfloat16), out_grad)
            dk_part = dk_new if dk_part is None else dk_part + dk_new
            dv_part = dv_new if h == 0 else dv_part + dv_new
            dqt_ref[h * HD : (h + 1) * HD, cols] += matmul(turned, score)
        dk_ref[rows, :] += dk_part
        dv_ref[rows, :] += dv_part

    key_no = lax.broadcasted_iota(jnp.int32, (blk, blk), 0)
    query_no = lax.broadcasted_iota(jnp.int32, (blk, blk), 1)
    for b in range(q_blocks):
        own = own_ref[b]
        count = block_lists(ids_ref, first, key_blocks, own, seq_blocks, reach, list_ref)

        def pair(step, carry):
            tile(b, list_ref[2 * step], None)
            tile(b, list_ref[2 * step + 1], None)
            return carry

        lax.fori_loop(0, count // 2, pair, 0)

        @pl.when(count % 2 == 1)
        def _():
            tile(b, list_ref[count - 1], None)

        diagonal = find_block(ids_ref, first, key_blocks, own)

        @pl.when(diagonal >= 0)
        def _():
            tile(b, diagonal, query_no >= key_no)

        if reach < seq_blocks:
            edge = find_block(ids_ref, first, key_blocks, own - reach)

            @pl.when((edge >= 0) & (own % seq_blocks >= reach))
            def _():
                tile(b, edge, query_no < key_no)

    dkv_ref[:, :HD] = dk_ref[...].astype(jnp.bfloat16)
    dkv_ref[:, HD:] = dv_ref[...].astype(jnp.bfloat16)

    @pl.when(chunk == pl.num_programs(0) - 1)
    def _():
        for h in range(heads):
            dq_ref[:, h * HD : (h + 1) * HD] = dqt_ref[h * HD : (h + 1) * HD, :].T


def attend_back(ids, own, queries, out_grad, lse, delta, kv_all, key_turned, blk, seq_blocks):
    rows, width = queries.shape
    heads = width // HD
    total = kv_all.shape[0]
    chunk_rows = min(total, 4096)
    kernel = partial(
        attend_back_kernel, blk=blk, heads=heads, key_blocks=chunk_rows // blk,
        seq_blocks=seq_blocks, reach=WINDOW // blk,
    )
    whole = lambda i, *_: (0, 0)
    return pl.pallas_call(
        kernel,
        out_shape=(
            jax.ShapeDtypeStruct((rows, width), jnp.float32),
            jax.ShapeDtypeStruct((total, 2 * HD), jnp.bfloat16),
        ),
        grid_spec=pltpu.PrefetchScalarGridSpec(
            num_scalar_prefetch=2,
            grid=(total // chunk_rows,),
            in_specs=[
                pl.BlockSpec((rows, width), whole),
                pl.BlockSpec((rows, width), whole),
                pl.BlockSpec((heads, rows), whole),
                pl.BlockSpec((heads, rows), whole),
                pl.BlockSpec((chunk_rows, HD), lambda i, *_: (i, 0)),
                pl.BlockSpec((chunk_rows, HD), lambda i, *_: (i, 1)),
                pl.BlockSpec((HD, chunk_rows), lambda i, *_: (0, i)),
            ],
            out_specs=[
                pl.BlockSpec((rows, width), whole),
                pl.BlockSpec((chunk_rows, 2 * HD), lambda i, *_: (i, 0)),
            ],
            scratch_shapes=[
                pltpu.VMEM((width, rows), jnp.float32),
                pltpu.VMEM((chunk_rows, HD), jnp.float32),
                pltpu.VMEM((chunk_rows, HD), jnp.float32),
                pltpu.SMEM((chunk_rows // blk + 1,), jnp.int32),
            ],
        ),
        compiler_params=pltpu.CompilerParams(vmem_limit_bytes=56 * 2**20),
        cost_estimate=pl.CostEstimate(
            flops=10 * rows * width * total, bytes_accessed=8 * rows * width + 10 * total * HD,
            transcendentals=2 * rows * heads * total,
        ),
        name="attend_back",
    )(ids, own, queries, out_grad, lse, delta, kv_all, kv_all, key_turned)


def swap(value, bit):
    pairs = [(i, i ^ bit) for i in range(lax.axis_size("ctx"))]
    return lax.ppermute(value, "ctx", pairs)


def paired():
    return lax.axis_size("ctx") == 8


def gather_relative(piece):
    half = piece.shape[0] // 2
    by_x = swap(piece, 2)
    by_y = swap(piece, 4)
    corner = (swap(by_x[:half], 4), swap(by_y[half:], 2))
    column = jnp.concatenate([piece, by_x, by_y, *corner], axis=0)
    return column, swap(column, 1)


def slots():
    return (0, 2, 4, 6, 1, 3, 5, 7)


def gather_rows(piece):
    if not paired():
        return lax.all_gather(piece, "ctx", axis=0, tiled=True)
    me = lax.axis_index("ctx")
    rows = piece.shape[0]
    column, other = gather_relative(piece)
    full = jnp.zeros((8 * rows, piece.shape[1]), piece.dtype)
    for source, base in ((column, 0), (other, 1)):
        for place, bits in enumerate((0, 2, 4, 6)):
            block = source[place * rows : (place + 1) * rows]
            full = lax.dynamic_update_slice(full, block, ((me ^ (bits + base)) * rows, 0))
    return full


def scatter_quads(own, by_x, by_y, corner):
    half = own.shape[0] // 2
    from_x = swap(corner[:half], 2)
    from_y = swap(corner[half:], 4)
    by_y = jnp.concatenate([by_y[:half] + from_x, by_y[half:]], axis=0)
    by_x = jnp.concatenate([by_x[:half], by_x[half:] + from_y], axis=0)
    last_x = swap(by_x, 2)
    last_y = swap(by_y, 4)
    return (
        own.astype(jnp.float32) + last_x.astype(jnp.float32) + last_y.astype(jnp.float32)
    )


def scatter_rows(whole):
    if not paired():
        return lax.psum_scatter(whole, "ctx", scatter_dimension=0, tiled=True).astype(jnp.float32)
    me = lax.axis_index("ctx")
    chip, core = me // 2, me % 2
    rows = whole.shape[0] // 8
    blocks = whole.reshape(4, 2, rows, whole.shape[1])
    theirs = lax.dynamic_index_in_dim(blocks, 1 - core, 1, keepdims=False)
    mine = lax.dynamic_index_in_dim(blocks, core, 1, keepdims=False)
    mine = mine + swap(theirs, 1)
    pick = lambda bits: lax.dynamic_index_in_dim(mine, chip ^ bits, 0, keepdims=False)
    return scatter_quads(pick(0), pick(1), pick(2), pick(3))


def scatter_relative(whole):
    rows = whole.shape[0] // 8
    mine = whole[: 4 * rows] + swap(whole[4 * rows :], 1)
    return scatter_quads(*(mine[k * rows : (k + 1) * rows] for k in range(4)))


def gather_gains(piece):
    if not paired():
        return lax.all_gather(piece, "ctx", axis=1, tiled=True)
    me = lax.axis_index("ctx")
    stack = piece[None]
    for bit in (1, 2, 4):
        other = swap(stack, bit)
        low = (me & bit) == 0
        stack = jnp.where(
            low, jnp.concatenate([stack, other], axis=0), jnp.concatenate([other, stack], axis=0)
        )
    return stack.transpose(1, 0, 2).reshape(piece.shape[0], 8 * piece.shape[1])


def scatter_gains(whole):
    if not paired():
        return lax.psum_scatter(
            whole.astype(jnp.bfloat16), "ctx", scatter_dimension=1, tiled=True
        ).astype(jnp.float32)
    me = lax.axis_index("ctx")
    columns = whole.shape[1] // 8
    stack = whole.reshape(whole.shape[0], 8, columns).transpose(1, 0, 2)
    for bit in (4, 2, 1):
        half = stack.shape[0] // 2
        low = (me & bit) == 0
        theirs = jnp.where(low, stack[half:], stack[:half])
        mine = jnp.where(low, stack[:half], stack[half:])
        stack = mine + swap(theirs, bit)
    return stack[0]


def body(
    tokens, block_map, w_query, w_key, w_value, w_out, w_gate, w_up, w_down, norm_gains, cotangent
):
    ctx_count = lax.axis_size("ctx")
    tok_dev = tokens.shape[0]
    block_rows = tok_dev // 2
    seq_count = max(1, ctx_count // 16)
    seq_len = tok_dev * ctx_count // seq_count
    seq_blocks = seq_len // block_rows
    me = lax.axis_index("ctx")
    heads_dev = w_query.shape[1] // HD
    own_ids = lax.dynamic_index_in_dim(block_map, me, 0, keepdims=False)
    offsets = jnp.arange(block_rows, dtype=jnp.int32)
    own_index = (own_ids[:, None] * block_rows + offsets[None, :]).reshape(-1)
    cosine, sine_table = angle_tables(own_index % seq_len)
    head_cos = cosine[:, None, :]
    head_sin = sine_table[:, None, :]

    full_gains = gather_gains(norm_gains)
    gains = full_gains.astype(jnp.float32)
    full_qkv = gather_rows(jnp.concatenate([w_query, w_key, w_value], axis=1))
    q_width = heads_dev * HD
    inputs = tokens.astype(jnp.float32)
    in_scale = rms_scale(inputs)
    normed_in = (inputs * in_scale * gains[0]).astype(jnp.bfloat16)
    projected = matmul(normed_in, full_qkv)
    query_raw = projected[:, :q_width].reshape(tok_dev, heads_dev, HD)
    key_raw = projected[:, q_width : q_width + HD]
    value_raw = projected[:, q_width + HD :]
    queries = (rotate(query_raw, head_cos, head_sin) * HD ** (-0.5)).astype(jnp.bfloat16)
    queries = queries.reshape(tok_dev, q_width)
    key_rows = rotate(key_raw, cosine, sine_table).astype(jnp.bfloat16)
    kv_local = jnp.concatenate([key_rows, value_raw.astype(jnp.bfloat16)], axis=-1)

    w_out = tie(w_out, full_qkv)
    full_out_t = gather_rows(w_out.T)
    if paired():
        column, other = gather_relative(kv_local)
        kv_all = jnp.concatenate([column, other], axis=0)
        key_ids = jnp.concatenate(
            [lax.dynamic_index_in_dim(block_map, me ^ k, 0, keepdims=False) for k in slots()]
        )
    else:
        kv_all = lax.all_gather(kv_local, "ctx", axis=0, tiled=True)
        key_ids = block_map.reshape(-1)
    w_gate, w_up, w_down, kv_all = lax.optimization_barrier((w_gate, w_up, w_down, kv_all))
    full_gate = lax.all_gather(w_gate, "ctx", axis=0, tiled=True)
    full_up = gather_rows(w_up)
    full_down = lax.all_gather(w_down, "ctx", axis=1, tiled=True)

    attended, totals = attend(key_ids, own_ids, queries, kv_all, block_rows, seq_blocks)
    attn_flat = attended.astype(jnp.bfloat16)
    branch_part = matmul_nt(attn_flat, full_out_t).astype(jnp.bfloat16)
    branch = lax.psum(branch_part, "tp")
    branch, full_gate, full_up = lax.optimization_barrier((branch, full_gate, full_up))
    branch = branch.astype(jnp.float32)
    branch_scale = rms_scale(branch)
    residual = inputs + branch * branch_scale * gains[1]
    resid_scale = rms_scale(residual)
    normed_mid = (residual * resid_scale * gains[2]).astype(jnp.bfloat16)
    gate_pre = matmul(normed_mid, full_gate)
    up_pre = matmul(normed_mid, full_up)
    active, gelu_back = jax.vjp(partial(jax.nn.gelu, approximate=True), gate_pre)
    hidden = (active * up_pre).astype(jnp.bfloat16)
    mlp_out = lax.psum(matmul(hidden, full_down).astype(jnp.bfloat16), "tp").astype(jnp.float32)
    mlp_scale = rms_scale(mlp_out)
    result = (residual + mlp_out * mlp_scale * gains[3]).astype(jnp.bfloat16)
    out_grad = cotangent.astype(jnp.float32)
    mlp_grad, gain_four = norm_back(mlp_out, mlp_scale, gains[3], out_grad)
    mlp_low = mlp_grad.astype(jnp.bfloat16)
    hidden_grad = matmul(mlp_low, full_down.T)
    gate_low = gelu_back(hidden_grad * up_pre)[0].astype(jnp.bfloat16)
    up_low = (hidden_grad * active).astype(jnp.bfloat16)
    mid_part = (matmul(gate_low, full_gate.T) + matmul(up_low, full_up.T)).astype(jnp.bfloat16)
    mid_part, hidden_t, mlp_t, gate_t, up_t = lax.optimization_barrier(
        (mid_part, hidden, mlp_low, gate_low, up_low)
    )
    mid_sum = lax.psum(mid_part, "tp")
    down_grad = matmul(hidden_t.T, mlp_t).astype(jnp.bfloat16)
    down_shard = lax.psum_scatter(down_grad, "ctx", scatter_dimension=1, tiled=True)
    gate_grad = matmul(normed_mid.T, gate_t).astype(jnp.bfloat16)
    gate_shard = scatter_rows(gate_grad)
    up_grad = matmul(normed_mid.T, up_t).astype(jnp.bfloat16)
    key_turned = kv_all[:, :HD].T
    log_total = jnp.log2(totals.reshape(tok_dev, heads_dev, 128)[:, :, 0]).T
    mid_sum, up_grad, key_turned, gate_shard = lax.optimization_barrier(
        (mid_sum, up_grad, key_turned, gate_shard)
    )
    mid_grad = mid_sum.astype(jnp.float32)
    up_shard = lax.psum_scatter(up_grad, "ctx", scatter_dimension=0, tiled=True)
    resid_part, gain_three = norm_back(residual, resid_scale, gains[2], mid_grad)
    resid_grad = out_grad + resid_part
    branch_grad, gain_two = norm_back(branch, branch_scale, gains[1], resid_grad)
    branch_low = branch_grad.astype(jnp.bfloat16)
    attn_grad = matmul(branch_low, full_out_t)
    attn_grad_low = attn_grad.astype(jnp.bfloat16)
    row_dot = jnp.sum(
        (attn_grad_low.astype(jnp.float32) * attended).reshape(tok_dev, heads_dev, HD), axis=-1
    ).T
    query_grad, kv_terms = attend_back(
        key_ids, own_ids, queries, attn_grad_low, log_total, row_dot, kv_all, key_turned,
        block_rows, seq_blocks,
    )
    kv_terms, down_shard = lax.optimization_barrier((kv_terms, down_shard))
    down_shard = down_shard.astype(jnp.float32)
    if paired():
        kv_grad = scatter_relative(kv_terms)
    else:
        kv_grad = lax.psum_scatter(
            kv_terms, "ctx", scatter_dimension=0, tiled=True
        ).astype(jnp.float32)
    key_low = unrotate(kv_grad[:, :HD], cosine, sine_table).astype(jnp.bfloat16)
    value_low = kv_grad[:, HD:].astype(jnp.bfloat16)
    query_low = (
        unrotate(query_grad.reshape(tok_dev, heads_dev, HD) * HD ** (-0.5), head_cos, head_sin)
        .astype(jnp.bfloat16)
        .reshape(tok_dev, q_width)
    )
    qkv_low = jnp.concatenate([query_low, key_low, value_low], axis=1)
    in_part = matmul(qkv_low, full_qkv.T).astype(jnp.bfloat16)
    in_part, qkv_low, branch_t = lax.optimization_barrier((in_part, qkv_low, branch_low))
    in_sum = lax.psum(in_part, "tp")
    qkv_grad = matmul(normed_in.T, qkv_low).astype(jnp.bfloat16)
    qkv_shard = scatter_rows(qkv_grad)
    out_weight_grad = matmul(branch_t.T, attn_flat).astype(jnp.bfloat16)
    out_shard = scatter_rows(out_weight_grad)
    in_sum, out_shard, up_shard, qkv_shard = lax.optimization_barrier(
        (in_sum, out_shard, up_shard, qkv_shard)
    )
    in_grad = in_sum.astype(jnp.float32)
    input_part, gain_one = norm_back(inputs, in_scale, gains[0], in_grad)
    input_grad = resid_grad + input_part
    gain_grads = jnp.stack([gain_one, gain_two, gain_three, gain_four])
    gains_shard = scatter_gains(gain_grads)
    return (
        result,
        input_grad,
        qkv_shard[:, :q_width],
        qkv_shard[:, q_width : q_width + HD],
        qkv_shard[:, q_width + HD :],
        out_shard.T,
        gate_shard,
        up_shard.astype(jnp.float32),
        down_shard,
        gains_shard,
    )


def solution(mesh):
    in_specs = (
        P("ctx", None),
        P(),
        P("ctx", "tp"),
        P("ctx", "tp"),
        P("ctx", "tp"),
        P("tp", "ctx"),
        P("ctx", "tp"),
        P("ctx", "tp"),
        P("tp", "ctx"),
        P(None, "ctx"),
        P("ctx", None),
    )
    out_specs = (
        P("ctx", None),
        P("ctx", None),
        P("ctx", "tp"),
        P("ctx", "tp"),
        P("ctx", "tp"),
        P("tp", "ctx"),
        P("ctx", "tp"),
        P("ctx", "tp"),
        P("tp", "ctx"),
        P(None, "ctx"),
    )
    return jax.shard_map(body, mesh=mesh, in_specs=in_specs, out_specs=out_specs, check_vma=False)
```

time: 1470 us -> 847 us (0.58)
  waiting for transfers between devices: 1090 us -> 378 us
  local copies, waits for them, and re-layouts: 47.9 us -> 146 us
  matrix products: 196 us -> 112 us
  Pallas kernels: 0 us -> 43.2 us
  starting transfers between devices: 1.99 us -> 40.8 us
    reduce_scatter x8 -> x2, waiting for transfers between devices: 425 us -> 5.12 us  [the longest x1 5.11 us: body(): up_shard = lax.psum_scatter(up_grad, 'ctx', scatter_dimension=0, tiled=True)]
    psum x3, waiting for transfers between devices: 274 us -> 22.3 us  [the longest x1 22.3 us: body(): in_sum = lax.psum(in_part, 'tp')]
    all_gather x8 -> x2, waiting for transfers between devices: 259 us -> 31.6 us  [the longest x1 31.6 us: body(): full_down = lax.all_gather(w_down, 'ctx', axis=1, tiled=True)]
    ppermute x0 -> x46, waiting for transfers between devices: none -> 222 us  [swap(): return lax.ppermute(value, 'ctx', pairs)]
    dot_general x28 -> x1, matrix products: 60.3 us -> 4.5 us  [matmul_nt(): lax.dot_general(left, right, (((1,), (1,)), ((), ())), preferred_element_...]
    unnamed x78 -> x172, local copies, waits for them, and re-layouts: 5.74 us -> 50.1 us
    pallas_call x0 -> x2, Pallas kernels: none -> 43.2 us  [the longest x1 28.8 us: attend_back(): pl.pallas_call(kernel, out_shape=(jax.ShapeDtypeStruct((rows, width), jnp...]
    ppermute x0 -> x46, starting transfers between devices: none -> 40.3 us  [swap(): return lax.ppermute(value, 'ctx', pairs)]
  transfers between devices with their start and end apart: 21 -> 54, of which waited for: 20 -> 31; matrix products, arithmetic and copies ran while one was open for 13% -> 26% of each run, Pallas kernels for 0% -> 3%
where the time goes in v1:
time: 847 us; the launch traced here: 836 us
  waiting for transfers between devices  378 us (45%)
  local copies, waits for them, and re-layouts  146 us (17%)
  matrix products  112 us (13%)
  other arithmetic  97.9 us (12%)
  Pallas kernels  43.2 us (5%)
  starting transfers between devices  40.8 us (5%)
  between operations  17.2 us (2%)
    ppermute x46, waiting for transfers between devices, swap(): return lax.ppermute(value, 'ctx', pairs)  222 us
    dot_general x14, matrix products, matmul(): return jnp.dot(left, right, preferred_element_type=jnp.float32)  108 us
    psum x1, waiting for transfers between devices, body(): lax.psum(matmul(hidden, full_down).astype(jnp.bfloat16), 'tp')  95.7 us
    unnamed x172, local copies, waits for them, and re-layouts  50.1 us
    ppermute x46, starting transfers between devices, swap(): return lax.ppermute(value, 'ctx', pairs)  40.3 us
    all_gather x1, waiting for transfers between devices, body(): full_down = lax.all_gather(w_down, 'ctx', axis=1, tiled=True)  31.6 us
    pallas_call x1, Pallas kernels, attend_back(): pl.pallas_call(kernel, out_shape=(jax.ShapeDtypeStruct((rows, width), jnp...  28.8 us
    dynamic_update_slice x13, local copies, waits for them, and re-layouts, gather_rows(): full = lax.dynamic_update_slice(full, block, ((me ^ bits + base) * rows, 0))  25.3 us
  transfers between devices with their start and end apart: 54, of which 31 were waited for; matrix products, arithmetic and copies ran while one was open for 26% of the time, Pallas kernels for 3%

profile of v1, /device:TPU:0, one launch (start us, length us, event | category | flops | bytes accessed | tf_op | source)
XLA Modules:
  0.0 835.9 jit_solution(1729270803825981424)
XLA Ops:
  17.4 11.8 %collective-permute-done.3 = bf16[288,1024]{1,0:T(8,128)(2,1)S(1)} collective-permute-done((bf16[288,1024]{1,0:T(8,128)(2,1)S(1)}, bf16[288,1024]{1,0:T(8,128)(2,1)S(1)}, u32[]{:S(2)}, u32[]{:S(2)}) %collective-permute-start.3) | collective-permute-done | bytes 589856 | tf_op jit(solution)/shard_map/ppermute | solution.py:330
  136.8 6.5 copy.63.k_ref.v_ref
  145.5 14.5 %attend.1 = (f32[512,512]{1,0:T(8,128)S(1)}, f32[512,256]{1,0:T(8,128)S(1)}) custom-call(s32[16]{0:T(128)S(1)} %concatenate.105.ids_ref, s32[2]{0:T(128)S(1)} %get-tuple-element.88.own_ref, bf16[512,512]{1,0:T(8,128)(2,1)S(1)} %multiply_convert_fusion.3.q_ref, bf16[4096,512]{1,0:T(8,128)(2,1)S(1)} %copy-done, bf16[4096,512]{1,0:T(8,128)(2,1)S(1)} %copy-done), custom_call_target="tpu_custom_call" | custom-call | flops 4294967296 | bytes 6291456 | tf_op jit(solution)/shard_map/attend/pallas_call | solution.py:166
  173.3 37.1 %collective-permute-done.19 = bf16[288,2304]{1,0:T(8,128)(2,1)S(1)} collective-permute-done((bf16[288,2304]{1,0:T(8,128)(2,1)}, bf16[288,2304]{1,0:T(8,128)(2,1)S(1)}, u32[]{:S(2)}, u32[]{:S(2)}) %collective-permute-start.19) | collective-permute-done | bytes 1327136 | tf_op jit(solution)/shard_map/ppermute | solution.py:330
  216.7 22.4 %collective-permute-done.20 = bf16[144,2304]{1,0:T(8,128)(2,1)S(1)} collective-permute-done((bf16[144,2304]{1,0:T(8,128)(2,1)S(1)}, bf16[144,2304]{1,0:T(8,128)(2,1)S(1)}, u32[]{:S(2)}, u32[]{:S(2)}) %collective-permute-start.20) | collective-permute-done | bytes 663584 | tf_op jit(solution)/shard_map/ppermute | solution.py:330
  244.5 7.5 collective-permute-done.22
  270.1 5.6 fusion.81
  277.9 11.8 %multiply_convert_fusion.1 = (bf16[512,2304]{1,0:T(8,128)(2,1)S(1)}, f32[512,2304]{1,0:T(8,128)}) fusion(f32[512,2304]{1,0:T(8,128)S(1)} %fusion.81, bf16[512,2304]{1,0:T(8,128)(2,1)S(1)} %multiply_convert_fusion.2, bf16[2304,2304]{1,0:T(8,128)(2,1)} %slice_dynamic-update-slice_fusion), kind=kOutput, calls=%fused_computation.67 | convolution fusion | flops 5447614464 | bytes 24772608 | tf_op jit(solution)/shard_map/dot_general | solution.py:55
  289.7 31.6 %all-gather.5.cloned.1.call-done = bf16[2304,2304]{0,1:T(8,128)(2,1)} async-done(((bf16[2304,288]{0,1:T(8,128)(2,1)}), bf16[2304,2304]{0,1:T(8,128)(2,1)}) %all-gather.5.cloned.1.call-update) | async-done | bytes 10616848 | tf_op jit(solution)/shard_map/all_gather | solution.py:476
  321.3 11.0 %convolution_convert_fusion.6 = bf16[512,2304]{1,0:T(8,128)(2,1)} fusion(bf16[512,2304]{1,0:T(8,128)(2,1)S(1)} %get-tuple-element.57, bf16[2304,2304]{0,1:T(8,128)(2,1)} %all-gather.5.cloned.1.call-done), kind=kOutput, calls=%fused_computation.72 | convolution fusion | flops 5436997632 | bytes 15335424 | tf_op jit(solution)/shard_map/dot_general | solution.py:55
  332.4 95.7 %all-reduce.7.cloned.1.call-done = bf16[512,2304]{1,0:T(8,128)(2,1)} async-done(((bf16[512,2304]{1,0:T(8,128)(2,1)}), bf16[512,2304]{1,0:T(8,128)(2,1)}) %all-reduce.7.cloned.1.call-update) | async-done | bytes 2359312 | tf_op jit(solution)/shard_map/psum | solution.py:492
  435.9 13.4 %multiply_convert_fusion = (bf16[512,2304]{1,0:T(8,128)(2,1)S(1)}, bf16[512,2304]{1,0:T(8,128)(2,1)S(1)}) fusion(f32[512,2304]{1,0:T(8,128)S(1)} %bitcast.150, f32[512,2304]{1,0:T(8,128)} %get-tuple-element.168, bf16[512,2304]{1,0:T(8,128)(2,1)S(1)} %fusion.16, bf16[2304,2304]{0,1:T(8,128)(2,1)} %all-gather.5.cloned.1.call-done), kind=kOutput, calls=%fused_computation.66 | convolution fusion | flops 5464129536 | bytes 27131904 | tf_op jit(solution)/shard_map/dot_general | solution.py:55
  449.3 7.4 fusion.82
  456.7 11.9 %fusion.44 = bf16[512,2304]{1,0:T(8,128)(2,1)} fusion(f32[512,2304]{1,0:T(8,128)} %fusion.82, bf16[512,2304]{1,0:T(8,128)(2,1)S(1)} %get-tuple-element.50, bf16[2304,2304]{1,0:T(8,128)(2,1)} %slice_dynamic-update-slice_fusion), kind=kOutput, calls=%fused_computation.74 | convolution fusion | flops 5438177280 | bytes 20054016 | tf_op jit(solution)/shard_map/dot_general | solution.py:55
  468.7 8.0 convolution_convert_fusion.1
  483.6 8.4 %convolution_convert_fusion = bf16[2304,2304]{0,1:T(8,128)(2,1)} fusion(bf16[512,2304]{1,0:T(8,128)(2,1)S(1)} %copy-done.66, bf16[512,2304]{1,0:T(8,128)(2,1)S(1)} %copy-done.32), kind=kOutput, calls=%fused_computation | convolution fusion | flops 5441126400 | bytes 15335424 | tf_op jit(solution)/shard_map/dot_general | solution.py:55
  492.7 4.8 bitcast_add_fusion
  504.2 10.4 %collective-permute-done.24 = bf16[144,2304]{1,0:T(8,128)(2,1)S(1)} collective-permute-done((bf16[144,2304]{1,0:T(8,128)(2,1)S(1)}, bf16[144,2304]{1,0:T(8,128)(2,1)S(1)}, u32[]{:S(2)}, u32[]{:S(2)}) %collective-permute-start.24) | collective-permute-done | bytes 663584 | tf_op jit(solution)/shard_map/ppermute | solution.py:330
  521.1 8.4 %convolution_convert_fusion.2 = bf16[2304,2304]{1,0:T(8,128)(2,1)} fusion(bf16[512,2304]{1,0:T(8,128)(2,1)S(1)} %copy-done.34, bf16[512,2304]{1,0:T(8,128)(2,1)S(1)} %copy-done.64), kind=kOutput, calls=%fused_computation.2 | convolution fusion | flops 5441126400 | bytes 15335424 | tf_op jit(solution)/shard_map/dot_general | solution.py:55
  529.5 46.5 %collective-permute-done.27 = bf16[288,2304]{1,0:T(8,128)(2,1)} collective-permute-done((bf16[288,2304]{1,0:T(8,128)(2,1)}, bf16[288,2304]{1,0:T(8,128)(2,1)}, u32[]{:S(2)}, u32[]{:S(2)}) %collective-permute-start.27) | collective-permute-done | bytes 1327136 | tf_op jit(solution)/shard_map/ppermute | solution.py:330
  586.5 6.9 fusion.25
  595.6 5.1 convert_multiply_fusion.11
  607.8 28.8 %attend_back.1 = (f32[512,512]{1,0:T(8,128)}, bf16[4096,512]{1,0:T(8,128)(2,1)}) custom-call(s32[16]{0:T(128)} %copy-done.3, s32[2]{0:T(128)} %copy-done.2, bf16[512,512]{1,0:T(8,128)(2,1)} %copy-done.1, bf16[512,512]{1,0:T(8,128)(2,1)} %get-tuple-element.170.do_ref, f32[2,512]{1,0:T(2,128)} %fusion.65.lse_ref, f32[2,512]{1,0:T(2,128)} %bitcast.144, ...), custom_call_target="tpu_custom_call" | custom-call | flops 10737418240 | bytes 12582912 | tf_op jit(solution)/shard_map/attend_back/pallas_call | solution.py:290
  636.5 6.4 copy.73
  649.6 8.3 collective-permute-done.31
  664.4 7.8 collective-permute-done.32
  699.2 6.6 convolution_convert_fusion.5
  716.5 4.8 collective-permute-done.33
  742.7 33.6 %collective-permute-done.35 = bf16[288,512]{1,0:T(8,128)(2,1)} collective-permute-done((bf16[288,512]{1,0:T(8,128)(2,1)S(1)}, bf16[288,512]{1,0:T(8,128)(2,1)}, u32[]{:S(2)}, u32[]{:S(2)}) %collective-permute-start.35) | collective-permute-done | bytes 294944 | tf_op jit(solution)/shard_map/ppermute | solution.py:330
  781.2 22.3 %all-reduce.11.cloned.1.call-done = bf16[512,2304]{1,0:T(8,128)(2,1)} async-done(((bf16[512,2304]{1,0:T(8,128)(2,1)}), bf16[512,2304]{1,0:T(8,128)(2,1)}) %all-reduce.11.cloned.1.call-update) | async-done | bytes 2359312 | tf_op jit(solution)/shard_map/psum | solution.py:549
  803.5 5.1 reduce-scatter.5.cloned.1.call-done
  817.3 6.6 fusion.18
  (424 shorter events, 301.6 us)
Async XLA Ops:
  8.0 254.0 %all-reduce.5.cloned.1.call-start = ((), (), s32[]{:S(2)}) async-start(), calls=%async_computation.2 | async-start | bytes 4718592 | tf_op jit(solution)/shard_map/psum | solution.py:481
  13.0 16.3 %collective-permute-start.3 = (bf16[288,1024]{1,0:T(8,128)(2,1)S(1)}, bf16[288,1024]{1,0:T(8,128)(2,1)S(1)}, u32[]{:S(2)}, u32[]{:S(2)}) collective-permute-start(bf16[288,1024]{1,0:T(8,128)(2,1)S(1)} %get-tuple-element.164), channel_id=1, source_target_pairs={{0,8},{4,12},{8,0},{12,4},{16,24},{20,28},{24,16},{28,20},{1,9},{5... | collective-permute-start | bytes 1769480 | tf_op jit(solution)/shard_map/ppermute | solution.py:330
  15.9 19.5 %collective-permute-start.4 = (bf16[288,1024]{1,0:T(8,128)(2,1)S(1)}, bf16[288,1024]{1,0:T(8,128)(2,1)}, u32[]{:S(2)}, u32[]{:S(2)}) collective-permute-start(bf16[288,1024]{1,0:T(8,128)(2,1)S(1)} %get-tuple-element.164), channel_id=1, source_target_pairs={{0,16},{4,20},{8,24},{12,28},{16,0},{20,4},{24,8},{28,12},{1,17},{... | collective-permute-start | bytes 1769480 | tf_op jit(solution)/shard_map/ppermute | solution.py:330
  30.0 12.5 %collective-permute-start.5 = (bf16[144,1024]{1,0:T(8,128)(2,1)}, bf16[144,1024]{1,0:T(8,128)(2,1)}, u32[]{:S(2)}, u32[]{:S(2)}) collective-permute-start(bf16[144,1024]{1,0:T(8,128)(2,1)} %slice.406), channel_id=1, source_target_pairs={{0,16},{4,20},{8,24},{12,28},{16,0},{20,4},{24,8},{28,12},{1,17},{... | collective-permute-start | bytes 884744 | tf_op jit(solution)/shard_map/ppermute | solution.py:330
  45.0 13.7 %collective-permute-start.7 = (bf16[1152,1024]{1,0:T(8,128)(2,1)}, bf16[1152,1024]{1,0:T(8,128)(2,1)}, u32[]{:S(2)}, u32[]{:S(2)}) collective-permute-start(bf16[1152,1024]{1,0:T(8,128)(2,1)} %constant_dynamic-update-slice_fusion.3), channel_id=1, source_target_pairs={{0,4},{4,0},{8,12},{12,8},{16,20},{20,16},{24,28},{28,24},{1,5},{5... | collective-permute-start | bytes 7077896 | tf_op jit(solution)/shard_map/ppermute | solution.py:330
  66.4 25.6 %collective-permute-start.13 = (bf16[288,512]{1,0:T(8,128)(2,1)}, bf16[288,512]{1,0:T(8,128)(2,1)}, u32[]{:S(2)}, u32[]{:S(2)}) collective-permute-start(bf16[288,512]{1,0:T(8,128)(2,1)} %bitcast.2), channel_id=1, source_target_pairs={{0,8},{4,12},{8,0},{12,4},{16,24},{20,28},{24,16},{28,20},{1,9},{5... | collective-permute-start | bytes 884744 | tf_op jit(solution)/shard_map/ppermute | solution.py:330
  67.9 25.6 %collective-permute-start.14 = (bf16[288,512]{1,0:T(8,128)(2,1)}, bf16[288,512]{1,0:T(8,128)(2,1)}, u32[]{:S(2)}, u32[]{:S(2)}) collective-permute-start(bf16[288,512]{1,0:T(8,128)(2,1)} %bitcast.2), channel_id=1, source_target_pairs={{0,16},{4,20},{8,24},{12,28},{16,0},{20,4},{24,8},{28,12},{1,17},{... | collective-permute-start | bytes 884744 | tf_op jit(solution)/shard_map/ppermute | solution.py:330
  86.6 16.3 %collective-permute-start.8 = (bf16[512,512]{0,1:T(8,128)(2,1)S(1)}, bf16[512,512]{0,1:T(8,128)(2,1)S(1)}, u32[]{:S(2)}, u32[]{:S(2)}) collective-permute-start(bf16[512,512]{0,1:T(8,128)(2,1)S(1)} %get-tuple-element.143), channel_id=1, source_target_pairs={{0,8},{4,12},{8,0},{12,4},{16,24},{20,28},{24,16},{28,20},{1,9},{5... | collective-permute-start | bytes 1572872 | tf_op jit(solution)/shard_map/ppermute | solution.py:330
  87.2 17.2 %collective-permute-start.9 = (bf16[512,512]{0,1:T(8,128)(2,1)S(1)}, bf16[512,512]{0,1:T(8,128)(2,1)S(1)}, u32[]{:S(2)}, u32[]{:S(2)}) collective-permute-start(bf16[512,512]{0,1:T(8,128)(2,1)S(1)} %get-tuple-element.143), channel_id=1, source_target_pairs={{0,16},{4,20},{8,24},{12,28},{16,0},{20,4},{24,8},{28,12},{1,17},{... | collective-permute-start | bytes 1572872 | tf_op jit(solution)/shard_map/ppermute | solution.py:330
  102.8 24.0 %collective-permute-start.17 = (bf16[1152,512]{1,0:T(8,128)(2,1)}, bf16[1152,512]{1,0:T(8,128)(2,1)}, u32[]{:S(2)}, u32[]{:S(2)}) collective-permute-start(bf16[1152,512]{1,0:T(8,128)(2,1)} %constant_dynamic-update-slice_fusion.21), channel_id=1, source_target_pairs={{0,4},{4,0},{8,12},{12,8},{16,20},{20,16},{24,28},{28,24},{1,5},{5... | collective-permute-start | bytes 3538952 | tf_op jit(solution)/shard_map/ppermute | solution.py:330
  113.8 19.8 %collective-permute-start.12 = (bf16[2048,512]{0,1:T(8,128)(2,1)}, bf16[2048,512]{0,1:T(8,128)(2,1)}, u32[]{:S(2)}, u32[]{:S(2)}) collective-permute-start(bf16[2048,512]{0,1:T(8,128)(2,1)} %get-tuple-element.156), channel_id=1, source_target_pairs={{0,4},{4,0},{8,12},{12,8},{16,20},{20,16},{24,28},{28,24},{1,5},{5... | collective-permute-start | bytes 6291464 | tf_op jit(solution)/shard_map/ppermute | solution.py:330
  165.5 96.5 %all-gather.3.cloned.1.call-start = ((), (), s32[]{:S(2)}) async-start(), calls=%async_computation.3 | async-start | bytes 11943936 | tf_op jit(solution)/shard_map/all_gather | solution.py:474
  166.1 155.2 %all-gather.5.cloned.1.call-start = ((), (), s32[]{:S(2)}) async-start(), calls=%async_computation.4 | async-start | bytes 11943936 | tf_op jit(solution)/shard_map/all_gather | solution.py:476
  166.7 261.4 %all-reduce.7.cloned.1.call-start = ((), (), s32[]{:S(2)}) async-start(), calls=%async_computation.5 | async-start | bytes 4718592 | tf_op jit(solution)/shard_map/psum | solution.py:492
  166.7 43.7 %collective-permute-start.19 = (bf16[288,2304]{1,0:T(8,128)(2,1)}, bf16[288,2304]{1,0:T(8,128)(2,1)S(1)}, u32[]{:S(2)}, u32[]{:S(2)}) collective-permute-start(bf16[288,2304]{1,0:T(8,128)(2,1)} %param.18), channel_id=1, source_target_pairs={{0,16},{4,20},{8,24},{12,28},{16,0},{20,4},{24,8},{28,12},{1,17},{... | collective-permute-start | bytes 3981320 | tf_op jit(solution)/shard_map/ppermute | solution.py:330
  166.8 43.7 %collective-permute-start.18 = (bf16[288,2304]{1,0:T(8,128)(2,1)}, bf16[288,2304]{1,0:T(8,128)(2,1)S(1)}, u32[]{:S(2)}, u32[]{:S(2)}) collective-permute-start(bf16[288,2304]{1,0:T(8,128)(2,1)} %param.18), channel_id=1, source_target_pairs={{0,8},{4,12},{8,0},{12,4},{16,24},{20,28},{24,16},{28,20},{1,9},{5... | collective-permute-start | bytes 3981320 | tf_op jit(solution)/shard_map/ppermute | solution.py:330
  210.4 29.6 %collective-permute-start.21 = (bf16[144,2304]{1,0:T(8,128)(2,1)S(1)}, bf16[144,2304]{1,0:T(8,128)(2,1)S(1)}, u32[]{:S(2)}, u32[]{:S(2)}) collective-permute-start(bf16[144,2304]{1,0:T(8,128)(2,1)S(1)} %slice.428), channel_id=1, source_target_pairs={{0,8},{4,12},{8,0},{12,4},{16,24},{20,28},{24,16},{28,20},{1,9},{5... | collective-permute-start | bytes 1990664 | tf_op jit(solution)/shard_map/ppermute | solution.py:330
  210.6 28.5 %collective-permute-start.20 = (bf16[144,2304]{1,0:T(8,128)(2,1)S(1)}, bf16[144,2304]{1,0:T(8,128)(2,1)S(1)}, u32[]{:S(2)}, u32[]{:S(2)}) collective-permute-start(bf16[144,2304]{1,0:T(8,128)(2,1)S(1)} %slice.427), channel_id=1, source_target_pairs={{0,16},{4,20},{8,24},{12,28},{16,0},{20,4},{24,8},{28,12},{1,17},{... | collective-permute-start | bytes 1990664 | tf_op jit(solution)/shard_map/ppermute | solution.py:330
  332.3 248.8 %all-reduce.9.cloned.1.call-start = ((), (), s32[]{:S(2)}) async-start(), calls=%async_computation.6 | async-start | bytes 4718592 | tf_op jit(solution)/shard_map/psum | solution.py:505
  468.6 168.0 %reduce-scatter.3.cloned.1.call-start = ((), (), s32[]{:S(2)}) async-start(), calls=%async_computation.7 | async-start | bytes 11943936 | tf_op jit(solution)/shard_map/reduce_scatter | solution.py:507
  492.0 311.5 %all-reduce.11.cloned.1.call-start = ((), (), s32[]{:S(2)}) async-start(), calls=%async_computation.8 | async-start | bytes 4718592 | tf_op jit(solution)/shard_map/psum | solution.py:549
  497.7 16.9 %collective-permute-start.24 = (bf16[144,2304]{1,0:T(8,128)(2,1)S(1)}, bf16[144,2304]{1,0:T(8,128)(2,1)S(1)}, u32[]{:S(2)}, u32[]{:S(2)}) collective-permute-start(bf16[144,2304]{1,0:T(8,128)(2,1)S(1)} %get-tuple-element.94), channel_id=1, source_target_pairs={{0,16},{4,20},{8,24},{12,28},{16,0},{20,4},{24,8},{28,12},{1,17},{... | collective-permute-start | bytes 1990664 | tf_op jit(solution)/shard_map/ppermute | solution.py:330
  499.1 16.7 %collective-permute-start.26 = (bf16[144,2304]{1,0:T(8,128)(2,1)S(1)}, bf16[144,2304]{1,0:T(8,128)(2,1)S(1)}, u32[]{:S(2)}, u32[]{:S(2)}) collective-permute-start(bf16[144,2304]{1,0:T(8,128)(2,1)S(1)} %get-tuple-element.96), channel_id=1, source_target_pairs={{0,8},{4,12},{8,0},{12,4},{16,24},{20,28},{24,16},{28,20},{1,9},{5... | collective-permute-start | bytes 1990664 | tf_op jit(solution)/shard_map/ppermute | solution.py:330
  517.3 58.8 %collective-permute-start.27 = (bf16[288,2304]{1,0:T(8,128)(2,1)}, bf16[288,2304]{1,0:T(8,128)(2,1)}, u32[]{:S(2)}, u32[]{:S(2)}) collective-permute-start(bf16[288,2304]{1,0:T(8,128)(2,1)} %pad_maximum_fusion.1), channel_id=1, source_target_pairs={{0,16},{4,20},{8,24},{12,28},{16,0},{20,4},{24,8},{28,12},{1,17},{... | collective-permute-start | bytes 3981320 | tf_op jit(solution)/shard_map/ppermute | solution.py:330
  519.0 57.9 %collective-permute-start.25 = (bf16[288,2304]{1,0:T(8,128)(2,1)}, bf16[288,2304]{1,0:T(8,128)(2,1)}, u32[]{:S(2)}, u32[]{:S(2)}) collective-permute-start(bf16[288,2304]{1,0:T(8,128)(2,1)} %pad_maximum_fusion), channel_id=1, source_target_pairs={{0,8},{4,12},{8,0},{12,4},{16,24},{20,28},{24,16},{28,20},{1,9},{5... | collective-permute-start | bytes 3981320 | tf_op jit(solution)/shard_map/ppermute | solution.py:330
  658.8 13.5 %collective-permute-start.32 = (bf16[512,512]{0,1:T(8,128)(2,1)}, bf16[512,512]{0,1:T(8,128)(2,1)}, u32[]{:S(2)}, u32[]{:S(2)}) collective-permute-start(bf16[512,512]{0,1:T(8,128)(2,1)} %pad_maximum_fusion.9), channel_id=1, source_target_pairs={{0,16},{4,20},{8,24},{12,28},{16,0},{20,4},{24,8},{28,12},{1,17},{... | collective-permute-start | bytes 1572872 | tf_op jit(solution)/shard_map/ppermute | solution.py:330
  659.9 13.5 %collective-permute-start.30 = (bf16[512,512]{0,1:T(8,128)(2,1)}, bf16[512,512]{0,1:T(8,128)(2,1)}, u32[]{:S(2)}, u32[]{:S(2)}) collective-permute-start(bf16[512,512]{0,1:T(8,128)(2,1)} %pad_maximum_fusion.8), channel_id=1, source_target_pairs={{0,8},{4,12},{8,0},{12,4},{16,24},{20,28},{24,16},{28,20},{1,9},{5... | collective-permute-start | bytes 1572872 | tf_op jit(solution)/shard_map/ppermute | solution.py:330
  708.1 100.5 %reduce-scatter.5.cloned.1.call-start = ((), (), s32[]{:S(2)}) async-start(), calls=%async_computation.9 | async-start | bytes 11943936 | tf_op jit(solution)/shard_map/reduce_scatter | solution.py:517
  730.6 12.1 %collective-permute-start.37 = (bf16[288,512]{1,0:T(8,128)(2,1)}, bf16[288,512]{1,0:T(8,128)(2,1)}, u32[]{:S(2)}, u32[]{:S(2)}) collective-permute-start(bf16[288,512]{1,0:T(8,128)(2,1)} %pad_maximum_fusion.11), channel_id=1, source_target_pairs={{0,16},{4,20},{8,24},{12,28},{16,0},{20,4},{24,8},{28,12},{1,17},{... | collective-permute-start | bytes 884744 | tf_op jit(solution)/shard_map/ppermute | solution.py:330
  735.3 43.2 %collective-permute-start.42 = (bf16[288,1024]{1,0:T(8,128)(2,1)S(1)}, bf16[288,1024]{1,0:T(8,128)(2,1)}, u32[]{:S(2)}, u32[]{:S(2)}) collective-permute-start(bf16[288,1024]{1,0:T(8,128)(2,1)S(1)} %pad_maximum_fusion.5), channel_id=1, source_target_pairs={{0,16},{4,20},{8,24},{12,28},{16,0},{20,4},{24,8},{28,12},{1,17},{... | collective-permute-start | bytes 1769480 | tf_op jit(solution)/shard_map/ppermute | solution.py:330
  737.3 41.2 %collective-permute-start.40 = (bf16[288,1024]{1,0:T(8,128)(2,1)}, bf16[288,1024]{1,0:T(8,128)(2,1)}, u32[]{:S(2)}, u32[]{:S(2)}) collective-permute-start(bf16[288,1024]{1,0:T(8,128)(2,1)} %pad_maximum_fusion.4), channel_id=1, source_target_pairs={{0,8},{4,12},{8,0},{12,4},{16,24},{20,28},{24,16},{28,20},{1,9},{5... | collective-permute-start | bytes 1769480 | tf_op jit(solution)/shard_map/ppermute | solution.py:330
  738.6 37.7 %collective-permute-start.35 = (bf16[288,512]{1,0:T(8,128)(2,1)S(1)}, bf16[288,512]{1,0:T(8,128)(2,1)}, u32[]{:S(2)}, u32[]{:S(2)}) collective-permute-start(bf16[288,512]{1,0:T(8,128)(2,1)S(1)} %pad_maximum_fusion.10), channel_id=1, source_target_pairs={{0,8},{4,12},{8,0},{12,4},{16,24},{20,28},{24,16},{28,20},{1,9},{5... | collective-permute-start | bytes 884744 | tf_op jit(solution)/shard_map/ppermute | solution.py:330
  (96 other events, 1180.5 us)
Sparse Core Ops, SparseCore 0:
  165.6 95.0 all-reduce.4
  332.4 95.6 all-reduce.6
  468.7 94.6 all-reduce.8
  708.2 95.2 all-reduce.10
Sparse Core Ops, SparseCore 1:
  167.8 87.4 all-gather.2
  257.1 64.1 all-gather.4
  492.1 108.5 reduce-scatter.2
  712.4 96.2 reduce-scatter.4

commit v2 on v1

v2 whole, which is shorter than its diff:
```python
from functools import partial

import jax
import jax.numpy as jnp
from jax import lax
from jax.experimental import pallas as pl
from jax.experimental.pallas import tpu as pltpu
from jax.sharding import PartitionSpec as P

HD = 256
HALF = 128
WINDOW = 4096
KEY_CHUNK = 4096


epsilon = 1e-06
soft_cap = 50.0
LOG2E = 1.4426950408889634


def rms_scale(values):
    return lax.rsqrt(jnp.mean(values * values, axis=-1, keepdims=True) + epsilon)


def angle_tables(positions):
    frequency = jnp.power(10000.0, -2.0 * jnp.arange(HALF, dtype=jnp.float32) / HD)
    phases = positions.astype(jnp.float32)[:, None] * frequency[None, :]
    return (jnp.cos(phases), jnp.sin(phases))


def matmul(left, right):
    return jnp.dot(left, right, preferred_element_type=jnp.float32)


def matmul_nt(left, right):
    return lax.dot_general(left, right, (((1,), (1,)), ((), ())), preferred_element_type=jnp.float32)


def tie(value, *others):
    return lax.optimization_barrier((value,) + others)[0]


def call(kernel, out_shape, args, name, scalars=0, scratch=(), flops=0, mem=60, space=None):
    spec = pl.BlockSpec(memory_space=pltpu.VMEM if space is None else space)
    outs = jax.tree.map(lambda _: spec, out_shape)
    size = sum(a.size * a.dtype.itemsize for a in args)
    size += sum(a.size * a.dtype.itemsize for a in jax.tree.leaves(out_shape))
    return pl.pallas_call(
        kernel,
        out_shape=out_shape,
        in_specs=[pl.BlockSpec(memory_space=pltpu.SMEM)] * scalars + [spec] * (len(args) - scalars),
        out_specs=outs,
        scratch_shapes=list(scratch),
        compiler_params=pltpu.CompilerParams(vmem_limit_bytes=mem * 2**20),
        cost_estimate=pl.CostEstimate(flops=flops, bytes_accessed=size, transcendentals=0),
        name=name,
    )(*args)


def swap(value, bit):
    pairs = [(i, i ^ bit) for i in range(lax.axis_size("ctx"))]
    return lax.ppermute(value, "ctx", pairs)


def paired():
    return lax.axis_size("ctx") == 8


def nearby(piece):
    return swap(piece, 2), swap(piece, 4)


def gather_pieces(piece, near=None):
    half = piece.shape[0] // 2
    by_x, by_y = nearby(piece) if near is None else near
    mine = (piece, by_x, by_y, swap(by_x[:half], 4), swap(by_y[half:], 2))
    return mine + tuple(swap(part, 1) for part in mine)


def piece_rows(rows):
    me = lax.axis_index("ctx")
    places = [(me ^ bit) * rows for bit in (0, 2, 4, 6, 6, 1, 3, 5, 7, 7)]
    shift = [0, 0, 0, 0, rows // 2] * 2
    return jnp.stack(places).astype(jnp.int32) + jnp.array(shift, jnp.int32)


def assemble_kernel(rows_ref, *refs):
    *pieces, whole, sems = refs
    copies = []
    for k, piece in enumerate(pieces):
        first = pl.multiple_of(rows_ref[k], 16)
        copy = pltpu.make_async_copy(piece, whole.at[pl.ds(first, piece.shape[0])], sems.at[k])
        copy.start()
        copies.append(copy)
    for copy in copies:
        copy.wait()


def assemble(pieces):
    rows, width = pieces[0].shape
    shape = jax.ShapeDtypeStruct((8 * rows, width), pieces[0].dtype)
    return call(
        assemble_kernel, shape, (piece_rows(rows), *pieces), "assemble", scalars=1,
        scratch=[pltpu.SemaphoreType.DMA((len(pieces),))], space=pl.ANY,
    )


def scatter_corner(own, by_x, by_y, corner):
    half = own.shape[0] // 2
    from_x = swap(corner[:half], 2)
    from_y = swap(corner[half:], 4)
    by_y = jnp.concatenate([by_y[:half] + from_x, by_y[half:]], axis=0)
    by_x = jnp.concatenate([by_x[:half], by_x[half:] + from_y], axis=0)
    return own, by_x, by_y


def scatter_start(whole):
    if not paired():
        return (lax.psum_scatter(whole, "ctx", scatter_dimension=0, tiled=True),)
    me = lax.axis_index("ctx")
    chip, core = me // 2, me % 2
    rows = whole.shape[0] // 8
    blocks = whole.reshape(4, 2, rows, whole.shape[1])
    theirs = lax.dynamic_index_in_dim(blocks, 1 - core, 1, keepdims=False)
    mine = lax.dynamic_index_in_dim(blocks, core, 1, keepdims=False)
    mine = mine + swap(theirs, 1)
    pick = lambda bits: lax.dynamic_index_in_dim(mine, chip ^ bits, 0, keepdims=False)
    return scatter_corner(pick(0), pick(1), pick(2), pick(3))


def scatter_finish(blocks):
    if len(blocks) == 1:
        return blocks
    own, by_x, by_y = blocks
    return own, swap(by_x, 2), swap(by_y, 4)


def add_terms(terms):
    total = terms[0].astype(jnp.float32)
    for term in terms[1:]:
        total = total + term.astype(jnp.float32)
    return total


def gather_gains(piece):
    if not paired():
        return lax.all_gather(piece, "ctx", axis=1, tiled=True)
    me = lax.axis_index("ctx")

    def ordered(bit, mine, other):
        low = (me & bit) == 0
        return jnp.concatenate([jnp.where(low, mine, other), jnp.where(low, other, mine)], axis=0)

    chip = ordered(1, piece[None], swap(piece[None], 1))
    row = ordered(2, chip, swap(chip, 2))
    stack = ordered(4, row, ordered(2, swap(chip, 4), swap(chip, 6)))
    return stack.transpose(1, 0, 2).reshape(piece.shape[0], 8 * piece.shape[1])


def scatter_gains(whole):
    if not paired():
        return lax.psum_scatter(whole, "ctx", scatter_dimension=1, tiled=True)
    me = lax.axis_index("ctx")
    columns = whole.shape[1] // 8
    stack = whole.reshape(whole.shape[0], 8, columns).transpose(1, 0, 2)
    for bit in (4, 2, 1):
        half = stack.shape[0] // 2
        low = (me & bit) == 0
        theirs = jnp.where(low, stack[half:], stack[:half])
        mine = jnp.where(low, stack[:half], stack[half:])
        stack = mine + swap(theirs, bit)
    return stack[0]


def sum_small_tp(value):
    count = lax.axis_size("tp")
    bit = 1
    while bit < count:
        value = value + lax.ppermute(value, "tp", [(i, i ^ bit) for i in range(count)])
        bit *= 2
    return value


def pack_kernel(a_ref, b_ref, c_ref, out_ref):
    one, two = a_ref.shape[1], a_ref.shape[1] + b_ref.shape[1]
    out_ref[:, :one] = a_ref[...]
    out_ref[:, one:two] = b_ref[...]
    out_ref[:, two:] = c_ref[...]


def pack(first, second, third):
    width = first.shape[1] + second.shape[1] + third.shape[1]
    shape = jax.ShapeDtypeStruct((first.shape[0], width), first.dtype)
    return call(pack_kernel, shape, (first, second, third), "pack")


def place(rows_ref, pieces, whole_ref):
    for k, piece in enumerate(pieces):
        whole_ref[pl.ds(pl.multiple_of(rows_ref[k], 16), piece.shape[0]), :] = piece[...]


def project_kernel(rows_ref, in_ref, cos_ref, sin_ref, *refs, heads, parts):
    pieces, (q_ref, kv_ref) = refs[:parts], refs[parts : parts + 2]
    if parts > 1:
        full_ref = refs[parts + 2]
        place(rows_ref, pieces, full_ref)
    else:
        full_ref = pieces[0]
    for n in range(heads + 2):
        raw = matmul(in_ref[...], full_ref[:, n * HD : (n + 1) * HD])
        if n <= heads:
            low, high = raw[:, :HALF], raw[:, HALF:]
            cosine, sine = cos_ref[...], sin_ref[...]
            low, high = low * cosine - high * sine, high * cosine + low * sine
            if n < heads:
                q_ref[:, n * HD : n * HD + HALF] = (low * HD ** (-0.5)).astype(jnp.bfloat16)
                q_ref[:, n * HD + HALF : (n + 1) * HD] = (high * HD ** (-0.5)).astype(jnp.bfloat16)
            else:
                kv_ref[:, :HALF] = low.astype(jnp.bfloat16)
                kv_ref[:, HALF:HD] = high.astype(jnp.bfloat16)
        else:
            kv_ref[:, HD:] = raw.astype(jnp.bfloat16)


def project(normed, cosine, sine, pieces, heads):
    rows, depth = normed.shape
    width = pieces[0].shape[1]
    low = lambda n: jax.ShapeDtypeStruct((rows, n), jnp.bfloat16)
    shapes = [low(heads * HD), low(2 * HD)]
    if len(pieces) > 1:
        shapes.append(jax.ShapeDtypeStruct((depth, width), jnp.bfloat16))
        places = piece_rows(pieces[0].shape[0])
    else:
        places = jnp.zeros((1,), jnp.int32)
    found = call(
        partial(project_kernel, heads=heads, parts=len(pieces)), tuple(shapes),
        (places, normed, cosine, sine, *pieces), "project", scalars=1,
        flops=2 * rows * depth * width,
    )
    return found if len(pieces) > 1 else (*found, pieces[0])


def out_project_kernel(rows_ref, attn_ref, *refs, parts):
    pieces, branch_ref = refs[:parts], refs[parts]
    if parts > 1:
        full_ref = refs[parts + 1]
        place(rows_ref, pieces, full_ref)
    else:
        full_ref = pieces[0]
    for n in range(0, branch_ref.shape[1], 256):
        part = matmul_nt(attn_ref[...], full_ref[n : n + 256, :])
        branch_ref[:, n : n + 256] = part.astype(jnp.bfloat16)


def out_project(attn, pieces, depth):
    rows, width = attn.shape
    shapes = [jax.ShapeDtypeStruct((rows, depth), jnp.bfloat16)]
    if len(pieces) > 1:
        shapes.append(jax.ShapeDtypeStruct((depth, width), jnp.bfloat16))
        places = piece_rows(pieces[0].shape[0])
    else:
        places = jnp.zeros((1,), jnp.int32)
    found = call(
        partial(out_project_kernel, parts=len(pieces)), tuple(shapes), (places, attn, *pieces),
        "out_project", scalars=1, flops=2 * rows * depth * width,
    )
    return found if len(pieces) > 1 else (*found, pieces[0])


def join_kernel(cos_ref, sin_ref, query_ref, full_ref, *refs):
    *terms, low_ref, part_ref = refs
    total = terms[0][...].astype(jnp.float32)
    for term in terms[1:]:
        total = total + term[...].astype(jnp.float32)
    width = query_ref.shape[1]
    cosine, sine = cos_ref[...], sin_ref[...]
    low, high = total[:, :HALF], total[:, HALF:HD]
    low_ref[:, :width] = query_ref[...]
    low_ref[:, width : width + HALF] = (low * cosine + high * sine).astype(jnp.bfloat16)
    low_ref[:, width + HALF : width + HD] = (high * cosine - low * sine).astype(jnp.bfloat16)
    low_ref[:, width + HD :] = total[:, HD:].astype(jnp.bfloat16)
    for n in range(0, part_ref.shape[1], 256):
        part = matmul_nt(low_ref[...], full_ref[n : n + 256, :])
        part_ref[:, n : n + 256] = part.astype(jnp.bfloat16)


def join(cosine, sine, query_low, full_qkv, terms):
    rows = query_low.shape[0]
    depth, width = full_qkv.shape
    low = lambda n: jax.ShapeDtypeStruct((rows, n), jnp.bfloat16)
    return call(
        join_kernel, (low(width), low(depth)), (cosine, sine, query_low, full_qkv, *terms), "join",
        flops=2 * rows * depth * width,
    )


GROUP = 16


def rms_of(values):
    return lax.rsqrt(jnp.mean(values * values, axis=-1, keepdims=True) + epsilon)


def norm_back(normed, scale, weighted):
    return scale * (weighted - normed * jnp.mean(weighted * normed, axis=-1, keepdims=True))


def fold(values):
    total = values[:8]
    for row in range(8, values.shape[0], 8):
        total = total + values[row : row + 8]
    return total


def wide(ref, rows):
    return ref[rows, :].astype(jnp.float32)


def walk(count, step):
    def run(index, carry):
        step(pl.ds(pl.multiple_of(index * GROUP, GROUP), GROUP))
        return carry

    lax.fori_loop(0, count // GROUP, run, 0, unroll=2)


def mid_kernel(tok_ref, branch_ref, gains_ref, out_ref):
    def step(rows):
        branch = wide(branch_ref, rows)
        residual = wide(tok_ref, rows) + branch * rms_of(branch) * gains_ref[1:2, :]
        out_ref[rows, :] = (residual * rms_of(residual) * gains_ref[2:3, :]).astype(jnp.bfloat16)

    walk(tok_ref.shape[0], step)


def top_kernel(tok_ref, branch_ref, mlp_ref, cot_ref, gains_ref, out_ref, grad_ref, sum_ref, acc_ref):
    @pl.when(pl.program_id(0) == 0)
    def _():
        acc_ref[...] = jnp.zeros_like(acc_ref)

    def step(rows):
        branch = wide(branch_ref, rows)
        residual = wide(tok_ref, rows) + branch * rms_of(branch) * gains_ref[1:2, :]
        mlp = wide(mlp_ref, rows)
        scale = rms_of(mlp)
        normed = mlp * scale
        out_ref[rows, :] = (residual + normed * gains_ref[3:4, :]).astype(jnp.bfloat16)
        out_grad = wide(cot_ref, rows)
        acc_ref[...] += fold(out_grad * normed)
        grad_ref[rows, :] = norm_back(normed, scale, out_grad * gains_ref[3:4, :]).astype(jnp.bfloat16)

    walk(tok_ref.shape[0], step)

    @pl.when(pl.program_id(0) == pl.num_programs(0) - 1)
    def _():
        sum_ref[...] = jnp.sum(acc_ref[...], axis=0, keepdims=True)


def low_kernel(
    tok_ref, branch_ref, mid_ref, cot_ref, gains_ref, resid_ref, grad_ref, sum_ref, acc_ref
):
    @pl.when(pl.program_id(0) == 0)
    def _():
        acc_ref[...] = jnp.zeros_like(acc_ref)

    def step(rows):
        branch = wide(branch_ref, rows)
        branch_scale = rms_of(branch)
        branch_normed = branch * branch_scale
        residual = wide(tok_ref, rows) + branch_normed * gains_ref[1:2, :]
        scale = rms_of(residual)
        normed = residual * scale
        mid_grad = wide(mid_ref, rows)
        acc_ref[:8, :] += fold(mid_grad * normed)
        grad = wide(cot_ref, rows) + norm_back(normed, scale, mid_grad * gains_ref[2:3, :])
        resid_ref[rows, :] = grad
        acc_ref[8:, :] += fold(grad * branch_normed)
        grad_ref[rows, :] = norm_back(
            branch_normed, branch_scale, grad * gains_ref[1:2, :]
        ).astype(jnp.bfloat16)

    walk(tok_ref.shape[0], step)

    @pl.when(pl.program_id(0) == pl.num_programs(0) - 1)
    def _():
        sum_ref[0:1, :] = jnp.sum(acc_ref[:8, :], axis=0, keepdims=True)
        sum_ref[1:2, :] = jnp.sum(acc_ref[8:, :], axis=0, keepdims=True)


def end_kernel(tok_ref, sum_ref, resid_ref, gains_ref, out_ref):
    def step(rows):
        values = wide(tok_ref, rows)
        scale = rms_of(values)
        weighted = wide(sum_ref, rows) * gains_ref[0:1, :]
        out_ref[rows, :] = resid_ref[rows, :] + norm_back(values * scale, scale, weighted)

    walk(tok_ref.shape[0], step)


def by_rows(kernel, args, gains, kinds, sums, name, block=128):
    rows, depth = args[0].shape
    tile = pl.BlockSpec((block, depth), lambda i: (i, 0))
    whole = lambda n: pl.BlockSpec((n, depth), lambda i: (0, 0))
    shapes = [jax.ShapeDtypeStruct((rows, depth), kind) for kind in kinds]
    out_specs = [tile] * len(kinds)
    scratch = []
    if sums:
        shapes.append(jax.ShapeDtypeStruct((sums, depth), jnp.float32))
        out_specs.append(whole(sums))
        scratch.append(pltpu.VMEM((8 * sums, depth), jnp.float32))
    size = sum(a.size * a.dtype.itemsize for a in (*args, *shapes))
    found = pl.pallas_call(
        kernel,
        out_shape=tuple(shapes),
        grid=(rows // block,),
        in_specs=[tile] * len(args) + [whole(gains.shape[0])],
        out_specs=out_specs,
        scratch_shapes=scratch,
        compiler_params=pltpu.CompilerParams(vmem_limit_bytes=60 * 2**20),
        cost_estimate=pl.CostEstimate(flops=0, bytes_accessed=size, transcendentals=0),
        name=name,
    )(*args, gains)
    return found if len(found) > 1 else found[0]


UNITS = 256


def units_kernel(in_ref, gate_ref, up_ref, hidden_ref, active_ref, slope_ref):
    gate = matmul(in_ref[...], gate_ref[...])
    up = matmul(in_ref[...], up_ref[...])
    root = (2.0 / jnp.pi) ** 0.5
    square = gate * gate
    bend = jnp.tanh(root * gate * (1.0 + 0.044715 * square))
    half = 0.5 * (1.0 + bend)
    active = gate * half
    slope = half + 0.5 * gate * (1.0 - bend * bend) * (root * (1.0 + 3 * 0.044715 * square))
    hidden_ref[...] = (active * up).astype(jnp.bfloat16)
    active_ref[...] = active.astype(jnp.bfloat16)
    slope_ref[...] = (slope * up).astype(jnp.bfloat16)


def units(normed, full_gate, full_up):
    rows, depth = normed.shape
    count = full_gate.shape[1]
    column = lambda n: pl.BlockSpec((n, UNITS), lambda i: (0, i))
    return pl.pallas_call(
        units_kernel,
        out_shape=tuple(jax.ShapeDtypeStruct((rows, count), jnp.bfloat16) for _ in range(3)),
        grid=(count // UNITS,),
        in_specs=[pl.BlockSpec((rows, depth), lambda i: (0, 0)), column(depth), column(depth)],
        out_specs=[column(rows)] * 3,
        compiler_params=pltpu.CompilerParams(vmem_limit_bytes=60 * 2**20),
        cost_estimate=pl.CostEstimate(
            flops=4 * rows * depth * count, bytes_accessed=4 * depth * count,
            transcendentals=rows * count,
        ),
        name="units",
    )(normed, full_gate, full_up)


def down_kernel(hidden_ref, down_ref, out_ref):
    out_ref[...] = matmul_nt(hidden_ref[...], down_ref[...]).astype(jnp.bfloat16)


def project_down(hidden, full_down_t):
    rows, count = hidden.shape
    depth = full_down_t.shape[0]
    return pl.pallas_call(
        down_kernel,
        out_shape=jax.ShapeDtypeStruct((rows, depth), jnp.bfloat16),
        grid=(depth // UNITS,),
        in_specs=[
            pl.BlockSpec((rows, count), lambda i: (0, 0)),
            pl.BlockSpec((UNITS, count), lambda i: (i, 0)),
        ],
        out_specs=pl.BlockSpec((rows, UNITS), lambda i: (0, i)),
        compiler_params=pltpu.CompilerParams(vmem_limit_bytes=60 * 2**20),
        cost_estimate=pl.CostEstimate(
            flops=2 * rows * depth * count, bytes_accessed=2 * depth * count, transcendentals=0
        ),
        name="project_down",
    )(hidden, full_down_t)


def units_back_kernel(
    grad_ref, down_ref, gate_ref, up_ref, active_ref, slope_ref, dg_ref, du_ref, out_ref, acc_ref
):
    @pl.when(pl.program_id(0) == 0)
    def _():
        acc_ref[...] = jnp.zeros_like(acc_ref)

    hidden_grad = matmul(grad_ref[...], down_ref[...])
    gate_low = (hidden_grad * slope_ref[...].astype(jnp.float32)).astype(jnp.bfloat16)
    up_low = (hidden_grad * active_ref[...].astype(jnp.float32)).astype(jnp.bfloat16)
    dg_ref[...] = gate_low
    du_ref[...] = up_low
    for n in range(0, acc_ref.shape[1], 256):
        acc_ref[:, n : n + 256] += matmul_nt(gate_low, gate_ref[n : n + 256, :]) + matmul_nt(
            up_low, up_ref[n : n + 256, :]
        )

    @pl.when(pl.program_id(0) == pl.num_programs(0) - 1)
    def _():
        out_ref[...] = acc_ref[...].astype(jnp.bfloat16)


def units_back(mlp_low, full_down_t, full_gate, full_up, active, slope):
    rows, depth = mlp_low.shape
    count = active.shape[1]
    column = lambda n: pl.BlockSpec((n, UNITS), lambda i: (0, i))
    whole = pl.BlockSpec((rows, depth), lambda i: (0, 0))
    low = lambda n: jax.ShapeDtypeStruct((rows, n), jnp.bfloat16)
    return pl.pallas_call(
        units_back_kernel,
        out_shape=(low(count), low(count), low(depth)),
        grid=(count // UNITS,),
        in_specs=[whole, column(depth), column(depth), column(depth), column(rows), column(rows)],
        out_specs=[column(rows), column(rows), whole],
        scratch_shapes=[pltpu.VMEM((rows, depth), jnp.float32)],
        compiler_params=pltpu.CompilerParams(vmem_limit_bytes=60 * 2**20),
        cost_estimate=pl.CostEstimate(
            flops=6 * rows * depth * count, bytes_accessed=6 * depth * count, transcendentals=0
        ),
        name="units_back",
    )(mlp_low, full_down_t, full_gate, full_up, active, slope)


def slot_block(map_ref, me, slot, swapped):
    device = slot >> 1
    if swapped:
        device = me ^ (((device & 3) << 1) | (device >> 2))
    return map_ref[device * 2 + (slot & 1)]


def block_list(lookup, key_blocks, own, seq_blocks, reach, list_ref):
    def look(slot, count):
        other = lookup(slot)
        gap = own - other
        whole = (gap > 0) & (gap < reach) & (own // seq_blocks == other // seq_blocks)
        list_ref[count] = slot
        return count + whole.astype(jnp.int32)

    return lax.fori_loop(0, key_blocks, look, jnp.int32(0))


def find_block(lookup, key_blocks, wanted):
    def look(slot, found):
        return jnp.where(lookup(slot) == wanted, slot, found)

    return lax.fori_loop(0, key_blocks, look, jnp.int32(-1))


def visit_blocks(map_ref, me, chunk, q_blocks, key_blocks, seq_blocks, reach, swapped, list_ref, tile, blk, keys_first):
    first = chunk * key_blocks
    lookup = lambda slot: slot_block(map_ref, me, first + slot, swapped)
    row_no = lax.broadcasted_iota(jnp.int32, (blk, blk), 0)
    col_no = lax.broadcasted_iota(jnp.int32, (blk, blk), 1)
    query_no, key_no = (col_no, row_no) if keys_first else (row_no, col_no)
    for b in range(q_blocks):
        own = map_ref[me * q_blocks + b]
        count = block_list(lookup, key_blocks, own, seq_blocks, reach, list_ref)

        def pair(step, carry):
            tile(b, list_ref[2 * step], None)
            tile(b, list_ref[2 * step + 1], None)
            return carry

        lax.fori_loop(0, count // 2, pair, 0)

        @pl.when(count % 2 == 1)
        def _():
            tile(b, list_ref[count - 1], None)

        diagonal = find_block(lookup, key_blocks, own)

        @pl.when(diagonal >= 0)
        def _():
            tile(b, diagonal, query_no >= key_no)

        if reach < seq_blocks:
            edge = find_block(lookup, key_blocks, own - reach)

            @pl.when((edge >= 0) & (own % seq_blocks >= reach))
            def _():
                tile(b, edge, query_no < key_no)


def attend_kernel(
    map_ref, me_ref, q_ref, *refs, blk, heads, parts, key_blocks, seq_blocks, reach
):
    pieces = refs[:parts]
    o_ref, low_ref, l_ref = refs[parts : parts + 3]
    chunk = pl.program_id(0)
    if parts > 1:
        kv_ref = refs[parts + 3]
        row = 0
        for piece in pieces:
            kv_ref[row : row + piece.shape[0], :] = piece[...]
            row += piece.shape[0]
    else:
        kv_ref = pieces[0]
    acc_ref, sum_ref, list_ref = refs[-3:]
    q_blocks = q_ref.shape[0] // blk

    @pl.when(chunk == 0)
    def _():
        acc_ref[...] = jnp.zeros_like(acc_ref)
        sum_ref[...] = jnp.zeros_like(sum_ref)

    def tile(b, slot, mask):
        rows = pl.ds(pl.multiple_of(slot * blk, blk), blk)
        keys = kv_ref[rows, :HD]
        vals = kv_ref[rows, HD:]
        for h in range(heads):
            query = q_ref[b * blk : (b + 1) * blk, h * HD : (h + 1) * HD]
            capped = jnp.tanh(matmul_nt(query, keys) * (1.0 / soft_cap))
            weights = jnp.exp2(capped * (soft_cap * LOG2E))
            if mask is not None:
                weights = jnp.where(mask, weights, 0.0)
            at = (slice(b * blk, (b + 1) * blk), slice(h * HD, (h + 1) * HD))
            lanes = (slice(b * blk, (b + 1) * blk), slice(h * 128, (h + 1) * 128))
            part = weights[:, :128]
            for piece in range(1, blk // 128):
                part = part + weights[:, piece * 128 : (piece + 1) * 128]
            sum_ref[lanes] += part
            acc_ref[at] += matmul(weights.astype(jnp.bfloat16), vals)

    visit_blocks(
        map_ref, me_ref[0], chunk, q_blocks, key_blocks, seq_blocks, reach, parts > 1, list_ref,
        tile, blk, False,
    )

    @pl.when(chunk == pl.num_programs(0) - 1)
    def _():
        for b in range(q_blocks):
            for h in range(heads):
                at = (slice(b * blk, (b + 1) * blk), slice(h * HD, (h + 1) * HD))
                lanes = (slice(b * blk, (b + 1) * blk), slice(h * 128, (h + 1) * 128))
                total = jnp.sum(sum_ref[lanes], axis=-1, keepdims=True)
                result = acc_ref[at] / total
                o_ref[at] = result
                low_ref[at] = result.astype(jnp.bfloat16)
                l_ref[lanes] = jnp.broadcast_to(total, (blk, 128))


def attend(block_map, me, queries, pieces, blk, seq_blocks):
    rows, width = queries.shape
    heads = width // HD
    total = sum(piece.shape[0] for piece in pieces)
    joined = len(pieces) > 1
    chunk_rows = total if joined else min(total, KEY_CHUNK)
    kernel = partial(
        attend_kernel, blk=blk, heads=heads, parts=len(pieces), key_blocks=chunk_rows // blk,
        seq_blocks=seq_blocks, reach=WINDOW // blk,
    )
    whole = lambda i, *_: (0, 0)
    if joined:
        kv_specs = [pl.BlockSpec(piece.shape, whole) for piece in pieces]
    else:
        kv_specs = [pl.BlockSpec((chunk_rows, 2 * HD), lambda i, *_: (i, 0))]
    out_shape = [
        jax.ShapeDtypeStruct((rows, width), jnp.float32),
        jax.ShapeDtypeStruct((rows, width), jnp.bfloat16),
        jax.ShapeDtypeStruct((rows, heads * 128), jnp.float32),
    ]
    if joined:
        out_shape.append(jax.ShapeDtypeStruct((total, 2 * HD), jnp.bfloat16))
    found = pl.pallas_call(
        kernel,
        out_shape=tuple(out_shape),
        grid_spec=pltpu.PrefetchScalarGridSpec(
            num_scalar_prefetch=2,
            grid=(total // chunk_rows,),
            in_specs=[pl.BlockSpec((rows, width), whole), *kv_specs],
            out_specs=[pl.BlockSpec(shape.shape, whole) for shape in out_shape],
            scratch_shapes=[
                pltpu.VMEM((rows, width), jnp.float32),
                pltpu.VMEM((rows, heads * 128), jnp.float32),
                pltpu.SMEM((chunk_rows // blk + 1,), jnp.int32),
            ],
        ),
        compiler_params=pltpu.CompilerParams(vmem_limit_bytes=60 * 2**20),
        cost_estimate=pl.CostEstimate(
            flops=4 * rows * width * total, bytes_accessed=8 * rows * width + 8 * total * HD,
            transcendentals=2 * rows * heads * total,
        ),
        name="attend",
    )(block_map, me, queries, *pieces)
    return found if joined else (*found, pieces[0])


def attend_back_kernel(
    map_ref, me_ref, da_ref, out_ref, o_ref, l_ref, q_ref, kv_ref, kt_ref, cos_ref, sin_ref, *refs,
    blk, heads, swapped, key_blocks, seq_blocks, reach
):
    dq_ref, *dkv_refs = refs[: 3 if swapped else 2]
    do_ref, stat_ref, dqt_ref, dk_ref, dv_ref, list_ref = refs[3 if swapped else 2 :]
    chunk = pl.program_id(0)
    q_blocks = q_ref.shape[0] // blk

    @pl.when(chunk == 0)
    def _():
        dqt_ref[...] = jnp.zeros_like(dqt_ref)
        for h in range(heads):
            at = slice(h * HD, (h + 1) * HD)
            out_grad = matmul(da_ref[...], out_ref[:, at]).astype(jnp.bfloat16)
            do_ref[:, at] = out_grad
            delta = jnp.sum(out_grad.astype(jnp.float32) * o_ref[:, at], axis=-1, keepdims=True)
            stat_ref[heads + h : heads + h + 1, :] = jnp.broadcast_to(
                delta, (delta.shape[0], 128)
            ).T[:1, :]
            stat_ref[h : h + 1, :] = jnp.log2(l_ref[:, h * 128 : (h + 1) * 128]).T[:1, :]

    dk_ref[...] = jnp.zeros_like(dk_ref)
    dv_ref[...] = jnp.zeros_like(dv_ref)

    def tile(b, slot, mask):
        rows = pl.ds(pl.multiple_of(slot * blk, blk), blk)
        keys = kv_ref[rows, :HD]
        vals = kv_ref[rows, HD:]
        turned = kt_ref[:, rows]
        cols = slice(b * blk, (b + 1) * blk)
        for h in range(heads):
            query = q_ref[cols, h * HD : (h + 1) * HD]
            out_grad = do_ref[cols, h * HD : (h + 1) * HD]
            tangent = jnp.tanh(matmul_nt(keys, query) * (1.0 / soft_cap))
            probs = jnp.exp2(tangent * (soft_cap * LOG2E) - stat_ref[h : h + 1, cols])
            if mask is not None:
                probs = jnp.where(mask, probs, 0.0)
            prob_grad = matmul_nt(vals, out_grad)
            score = (
                probs * (prob_grad - stat_ref[heads + h : heads + h + 1, cols])
                * (1.0 - tangent * tangent)
            ).astype(jnp.bfloat16)
            dk_new = matmul(score, query)
            dv_new = matmul(probs.astype(jnp.bfloat16), out_grad)
            dk_part = dk_new if h == 0 else dk_part + dk_new
            dv_part = dv_new if h == 0 else dv_part + dv_new
            dqt_ref[h * HD : (h + 1) * HD, cols] += matmul(turned, score)
        dk_ref[rows, :] += dk_part
        dv_ref[rows, :] += dv_part

    visit_blocks(
        map_ref, me_ref[0], chunk, q_blocks, key_blocks, seq_blocks, reach, swapped, list_ref,
        tile, blk, True,
    )

    row = 0
    for dkv_ref in dkv_refs:
        count = dkv_ref.shape[0]
        dkv_ref[:, :HD] = dk_ref[row : row + count, :].astype(jnp.bfloat16)
        dkv_ref[:, HD:] = dv_ref[row : row + count, :].astype(jnp.bfloat16)
        row += count

    @pl.when(chunk == pl.num_programs(0) - 1)
    def _():
        cosine, sine = cos_ref[...], sin_ref[...]
        for h in range(heads):
            low = dqt_ref[h * HD : h * HD + HALF, :].T * HD ** (-0.5)
            high = dqt_ref[h * HD + HALF : (h + 1) * HD, :].T * HD ** (-0.5)
            dq_ref[:, h * HD : h * HD + HALF] = (low * cosine + high * sine).astype(jnp.bfloat16)
            dq_ref[:, h * HD + HALF : (h + 1) * HD] = (high * cosine - low * sine).astype(
                jnp.bfloat16
            )


def attend_back(
    block_map, me, branch_low, full_out_t, attended, totals, queries, kv_all, key_turned, cosine,
    sine, blk, seq_blocks, swapped
):
    rows, width = queries.shape
    heads = width // HD
    depth = branch_low.shape[1]
    total = kv_all.shape[0]
    chunk_rows = total if swapped else min(total, KEY_CHUNK)
    kernel = partial(
        attend_back_kernel, blk=blk, heads=heads, swapped=swapped, key_blocks=chunk_rows // blk,
        seq_blocks=seq_blocks, reach=WINDOW // blk,
    )
    whole = lambda i, *_: (0, 0)
    part = total // 2 if swapped else total
    dkv_shapes = [jax.ShapeDtypeStruct((part, 2 * HD), jnp.bfloat16)] * (2 if swapped else 1)
    dkv_specs = [pl.BlockSpec((min(part, chunk_rows), 2 * HD), lambda i, *_: (i, 0))] * len(dkv_shapes)
    return pl.pallas_call(
        kernel,
        out_shape=(jax.ShapeDtypeStruct((rows, width), jnp.bfloat16), *dkv_shapes),
        grid_spec=pltpu.PrefetchScalarGridSpec(
            num_scalar_prefetch=2,
            grid=(total // chunk_rows,),
            in_specs=[
                pl.BlockSpec((rows, depth), whole),
                pl.BlockSpec((depth, width), whole),
                pl.BlockSpec((rows, width), whole),
                pl.BlockSpec((rows, heads * 128), whole),
                pl.BlockSpec((rows, width), whole),
                pl.BlockSpec((chunk_rows, 2 * HD), lambda i, *_: (i, 0)),
                pl.BlockSpec((HD, chunk_rows), lambda i, *_: (0, i)),
                pl.BlockSpec((rows, HALF), whole),
                pl.BlockSpec((rows, HALF), whole),
            ],
            out_specs=[pl.BlockSpec((rows, width), whole), *dkv_specs],
            scratch_shapes=[
                pltpu.VMEM((rows, width), jnp.bfloat16),
                pltpu.VMEM((2 * heads, rows), jnp.float32),
                pltpu.VMEM((width, rows), jnp.float32),
                pltpu.VMEM((chunk_rows, HD), jnp.float32),
                pltpu.VMEM((chunk_rows, HD), jnp.float32),
                pltpu.SMEM((chunk_rows // blk + 1,), jnp.int32),
            ],
        ),
        compiler_params=pltpu.CompilerParams(vmem_limit_bytes=60 * 2**20),
        cost_estimate=pl.CostEstimate(
            flops=10 * rows * width * total, bytes_accessed=16 * rows * width + 10 * total * HD,
            transcendentals=2 * rows * heads * total,
        ),
        name="attend_back",
    )(
        block_map, me, branch_low, full_out_t, attended, totals, queries, kv_all, key_turned,
        cosine, sine,
    )


def body(
    tokens, block_map, w_query, w_key, w_value, w_out, w_gate, w_up, w_down, norm_gains, cotangent
):
    ctx_count = lax.axis_size("ctx")
    tok_dev, depth = tokens.shape
    block_rows = tok_dev // 2
    seq_count = max(1, ctx_count // 16)
    seq_len = tok_dev * ctx_count // seq_count
    seq_blocks = seq_len // block_rows
    me = lax.axis_index("ctx")
    me_list = me.reshape(1).astype(jnp.int32)
    heads_dev = w_query.shape[1] // HD
    q_width = heads_dev * HD
    flat_map = block_map.reshape(-1).astype(jnp.int32)
    pairs = paired()

    gains = gather_gains(norm_gains).astype(jnp.float32)
    if pairs:
        qkv_shard = pack(w_query, w_key, w_value)
        near = lax.optimization_barrier((*nearby(qkv_shard), gains))
        gains = near[2]
        qkv_pieces = gather_pieces(qkv_shard, near[:2])
        out_shard = tie(w_out, qkv_pieces[3], qkv_pieces[4]).T
        out_near = nearby(out_shard)
    else:
        qkv_shard = jnp.concatenate([w_query, w_key, w_value], axis=1)
        qkv_pieces = (lax.all_gather(qkv_shard, "ctx", axis=0, tiled=True),)
        out_pieces = (lax.all_gather(w_out.T, "ctx", axis=0, tiled=True),)
    own_ids = lax.dynamic_index_in_dim(block_map, me, 0, keepdims=False)
    offsets = jnp.arange(block_rows, dtype=jnp.int32)
    own_index = (own_ids[:, None] * block_rows + offsets[None, :]).reshape(-1)
    cosine, sine = angle_tables(own_index % seq_len)
    inputs = tokens.astype(jnp.float32)
    in_scale = rms_scale(inputs)
    normed_in = (inputs * in_scale * gains[0]).astype(jnp.bfloat16)
    queries, kv_local, full_qkv = project(normed_in, cosine, sine, qkv_pieces, heads_dev)
    if pairs:
        kv_local, *out_near = lax.optimization_barrier((kv_local, *out_near))
        kv_pieces = gather_pieces(kv_local)
        out_pieces = gather_pieces(tie(out_shard, *kv_pieces[1:3]), out_near)
        late = (*kv_pieces[3:5], *out_pieces[3:5])
    else:
        kv_pieces = (lax.all_gather(kv_local, "ctx", axis=0, tiled=True),)
        late = kv_pieces
    w_gate, w_up, w_down, *_ = lax.optimization_barrier((w_gate, w_up, w_down, *late))
    if pairs:
        gate_near = nearby(w_gate)
    attended, attn_flat, totals, kv_all = attend(
        flat_map, me_list, queries, kv_pieces, block_rows, seq_blocks
    )
    branch_part, full_out_t = out_project(attn_flat, out_pieces, depth)
    if pairs:
        branch_part, *gate_near = lax.optimization_barrier((branch_part, *gate_near))
        full_gate = assemble(gather_pieces(w_gate, gate_near))
    else:
        full_gate = lax.all_gather(w_gate, "ctx", axis=0, tiled=True)
    branch = lax.psum(branch_part, "tp")
    full_up = lax.all_gather(w_up, "ctx", axis=0, tiled=True)
    if pairs:
        full_down_t = assemble(gather_pieces(w_down.T))
    else:
        full_down_t = lax.all_gather(w_down.T, "ctx", axis=0, tiled=True)
    branch, full_gate, full_up, full_down_t = lax.optimization_barrier(
        (branch, full_gate, full_up, full_down_t)
    )
    normed_mid = by_rows(mid_kernel, (tokens, branch), gains, (jnp.bfloat16,), 0, "mid_norms")
    hidden, active, slope = units(normed_mid, full_gate, full_up)
    mlp_out = lax.psum(project_down(hidden, full_down_t), "tp")
    result, mlp_low, gain_four = by_rows(
        top_kernel, (tokens, branch, mlp_out, cotangent), gains, (jnp.bfloat16, jnp.bfloat16), 1,
        "top_norms",
    )
    gate_low, up_low, mid_part = units_back(mlp_low, full_down_t, full_gate, full_up, active, slope)
    mid_part, hidden_t, mlp_t, gate_t, up_t = lax.optimization_barrier(
        (mid_part, hidden, mlp_low, gate_low, up_low)
    )
    mid_sum = lax.psum(mid_part, "tp")
    down_grad = matmul(hidden_t.T, mlp_t).astype(jnp.bfloat16)
    down_shard = lax.psum_scatter(down_grad, "ctx", scatter_dimension=1, tiled=True)
    gate_grad = matmul(normed_mid.T, gate_t).astype(jnp.bfloat16)
    gate_blocks = scatter_start(gate_grad)
    up_grad = matmul(normed_mid.T, up_t).astype(jnp.bfloat16)
    key_turned = kv_all[:, :HD].T
    mid_sum, up_grad, key_turned, gate_blocks = lax.optimization_barrier(
        (mid_sum, up_grad, key_turned, gate_blocks)
    )
    gate_terms = scatter_finish(gate_blocks)
    resid_grad, branch_low, gain_mid = by_rows(
        low_kernel, (tokens, branch, mid_sum, cotangent), gains, (jnp.float32, jnp.bfloat16), 2,
        "low_norms",
    )
    query_low, *kv_terms = attend_back(
        flat_map, me_list, branch_low, full_out_t, attended, totals, queries, kv_all, key_turned,
        cosine, sine, block_rows, seq_blocks, pairs,
    )
    *kv_terms, down_shard, gate_terms = lax.optimization_barrier((*kv_terms, down_shard, gate_terms))
    gate_shard = add_terms(gate_terms)
    if pairs:
        mine = kv_terms[0] + swap(kv_terms[1], 1)
        kv_sums = scatter_finish(
            scatter_corner(*(mine[k * tok_dev : (k + 1) * tok_dev] for k in range(4)))
        )
    else:
        kv_sums = (lax.psum_scatter(kv_terms[0], "ctx", scatter_dimension=0, tiled=True),)
    qkv_low, in_part = join(cosine, sine, query_low, full_qkv, kv_sums)
    in_part, qkv_low, branch_t, up_grad = lax.optimization_barrier(
        (in_part, qkv_low, branch_low, up_grad)
    )
    in_sum = lax.psum(in_part, "tp")
    up_shard = lax.psum_scatter(up_grad, "ctx", scatter_dimension=0, tiled=True)
    gain_one = jnp.sum(in_part.astype(jnp.float32) * (inputs * in_scale), axis=0)
    gain_one = sum_small_tp(gain_one)
    gains_shard = scatter_gains(jnp.concatenate([gain_one[None], gain_mid[1:], gain_mid[:1], gain_four]))
    qkv_grad = matmul(normed_in.T, qkv_low).astype(jnp.bfloat16)
    qkv_shard = add_terms(scatter_finish(scatter_start(qkv_grad)))
    out_weight_grad = matmul(branch_t.T, attn_flat).astype(jnp.bfloat16)
    out_grad_t = add_terms(scatter_finish(scatter_start(out_weight_grad)))
    shards = (
        qkv_shard[:, :q_width],
        qkv_shard[:, q_width : q_width + HD],
        qkv_shard[:, q_width + HD :],
        out_grad_t.T,
        gate_shard,
        up_shard.astype(jnp.float32),
        down_shard.astype(jnp.float32),
        gains_shard,
    )
    in_sum, shards = lax.optimization_barrier((in_sum, shards))
    input_grad = by_rows(
        end_kernel, (tokens, in_sum, resid_grad), gains, (jnp.float32,), 0, "end_norms"
    )
    return (result, input_grad, *shards)


def solution(mesh):
    in_specs = (
        P("ctx", None),
        P(),
        P("ctx", "tp"),
        P("ctx", "tp"),
        P("ctx", "tp"),
        P("tp", "ctx"),
        P("ctx", "tp"),
        P("ctx", "tp"),
        P("tp", "ctx"),
        P(None, "ctx"),
        P("ctx", None),
    )
    out_specs = (
        P("ctx", None),
        P("ctx", None),
        P("ctx", "tp"),
        P("ctx", "tp"),
        P("ctx", "tp"),
        P("tp", "ctx"),
        P("ctx", "tp"),
        P("ctx", "tp"),
        P("tp", "ctx"),
        P(None, "ctx"),
    )
    return jax.shard_map(body, mesh=mesh, in_specs=in_specs, out_specs=out_specs, check_vma=False)
```

time: 847 us -> 1380 us (1.63)
  Pallas kernels: 43.2 us -> 814 us
  local copies, waits for them, and re-layouts: 146 us -> 44.6 us
  matrix products: 112 us -> 33.6 us
  other arithmetic: 97.9 us -> 33.1 us
  starting transfers between devices: 40.8 us -> 55.4 us
    pallas_call x1 -> x14, Pallas kernels: 14.5 us -> 787 us  [the longest x6 669 us: call(): pl.pallas_call(kernel, out_shape=out_shape, in_specs=[pl.BlockSpec(memory...]
    dot_general x14 -> x5, matrix products: 108 us -> 33.6 us  [matmul(): return jnp.dot(left, right, preferred_element_type=jnp.float32)]
    all_gather x2 -> x1, waiting for transfers between devices: 31.6 us -> 0.03 us  [body(): full_up = lax.all_gather(w_up, 'ctx', axis=0, tiled=True)]
    unnamed x172 -> x96, local copies, waits for them, and re-layouts: 50.1 us -> 20.2 us
    dynamic_update_slice x13 -> x0, local copies, waits for them, and re-layouts: 25.3 us -> none  [gather_rows(): full = lax.dynamic_update_slice(full, block, ((me ^ bits + base) * rows, 0))]
    reduce_sum x5 -> x1, other arithmetic: 21.2 us -> 1.02 us  [body(): jnp.sum(in_part.astype(jnp.float32) * (inputs * in_scale), axis=0)]
    ppermute x46 -> x72, waiting for transfers between devices: 222 us -> 237 us  [swap(): return lax.ppermute(value, 'ctx', pairs)]
    reduce_scatter x1, waiting for transfers between devices: 5.11 us -> 19.3 us  [body(): up_shard = lax.psum_scatter(up_grad, 'ctx', scatter_dimension=0, tiled=True)]
  transfers between devices with their start and end apart: 54 -> 81, of which waited for: 31 -> 39; matrix products, arithmetic and copies ran while one was open for 26% -> 6% of each run, Pallas kernels for 3% -> 52%
where the time goes in v2:
time: 1380 us; the launch traced here: 1370 us
  Pallas kernels  814 us (59%)
  waiting for transfers between devices  376 us (27%)
  starting transfers between devices  55.4 us (4%)
  local copies, waits for them, and re-layouts  44.6 us (3%)
  matrix products  33.6 us (2%)
  other arithmetic  33.1 us (2%)
  between operations  16.7 us (1%)
    pallas_call x6, Pallas kernels, call(): pl.pallas_call(kernel, out_shape=out_shape, in_specs=[pl.BlockSpec(memory...  669 us
    ppermute x72, waiting for transfers between devices, swap(): return lax.ppermute(value, 'ctx', pairs)  237 us
    psum x1, waiting for transfers between devices, body(): mlp_out = lax.psum(project_down(hidden, full_down_t), 'tp')  95 us
    ppermute x72, starting transfers between devices, swap(): return lax.ppermute(value, 'ctx', pairs)  52.5 us
    pallas_call x4, Pallas kernels, by_rows(): pl.pallas_call(kernel, out_shape=tuple(shapes), grid=(rows // block,), in...  35.1 us
    pallas_call x1, Pallas kernels, units_back(): pl.pallas_call(units_back_kernel, out_shape=(low(count), low(count), low(...  34.9 us
    dot_general x5, matrix products, matmul(): return jnp.dot(left, right, preferred_element_type=jnp.float32)  33.6 us
  transfers between devices with their start and end apart: 81, of which 39 were waited for; matrix products, arithmetic and copies ran while one was open for 6% of the time, Pallas kernels for 52%

profile of v2, /device:TPU:0, one launch (start us, length us, event | category | flops | bytes accessed | tf_op | source)
XLA Modules:
  0.0 1374.3 jit_solution(11515264146697063790)
XLA Ops:
  17.9 8.9 collective-permute-done.3
  49.6 8.5 project.1
  60.6 12.2 collective-permute-done.15.refs_1_
  94.8 16.2 %attend.1 = (f32[512,512]{1,0:T(8,128)}, bf16[512,512]{1,0:T(8,128)(2,1)}, f32[512,256]{1,0:T(8,128)}, bf16[4096,512]{1,0:T(8,128)(2,1)}) custom-call(s32[16]{0:T(128)} %reshape.114.map_ref, s32[1]{0:T(128)} %bitcast.8.me_ref, bf16[512,512]{1,0:T(8,128)(2,1)} %get-tuple-element.87.q_ref, bf16[512,512]{1,0:T(8,128)(2,1)} %get-tuple-element.90.refs_0_, ...), custom_call_target="tpu_custom_call" | custom-call | flops 4294967296 | bytes 10485760 | tf_op jit(solution)/shard_map/attend/pallas_call | solution.py:669
  120.1 43.8 %collective-permute-done.40.refs_1_ = bf16[288,2304]{1,0:T(8,128)(2,1)S(1)} collective-permute-done((bf16[288,2304]{1,0:T(8,128)(2,1)}, bf16[288,2304]{1,0:T(8,128)(2,1)S(1)}, u32[]{:S(2)}, u32[]{:S(2)}) %collective-permute-start.40) | collective-permute-done | bytes 1327136 | tf_op jit(solution)/shard_map/ppermute | solution.py:62
  168.4 27.4 %collective-permute-done.42.refs_3_ = bf16[144,2304]{1,0:T(8,128)(2,1)S(1)} collective-permute-done((bf16[144,2304]{1,0:T(8,128)(2,1)S(1)}, bf16[144,2304]{1,0:T(8,128)(2,1)S(1)}, u32[]{:S(2)}, u32[]{:S(2)}) %collective-permute-start.42) | collective-permute-done | bytes 663584 | tf_op jit(solution)/shard_map/ppermute | solution.py:62
  197.2 27.1 %collective-permute-done.33.refs_3_ = bf16[144,2304]{1,0:T(8,128)(2,1)S(1)} collective-permute-done((bf16[144,2304]{1,0:T(8,128)(2,1)S(1)}, bf16[144,2304]{1,0:T(8,128)(2,1)S(1)}, u32[]{:S(2)}, u32[]{:S(2)}) %collective-permute-start.33) | collective-permute-done | bytes 663584 | tf_op jit(solution)/shard_map/ppermute | solution.py:62
  231.3 323.5 %assemble.3.down_ref = bf16[2304,2304]{1,0:T(8,128)(2,1)} custom-call(s32[10]{0:T(128)} %add.183.rows_ref, bf16[288,2304]{1,0:T(8,128)(2,1)} %bitcast.121, bf16[288,2304]{1,0:T(8,128)(2,1)} %copy-done.8, bf16[288,2304]{1,0:T(8,128)(2,1)} %copy-done.9, bf16[144,2304]{1,0:T(8,128)(2,1)} %copy-done.19, bf16[144,2304]{1,0:T(8,128)(2,1)} %copy-done.20, ...), custom_call_target="tpu_custom_call" | custom-call | bytes 21233704 | tf_op jit(solution)/shard_map/assemble/pallas_call | solution.py:48
  554.8 323.5 %assemble.2.gate_ref = bf16[2304,2304]{1,0:T(8,128)(2,1)} custom-call(s32[10]{0:T(128)} %add.183.rows_ref, bf16[288,2304]{1,0:T(8,128)(2,1)} %refs_0_, bf16[288,2304]{1,0:T(8,128)(2,1)} %copy-done.6, bf16[288,2304]{1,0:T(8,128)(2,1)} %copy-done.7, bf16[144,2304]{1,0:T(8,128)(2,1)} %copy-done.18, bf16[144,2304]{1,0:T(8,128)(2,1)} %collective-permute-done.34.refs_4_, ...), custom_call_target="tpu_custom_call" | custom-call | bytes 21233704 | tf_op jit(solution)/shard_map/assemble/pallas_call | solution.py:48
  878.3 6.8 mid_norms.1.in_ref
  885.2 19.4 %units.1 = (bf16[512,2304]{1,0:T(8,128)(2,1)}, bf16[512,2304]{1,0:T(8,128)(2,1)}, bf16[512,2304]{1,0:T(8,128)(2,1)}) custom-call(bf16[512,2304]{1,0:T(8,128)(2,1)} %mid_norms.1.in_ref, bf16[2304,2304]{1,0:T(8,128)(2,1)} %assemble.2.gate_ref, bf16[2304,2304]{1,0:T(8,128)(2,1)} %all-gather.2.cloned.1.call-done.up_ref), custom_call_target="tpu_custom_call" | custom-call | flops 10871635968 | bytes 21233664 | tf_op jit(solution)/shard_map/units/pallas_call | solution.py:447
  904.6 12.4 project_down.1
  917.0 95.0 %all-reduce.7.cloned.1.call-done.mlp_ref = bf16[512,2304]{1,0:T(8,128)(2,1)} async-done(((bf16[512,2304]{1,0:T(8,128)(2,1)}), bf16[512,2304]{1,0:T(8,128)(2,1)}) %all-reduce.7.cloned.1.call-update) | async-done | bytes 2359312 | tf_op jit(solution)/shard_map/psum | solution.py:891
  1012.0 8.5 top_norms.1
  1020.5 34.9 %units_back.1 = (bf16[512,2304]{1,0:T(8,128)(2,1)}, bf16[512,2304]{1,0:T(8,128)(2,1)}, bf16[512,2304]{1,0:T(8,128)(2,1)}) custom-call(bf16[512,2304]{1,0:T(8,128)(2,1)} %get-tuple-element.129.grad_ref, bf16[2304,2304]{1,0:T(8,128)(2,1)} %assemble.3.down_ref, bf16[2304,2304]{1,0:T(8,128)(2,1)} %assemble.2.gate_ref, ...), custom_call_target="tpu_custom_call" | custom-call | flops 16307453952 | bytes 31850496 | tf_op jit(solution)/shard_map/units_back/pallas_call | solution.py:514
  1057.1 10.0 convolution_convert_fusion
  1068.8 7.6 convolution_convert_fusion.1
  1084.6 6.5 copy.33
  1105.3 8.2 convolution_convert_fusion.2
  1115.0 19.3 %collective-permute-done.50 = bf16[144,2304]{1,0:T(8,128)(2,1)S(1)} collective-permute-done((bf16[144,2304]{1,0:T(8,128)(2,1)}, bf16[144,2304]{1,0:T(8,128)(2,1)S(1)}, u32[]{:S(2)}, u32[]{:S(2)}) %collective-permute-start.50) | collective-permute-done | bytes 663584 | tf_op jit(solution)/shard_map/ppermute | solution.py:62
  1139.3 10.9 all-reduce.9.cloned.1.call-done.mid_ref
  1153.2 11.5 low_norms.1
  1164.8 27.0 %attend_back.1 = (bf16[512,512]{1,0:T(8,128)(2,1)}, bf16[2048,512]{1,0:T(8,128)(2,1)}, bf16[2048,512]{1,0:T(8,128)(2,1)}) custom-call(s32[16]{0:T(128)} %reshape.114.map_ref, s32[1]{0:T(128)} %bitcast.8.me_ref, bf16[512,2304]{1,0:T(8,128)(2,1)} %get-tuple-element.140.da_ref, bf16[2304,512]{1,0:T(8,128)(2,1)} %get-tuple-element.120.out_ref, ...), custom_call_target="tpu_custom_call" | custom-call | flops 10737418240 | bytes 14680064 | tf_op jit(solution)/shard_map/attend_back/pallas_call | solution.py:785
  1200.5 8.3 collective-permute-done.57
  1211.1 7.1 collective-permute-done.55
  1219.4 8.5 collective-permute-done.58.refs_2_
  1230.1 7.2 join.1
  1280.8 10.0 collective-permute-done.60
  1304.9 17.7 %collective-permute-done.61 = bf16[288,1024]{1,0:T(8,128)(2,1)S(1)} collective-permute-done((bf16[288,1024]{1,0:T(8,128)(2,1)S(1)}, bf16[288,1024]{1,0:T(8,128)(2,1)S(1)}, u32[]{:S(2)}, u32[]{:S(2)}) %collective-permute-start.61) | collective-permute-done | bytes 589856 | tf_op jit(solution)/shard_map/ppermute | solution.py:62
  1324.6 19.3 %reduce-scatter.5.cloned.1.call-done = bf16[288,2304]{1,0:T(8,128)(2,1)} async-done(((bf16[2304,2304]{1,0:T(8,128)(2,1)}), bf16[288,2304]{1,0:T(8,128)(2,1)}) %reduce-scatter.5.cloned.1.call-update) | async-done | bytes 1327120 | tf_op jit(solution)/shard_map/reduce_scatter | solution.py:933
  1346.9 11.5 all-reduce.11.cloned.1.call-done.sum_ref
  1358.3 8.2 end_norms.1
  (333 shorter events, 190.8 us)
Async XLA Ops:
  8.0 870.3 %all-reduce.5.cloned.1.call-start = ((), (), s32[]{:S(2)}) async-start(), calls=%async_computation.2 | async-start | bytes 4718592 | tf_op jit(solution)/shard_map/psum | solution.py:880
  14.6 31.6 %collective-permute-start.8 = (bf16[288,1024]{1,0:T(8,128)(2,1)}, bf16[288,1024]{1,0:T(8,128)(2,1)}, u32[]{:S(2)}, u32[]{:S(2)}) collective-permute-start(bf16[288,1024]{1,0:T(8,128)(2,1)} %pack.1.refs_0_), channel_id=1, source_target_pairs={{0,4},{4,0},{8,12},{12,8},{16,20},{20,16},{24,28},{28,24},{1,5},{5... | collective-permute-start | bytes 1769480 | tf_op jit(solution)/shard_map/ppermute | solution.py:62
  86.7 29.9 %collective-permute-start.31 = (bf16[288,2304]{1,0:T(8,128)(2,1)}, bf16[288,2304]{1,0:T(8,128)(2,1)S(1)}, u32[]{:S(2)}, u32[]{:S(2)}) collective-permute-start(bf16[288,2304]{1,0:T(8,128)(2,1)} %refs_0_), channel_id=1, source_target_pairs={{0,8},{4,12},{8,0},{12,4},{16,24},{20,28},{24,16},{28,20},{1,9},{5... | collective-permute-start | bytes 3981320 | tf_op jit(solution)/shard_map/ppermute | solution.py:62
  87.3 29.6 %collective-permute-start.32 = (bf16[288,2304]{1,0:T(8,128)(2,1)}, bf16[288,2304]{1,0:T(8,128)(2,1)S(1)}, u32[]{:S(2)}, u32[]{:S(2)}) collective-permute-start(bf16[288,2304]{1,0:T(8,128)(2,1)} %refs_0_), channel_id=1, source_target_pairs={{0,16},{4,20},{8,24},{12,28},{16,0},{20,4},{24,8},{28,12},{1,17},{... | collective-permute-start | bytes 3981320 | tf_op jit(solution)/shard_map/ppermute | solution.py:62
  116.9 761.4 %all-gather.2.cloned.1.call-start = ((), (), s32[]{:S(2)}) async-start(), calls=%async_computation.3 | async-start | bytes 11943936 | tf_op jit(solution)/shard_map/all_gather | solution.py:881
  117.5 894.5 %all-reduce.7.cloned.1.call-start = ((), (), s32[]{:S(2)}) async-start(), calls=%async_computation.4 | async-start | bytes 4718592 | tf_op jit(solution)/shard_map/psum | solution.py:891
  118.0 45.8 %collective-permute-start.40 = (bf16[288,2304]{1,0:T(8,128)(2,1)}, bf16[288,2304]{1,0:T(8,128)(2,1)S(1)}, u32[]{:S(2)}, u32[]{:S(2)}) collective-permute-start(bf16[288,2304]{1,0:T(8,128)(2,1)} %bitcast.118), channel_id=1, source_target_pairs={{0,8},{4,12},{8,0},{12,4},{16,24},{20,28},{24,16},{28,20},{1,9},{5... | collective-permute-start | bytes 3981320 | tf_op jit(solution)/shard_map/ppermute | solution.py:62
  119.5 45.7 %collective-permute-start.41 = (bf16[288,2304]{1,0:T(8,128)(2,1)}, bf16[288,2304]{1,0:T(8,128)(2,1)S(1)}, u32[]{:S(2)}, u32[]{:S(2)}) collective-permute-start(bf16[288,2304]{1,0:T(8,128)(2,1)} %bitcast.119), channel_id=1, source_target_pairs={{0,16},{4,20},{8,24},{12,28},{16,0},{20,4},{24,8},{28,12},{1,17},{... | collective-permute-start | bytes 3981320 | tf_op jit(solution)/shard_map/ppermute | solution.py:62
  120.1 48.3 %collective-permute-start.44 = (bf16[288,2304]{1,0:T(8,128)(2,1)}, bf16[288,2304]{1,0:T(8,128)(2,1)S(1)}, u32[]{:S(2)}, u32[]{:S(2)}) collective-permute-start(bf16[288,2304]{1,0:T(8,128)(2,1)} %bitcast.120), channel_id=1, source_target_pairs={{0,4},{4,0},{8,12},{12,8},{16,20},{20,16},{24,28},{28,24},{1,5},{5... | collective-permute-start | bytes 3981320 | tf_op jit(solution)/shard_map/ppermute | solution.py:62
  163.9 31.9 %collective-permute-start.42 = (bf16[144,2304]{1,0:T(8,128)(2,1)S(1)}, bf16[144,2304]{1,0:T(8,128)(2,1)S(1)}, u32[]{:S(2)}, u32[]{:S(2)}) collective-permute-start(bf16[144,2304]{1,0:T(8,128)(2,1)S(1)} %slice.281), channel_id=1, source_target_pairs={{0,16},{4,20},{8,24},{12,28},{16,0},{20,4},{24,8},{28,12},{1,17},{... | collective-permute-start | bytes 1990664 | tf_op jit(solution)/shard_map/ppermute | solution.py:62
  165.3 31.8 %collective-permute-start.43 = (bf16[144,2304]{1,0:T(8,128)(2,1)S(1)}, bf16[144,2304]{1,0:T(8,128)(2,1)S(1)}, u32[]{:S(2)}, u32[]{:S(2)}) collective-permute-start(bf16[144,2304]{1,0:T(8,128)(2,1)S(1)} %slice.282), channel_id=1, source_target_pairs={{0,8},{4,12},{8,0},{12,4},{16,24},{20,28},{24,16},{28,20},{1,9},{5... | collective-permute-start | bytes 1990664 | tf_op jit(solution)/shard_map/ppermute | solution.py:62
  166.3 57.9 %collective-permute-start.33 = (bf16[144,2304]{1,0:T(8,128)(2,1)S(1)}, bf16[144,2304]{1,0:T(8,128)(2,1)S(1)}, u32[]{:S(2)}, u32[]{:S(2)}) collective-permute-start(bf16[144,2304]{1,0:T(8,128)(2,1)S(1)} %slice.220), channel_id=1, source_target_pairs={{0,16},{4,20},{8,24},{12,28},{16,0},{20,4},{24,8},{28,12},{1,17},{... | collective-permute-start | bytes 1990664 | tf_op jit(solution)/shard_map/ppermute | solution.py:62
  167.9 56.5 %collective-permute-start.34 = (bf16[144,2304]{1,0:T(8,128)(2,1)S(1)}, bf16[144,2304]{1,0:T(8,128)(2,1)}, u32[]{:S(2)}, u32[]{:S(2)}) collective-permute-start(bf16[144,2304]{1,0:T(8,128)(2,1)S(1)} %slice.221), channel_id=1, source_target_pairs={{0,8},{4,12},{8,0},{12,4},{16,24},{20,28},{24,16},{28,20},{1,9},{5... | collective-permute-start | bytes 1990664 | tf_op jit(solution)/shard_map/ppermute | solution.py:62
  168.4 60.3 %collective-permute-start.45 = (bf16[288,2304]{1,0:T(8,128)(2,1)S(1)}, bf16[288,2304]{1,0:T(8,128)(2,1)S(1)}, u32[]{:S(2)}, u32[]{:S(2)}) collective-permute-start(bf16[288,2304]{1,0:T(8,128)(2,1)S(1)} %collective-permute-done.40.refs_1_), channel_id=1, source_target_pairs={{0,4},{4,0},{8,12},{12,8},{16,20},{20,16},{24,28},{28,24},{1,5},{5... | collective-permute-start | bytes 3981320 | tf_op jit(solution)/shard_map/ppermute | solution.py:62
  195.8 33.3 %collective-permute-start.46 = (bf16[288,2304]{1,0:T(8,128)(2,1)S(1)}, bf16[288,2304]{1,0:T(8,128)(2,1)S(1)}, u32[]{:S(2)}, u32[]{:S(2)}) collective-permute-start(bf16[288,2304]{1,0:T(8,128)(2,1)S(1)} %collective-permute-done.41.refs_2_), channel_id=1, source_target_pairs={{0,4},{4,0},{8,12},{12,8},{16,20},{20,16},{24,28},{28,24},{1,5},{5... | collective-permute-start | bytes 3981320 | tf_op jit(solution)/shard_map/ppermute | solution.py:62
  197.1 27.6 %collective-permute-start.47 = (bf16[144,2304]{1,0:T(8,128)(2,1)S(1)}, bf16[144,2304]{1,0:T(8,128)(2,1)S(1)}, u32[]{:S(2)}, u32[]{:S(2)}) collective-permute-start(bf16[144,2304]{1,0:T(8,128)(2,1)S(1)} %collective-permute-done.42.refs_3_), channel_id=1, source_target_pairs={{0,4},{4,0},{8,12},{12,8},{16,20},{20,16},{24,28},{28,24},{1,5},{5... | collective-permute-start | bytes 1990664 | tf_op jit(solution)/shard_map/ppermute | solution.py:62
  224.4 330.3 %collective-permute-start.35 = (bf16[288,2304]{1,0:T(8,128)(2,1)}, bf16[288,2304]{1,0:T(8,128)(2,1)}, u32[]{:S(2)}, u32[]{:S(2)}) collective-permute-start(bf16[288,2304]{1,0:T(8,128)(2,1)} %refs_0_), channel_id=1, source_target_pairs={{0,4},{4,0},{8,12},{12,8},{16,20},{20,16},{24,28},{28,24},{1,5},{5... | collective-permute-start | bytes 3981320 | tf_op jit(solution)/shard_map/ppermute | solution.py:62
  224.7 330.0 %collective-permute-start.36 = (bf16[288,2304]{1,0:T(8,128)(2,1)S(1)}, bf16[288,2304]{1,0:T(8,128)(2,1)}, u32[]{:S(2)}, u32[]{:S(2)}) collective-permute-start(bf16[288,2304]{1,0:T(8,128)(2,1)S(1)} %collective-permute-done.31.refs_1_), channel_id=1, source_target_pairs={{0,4},{4,0},{8,12},{12,8},{16,20},{20,16},{24,28},{28,24},{1,5},{5... | collective-permute-start | bytes 3981320 | tf_op jit(solution)/shard_map/ppermute | solution.py:62
  228.5 326.2 %collective-permute-start.37 = (bf16[288,2304]{1,0:T(8,128)(2,1)S(1)}, bf16[288,2304]{1,0:T(8,128)(2,1)}, u32[]{:S(2)}, u32[]{:S(2)}) collective-permute-start(bf16[288,2304]{1,0:T(8,128)(2,1)S(1)} %collective-permute-done.32.refs_2_), channel_id=1, source_target_pairs={{0,4},{4,0},{8,12},{12,8},{16,20},{20,16},{24,28},{28,24},{1,5},{5... | collective-permute-start | bytes 3981320 | tf_op jit(solution)/shard_map/ppermute | solution.py:62
  228.7 326.1 %collective-permute-start.38 = (bf16[144,2304]{1,0:T(8,128)(2,1)S(1)}, bf16[144,2304]{1,0:T(8,128)(2,1)}, u32[]{:S(2)}, u32[]{:S(2)}) collective-permute-start(bf16[144,2304]{1,0:T(8,128)(2,1)S(1)} %collective-permute-done.33.refs_3_), channel_id=1, source_target_pairs={{0,4},{4,0},{8,12},{12,8},{16,20},{20,16},{24,28},{28,24},{1,5},{5... | collective-permute-start | bytes 1990664 | tf_op jit(solution)/shard_map/ppermute | solution.py:62
  230.9 323.8 %collective-permute-start.39 = (bf16[144,2304]{1,0:T(8,128)(2,1)}, bf16[144,2304]{1,0:T(8,128)(2,1)}, u32[]{:S(2)}, u32[]{:S(2)}) collective-permute-start(bf16[144,2304]{1,0:T(8,128)(2,1)} %collective-permute-done.34.refs_4_), channel_id=1, source_target_pairs={{0,4},{4,0},{8,12},{12,8},{16,20},{20,16},{24,28},{28,24},{1,5},{5... | collective-permute-start | bytes 1990664 | tf_op jit(solution)/shard_map/ppermute | solution.py:62
  917.0 233.3 %all-reduce.9.cloned.1.call-start = ((), (), s32[]{:S(2)}) async-start(), calls=%async_computation.5 | async-start | bytes 4718592 | tf_op jit(solution)/shard_map/psum | solution.py:900
  1055.4 136.3 %reduce-scatter.3.cloned.1.call-start = ((), (), s32[]{:S(2)}) async-start(), calls=%async_computation.6 | async-start | bytes 11943936 | tf_op jit(solution)/shard_map/reduce_scatter | solution.py:902
  1067.1 276.8 %reduce-scatter.5.cloned.1.call-start = ((), (), s32[]{:S(2)}) async-start(), calls=%async_computation.8 | async-start | bytes 11943936 | tf_op jit(solution)/shard_map/reduce_scatter | solution.py:933
  1102.3 32.0 %collective-permute-start.50 = (bf16[144,2304]{1,0:T(8,128)(2,1)}, bf16[144,2304]{1,0:T(8,128)(2,1)S(1)}, u32[]{:S(2)}, u32[]{:S(2)}) collective-permute-start(bf16[144,2304]{1,0:T(8,128)(2,1)} %get-tuple-element.163), channel_id=1, source_target_pairs={{0,16},{4,20},{8,24},{12,28},{16,0},{20,4},{24,8},{28,12},{1,17},{... | collective-permute-start | bytes 1990664 | tf_op jit(solution)/shard_map/ppermute | solution.py:62
  1103.8 32.0 %collective-permute-start.51 = (bf16[144,2304]{1,0:T(8,128)(2,1)}, bf16[144,2304]{1,0:T(8,128)(2,1)}, u32[]{:S(2)}, u32[]{:S(2)}) collective-permute-start(bf16[144,2304]{1,0:T(8,128)(2,1)} %get-tuple-element.162), channel_id=1, source_target_pairs={{0,8},{4,12},{8,0},{12,4},{16,24},{20,28},{24,16},{28,20},{1,9},{5... | collective-permute-start | bytes 1990664 | tf_op jit(solution)/shard_map/ppermute | solution.py:62
  1150.3 41.5 %collective-permute-start.52 = (bf16[288,2304]{1,0:T(8,128)(2,1)}, bf16[288,2304]{1,0:T(8,128)(2,1)S(1)}, u32[]{:S(2)}, u32[]{:S(2)}) collective-permute-start(bf16[288,2304]{1,0:T(8,128)(2,1)} %get-tuple-element.131), channel_id=1, source_target_pairs={{0,8},{4,12},{8,0},{12,4},{16,24},{20,28},{24,16},{28,20},{1,9},{5... | collective-permute-start | bytes 3981320 | tf_op jit(solution)/shard_map/ppermute | solution.py:62
  1151.7 40.0 %collective-permute-start.53 = (bf16[288,2304]{1,0:T(8,128)(2,1)}, bf16[288,2304]{1,0:T(8,128)(2,1)}, u32[]{:S(2)}, u32[]{:S(2)}) collective-permute-start(bf16[288,2304]{1,0:T(8,128)(2,1)} %get-tuple-element.132), channel_id=1, source_target_pairs={{0,16},{4,20},{8,24},{12,28},{16,0},{20,4},{24,8},{28,12},{1,17},{... | collective-permute-start | bytes 3981320 | tf_op jit(solution)/shard_map/ppermute | solution.py:62
  1249.8 108.6 %all-reduce.11.cloned.1.call-start = ((), (), s32[]{:S(2)}) async-start(), calls=%async_computation.7 | async-start | bytes 4718592 | tf_op jit(solution)/shard_map/psum | solution.py:932
  1266.3 32.2 %collective-permute-start.73 = (f32[1,4,288]{2,1,0:T(4,128)S(1)}, f32[1,4,288]{2,1,0:T(4,128)S(1)}, u32[]{:S(2)}, u32[]{:S(2)}) collective-permute-start(f32[1,4,288]{2,1,0:T(4,128)S(1)} %slice_select_fusion.2), channel_id=1, source_target_pairs={{0,4},{4,0},{8,12},{12,8},{16,20},{20,16},{24,28},{28,24},{1,5},{5... | collective-permute-start | bytes 13832 | tf_op jit(solution)/shard_map/ppermute | solution.py:62
  1291.6 31.0 %collective-permute-start.61 = (bf16[288,1024]{1,0:T(8,128)(2,1)S(1)}, bf16[288,1024]{1,0:T(8,128)(2,1)S(1)}, u32[]{:S(2)}, u32[]{:S(2)}) collective-permute-start(bf16[288,1024]{1,0:T(8,128)(2,1)S(1)} %pad_maximum_fusion.2), channel_id=1, source_target_pairs={{0,8},{4,12},{8,0},{12,4},{16,24},{20,28},{24,16},{28,20},{1,9},{5... | collective-permute-start | bytes 1769480 | tf_op jit(solution)/shard_map/ppermute | solution.py:62
  1292.1 30.5 %collective-permute-start.63 = (bf16[288,1024]{1,0:T(8,128)(2,1)S(1)}, bf16[288,1024]{1,0:T(8,128)(2,1)S(1)}, u32[]{:S(2)}, u32[]{:S(2)}) collective-permute-start(bf16[288,1024]{1,0:T(8,128)(2,1)S(1)} %pad_maximum_fusion.3), channel_id=1, source_target_pairs={{0,16},{4,20},{8,24},{12,28},{16,0},{20,4},{24,8},{28,12},{1,17},{... | collective-permute-start | bytes 1769480 | tf_op jit(solution)/shard_map/ppermute | solution.py:62
  (96 other events, 1578.2 us)
Sparse Core Ops, SparseCore 0:
  117.0 96.3 all-reduce.4
  917.1 94.8 all-reduce.6
  1055.6 94.6 all-reduce.8
  1263.1 95.1 all-reduce.10
Sparse Core Ops, SparseCore 1:
  119.3 109.2 all-gather.1
  1067.2 103.1 reduce-scatter.2
  1237.4 106.4 reduce-scatter.4

commit v3 on v2

--- a/solution.py
+++ b/solution.py
@@ -11,6 +11,7 @@
 HALF = 128
 WINDOW = 4096
 KEY_CHUNK = 4096
+MOST = 60 * 2**20
 
 
 epsilon = 1e-06
@@ -40,7 +41,11 @@
     return lax.optimization_barrier((value,) + others)[0]
 
 
-def call(kernel, out_shape, args, name, scalars=0, scratch=(), flops=0, mem=60, space=None):
+def tie_all(values, *others):
+    return lax.optimization_barrier((*values, *others))[: len(values)]
+
+
+def call(kernel, out_shape, args, name, scalars=0, scratch=(), flops=0, mem=32, space=None):
     spec = pl.BlockSpec(memory_space=pltpu.VMEM if space is None else space)
     outs = jax.tree.map(lambda _: spec, out_shape)
     size = sum(a.size * a.dtype.itemsize for a in args)
@@ -84,25 +89,34 @@
     return jnp.stack(places).astype(jnp.int32) + jnp.array(shift, jnp.int32)
 
 
+def places_of(pieces):
+    return piece_rows(pieces[0].shape[0]) if len(pieces) > 1 else jnp.zeros((1,), jnp.int32)
+
+
+def place(rows_ref, pieces, whole_ref):
+    for k, piece in enumerate(pieces):
+        whole_ref[pl.ds(pl.multiple_of(rows_ref[k], 16), piece.shape[0]), :] = piece[...]
+
+
 def assemble_kernel(rows_ref, *refs):
-    *pieces, whole, sems = refs
-    copies = []
-    for k, piece in enumerate(pieces):
-        first = pl.multiple_of(rows_ref[k], 16)
-        copy = pltpu.make_async_copy(piece, whole.at[pl.ds(first, piece.shape[0])], sems.at[k])
-        copy.start()
-        copies.append(copy)
-    for copy in copies:
-        copy.wait()
-
-
-def assemble(pieces):
+    place(rows_ref, refs[:-1], refs[-1])
+
+
+def assemble(pieces, grid=1):
+    if len(pieces) == 1:
+        return pieces[0]
     rows, width = pieces[0].shape
-    shape = jax.ShapeDtypeStruct((8 * rows, width), pieces[0].dtype)
-    return call(
-        assemble_kernel, shape, (piece_rows(rows), *pieces), "assemble", scalars=1,
-        scratch=[pltpu.SemaphoreType.DMA((len(pieces),))], space=pl.ANY,
-    )
+    column = lambda n: pl.BlockSpec((n, width // grid), lambda i: (0, i))
+    return pl.pallas_call(
+        assemble_kernel,
+        out_shape=jax.ShapeDtypeStruct((8 * rows, width), pieces[0].dtype),
+        grid=(grid,),
+        in_specs=[pl.BlockSpec(memory_space=pltpu.SMEM)] + [column(p.shape[0]) for p in pieces],
+        out_specs=column(8 * rows),
+        compiler_params=pltpu.CompilerParams(vmem_limit_bytes=MOST),
+        cost_estimate=pl.CostEstimate(flops=0, bytes_accessed=32 * rows * width, transcendentals=0),
+        name="assemble",
+    )(piece_rows(rows), *pieces)
 
 
 def scatter_corner(own, by_x, by_y, corner):
@@ -140,21 +154,6 @@
     for term in terms[1:]:
         total = total + term.astype(jnp.float32)
     return total
-
-
-def gather_gains(piece):
-    if not paired():
-        return lax.all_gather(piece, "ctx", axis=1, tiled=True)
-    me = lax.axis_index("ctx")
-
-    def ordered(bit, mine, other):
-        low = (me & bit) == 0
-        return jnp.concatenate([jnp.where(low, mine, other), jnp.where(low, other, mine)], axis=0)
-
-    chip = ordered(1, piece[None], swap(piece[None], 1))
-    row = ordered(2, chip, swap(chip, 2))
-    stack = ordered(4, row, ordered(2, swap(chip, 4), swap(chip, 6)))
-    return stack.transpose(1, 0, 2).reshape(piece.shape[0], 8 * piece.shape[1])
 
 
 def scatter_gains(whole):
@@ -181,22 +180,23 @@
     return value
 
 
-def pack_kernel(a_ref, b_ref, c_ref, out_ref):
+def pack_kernel(a_ref, b_ref, c_ref, gains_ref, out_ref):
     one, two = a_ref.shape[1], a_ref.shape[1] + b_ref.shape[1]
+    three = two + c_ref.shape[1]
     out_ref[:, :one] = a_ref[...]
     out_ref[:, one:two] = b_ref[...]
-    out_ref[:, two:] = c_ref[...]
-
-
-def pack(first, second, third):
-    width = first.shape[1] + second.shape[1] + third.shape[1]
+    out_ref[:, two:three] = c_ref[...]
+    out_ref[:, three:] = jnp.broadcast_to(gains_ref[:, :1], (gains_ref.shape[0], HALF))
+    for k in range(1, gains_ref.shape[1]):
+        lane = lax.broadcasted_iota(jnp.int32, (gains_ref.shape[0], HALF), 1)
+        column = jnp.broadcast_to(gains_ref[:, k : k + 1], lane.shape)
+        out_ref[:, three:] = jnp.where(lane == k, column, out_ref[:, three:])
+
+
+def pack(first, second, third, gains):
+    width = first.shape[1] + second.shape[1] + third.shape[1] + HALF
     shape = jax.ShapeDtypeStruct((first.shape[0], width), first.dtype)
-    return call(pack_kernel, shape, (first, second, third), "pack")
-
-
-def place(rows_ref, pieces, whole_ref):
-    for k, piece in enumerate(pieces):
-        whole_ref[pl.ds(pl.multiple_of(rows_ref[k], 16), piece.shape[0]), :] = piece[...]
+    return call(pack_kernel, shape, (first, second, third, gains), "pack")
 
 
 def project_kernel(rows_ref, in_ref, cos_ref, sin_ref, *refs, heads, parts):
@@ -206,8 +206,10 @@
         place(rows_ref, pieces, full_ref)
     else:
         full_ref = pieces[0]
+    gain = full_ref[:, (heads + 2) * HD : (heads + 2) * HD + 1].astype(jnp.float32)
     for n in range(heads + 2):
-        raw = matmul(in_ref[...], full_ref[:, n * HD : (n + 1) * HD])
+        weight = (full_ref[:, n * HD : (n + 1) * HD].astype(jnp.float32) * gain).astype(jnp.bfloat16)
+        raw = matmul(in_ref[...], weight)
         if n <= heads:
             low, high = raw[:, :HALF], raw[:, HALF:]
             cosine, sine = cos_ref[...], sin_ref[...]
@@ -226,18 +228,12 @@
     rows, depth = normed.shape
     width = pieces[0].shape[1]
     low = lambda n: jax.ShapeDtypeStruct((rows, n), jnp.bfloat16)
-    shapes = [low(heads * HD), low(2 * HD)]
-    if len(pieces) > 1:
-        shapes.append(jax.ShapeDtypeStruct((depth, width), jnp.bfloat16))
-        places = piece_rows(pieces[0].shape[0])
-    else:
-        places = jnp.zeros((1,), jnp.int32)
-    found = call(
-        partial(project_kernel, heads=heads, parts=len(pieces)), tuple(shapes),
-        (places, normed, cosine, sine, *pieces), "project", scalars=1,
+    scratch = [pltpu.VMEM((depth, width), jnp.bfloat16)] if len(pieces) > 1 else []
+    return call(
+        partial(project_kernel, heads=heads, parts=len(pieces)), (low(heads * HD), low(2 * HD)),
+        (places_of(pieces), normed, cosine, sine, *pieces), "project", scalars=1, scratch=scratch,
         flops=2 * rows * depth * width,
     )
-    return found if len(pieces) > 1 else (*found, pieces[0])
 
 
 def out_project_kernel(rows_ref, attn_ref, *refs, parts):
@@ -254,17 +250,12 @@
 
 def out_project(attn, pieces, depth):
     rows, width = attn.shape
-    shapes = [jax.ShapeDtypeStruct((rows, depth), jnp.bfloat16)]
-    if len(pieces) > 1:
-        shapes.append(jax.ShapeDtypeStruct((depth, width), jnp.bfloat16))
-        places = piece_rows(pieces[0].shape[0])
-    else:
-        places = jnp.zeros((1,), jnp.int32)
-    found = call(
-        partial(out_project_kernel, parts=len(pieces)), tuple(shapes), (places, attn, *pieces),
-        "out_project", scalars=1, flops=2 * rows * depth * width,
-    )
-    return found if len(pieces) > 1 else (*found, pieces[0])
+    scratch = [pltpu.VMEM((depth, width), jnp.bfloat16)] if len(pieces) > 1 else []
+    return call(
+        partial(out_project_kernel, parts=len(pieces)),
+        jax.ShapeDtypeStruct((rows, depth), jnp.bfloat16), (places_of(pieces), attn, *pieces),
+        "out_project", scalars=1, scratch=scratch, flops=2 * rows * depth * width,
+    )
 
 
 def join_kernel(cos_ref, sin_ref, query_ref, full_ref, *refs):
@@ -280,13 +271,13 @@
     low_ref[:, width + HALF : width + HD] = (high * cosine - low * sine).astype(jnp.bfloat16)
     low_ref[:, width + HD :] = total[:, HD:].astype(jnp.bfloat16)
     for n in range(0, part_ref.shape[1], 256):
-        part = matmul_nt(low_ref[...], full_ref[n : n + 256, :])
+        part = matmul_nt(low_ref[...], full_ref[n : n + 256, : low_ref.shape[1]])
         part_ref[:, n : n + 256] = part.astype(jnp.bfloat16)
 
 
 def join(cosine, sine, query_low, full_qkv, terms):
     rows = query_low.shape[0]
-    depth, width = full_qkv.shape
+    depth, width = full_qkv.shape[0], query_low.shape[1] + 2 * HD
     low = lambda n: jax.ShapeDtypeStruct((rows, n), jnp.bfloat16)
     return call(
         join_kernel, (low(width), low(depth)), (cosine, sine, query_low, full_qkv, *terms), "join",
@@ -400,6 +391,7 @@
 def by_rows(kernel, args, gains, kinds, sums, name, block=128):
     rows, depth = args[0].shape
     tile = pl.BlockSpec((block, depth), lambda i: (i, 0))
+    ahead = pl.BlockSpec((block, depth), lambda i: (i, 0))
     whole = lambda n: pl.BlockSpec((n, depth), lambda i: (0, 0))
     shapes = [jax.ShapeDtypeStruct((rows, depth), kind) for kind in kinds]
     out_specs = [tile] * len(kinds)
@@ -413,44 +405,48 @@
         kernel,
         out_shape=tuple(shapes),
         grid=(rows // block,),
-        in_specs=[tile] * len(args) + [whole(gains.shape[0])],
+        in_specs=[ahead] * len(args) + [whole(gains.shape[0])],
         out_specs=out_specs,
         scratch_shapes=scratch,
-        compiler_params=pltpu.CompilerParams(vmem_limit_bytes=60 * 2**20),
+        compiler_params=pltpu.CompilerParams(vmem_limit_bytes=MOST),
         cost_estimate=pl.CostEstimate(flops=0, bytes_accessed=size, transcendentals=0),
         name=name,
     )(*args, gains)
     return found if len(found) > 1 else found[0]
 
 
-UNITS = 256
+UNITS = 768
+STEP = 256
 
 
 def units_kernel(in_ref, gate_ref, up_ref, hidden_ref, active_ref, slope_ref):
-    gate = matmul(in_ref[...], gate_ref[...])
-    up = matmul(in_ref[...], up_ref[...])
-    root = (2.0 / jnp.pi) ** 0.5
-    square = gate * gate
-    bend = jnp.tanh(root * gate * (1.0 + 0.044715 * square))
-    half = 0.5 * (1.0 + bend)
-    active = gate * half
-    slope = half + 0.5 * gate * (1.0 - bend * bend) * (root * (1.0 + 3 * 0.044715 * square))
-    hidden_ref[...] = (active * up).astype(jnp.bfloat16)
-    active_ref[...] = active.astype(jnp.bfloat16)
-    slope_ref[...] = (slope * up).astype(jnp.bfloat16)
+    for n in range(0, UNITS, STEP):
+        at = slice(n, n + STEP)
+        gate = matmul(in_ref[...], gate_ref[:, at])
+        up = matmul(in_ref[...], up_ref[:, at])
+        root = (2.0 / jnp.pi) ** 0.5
+        square = gate * gate
+        bend = jnp.tanh(root * gate * (1.0 + 0.044715 * square))
+        half = 0.5 * (1.0 + bend)
+        active = gate * half
+        slope = half + 0.5 * gate * (1.0 - bend * bend) * (root * (1.0 + 3 * 0.044715 * square))
+        hidden_ref[:, at] = (active * up).astype(jnp.bfloat16)
+        active_ref[:, at] = active.astype(jnp.bfloat16)
+        slope_ref[:, at] = (slope * up).astype(jnp.bfloat16)
 
 
 def units(normed, full_gate, full_up):
     rows, depth = normed.shape
     count = full_gate.shape[1]
     column = lambda n: pl.BlockSpec((n, UNITS), lambda i: (0, i))
+    ahead = pl.BlockSpec((depth, UNITS), lambda i: (0, i))
     return pl.pallas_call(
         units_kernel,
         out_shape=tuple(jax.ShapeDtypeStruct((rows, count), jnp.bfloat16) for _ in range(3)),
         grid=(count // UNITS,),
-        in_specs=[pl.BlockSpec((rows, depth), lambda i: (0, 0)), column(depth), column(depth)],
+        in_specs=[pl.BlockSpec((rows, depth), lambda i: (0, 0)), ahead, ahead],
         out_specs=[column(rows)] * 3,
-        compiler_params=pltpu.CompilerParams(vmem_limit_bytes=60 * 2**20),
+        compiler_params=pltpu.CompilerParams(vmem_limit_bytes=MOST),
         cost_estimate=pl.CostEstimate(
             flops=4 * rows * depth * count, bytes_accessed=4 * depth * count,
             transcendentals=rows * count,
@@ -460,7 +456,9 @@
 
 
 def down_kernel(hidden_ref, down_ref, out_ref):
-    out_ref[...] = matmul_nt(hidden_ref[...], down_ref[...]).astype(jnp.bfloat16)
+    for n in range(0, UNITS, STEP):
+        part = matmul_nt(hidden_ref[...], down_ref[n : n + STEP, :])
+        out_ref[:, n : n + STEP] = part.astype(jnp.bfloat16)
 
 
 def project_down(hidden, full_down_t):
@@ -475,7 +473,7 @@
             pl.BlockSpec((UNITS, count), lambda i: (i, 0)),
         ],
         out_specs=pl.BlockSpec((rows, UNITS), lambda i: (0, i)),
-        compiler_params=pltpu.CompilerParams(vmem_limit_bytes=60 * 2**20),
+        compiler_params=pltpu.CompilerParams(vmem_limit_bytes=MOST),
         cost_estimate=pl.CostEstimate(
             flops=2 * rows * depth * count, bytes_accessed=2 * depth * count, transcendentals=0
         ),
@@ -483,47 +481,57 @@
     )(hidden, full_down_t)
 
 
-def units_back_kernel(
-    grad_ref, down_ref, gate_ref, up_ref, active_ref, slope_ref, dg_ref, du_ref, out_ref, acc_ref
-):
-    @pl.when(pl.program_id(0) == 0)
-    def _():
-        acc_ref[...] = jnp.zeros_like(acc_ref)
-
-    hidden_grad = matmul(grad_ref[...], down_ref[...])
-    gate_low = (hidden_grad * slope_ref[...].astype(jnp.float32)).astype(jnp.bfloat16)
-    up_low = (hidden_grad * active_ref[...].astype(jnp.float32)).astype(jnp.bfloat16)
-    dg_ref[...] = gate_low
-    du_ref[...] = up_low
-    for n in range(0, acc_ref.shape[1], 256):
-        acc_ref[:, n : n + 256] += matmul_nt(gate_low, gate_ref[n : n + 256, :]) + matmul_nt(
-            up_low, up_ref[n : n + 256, :]
-        )
-
-    @pl.when(pl.program_id(0) == pl.num_programs(0) - 1)
-    def _():
-        out_ref[...] = acc_ref[...].astype(jnp.bfloat16)
-
-
-def units_back(mlp_low, full_down_t, full_gate, full_up, active, slope):
+def units_back_kernel(grad_ref, down_ref, active_ref, slope_ref, dg_ref, du_ref):
+    for n in range(0, UNITS, STEP):
+        at = slice(n, n + STEP)
+        hidden_grad = matmul(grad_ref[...], down_ref[:, at])
+        dg_ref[:, at] = (hidden_grad * slope_ref[:, at].astype(jnp.float32)).astype(jnp.bfloat16)
+        du_ref[:, at] = (hidden_grad * active_ref[:, at].astype(jnp.float32)).astype(jnp.bfloat16)
+
+
+def units_back(mlp_low, full_down_t, active, slope):
     rows, depth = mlp_low.shape
     count = active.shape[1]
     column = lambda n: pl.BlockSpec((n, UNITS), lambda i: (0, i))
-    whole = pl.BlockSpec((rows, depth), lambda i: (0, 0))
-    low = lambda n: jax.ShapeDtypeStruct((rows, n), jnp.bfloat16)
+    ahead = pl.BlockSpec((depth, UNITS), lambda i: (0, i))
     return pl.pallas_call(
         units_back_kernel,
-        out_shape=(low(count), low(count), low(depth)),
+        out_shape=tuple(jax.ShapeDtypeStruct((rows, count), jnp.bfloat16) for _ in range(2)),
         grid=(count // UNITS,),
-        in_specs=[whole, column(depth), column(depth), column(depth), column(rows), column(rows)],
-        out_specs=[column(rows), column(rows), whole],
-        scratch_shapes=[pltpu.VMEM((rows, depth), jnp.float32)],
-        compiler_params=pltpu.CompilerParams(vmem_limit_bytes=60 * 2**20),
+        in_specs=[pl.BlockSpec((rows, depth), lambda i: (0, 0)), ahead, column(rows), column(rows)],
+        out_specs=[column(rows)] * 2,
+        compiler_params=pltpu.CompilerParams(vmem_limit_bytes=MOST),
         cost_estimate=pl.CostEstimate(
-            flops=6 * rows * depth * count, bytes_accessed=6 * depth * count, transcendentals=0
+            flops=2 * rows * depth * count, bytes_accessed=2 * depth * count, transcendentals=0
         ),
         name="units_back",
-    )(mlp_low, full_down_t, full_gate, full_up, active, slope)
+    )(mlp_low, full_down_t, active, slope)
+
+
+def features_back_kernel(dg_ref, du_ref, gate_ref, up_ref, out_ref):
+    for n in range(0, UNITS, STEP):
+        at = slice(n, n + STEP)
+        part = matmul_nt(dg_ref[...], gate_ref[at, :]) + matmul_nt(du_ref[...], up_ref[at, :])
+        out_ref[:, at] = part.astype(jnp.bfloat16)
+
+
+def features_back(gate_low, up_low, full_gate, full_up):
+    rows, count = gate_low.shape
+    depth = full_gate.shape[0]
+    whole = pl.BlockSpec((rows, count), lambda i: (0, 0))
+    tile = pl.BlockSpec((UNITS, count), lambda i: (i, 0))
+    return pl.pallas_call(
+        features_back_kernel,
+        out_shape=jax.ShapeDtypeStruct((rows, depth), jnp.bfloat16),
+        grid=(depth // UNITS,),
+        in_specs=[whole, whole, tile, tile],
+        out_specs=pl.BlockSpec((rows, UNITS), lambda i: (0, i)),
+        compiler_params=pltpu.CompilerParams(vmem_limit_bytes=MOST),
+        cost_estimate=pl.CostEstimate(
+            flops=4 * rows * depth * count, bytes_accessed=4 * depth * count, transcendentals=0
+        ),
+        name="features_back",
+    )(gate_low, up_low, full_gate, full_up)
 
 
 def slot_block(map_ref, me, slot, swapped):
@@ -562,28 +570,45 @@
         count = block_list(lookup, key_blocks, own, seq_blocks, reach, list_ref)
 
         def pair(step, carry):
-            tile(b, list_ref[2 * step], None)
-            tile(b, list_ref[2 * step + 1], None)
+            tile(b, (list_ref[2 * step], list_ref[2 * step + 1]), None)
             return carry
 
         lax.fori_loop(0, count // 2, pair, 0)
 
         @pl.when(count % 2 == 1)
         def _():
-            tile(b, list_ref[count - 1], None)
+            tile(b, (list_ref[count - 1],), None)
 
         diagonal = find_block(lookup, key_blocks, own)
 
         @pl.when(diagonal >= 0)
         def _():
-            tile(b, diagonal, query_no >= key_no)
+            tile(b, (diagonal,), query_no >= key_no)
 
         if reach < seq_blocks:
             edge = find_block(lookup, key_blocks, own - reach)
 
             @pl.when((edge >= 0) & (own % seq_blocks >= reach))
             def _():
-                tile(b, edge, query_no < key_no)
+                tile(b, (edge,), query_no < key_no)
+
+
+def turn_kernel(*refs):
+    *pieces, whole_ref, turned_ref = refs
+    row = 0
+    for piece in pieces:
+        count = piece.shape[0]
+        whole_ref[row : row + count, :] = piece[...]
+        turned_ref[:, row : row + count] = piece[:, :HD].T
+        row += count
+
+
+def turn(pieces):
+    if len(pieces) == 1:
+        return pieces[0], pieces[0][:, :HD].T
+    total = sum(piece.shape[0] for piece in pieces)
+    low = lambda a, b: jax.ShapeDtypeStruct((a, b), jnp.bfloat16)
+    return call(turn_kernel, (low(total, 2 * HD), low(HD, total)), pieces, "turn")
 
 
 def attend_kernel(
@@ -608,23 +633,24 @@
         acc_ref[...] = jnp.zeros_like(acc_ref)
         sum_ref[...] = jnp.zeros_like(sum_ref)
 
-    def tile(b, slot, mask):
-        rows = pl.ds(pl.multiple_of(slot * blk, blk), blk)
-        keys = kv_ref[rows, :HD]
-        vals = kv_ref[rows, HD:]
+    def tile(b, slots, mask):
+        rows = [pl.ds(pl.multiple_of(slot * blk, blk), blk) for slot in slots]
+        cols = slice(b * blk, (b + 1) * blk)
         for h in range(heads):
-            query = q_ref[b * blk : (b + 1) * blk, h * HD : (h + 1) * HD]
-            capped = jnp.tanh(matmul_nt(query, keys) * (1.0 / soft_cap))
-            weights = jnp.exp2(capped * (soft_cap * LOG2E))
-            if mask is not None:
-                weights = jnp.where(mask, weights, 0.0)
-            at = (slice(b * blk, (b + 1) * blk), slice(h * HD, (h + 1) * HD))
-            lanes = (slice(b * blk, (b + 1) * blk), slice(h * 128, (h + 1) * 128))
-            part = weights[:, :128]
-            for piece in range(1, blk // 128):
-                part = part + weights[:, piece * 128 : (piece + 1) * 128]
-            sum_ref[lanes] += part
-            acc_ref[at] += matmul(weights.astype(jnp.bfloat16), vals)
+            query = q_ref[cols, h * HD : (h + 1) * HD]
+            part = result = None
+            for row in rows:
+                capped = jnp.tanh(matmul_nt(query, kv_ref[row, :HD]) * (1.0 / soft_cap))
+                weights = jnp.exp2(capped * (soft_cap * LOG2E))
+                if mask is not None:
+                    weights = jnp.where(mask, weights, 0.0)
+                for piece in range(0, blk, 128):
+                    term = weights[:, piece : piece + 128]
+                    part = term if part is None else part + term
+                term = matmul(weights.astype(jnp.bfloat16), kv_ref[row, HD:])
+                result = term if result is None else result + term
+            sum_ref[cols, h * 128 : (h + 1) * 128] += part
+            acc_ref[cols, h * HD : (h + 1) * HD] += result
 
     visit_blocks(
         map_ref, me_ref[0], chunk, q_blocks, key_blocks, seq_blocks, reach, parts > 1, list_ref,
@@ -664,9 +690,8 @@
         jax.ShapeDtypeStruct((rows, width), jnp.bfloat16),
         jax.ShapeDtypeStruct((rows, heads * 128), jnp.float32),
     ]
-    if joined:
-        out_shape.append(jax.ShapeDtypeStruct((total, 2 * HD), jnp.bfloat16))
-    found = pl.pallas_call(
+    held = [pltpu.VMEM((total, 2 * HD), jnp.bfloat16)] if joined else []
+    return pl.pallas_call(
         kernel,
         out_shape=tuple(out_shape),
         grid_spec=pltpu.PrefetchScalarGridSpec(
@@ -675,27 +700,27 @@
             in_specs=[pl.BlockSpec((rows, width), whole), *kv_specs],
             out_specs=[pl.BlockSpec(shape.shape, whole) for shape in out_shape],
             scratch_shapes=[
+                *held,
                 pltpu.VMEM((rows, width), jnp.float32),
                 pltpu.VMEM((rows, heads * 128), jnp.float32),
                 pltpu.SMEM((chunk_rows // blk + 1,), jnp.int32),
             ],
         ),
-        compiler_params=pltpu.CompilerParams(vmem_limit_bytes=60 * 2**20),
+        compiler_params=pltpu.CompilerParams(vmem_limit_bytes=MOST),
         cost_estimate=pl.CostEstimate(
             flops=4 * rows * width * total, bytes_accessed=8 * rows * width + 8 * total * HD,
             transcendentals=2 * rows * heads * total,
         ),
         name="attend",
     )(block_map, me, queries, *pieces)
-    return found if joined else (*found, pieces[0])
 
 
 def attend_back_kernel(
     map_ref, me_ref, da_ref, out_ref, o_ref, l_ref, q_ref, kv_ref, kt_ref, cos_ref, sin_ref, *refs,
     blk, heads, swapped, key_blocks, seq_blocks, reach
 ):
-    dq_ref, *dkv_refs = refs[: 3 if swapped else 2]
-    do_ref, stat_ref, dqt_ref, dk_ref, dv_ref, list_ref = refs[3 if swapped else 2 :]
+    dq_ref, *dkv_refs = refs[: 5 if swapped else 2]
+    do_ref, stat_ref, dqt_ref, dk_ref, dv_ref, list_ref = refs[5 if swapped else 2 :]
     chunk = pl.program_id(0)
     q_blocks = q_ref.shape[0] // blk
 
@@ -715,31 +740,32 @@
     dk_ref[...] = jnp.zeros_like(dk_ref)
     dv_ref[...] = jnp.zeros_like(dv_ref)
 
-    def tile(b, slot, mask):
-        rows = pl.ds(pl.multiple_of(slot * blk, blk), blk)
-        keys = kv_ref[rows, :HD]
-        vals = kv_ref[rows, HD:]
-        turned = kt_ref[:, rows]
+    def tile(b, slots, mask):
+        rows = [pl.ds(pl.multiple_of(slot * blk, blk), blk) for slot in slots]
         cols = slice(b * blk, (b + 1) * blk)
+        dk_parts, dv_parts = [None] * len(rows), [None] * len(rows)
+        dq_parts = [None] * heads
+        add = lambda total, term: term if total is None else total + term
         for h in range(heads):
             query = q_ref[cols, h * HD : (h + 1) * HD]
             out_grad = do_ref[cols, h * HD : (h + 1) * HD]
-            tangent = jnp.tanh(matmul_nt(keys, query) * (1.0 / soft_cap))
-            probs = jnp.exp2(tangent * (soft_cap * LOG2E) - stat_ref[h : h + 1, cols])
-            if mask is not None:
-                probs = jnp.where(mask, probs, 0.0)
-            prob_grad = matmul_nt(vals, out_grad)
-            score = (
-                probs * (prob_grad - stat_ref[heads + h : heads + h + 1, cols])
-                * (1.0 - tangent * tangent)
-            ).astype(jnp.bfloat16)
-            dk_new = matmul(score, query)
-            dv_new = matmul(probs.astype(jnp.bfloat16), out_grad)
-            dk_part = dk_new if h == 0 else dk_part + dk_new
-            dv_part = dv_new if h == 0 else dv_part + dv_new
-            dqt_ref[h * HD : (h + 1) * HD, cols] += matmul(turned, score)
-        dk_ref[rows, :] += dk_part
-        dv_ref[rows, :] += dv_part
+            log_total = stat_ref[h : h + 1, cols]
+            delta = stat_ref[heads + h : heads + h + 1, cols]
+            for k, row in enumerate(rows):
+                tangent = jnp.tanh(matmul_nt(kv_ref[row, :HD], query) * (1.0 / soft_cap))
+                probs = jnp.exp2(tangent * (soft_cap * LOG2E) - log_total)
+                if mask is not None:
+                    probs = jnp.where(mask, probs, 0.0)
+                prob_grad = matmul_nt(kv_ref[row, HD:], out_grad)
+                score = (probs * (prob_grad - delta) * (1.0 - tangent * tangent)).astype(jnp.bfloat16)
+                dk_parts[k] = add(dk_parts[k], matmul(score, query))
+                dv_parts[k] = add(dv_parts[k], matmul(probs.astype(jnp.bfloat16), out_grad))
+                dq_parts[h] = add(dq_parts[h], matmul(kt_ref[:, row], score))
+        for h in range(heads):
+            dqt_ref[h * HD : (h + 1) * HD, cols] += dq_parts[h]
+        for k, row in enumerate(rows):
+            dk_ref[row, :] += dk_parts[k]
+            dv_ref[row, :] += dv_parts[k]
 
     visit_blocks(
         map_ref, me_ref[0], chunk, q_blocks, key_blocks, seq_blocks, reach, swapped, list_ref,
@@ -779,9 +805,11 @@
         seq_blocks=seq_blocks, reach=WINDOW // blk,
     )
     whole = lambda i, *_: (0, 0)
-    part = total // 2 if swapped else total
-    dkv_shapes = [jax.ShapeDtypeStruct((part, 2 * HD), jnp.bfloat16)] * (2 if swapped else 1)
-    dkv_specs = [pl.BlockSpec((min(part, chunk_rows), 2 * HD), lambda i, *_: (i, 0))] * len(dkv_shapes)
+    parts = [3 * rows, rows, 3 * rows, rows] if swapped else [total]
+    dkv_shapes = [jax.ShapeDtypeStruct((part, 2 * HD), jnp.bfloat16) for part in parts]
+    dkv_specs = [
+        pl.BlockSpec((min(part, chunk_rows), 2 * HD), lambda i, *_: (i, 0)) for part in parts
+    ]
     return pl.pallas_call(
         kernel,
         out_shape=(jax.ShapeDtypeStruct((rows, width), jnp.bfloat16), *dkv_shapes),
@@ -809,7 +837,7 @@
                 pltpu.SMEM((chunk_rows // blk + 1,), jnp.int32),
             ],
         ),
-        compiler_params=pltpu.CompilerParams(vmem_limit_bytes=60 * 2**20),
+        compiler_params=pltpu.CompilerParams(vmem_limit_bytes=MOST),
         cost_estimate=pl.CostEstimate(
             flops=10 * rows * width * total, bytes_accessed=16 * rows * width + 10 * total * HD,
             transcendentals=2 * rows * heads * total,
@@ -837,16 +865,12 @@
     flat_map = block_map.reshape(-1).astype(jnp.int32)
     pairs = paired()
 
-    gains = gather_gains(norm_gains).astype(jnp.float32)
+    qkv_shard = pack(w_query, w_key, w_value, norm_gains.T)
     if pairs:
-        qkv_shard = pack(w_query, w_key, w_value)
-        near = lax.optimization_barrier((*nearby(qkv_shard), gains))
-        gains = near[2]
-        qkv_pieces = gather_pieces(qkv_shard, near[:2])
+        qkv_pieces = gather_pieces(qkv_shard)
         out_shard = tie(w_out, qkv_pieces[3], qkv_pieces[4]).T
         out_near = nearby(out_shard)
     else:
-        qkv_shard = jnp.concatenate([w_query, w_key, w_value], axis=1)
         qkv_pieces = (lax.all_gather(qkv_shard, "ctx", axis=0, tiled=True),)
         out_pieces = (lax.all_gather(w_out.T, "ctx", axis=0, tiled=True),)
     own_ids = lax.dynamic_index_in_dim(block_map, me, 0, keepdims=False)
@@ -855,8 +879,8 @@
     cosine, sine = angle_tables(own_index % seq_len)
     inputs = tokens.astype(jnp.float32)
     in_scale = rms_scale(inputs)
-    normed_in = (inputs * in_scale * gains[0]).astype(jnp.bfloat16)
-    queries, kv_local, full_qkv = project(normed_in, cosine, sine, qkv_pieces, heads_dev)
+    unit_in = (inputs * in_scale).astype(jnp.bfloat16)
+    queries, kv_local = project(unit_in, cosine, sine, qkv_pieces, heads_dev)
     if pairs:
         kv_local, *out_near = lax.optimization_barrier((kv_local, *out_near))
         kv_pieces = gather_pieces(kv_local)
@@ -868,32 +892,52 @@
     w_gate, w_up, w_down, *_ = lax.optimization_barrier((w_gate, w_up, w_down, *late))
     if pairs:
         gate_near = nearby(w_gate)
-    attended, attn_flat, totals, kv_all = attend(
+    attended, attn_flat, totals = attend(
         flat_map, me_list, queries, kv_pieces, block_rows, seq_blocks
     )
-    branch_part, full_out_t = out_project(attn_flat, out_pieces, depth)
+    branch_part = out_project(attn_flat, out_pieces, depth)
     if pairs:
         branch_part, *gate_near = lax.optimization_barrier((branch_part, *gate_near))
-        full_gate = assemble(gather_pieces(w_gate, gate_near))
+        gate_pieces = gather_pieces(w_gate, gate_near)
+        qkv_pieces = tie_all(qkv_pieces, branch_part)
+    branch = lax.psum(branch_part, "tp")
+    full_up = lax.all_gather(w_up, "ctx", axis=0, tiled=True)
+    full_qkv = assemble(qkv_pieces)
+    gains = full_qkv[:, q_width + 2 * HD : q_width + 2 * HD + 4].T.astype(jnp.float32)
+    normed_in = (inputs * in_scale * gains[0]).astype(jnp.bfloat16)
+    if pairs:
+        down_shard, gains, normed_in, *far = lax.optimization_barrier(
+            (w_down.T, gains, normed_in, *gate_pieces[3:5])
+        )
+        gate_pieces = (*gate_pieces[:3], *far, *gate_pieces[5:])
+        down_near = nearby(down_shard)
+        full_gate = assemble(gate_pieces, 3)
+        full_gate, *down_near = lax.optimization_barrier((full_gate, *down_near))
+        down_pieces = gather_pieces(down_shard, down_near)
     else:
         full_gate = lax.all_gather(w_gate, "ctx", axis=0, tiled=True)
-    branch = lax.psum(branch_part, "tp")
-    full_up = lax.all_gather(w_up, "ctx", axis=0, tiled=True)
-    if pairs:
-        full_down_t = assemble(gather_pieces(w_down.T))
-    else:
-        full_down_t = lax.all_gather(w_down.T, "ctx", axis=0, tiled=True)
-    branch, full_gate, full_up, full_down_t = lax.optimization_barrier(
-        (branch, full_gate, full_up, full_down_t)
-    )
+        down_pieces = (lax.all_gather(w_down.T, "ctx", axis=0, tiled=True),)
+    branch, full_gate, full_up, *mine = lax.optimization_barrier(
+        (branch, full_gate, full_up, *down_pieces[:5])
+    )
+    down_pieces = (*mine, *down_pieces[5:])
     normed_mid = by_rows(mid_kernel, (tokens, branch), gains, (jnp.bfloat16,), 0, "mid_norms")
     hidden, active, slope = units(normed_mid, full_gate, full_up)
-    mlp_out = lax.psum(project_down(hidden, full_down_t), "tp")
+    full_down_t = assemble(down_pieces, 3)
+    mlp_part = project_down(hidden, full_down_t)
+    mlp_part, out_pieces, kv_pieces = lax.optimization_barrier((mlp_part, out_pieces, kv_pieces))
+    full_out_t = assemble(out_pieces)
+    kv_all, key_turned = turn(kv_pieces)
+    mlp_out = lax.psum(mlp_part, "tp")
+    mlp_out, full_out_t, kv_all, key_turned = lax.optimization_barrier(
+        (mlp_out, full_out_t, kv_all, key_turned)
+    )
     result, mlp_low, gain_four = by_rows(
         top_kernel, (tokens, branch, mlp_out, cotangent), gains, (jnp.bfloat16, jnp.bfloat16), 1,
         "top_norms",
     )
-    gate_low, up_low, mid_part = units_back(mlp_low, full_down_t, full_gate, full_up, active, slope)
+    gate_low, up_low = units_back(mlp_low, full_down_t, active, slope)
+    mid_part = features_back(gate_low, up_low, full_gate, full_up)
     mid_part, hidden_t, mlp_t, gate_t, up_t = lax.optimization_barrier(
         (mid_part, hidden, mlp_low, gate_low, up_low)
     )
@@ -903,11 +947,9 @@
     gate_grad = matmul(normed_mid.T, gate_t).astype(jnp.bfloat16)
     gate_blocks = scatter_start(gate_grad)
     up_grad = matmul(normed_mid.T, up_t).astype(jnp.bfloat16)
-    key_turned = kv_all[:, :HD].T
-    mid_sum, up_grad, key_turned, gate_blocks = lax.optimization_barrier(
-        (mid_sum, up_grad, key_turned, gate_blocks)
-    )
+    up_grad, gate_blocks = lax.optimization_barrier((up_grad, gate_blocks))
     gate_terms = scatter_finish(gate_blocks)
+    mid_sum, up_grad = lax.optimization_barrier((mid_sum, up_grad))
     resid_grad, branch_low, gain_mid = by_rows(
         low_kernel, (tokens, branch, mid_sum, cotangent), gains, (jnp.float32, jnp.bfloat16), 2,
         "low_norms",
@@ -919,10 +961,10 @@
     *kv_terms, down_shard, gate_terms = lax.optimization_barrier((*kv_terms, down_shard, gate_terms))
     gate_shard = add_terms(gate_terms)
     if pairs:
-        mine = kv_terms[0] + swap(kv_terms[1], 1)
-        kv_sums = scatter_finish(
-            scatter_corner(*(mine[k * tok_dev : (k + 1) * tok_dev] for k in range(4)))
-        )
+        far = kv_terms[1] + swap(kv_terms[3], 1)
+        near = kv_terms[0] + swap(kv_terms[2], 1)
+        blocks = (near[k * tok_dev : (k + 1) * tok_dev] for k in range(3))
+        kv_sums = scatter_finish(scatter_corner(*blocks, far))
     else:
         kv_sums = (lax.psum_scatter(kv_terms[0], "ctx", scatter_dimension=0, tiled=True),)
     qkv_low, in_part = join(cosine, sine, query_low, full_qkv, kv_sums)

time: 1380 us -> 730 us (0.53)
  Pallas kernels: 814 us -> 166 us
  waiting for transfers between devices: 376 us -> 358 us
    pallas_call x6 -> x5, Pallas kernels: 669 us -> 15.6 us  [call(): pl.pallas_call(kernel, out_shape=out_shape, in_specs=[pl.BlockSpec(memory...]
    pallas_call x1 -> x6, Pallas kernels: 34.9 us -> 56.1 us  [the longest x4 27.2 us: assemble(): pl.pallas_call(assemble_kernel, out_shape=jax.ShapeDtypeStruct((8 * rows,...]
    unnamed x96 -> x144, local copies, waits for them, and re-layouts: 20.2 us -> 33.4 us
    ppermute x72 -> x69, waiting for transfers between devices: 237 us -> 232 us  [swap(): return lax.ppermute(value, 'ctx', pairs)]
    ppermute x72 -> x69, starting transfers between devices: 52.5 us -> 55.8 us  [swap(): return lax.ppermute(value, 'ctx', pairs)]
  transfers between devices with their start and end apart: 81 -> 78, of which waited for: 39 -> 42; matrix products, arithmetic and copies ran while one was open for 6% -> 12% of each run, Pallas kernels for 52% -> 13%
where the time goes in v3:
time: 730 us; the launch traced here: 720 us
  waiting for transfers between devices  358 us (49%)
  Pallas kernels  166 us (23%)
  starting transfers between devices  58.3 us (8%)
  local copies, waits for them, and re-layouts  53.4 us (7%)
  other arithmetic  36 us (5%)
  matrix products  32.2 us (4%)
  between operations  16.8 us (2%)
    ppermute x69, waiting for transfers between devices, swap(): return lax.ppermute(value, 'ctx', pairs)  232 us
    psum x1, waiting for transfers between devices, body(): mlp_out = lax.psum(mlp_part, 'tp')  85 us
    ppermute x69, starting transfers between devices, swap(): return lax.ppermute(value, 'ctx', pairs)  55.8 us
    pallas_call x4, Pallas kernels, by_rows(): pl.pallas_call(kernel, out_shape=tuple(shapes), grid=(rows // block,), in...  35.1 us
    unnamed x144, local copies, waits for them, and re-layouts  33.4 us
    dot_general x5, matrix products, matmul(): return jnp.dot(left, right, preferred_element_type=jnp.float32)  32.2 us
    pallas_call x4, Pallas kernels, assemble(): pl.pallas_call(assemble_kernel, out_shape=jax.ShapeDtypeStruct((8 * rows,...  27.2 us
    reduce_scatter x1, waiting for transfers between devices, body(): up_shard = lax.psum_scatter(up_grad, 'ctx', scatter_dimension=0, tiled=True)  21.9 us
  transfers between devices with their start and end apart: 78, of which 42 were waited for; matrix products, arithmetic and copies ran while one was open for 12% of the time, Pallas kernels for 13%

profile of v3, /device:TPU:0, one launch (start us, length us, event | category | flops | bytes accessed | tf_op | source)
XLA Modules:
  0.0 720.1 jit_solution(14196166960091144711)
XLA Ops:
  18.6 11.2 %collective-permute-done.refs_1_ = bf16[288,1152]{1,0:T(8,128)(2,1)S(1)} collective-permute-done((bf16[288,1152]{1,0:T(8,128)(2,1)S(1)}, bf16[288,1152]{1,0:T(8,128)(2,1)S(1)}, u32[]{:S(2)}, u32[]{:S(2)}) %collective-permute-start) | collective-permute-done | bytes 663584 | tf_op jit(solution)/shard_map/ppermute | solution.py:67
  59.8 11.7 %collective-permute-done.11.refs_1_ = bf16[512,512]{1,0:T(8,128)(2,1)S(1)} collective-permute-done((bf16[512,512]{1,0:T(8,128)(2,1)S(1)}, bf16[512,512]{1,0:T(8,128)(2,1)S(1)}, u32[]{:S(2)}, u32[]{:S(2)}) %collective-permute-start.11) | collective-permute-done | bytes 524320 | tf_op jit(solution)/shard_map/ppermute | solution.py:67
  90.7 10.7 %attend.1 = (f32[512,512]{1,0:T(8,128)}, bf16[512,512]{1,0:T(8,128)(2,1)}, f32[512,256]{1,0:T(8,128)}) custom-call(s32[16]{0:T(128)} %reshape.111.map_ref, s32[1]{0:T(128)} %bitcast.8.me_ref, bf16[512,512]{1,0:T(8,128)(2,1)} %copy-done.42, bf16[512,512]{1,0:T(8,128)(2,1)} %copy-done.19, bf16[512,512]{1,0:T(8,128)(2,1)} %copy-done.9, ...), custom_call_target="tpu_custom_call" | custom-call | flops 4294967296 | bytes 10485760 | tf_op jit(solution)/shard_map/attend/pallas_call | solution.py:694
  106.7 6.8 collective-permute-done.27.refs_1_
  119.3 5.8 assemble.4.full_ref
  132.1 24.4 %collective-permute-done.29.refs_3_ = bf16[144,2304]{1,0:T(8,128)(2,1)S(1)} collective-permute-done((bf16[144,2304]{1,0:T(8,128)(2,1)}, bf16[144,2304]{1,0:T(8,128)(2,1)S(1)}, u32[]{:S(2)}, u32[]{:S(2)}) %collective-permute-start.29) | collective-permute-done | bytes 663584 | tf_op jit(solution)/shard_map/ppermute | solution.py:67
  162.6 9.2 %assemble.5.gate_ref = bf16[2304,2304]{1,0:T(8,128)(2,1)} custom-call(s32[10]{0:T(128)} %copy-done.38, bf16[288,2304]{1,0:T(8,128)(2,1)} %refs_0_, bf16[288,2304]{1,0:T(8,128)(2,1)} %collective-permute-done.27.refs_1_, bf16[288,2304]{1,0:T(8,128)(2,1)} %collective-permute-done.28.refs_2_, bf16[144,2304]{1,0:T(8,128)(2,1)} %copy-done.60, ...), custom_call_target="tpu_custom_call" | custom-call | bytes 21233664 | tf_op jit(solution)/shard_map/assemble/pallas_call | solution.py:110
  171.8 44.0 %collective-permute-done.36.refs_1_ = bf16[288,2304]{1,0:T(8,128)(2,1)S(1)} collective-permute-done((bf16[288,2304]{1,0:T(8,128)(2,1)}, bf16[288,2304]{1,0:T(8,128)(2,1)S(1)}, u32[]{:S(2)}, u32[]{:S(2)}) %collective-permute-start.36) | collective-permute-done | bytes 1327136 | tf_op jit(solution)/shard_map/ppermute | solution.py:67
  219.4 14.1 %collective-permute-done.38.refs_3_ = bf16[144,2304]{1,0:T(8,128)(2,1)S(1)} collective-permute-done((bf16[144,2304]{1,0:T(8,128)(2,1)S(1)}, bf16[144,2304]{1,0:T(8,128)(2,1)S(1)}, u32[]{:S(2)}, u32[]{:S(2)}) %collective-permute-start.38) | collective-permute-done | bytes 663584 | tf_op jit(solution)/shard_map/ppermute | solution.py:67
  234.7 6.8 mid_norms.1.in_ref
  241.6 18.6 %units.1 = (bf16[512,2304]{1,0:T(8,128)(2,1)}, bf16[512,2304]{1,0:T(8,128)(2,1)}, bf16[512,2304]{1,0:T(8,128)(2,1)}) custom-call(bf16[512,2304]{1,0:T(8,128)(2,1)} %mid_norms.1.in_ref, bf16[2304,2304]{1,0:T(8,128)(2,1)} %assemble.5.gate_ref, bf16[2304,2304]{1,0:T(8,128)(2,1)} %all-gather.2.cloned.1.call-done.up_ref), custom_call_target="tpu_custom_call" | custom-call | flops 10871635968 | bytes 21233664 | tf_op jit(solution)/shard_map/units/pallas_call | solution.py:443
  260.2 9.1 %assemble.6.down_ref = bf16[2304,2304]{1,0:T(8,128)(2,1)} custom-call(s32[10]{0:T(128)} %copy-done.38, bf16[288,2304]{1,0:T(8,128)(2,1)} %bitcast.11.refs_0_, bf16[288,2304]{1,0:T(8,128)(2,1)} %copy-done.50, bf16[288,2304]{1,0:T(8,128)(2,1)} %copy-done.51, bf16[144,2304]{1,0:T(8,128)(2,1)} %copy-done.59, bf16[144,2304]{1,0:T(8,128)(2,1)} %collective-permute-done.39.refs_4_, ...), custom_call_target="tpu_custom_call" | custom-call | bytes 21233664 | tf_op jit(solution)/shard_map/assemble/pallas_call | solution.py:110
  269.3 10.0 %project_down.1 = bf16[512,2304]{1,0:T(8,128)(2,1)} custom-call(bf16[512,2304]{1,0:T(8,128)(2,1)} %get-tuple-element.215.hidden_ref, bf16[2304,2304]{1,0:T(8,128)(2,1)} %assemble.6.down_ref), custom_call_target="tpu_custom_call" | custom-call | flops 5435817984 | bytes 10616832 | tf_op jit(solution)/shard_map/project_down/pallas_call | solution.py:467
  289.6 85.0 %all-reduce.7.cloned.1.call-done.mlp_ref = bf16[512,2304]{1,0:T(8,128)(2,1)} async-done(((bf16[512,2304]{1,0:T(8,128)(2,1)}), bf16[512,2304]{1,0:T(8,128)(2,1)}) %all-reduce.7.cloned.1.call-update) | async-done | bytes 2359312 | tf_op jit(solution)/shard_map/psum | solution.py:931
  374.6 8.5 %top_norms.1 = (bf16[512,2304]{1,0:T(8,128)(2,1)}, bf16[512,2304]{1,0:T(8,128)(2,1)}, f32[1,2304]{1,0:T(1,128)}) custom-call(bf16[512,2304]{1,0:T(8,128)(2,1)} %tok_ref.7, bf16[512,2304]{1,0:T(8,128)(2,1)} %all-reduce.5.cloned.1.call-done.branch_ref, bf16[512,2304]{1,0:T(8,128)(2,1)} %all-reduce.7.cloned.1.call-done.mlp_ref, bf16[512,2304]{1,0:T(8,128)(2,1)} %cot_ref.3, ...), custom_call_target="tpu_custom_call" | custom-call | bytes 14164992 | tf_op jit(solution)/shard_map/top_norms/pallas_call | solution.py:404
  383.1 12.0 %units_back.1 = (bf16[512,2304]{1,0:T(8,128)(2,1)}, bf16[512,2304]{1,0:T(8,128)(2,1)}) custom-call(bf16[512,2304]{1,0:T(8,128)(2,1)} %get-tuple-element.216.grad_ref, bf16[2304,2304]{1,0:T(8,128)(2,1)} %assemble.6.down_ref, bf16[512,2304]{1,0:T(8,128)(2,1)} %get-tuple-element.195.active_ref, bf16[512,2304]{1,0:T(8,128)(2,1)} %get-tuple-element.196.slope_ref), custom_call_target="tpu_custom_call" | custom-call | flops 5435817984 | bytes 10616832 | tf_op jit(solution)/shard_map/units_back/pallas_call | solution.py:497
  395.0 16.9 %features_back.1 = bf16[512,2304]{1,0:T(8,128)(2,1)} custom-call(bf16[512,2304]{1,0:T(8,128)(2,1)} %get-tuple-element.201.dg_ref, bf16[512,2304]{1,0:T(8,128)(2,1)} %get-tuple-element.200.du_ref, bf16[2304,2304]{1,0:T(8,128)(2,1)} %assemble.5.gate_ref, bf16[2304,2304]{1,0:T(8,128)(2,1)} %all-gather.2.cloned.1.call-done.up_ref), custom_call_target="tpu_custom_call" | custom-call | flops 10871635968 | bytes 21233664 | tf_op jit(solution)/shard_map/features_back/pallas_call | solution.py:523
  413.6 9.9 %convolution_convert_fusion = bf16[2304,2304]{0,1:T(8,128)(2,1)} fusion(bf16[512,2304]{1,0:T(8,128)(2,1)} %get-tuple-element.215.hidden_ref, bf16[512,2304]{1,0:T(8,128)(2,1)S(1)} %copy-done.67), kind=kOutput, calls=%fused_computation | convolution fusion | flops 5441126400 | bytes 15335424 | tf_op jit(solution)/shard_map/dot_general | solution.py:33
  425.2 7.6 %convolution_convert_fusion.1 = bf16[2304,2304]{1,0:T(8,128)(2,1)S(1)} fusion(bf16[512,2304]{1,0:T(8,128)(2,1)S(1)} %copy-done.52, bf16[512,2304]{1,0:T(8,128)(2,1)} %get-tuple-element.201.dg_ref), kind=kOutput, calls=%fused_computation.1 | convolution fusion | flops 5441126400 | bytes 15335424 | tf_op jit(solution)/shard_map/dot_general | solution.py:33
  441.1 9.1 %collective-permute-done.45 = bf16[4,288,2304]{2,1,0:T(8,128)(2,1)} collective-permute-done((bf16[4,288,2304]{2,1,0:T(8,128)(2,1)}, bf16[4,288,2304]{2,1,0:T(8,128)(2,1)}, u32[]{:S(2)}, u32[]{:S(2)}) %collective-permute-start.45) | collective-permute-done | bytes 5308448 | tf_op jit(solution)/shard_map/ppermute | solution.py:67
  461.3 8.3 %convolution_convert_fusion.2 = bf16[2304,2304]{1,0:T(8,128)(2,1)} fusion(bf16[512,2304]{1,0:T(8,128)(2,1)S(1)} %copy-done.53, bf16[512,2304]{1,0:T(8,128)(2,1)S(1)} %copy-done.69), kind=kOutput, calls=%fused_computation.2 | convolution fusion | flops 5441126400 | bytes 15335424 | tf_op jit(solution)/shard_map/dot_general | solution.py:33
  472.0 18.1 %collective-permute-done.46 = bf16[144,2304]{1,0:T(8,128)(2,1)S(1)} collective-permute-done((bf16[144,2304]{1,0:T(8,128)(2,1)}, bf16[144,2304]{1,0:T(8,128)(2,1)S(1)}, u32[]{:S(2)}, u32[]{:S(2)}) %collective-permute-start.46) | collective-permute-done | bytes 663584 | tf_op jit(solution)/shard_map/ppermute | solution.py:67
  496.8 10.0 %all-reduce.9.cloned.1.call-done.mid_ref = bf16[512,2304]{1,0:T(8,128)(2,1)} async-done(((bf16[512,2304]{1,0:T(8,128)(2,1)}), bf16[512,2304]{1,0:T(8,128)(2,1)}) %all-reduce.9.cloned.1.call-update) | async-done | bytes 2359312 | tf_op jit(solution)/shard_map/psum | solution.py:944
  506.8 11.6 %low_norms.1 = (f32[512,2304]{1,0:T(8,128)}, bf16[512,2304]{1,0:T(8,128)(2,1)}, f32[2,2304]{1,0:T(2,128)}) custom-call(bf16[512,2304]{1,0:T(8,128)(2,1)} %tok_ref.7, bf16[512,2304]{1,0:T(8,128)(2,1)} %all-reduce.5.cloned.1.call-done.branch_ref, bf16[512,2304]{1,0:T(8,128)(2,1)} %all-reduce.9.cloned.1.call-done.mid_ref, bf16[512,2304]{1,0:T(8,128)(2,1)} %cot_ref.3, ...), custom_call_target="tpu_custom_call" | custom-call | bytes 16533504 | tf_op jit(solution)/shard_map/low_norms/pallas_call | solution.py:404
  518.4 19.4 %attend_back.1 = (bf16[512,512]{1,0:T(8,128)(2,1)}, bf16[1536,512]{1,0:T(8,128)(2,1)}, bf16[512,512]{1,0:T(8,128)(2,1)}, bf16[1536,512]{1,0:T(8,128)(2,1)}, bf16[512,512]{1,0:T(8,128)(2,1)}) custom-call(s32[16]{0:T(128)} %reshape.111.map_ref, s32[1]{0:T(128)} %bitcast.8.me_ref, bf16[512,2304]{1,0:T(8,128)(2,1)} %get-tuple-element.230.da_ref, ...), custom_call_target="tpu_custom_call" | custom-call | flops 10737418240 | bytes 14680064 | tf_op jit(solution)/shard_map/attend_back/pallas_call | solution.py:813
  549.9 6.3 collective-permute-start.54
  565.1 11.1 %collective-permute-done.55.refs_2_ = bf16[512,512]{1,0:T(8,128)(2,1)S(1)} collective-permute-done((bf16[512,512]{1,0:T(8,128)(2,1)S(1)}, bf16[512,512]{1,0:T(8,128)(2,1)S(1)}, u32[]{:S(2)}, u32[]{:S(2)}) %collective-permute-start.55) | collective-permute-done | bytes 524320 | tf_op jit(solution)/shard_map/ppermute | solution.py:67
  626.9 9.1 %collective-permute-done.57 = bf16[144,1024]{1,0:T(8,128)(2,1)S(1)} collective-permute-done((bf16[144,1024]{1,0:T(8,128)(2,1)S(1)}, bf16[144,1024]{1,0:T(8,128)(2,1)S(1)}, u32[]{:S(2)}, u32[]{:S(2)}) %collective-permute-start.57) | collective-permute-done | bytes 294944 | tf_op jit(solution)/shard_map/ppermute | solution.py:67
  650.7 20.3 %collective-permute-done.58 = bf16[288,1024]{1,0:T(8,128)(2,1)S(1)} collective-permute-done((bf16[288,1024]{1,0:T(8,128)(2,1)S(1)}, bf16[288,1024]{1,0:T(8,128)(2,1)S(1)}, u32[]{:S(2)}, u32[]{:S(2)}) %collective-permute-start.58) | collective-permute-done | bytes 589856 | tf_op jit(solution)/shard_map/ppermute | solution.py:67
  673.1 21.9 %reduce-scatter.5.cloned.1.call-done = bf16[288,2304]{1,0:T(8,128)(2,1)} async-done(((bf16[2304,2304]{1,0:T(8,128)(2,1)}), bf16[288,2304]{1,0:T(8,128)(2,1)}) %reduce-scatter.5.cloned.1.call-update) | async-done | bytes 1327120 | tf_op jit(solution)/shard_map/reduce_scatter | solution.py:975
  697.9 6.2 all-reduce.11.cloned.1.call-done.sum_ref
  704.1 8.2 %end_norms.1 = f32[512,2304]{1,0:T(8,128)} custom-call(bf16[512,2304]{1,0:T(8,128)(2,1)} %tok_ref.7, bf16[512,2304]{1,0:T(8,128)(2,1)} %all-reduce.11.cloned.1.call-done.sum_ref, f32[512,2304]{1,0:T(8,128)} %get-tuple-element.239.resid_ref, f32[4,2304]{1,0:T(4,128)} %bitcast.119), custom_call_target="tpu_custom_call" | custom-call | bytes 14155776 | tf_op jit(solution)/shard_map/end_norms/pallas_call | solution.py:404
  (371 shorter events, 221.5 us)
Async XLA Ops:
  8.0 226.7 %all-reduce.5.cloned.1.call-start = ((), (), s32[]{:S(2)}) async-start(), calls=%async_computation.2 | async-start | bytes 4718592 | tf_op jit(solution)/shard_map/psum | solution.py:903
  16.4 26.5 %collective-permute-start.4 = (bf16[288,1152]{1,0:T(8,128)(2,1)S(1)}, bf16[288,1152]{1,0:T(8,128)(2,1)}, u32[]{:S(2)}, u32[]{:S(2)}) collective-permute-start(bf16[288,1152]{1,0:T(8,128)(2,1)S(1)} %pack.1.refs_0_), channel_id=1, source_target_pairs={{0,4},{4,0},{8,12},{12,8},{16,20},{20,16},{24,28},{28,24},{1,5},{5... | collective-permute-start | bytes 1990664 | tf_op jit(solution)/shard_map/ppermute | solution.py:67
  83.4 30.1 %collective-permute-start.27 = (bf16[288,2304]{1,0:T(8,128)(2,1)}, bf16[288,2304]{1,0:T(8,128)(2,1)}, u32[]{:S(2)}, u32[]{:S(2)}) collective-permute-start(bf16[288,2304]{1,0:T(8,128)(2,1)} %refs_0_), channel_id=1, source_target_pairs={{0,8},{4,12},{8,0},{12,4},{16,24},{20,28},{24,16},{28,20},{1,9},{5... | collective-permute-start | bytes 3981320 | tf_op jit(solution)/shard_map/ppermute | solution.py:67
  84.0 30.1 %collective-permute-start.28 = (bf16[288,2304]{1,0:T(8,128)(2,1)}, bf16[288,2304]{1,0:T(8,128)(2,1)}, u32[]{:S(2)}, u32[]{:S(2)}) collective-permute-start(bf16[288,2304]{1,0:T(8,128)(2,1)} %refs_0_), channel_id=1, source_target_pairs={{0,16},{4,20},{8,24},{12,28},{16,0},{20,4},{24,8},{28,12},{1,17},{... | collective-permute-start | bytes 3981320 | tf_op jit(solution)/shard_map/ppermute | solution.py:67
  114.1 120.6 %all-gather.2.cloned.1.call-start = ((), (), s32[]{:S(2)}) async-start(), calls=%async_computation.3 | async-start | bytes 11943936 | tf_op jit(solution)/shard_map/all_gather | solution.py:904
  114.7 259.9 %all-reduce.7.cloned.1.call-start = ((), (), s32[]{:S(2)}) async-start(), calls=%async_computation.4 | async-start | bytes 4718592 | tf_op jit(solution)/shard_map/psum | solution.py:931
  114.8 43.3 %collective-permute-start.31 = (bf16[288,2304]{1,0:T(8,128)(2,1)}, bf16[288,2304]{1,0:T(8,128)(2,1)}, u32[]{:S(2)}, u32[]{:S(2)}) collective-permute-start(bf16[288,2304]{1,0:T(8,128)(2,1)} %refs_0_), channel_id=1, source_target_pairs={{0,4},{4,0},{8,12},{12,8},{16,20},{20,16},{24,28},{28,24},{1,5},{5... | collective-permute-start | bytes 3981320 | tf_op jit(solution)/shard_map/ppermute | solution.py:67
  116.8 44.9 %collective-permute-start.32 = (bf16[288,2304]{1,0:T(8,128)(2,1)}, bf16[288,2304]{1,0:T(8,128)(2,1)}, u32[]{:S(2)}, u32[]{:S(2)}) collective-permute-start(bf16[288,2304]{1,0:T(8,128)(2,1)} %collective-permute-done.27.refs_1_), channel_id=1, source_target_pairs={{0,4},{4,0},{8,12},{12,8},{16,20},{20,16},{24,28},{28,24},{1,5},{5... | collective-permute-start | bytes 3981320 | tf_op jit(solution)/shard_map/ppermute | solution.py:67
  119.3 43.3 %collective-permute-start.33 = (bf16[288,2304]{1,0:T(8,128)(2,1)}, bf16[288,2304]{1,0:T(8,128)(2,1)}, u32[]{:S(2)}, u32[]{:S(2)}) collective-permute-start(bf16[288,2304]{1,0:T(8,128)(2,1)} %collective-permute-done.28.refs_2_), channel_id=1, source_target_pairs={{0,4},{4,0},{8,12},{12,8},{16,20},{20,16},{24,28},{28,24},{1,5},{5... | collective-permute-start | bytes 3981320 | tf_op jit(solution)/shard_map/ppermute | solution.py:67
  127.4 29.1 %collective-permute-start.29 = (bf16[144,2304]{1,0:T(8,128)(2,1)}, bf16[144,2304]{1,0:T(8,128)(2,1)S(1)}, u32[]{:S(2)}, u32[]{:S(2)}) collective-permute-start(bf16[144,2304]{1,0:T(8,128)(2,1)} %slice.218), channel_id=1, source_target_pairs={{0,16},{4,20},{8,24},{12,28},{16,0},{20,4},{24,8},{28,12},{1,17},{... | collective-permute-start | bytes 1990664 | tf_op jit(solution)/shard_map/ppermute | solution.py:67
  129.1 27.5 %collective-permute-start.30 = (bf16[144,2304]{1,0:T(8,128)(2,1)}, bf16[144,2304]{1,0:T(8,128)(2,1)S(1)}, u32[]{:S(2)}, u32[]{:S(2)}) collective-permute-start(bf16[144,2304]{1,0:T(8,128)(2,1)} %slice.219), channel_id=1, source_target_pairs={{0,8},{4,12},{8,0},{12,4},{16,24},{20,28},{24,16},{28,20},{1,9},{5... | collective-permute-start | bytes 1990664 | tf_op jit(solution)/shard_map/ppermute | solution.py:67
  156.5 59.2 %collective-permute-start.36 = (bf16[288,2304]{1,0:T(8,128)(2,1)}, bf16[288,2304]{1,0:T(8,128)(2,1)S(1)}, u32[]{:S(2)}, u32[]{:S(2)}) collective-permute-start(bf16[288,2304]{1,0:T(8,128)(2,1)} %bitcast.11.refs_0_), channel_id=1, source_target_pairs={{0,8},{4,12},{8,0},{12,4},{16,24},{20,28},{24,16},{28,20},{1,9},{5... | collective-permute-start | bytes 3981320 | tf_op jit(solution)/shard_map/ppermute | solution.py:67
  158.1 59.8 %collective-permute-start.37 = (bf16[288,2304]{1,0:T(8,128)(2,1)}, bf16[288,2304]{1,0:T(8,128)(2,1)S(1)}, u32[]{:S(2)}, u32[]{:S(2)}) collective-permute-start(bf16[288,2304]{1,0:T(8,128)(2,1)} %bitcast.11.refs_0_), channel_id=1, source_target_pairs={{0,16},{4,20},{8,24},{12,28},{16,0},{20,4},{24,8},{28,12},{1,17},{... | collective-permute-start | bytes 3981320 | tf_op jit(solution)/shard_map/ppermute | solution.py:67
  218.8 41.4 %collective-permute-start.40 = (bf16[288,2304]{1,0:T(8,128)(2,1)}, bf16[288,2304]{1,0:T(8,128)(2,1)}, u32[]{:S(2)}, u32[]{:S(2)}) collective-permute-start(bf16[288,2304]{1,0:T(8,128)(2,1)} %bitcast.11.refs_0_), channel_id=1, source_target_pairs={{0,4},{4,0},{8,12},{12,8},{16,20},{20,16},{24,28},{28,24},{1,5},{5... | collective-permute-start | bytes 3981320 | tf_op jit(solution)/shard_map/ppermute | solution.py:67
  218.8 41.4 %collective-permute-start.41 = (bf16[288,2304]{1,0:T(8,128)(2,1)S(1)}, bf16[288,2304]{1,0:T(8,128)(2,1)}, u32[]{:S(2)}, u32[]{:S(2)}) collective-permute-start(bf16[288,2304]{1,0:T(8,128)(2,1)S(1)} %collective-permute-done.36.refs_1_), channel_id=1, source_target_pairs={{0,4},{4,0},{8,12},{12,8},{16,20},{20,16},{24,28},{28,24},{1,5},{5... | collective-permute-start | bytes 3981320 | tf_op jit(solution)/shard_map/ppermute | solution.py:67
  219.3 40.9 %collective-permute-start.42 = (bf16[288,2304]{1,0:T(8,128)(2,1)S(1)}, bf16[288,2304]{1,0:T(8,128)(2,1)}, u32[]{:S(2)}, u32[]{:S(2)}) collective-permute-start(bf16[288,2304]{1,0:T(8,128)(2,1)S(1)} %collective-permute-done.37.refs_2_), channel_id=1, source_target_pairs={{0,4},{4,0},{8,12},{12,8},{16,20},{20,16},{24,28},{28,24},{1,5},{5... | collective-permute-start | bytes 3981320 | tf_op jit(solution)/shard_map/ppermute | solution.py:67
  233.5 26.7 %collective-permute-start.43 = (bf16[144,2304]{1,0:T(8,128)(2,1)S(1)}, bf16[144,2304]{1,0:T(8,128)(2,1)}, u32[]{:S(2)}, u32[]{:S(2)}) collective-permute-start(bf16[144,2304]{1,0:T(8,128)(2,1)S(1)} %collective-permute-done.38.refs_3_), channel_id=1, source_target_pairs={{0,4},{4,0},{8,12},{12,8},{16,20},{20,16},{24,28},{28,24},{1,5},{5... | collective-permute-start | bytes 1990664 | tf_op jit(solution)/shard_map/ppermute | solution.py:67
  234.7 25.5 %collective-permute-start.44 = (bf16[144,2304]{1,0:T(8,128)(2,1)}, bf16[144,2304]{1,0:T(8,128)(2,1)}, u32[]{:S(2)}, u32[]{:S(2)}) collective-permute-start(bf16[144,2304]{1,0:T(8,128)(2,1)} %collective-permute-done.39.refs_4_), channel_id=1, source_target_pairs={{0,4},{4,0},{8,12},{12,8},{16,20},{20,16},{24,28},{28,24},{1,5},{5... | collective-permute-start | bytes 1990664 | tf_op jit(solution)/shard_map/ppermute | solution.py:67
  279.4 227.4 %all-reduce.9.cloned.1.call-start = ((), (), s32[]{:S(2)}) async-start(), calls=%async_computation.5 | async-start | bytes 4718592 | tf_op jit(solution)/shard_map/psum | solution.py:944
  411.9 128.6 %reduce-scatter.3.cloned.1.call-start = ((), (), s32[]{:S(2)}) async-start(), calls=%async_computation.6 | async-start | bytes 11943936 | tf_op jit(solution)/shard_map/reduce_scatter | solution.py:946
  423.6 271.4 %reduce-scatter.5.cloned.1.call-start = ((), (), s32[]{:S(2)}) async-start(), calls=%async_computation.8 | async-start | bytes 11943936 | tf_op jit(solution)/shard_map/reduce_scatter | solution.py:975
  458.2 31.9 %collective-permute-start.46 = (bf16[144,2304]{1,0:T(8,128)(2,1)}, bf16[144,2304]{1,0:T(8,128)(2,1)S(1)}, u32[]{:S(2)}, u32[]{:S(2)}) collective-permute-start(bf16[144,2304]{1,0:T(8,128)(2,1)} %get-tuple-element.253), channel_id=1, source_target_pairs={{0,16},{4,20},{8,24},{12,28},{16,0},{20,4},{24,8},{28,12},{1,17},{... | collective-permute-start | bytes 1990664 | tf_op jit(solution)/shard_map/ppermute | solution.py:67
  459.8 31.6 %collective-permute-start.47 = (bf16[144,2304]{1,0:T(8,128)(2,1)S(1)}, bf16[144,2304]{1,0:T(8,128)(2,1)S(1)}, u32[]{:S(2)}, u32[]{:S(2)}) collective-permute-start(bf16[144,2304]{1,0:T(8,128)(2,1)S(1)} %get-tuple-element.252), channel_id=1, source_target_pairs={{0,8},{4,12},{8,0},{12,4},{16,24},{20,28},{24,16},{28,20},{1,9},{5... | collective-permute-start | bytes 1990664 | tf_op jit(solution)/shard_map/ppermute | solution.py:67
  494.8 44.5 %collective-permute-start.48 = (bf16[288,2304]{1,0:T(8,128)(2,1)}, bf16[288,2304]{1,0:T(8,128)(2,1)S(1)}, u32[]{:S(2)}, u32[]{:S(2)}) collective-permute-start(bf16[288,2304]{1,0:T(8,128)(2,1)} %get-tuple-element.218), channel_id=1, source_target_pairs={{0,8},{4,12},{8,0},{12,4},{16,24},{20,28},{24,16},{28,20},{1,9},{5... | collective-permute-start | bytes 3981320 | tf_op jit(solution)/shard_map/ppermute | solution.py:67
  496.2 44.4 %collective-permute-start.49 = (bf16[288,2304]{1,0:T(8,128)(2,1)}, bf16[288,2304]{1,0:T(8,128)(2,1)}, u32[]{:S(2)}, u32[]{:S(2)}) collective-permute-start(bf16[288,2304]{1,0:T(8,128)(2,1)} %get-tuple-element.219), channel_id=1, source_target_pairs={{0,16},{4,20},{8,24},{12,28},{16,0},{20,4},{24,8},{28,12},{1,17},{... | collective-permute-start | bytes 3981320 | tf_op jit(solution)/shard_map/ppermute | solution.py:67
  591.8 24.3 %collective-permute-start.56 = (bf16[4,288,1024]{2,1,0:T(8,128)(2,1)}, bf16[4,288,1024]{2,1,0:T(8,128)(2,1)}, u32[]{:S(2)}, u32[]{:S(2)}) collective-permute-start(bf16[4,288,1024]{2,1,0:T(8,128)(2,1)} %dynamic-slice_bitcast_fusion.1), channel_id=1, source_target_pairs={{0,4},{4,0},{8,12},{12,8},{16,20},{20,16},{24,28},{28,24},{1,5},{5... | collective-permute-start | bytes 7077896 | tf_op jit(solution)/shard_map/ppermute | solution.py:67
  595.0 109.1 %all-reduce.11.cloned.1.call-start = ((), (), s32[]{:S(2)}) async-start(), calls=%async_computation.7 | async-start | bytes 4718592 | tf_op jit(solution)/shard_map/psum | solution.py:974
  611.6 33.3 %collective-permute-start.70 = (f32[1,4,288]{2,1,0:T(4,128)S(1)}, f32[1,4,288]{2,1,0:T(4,128)S(1)}, u32[]{:S(2)}, u32[]{:S(2)}) collective-permute-start(f32[1,4,288]{2,1,0:T(4,128)S(1)} %slice_select_fusion.2), channel_id=1, source_target_pairs={{0,4},{4,0},{8,12},{12,8},{16,20},{20,16},{24,28},{28,24},{1,5},{5... | collective-permute-start | bytes 13832 | tf_op jit(solution)/shard_map/ppermute | solution.py:67
  624.6 25.2 %collective-permute-start.63 = (bf16[288,512]{1,0:T(8,128)(2,1)S(1)}, bf16[288,512]{1,0:T(8,128)(2,1)S(1)}, u32[]{:S(2)}, u32[]{:S(2)}) collective-permute-start(bf16[288,512]{1,0:T(8,128)(2,1)S(1)} %pad_maximum_fusion.6), channel_id=1, source_target_pairs={{0,8},{4,12},{8,0},{12,4},{16,24},{20,28},{24,16},{28,20},{1,9},{5... | collective-permute-start | bytes 884744 | tf_op jit(solution)/shard_map/ppermute | solution.py:67
  626.1 23.7 %collective-permute-start.65 = (bf16[288,512]{1,0:T(8,128)(2,1)S(1)}, bf16[288,512]{1,0:T(8,128)(2,1)S(1)}, u32[]{:S(2)}, u32[]{:S(2)}) collective-permute-start(bf16[288,512]{1,0:T(8,128)(2,1)S(1)} %pad_maximum_fusion.7), channel_id=1, source_target_pairs={{0,16},{4,20},{8,24},{12,28},{16,0},{20,4},{24,8},{28,12},{1,17},{... | collective-permute-start | bytes 884744 | tf_op jit(solution)/shard_map/ppermute | solution.py:67
  637.4 33.6 %collective-permute-start.58 = (bf16[288,1024]{1,0:T(8,128)(2,1)S(1)}, bf16[288,1024]{1,0:T(8,128)(2,1)S(1)}, u32[]{:S(2)}, u32[]{:S(2)}) collective-permute-start(bf16[288,1024]{1,0:T(8,128)(2,1)S(1)} %pad_maximum_fusion.2), channel_id=1, source_target_pairs={{0,8},{4,12},{8,0},{12,4},{16,24},{20,28},{24,16},{28,20},{1,9},{5... | collective-permute-start | bytes 1769480 | tf_op jit(solution)/shard_map/ppermute | solution.py:67
  639.0 32.1 %collective-permute-start.60 = (bf16[288,1024]{1,0:T(8,128)(2,1)S(1)}, bf16[288,1024]{1,0:T(8,128)(2,1)S(1)}, u32[]{:S(2)}, u32[]{:S(2)}) collective-permute-start(bf16[288,1024]{1,0:T(8,128)(2,1)S(1)} %pad_maximum_fusion.3), channel_id=1, source_target_pairs={{0,16},{4,20},{8,24},{12,28},{16,0},{20,4},{24,8},{28,12},{1,17},{... | collective-permute-start | bytes 1769480 | tf_op jit(solution)/shard_map/ppermute | solution.py:67
  (116 other events, 1067.9 us)
Sparse Core Ops, SparseCore 0:
  114.2 95.9 all-reduce.4
  279.5 95.0 all-reduce.6
  412.1 94.6 all-reduce.8
  609.3 94.7 all-reduce.10
Sparse Core Ops, SparseCore 1:
  116.5 103.8 all-gather.1
  423.6 109.6 reduce-scatter.2
  583.4 111.5 reduce-scatter.4

commit v4 on v3

--- a/solution.py
+++ b/solution.py
@@ -82,15 +82,34 @@
     return mine + tuple(swap(part, 1) for part in mine)
 
 
-def piece_rows(rows):
+def nearby_halves(low, high):
+    first = (swap(low, 2), swap(high, 4))
+    return first[0], swap(high, 2), swap(low, 4), first[1]
+
+
+def gather_halves(low, high, near=None):
+    near = nearby_halves(low, high) if near is None else near
+    mine = (low, high, *near, swap(near[0], 4), swap(near[3], 2))
+    return mine + tuple(swap(part, 1) for part in mine)
+
+
+def piece_rows(rows, halves):
     me = lax.axis_index("ctx")
-    places = [(me ^ bit) * rows for bit in (0, 2, 4, 6, 6, 1, 3, 5, 7, 7)]
-    shift = [0, 0, 0, 0, rows // 2] * 2
+    if halves:
+        bits = [bit for core in (0, 1) for bit in (0, 2, 4, 6) for _ in range(2)]
+        shift = [0, rows // 2] * 8
+        places = [(me ^ (bit + k // 8)) * rows for k, bit in enumerate(bits)]
+    else:
+        places = [(me ^ bit) * rows for bit in (0, 2, 4, 6, 6, 1, 3, 5, 7, 7)]
+        shift = [0, 0, 0, 0, rows // 2] * 2
     return jnp.stack(places).astype(jnp.int32) + jnp.array(shift, jnp.int32)
 
 
 def places_of(pieces):
-    return piece_rows(pieces[0].shape[0]) if len(pieces) > 1 else jnp.zeros((1,), jnp.int32)
+    if len(pieces) == 1:
+        return jnp.zeros((1,), jnp.int32)
+    rows = sum(piece.shape[0] for piece in pieces) // 8
+    return piece_rows(rows, len(pieces) == 16)
 
 
 def place(rows_ref, pieces, whole_ref):
@@ -105,7 +124,7 @@
 def assemble(pieces, grid=1):
     if len(pieces) == 1:
         return pieces[0]
-    rows, width = pieces[0].shape
+    rows, width = sum(piece.shape[0] for piece in pieces) // 8, pieces[0].shape[1]
     column = lambda n: pl.BlockSpec((n, width // grid), lambda i: (0, i))
     return pl.pallas_call(
         assemble_kernel,
@@ -116,7 +135,7 @@
         compiler_params=pltpu.CompilerParams(vmem_limit_bytes=MOST),
         cost_estimate=pl.CostEstimate(flops=0, bytes_accessed=32 * rows * width, transcendentals=0),
         name="assemble",
-    )(piece_rows(rows), *pieces)
+    )(places_of(pieces), *pieces)
 
 
 def scatter_corner(own, by_x, by_y, corner):
@@ -186,11 +205,11 @@
     out_ref[:, :one] = a_ref[...]
     out_ref[:, one:two] = b_ref[...]
     out_ref[:, two:three] = c_ref[...]
-    out_ref[:, three:] = jnp.broadcast_to(gains_ref[:, :1], (gains_ref.shape[0], HALF))
+    lane = lax.broadcasted_iota(jnp.int32, (gains_ref.shape[0], HALF), 1)
+    columns = jnp.broadcast_to(gains_ref[:, :1], lane.shape)
     for k in range(1, gains_ref.shape[1]):
-        lane = lax.broadcasted_iota(jnp.int32, (gains_ref.shape[0], HALF), 1)
-        column = jnp.broadcast_to(gains_ref[:, k : k + 1], lane.shape)
-        out_ref[:, three:] = jnp.where(lane == k, column, out_ref[:, three:])
+        columns = jnp.where(lane == k, jnp.broadcast_to(gains_ref[:, k : k + 1], lane.shape), columns)
+    out_ref[:, three:] = columns
 
 
 def pack(first, second, third, gains):
@@ -200,9 +219,10 @@
 
 
 def project_kernel(rows_ref, in_ref, cos_ref, sin_ref, *refs, heads, parts):
-    pieces, (q_ref, kv_ref) = refs[:parts], refs[parts : parts + 2]
+    pieces, q_ref, kv_refs = refs[:parts], refs[parts], refs[parts + 1 : parts + 3]
+    block = kv_refs[0].shape[0]
     if parts > 1:
-        full_ref = refs[parts + 2]
+        full_ref = refs[parts + 3]
         place(rows_ref, pieces, full_ref)
     else:
         full_ref = pieces[0]
@@ -218,19 +238,23 @@
                 q_ref[:, n * HD : n * HD + HALF] = (low * HD ** (-0.5)).astype(jnp.bfloat16)
                 q_ref[:, n * HD + HALF : (n + 1) * HD] = (high * HD ** (-0.5)).astype(jnp.bfloat16)
             else:
-                kv_ref[:, :HALF] = low.astype(jnp.bfloat16)
-                kv_ref[:, HALF:HD] = high.astype(jnp.bfloat16)
+                for k, kv_ref in enumerate(kv_refs):
+                    rows = slice(k * block, (k + 1) * block)
+                    kv_ref[:, :HALF] = low[rows].astype(jnp.bfloat16)
+                    kv_ref[:, HALF:HD] = high[rows].astype(jnp.bfloat16)
         else:
-            kv_ref[:, HD:] = raw.astype(jnp.bfloat16)
+            for k, kv_ref in enumerate(kv_refs):
+                kv_ref[:, HD:] = raw[k * block : (k + 1) * block].astype(jnp.bfloat16)
 
 
 def project(normed, cosine, sine, pieces, heads):
     rows, depth = normed.shape
     width = pieces[0].shape[1]
-    low = lambda n: jax.ShapeDtypeStruct((rows, n), jnp.bfloat16)
+    low = lambda m, n: jax.ShapeDtypeStruct((m, n), jnp.bfloat16)
     scratch = [pltpu.VMEM((depth, width), jnp.bfloat16)] if len(pieces) > 1 else []
     return call(
-        partial(project_kernel, heads=heads, parts=len(pieces)), (low(heads * HD), low(2 * HD)),
+        partial(project_kernel, heads=heads, parts=len(pieces)),
+        (low(rows, heads * HD), low(rows // 2, 2 * HD), low(rows // 2, 2 * HD)),
         (places_of(pieces), normed, cosine, sine, *pieces), "project", scalars=1, scratch=scratch,
         flops=2 * rows * depth * width,
     )
@@ -248,13 +272,13 @@
         branch_ref[:, n : n + 256] = part.astype(jnp.bfloat16)
 
 
-def out_project(attn, pieces, depth):
+def out_project(attn, pieces, depth, name="out_project"):
     rows, width = attn.shape
     scratch = [pltpu.VMEM((depth, width), jnp.bfloat16)] if len(pieces) > 1 else []
     return call(
         partial(out_project_kernel, parts=len(pieces)),
         jax.ShapeDtypeStruct((rows, depth), jnp.bfloat16), (places_of(pieces), attn, *pieces),
-        "out_project", scalars=1, scratch=scratch, flops=2 * rows * depth * width,
+        name, scalars=1, scratch=scratch, flops=2 * rows * depth * width,
     )
 
 
@@ -453,32 +477,6 @@
         ),
         name="units",
     )(normed, full_gate, full_up)
-
-
-def down_kernel(hidden_ref, down_ref, out_ref):
-    for n in range(0, UNITS, STEP):
-        part = matmul_nt(hidden_ref[...], down_ref[n : n + STEP, :])
-        out_ref[:, n : n + STEP] = part.astype(jnp.bfloat16)
-
-
-def project_down(hidden, full_down_t):
-    rows, count = hidden.shape
-    depth = full_down_t.shape[0]
-    return pl.pallas_call(
-        down_kernel,
-        out_shape=jax.ShapeDtypeStruct((rows, depth), jnp.bfloat16),
-        grid=(depth // UNITS,),
-        in_specs=[
-            pl.BlockSpec((rows, count), lambda i: (0, 0)),
-            pl.BlockSpec((UNITS, count), lambda i: (i, 0)),
-        ],
-        out_specs=pl.BlockSpec((rows, UNITS), lambda i: (0, i)),
-        compiler_params=pltpu.CompilerParams(vmem_limit_bytes=MOST),
-        cost_estimate=pl.CostEstimate(
-            flops=2 * rows * depth * count, bytes_accessed=2 * depth * count, transcendentals=0
-        ),
-        name="project_down",
-    )(hidden, full_down_t)
 
 
 def units_back_kernel(grad_ref, down_ref, active_ref, slope_ref, dg_ref, du_ref):
@@ -880,14 +878,15 @@
     inputs = tokens.astype(jnp.float32)
     in_scale = rms_scale(inputs)
     unit_in = (inputs * in_scale).astype(jnp.bfloat16)
-    queries, kv_local = project(unit_in, cosine, sine, qkv_pieces, heads_dev)
+    queries, *kv_local = project(unit_in, cosine, sine, qkv_pieces, heads_dev)
     if pairs:
-        kv_local, *out_near = lax.optimization_barrier((kv_local, *out_near))
-        kv_pieces = gather_pieces(kv_local)
-        out_pieces = gather_pieces(tie(out_shard, *kv_pieces[1:3]), out_near)
-        late = (*kv_pieces[3:5], *out_pieces[3:5])
+        kv_local, out_near = lax.optimization_barrier((kv_local, out_near))
+        kv_near = nearby_halves(*kv_local)
+        kv_pieces = gather_halves(*kv_local, kv_near)
+        out_pieces = gather_pieces(tie(out_shard, *kv_near), out_near)
+        late = (*kv_pieces[2:8], *out_pieces[3:5])
     else:
-        kv_pieces = (lax.all_gather(kv_local, "ctx", axis=0, tiled=True),)
+        kv_pieces = (lax.all_gather(jnp.concatenate(kv_local), "ctx", axis=0, tiled=True),)
         late = kv_pieces
     w_gate, w_up, w_down, *_ = lax.optimization_barrier((w_gate, w_up, w_down, *late))
     if pairs:
@@ -917,20 +916,25 @@
     else:
         full_gate = lax.all_gather(w_gate, "ctx", axis=0, tiled=True)
         down_pieces = (lax.all_gather(w_down.T, "ctx", axis=0, tiled=True),)
-    branch, full_gate, full_up, *mine = lax.optimization_barrier(
-        (branch, full_gate, full_up, *down_pieces[:5])
-    )
-    down_pieces = (*mine, *down_pieces[5:])
+    branch, full_gate, full_up, *near = lax.optimization_barrier(
+        (branch, full_gate, full_up, *down_pieces[:3])
+    )
     normed_mid = by_rows(mid_kernel, (tokens, branch), gains, (jnp.bfloat16,), 0, "mid_norms")
+    if pairs:
+        normed_mid, *far = lax.optimization_barrier((normed_mid, *down_pieces[3:5]))
+        mine = (*near, *far)
+        down_pieces = (*mine, *(swap(part, 1) for part in mine))
     hidden, active, slope = units(normed_mid, full_gate, full_up)
+    mlp_part = out_project(hidden, down_pieces, depth, "project_down")
+    mlp_part, out_pieces, kv_pieces, down_pieces = lax.optimization_barrier(
+        (mlp_part, out_pieces, kv_pieces, down_pieces)
+    )
     full_down_t = assemble(down_pieces, 3)
-    mlp_part = project_down(hidden, full_down_t)
-    mlp_part, out_pieces, kv_pieces = lax.optimization_barrier((mlp_part, out_pieces, kv_pieces))
     full_out_t = assemble(out_pieces)
     kv_all, key_turned = turn(kv_pieces)
     mlp_out = lax.psum(mlp_part, "tp")
-    mlp_out, full_out_t, kv_all, key_turned = lax.optimization_barrier(
-        (mlp_out, full_out_t, kv_all, key_turned)
+    mlp_out, full_out_t, kv_all, key_turned, full_down_t = lax.optimization_barrier(
+        (mlp_out, full_out_t, kv_all, key_turned, full_down_t)
     )
     result, mlp_low, gain_four = by_rows(
         top_kernel, (tokens, branch, mlp_out, cotangent), gains, (jnp.bfloat16, jnp.bfloat16), 1,

time: 730 us -> 713 us (0.977)
  waiting for transfers between devices: 358 us -> 334 us
  Pallas kernels: 166 us -> 174 us
    ppermute x69 -> x74, waiting for transfers between devices: 232 us -> 215 us  [swap(): return lax.ppermute(value, 'ctx', pairs)]
    pallas_call x1 -> x0, Pallas kernels: 10 us -> none  [project_down(): pl.pallas_call(down_kernel, out_shape=jax.ShapeDtypeStruct((rows, depth),...]
    pallas_call x5 -> x6, Pallas kernels: 15.6 us -> 24.8 us  [call(): pl.pallas_call(kernel, out_shape=out_shape, in_specs=[pl.BlockSpec(memory...]
    psum x1, waiting for transfers between devices: 85 us -> 77 us  [body(): mlp_out = lax.psum(mlp_part, 'tp')]
    ppermute x69 -> x74, starting transfers between devices: 55.8 us -> 49.2 us  [swap(): return lax.ppermute(value, 'ctx', pairs)]
    unnamed x144 -> x178, local copies, waits for them, and re-layouts: 33.4 us -> 37 us
  transfers between devices with their start and end apart: 78 -> 83, of which waited for: 42 -> 43; matrix products, arithmetic and copies ran while one was open for 12% -> 13% of each run, Pallas kernels for 13% -> 16%
where the time goes in v4:
time: 713 us; the launch traced here: 704 us
  waiting for transfers between devices  334 us (47%)
  Pallas kernels  174 us (24%)
  local copies, waits for them, and re-layouts  58.8 us (8%)
  starting transfers between devices  52.2 us (7%)
  other arithmetic  35.8 us (5%)
  matrix products  31.6 us (4%)
  between operations  17 us (2%)
    ppermute x74, waiting for transfers between devices, swap(): return lax.ppermute(value, 'ctx', pairs)  215 us
    psum x1, waiting for transfers between devices, body(): mlp_out = lax.psum(mlp_part, 'tp')  77 us
    ppermute x74, starting transfers between devices, swap(): return lax.ppermute(value, 'ctx', pairs)  49.2 us
    unnamed x178, local copies, waits for them, and re-layouts  37 us
    pallas_call x4, Pallas kernels, by_rows(): pl.pallas_call(kernel, out_shape=tuple(shapes), grid=(rows // block,), in...  35.1 us
    dot_general x5, matrix products, matmul(): return jnp.dot(left, right, preferred_element_type=jnp.float32)  31.6 us
    pallas_call x4, Pallas kernels, assemble(): pl.pallas_call(assemble_kernel, out_shape=jax.ShapeDtypeStruct((8 * rows,...  27.4 us
    pallas_call x1, Pallas kernels, attend_back(): pl.pallas_call(kernel, out_shape=(jax.ShapeDtypeStruct((rows, width), jnp...  25.2 us
  transfers between devices with their start and end apart: 83, of which 43 were waited for; matrix products, arithmetic and copies ran while one was open for 13% of the time, Pallas kernels for 16%

profile of v4, /device:TPU:0, one launch (start us, length us, event | category | flops | bytes accessed | tf_op | source)
XLA Modules:
  0.0 703.5 jit_solution(1436798488408228781)
XLA Ops:
  18.7 11.2 %collective-permute-done.refs_1_ = bf16[288,1152]{1,0:T(8,128)(2,1)S(1)} collective-permute-done((bf16[288,1152]{1,0:T(8,128)(2,1)S(1)}, bf16[288,1152]{1,0:T(8,128)(2,1)S(1)}, u32[]{:S(2)}, u32[]{:S(2)}) %collective-permute-start) | collective-permute-done | bytes 663584 | tf_op jit(solution)/shard_map/ppermute | solution.py:67
  63.5 5.9 collective-permute-done.25.refs_3_
  91.7 14.1 %attend.1 = (f32[512,512]{1,0:T(8,128)}, bf16[512,512]{1,0:T(8,128)(2,1)}, f32[512,256]{1,0:T(8,128)}) custom-call(s32[16]{0:T(128)} %reshape.111.map_ref, s32[1]{0:T(128)} %bitcast.8.me_ref, bf16[512,512]{1,0:T(8,128)(2,1)} %copy-done.61, bf16[256,512]{1,0:T(8,128)(2,1)} %copy-done.22, bf16[256,512]{1,0:T(8,128)(2,1)} %copy-done.24, ...), custom_call_target="tpu_custom_call" | custom-call | flops 4294967296 | bytes 10485760 | tf_op jit(solution)/shard_map/attend/pallas_call | solution.py:692
  117.6 5.8 assemble.4.full_ref
  130.4 24.3 %collective-permute-done.34.refs_3_ = bf16[144,2304]{1,0:T(8,128)(2,1)S(1)} collective-permute-done((bf16[144,2304]{1,0:T(8,128)(2,1)}, bf16[144,2304]{1,0:T(8,128)(2,1)S(1)}, u32[]{:S(2)}, u32[]{:S(2)}) %collective-permute-start.34) | collective-permute-done | bytes 663584 | tf_op jit(solution)/shard_map/ppermute | solution.py:67
  159.9 9.2 %assemble.5.gate_ref = bf16[2304,2304]{1,0:T(8,128)(2,1)} custom-call(s32[10]{0:T(128)} %copy-done.56, bf16[288,2304]{1,0:T(8,128)(2,1)} %refs_0_, bf16[288,2304]{1,0:T(8,128)(2,1)} %collective-permute-done.32.refs_1_, bf16[288,2304]{1,0:T(8,128)(2,1)} %collective-permute-done.33.refs_2_, bf16[144,2304]{1,0:T(8,128)(2,1)} %copy-done.78, ...), custom_call_target="tpu_custom_call" | custom-call | bytes 21233664 | tf_op jit(solution)/shard_map/assemble/pallas_call | solution.py:129
  169.0 44.1 %collective-permute-done.41.refs_1_ = bf16[288,2304]{1,0:T(8,128)(2,1)S(1)} collective-permute-done((bf16[288,2304]{1,0:T(8,128)(2,1)}, bf16[288,2304]{1,0:T(8,128)(2,1)S(1)}, u32[]{:S(2)}, u32[]{:S(2)}) %collective-permute-start.41) | collective-permute-done | bytes 1327136 | tf_op jit(solution)/shard_map/ppermute | solution.py:67
  219.0 6.8 mid_norms.1.in_ref
  225.9 5.6 collective-permute-done.43.refs_3_
  233.5 18.6 %units.1 = (bf16[512,2304]{1,0:T(8,128)(2,1)}, bf16[512,2304]{1,0:T(8,128)(2,1)}, bf16[512,2304]{1,0:T(8,128)(2,1)}) custom-call(bf16[512,2304]{1,0:T(8,128)(2,1)} %mid_norms.1.in_ref, bf16[2304,2304]{1,0:T(8,128)(2,1)} %assemble.5.gate_ref, bf16[2304,2304]{1,0:T(8,128)(2,1)} %all-gather.2.cloned.1.call-done.up_ref), custom_call_target="tpu_custom_call" | custom-call | flops 10871635968 | bytes 21233664 | tf_op jit(solution)/shard_map/units/pallas_call | solution.py:467
  253.8 9.4 %project_down.1 = bf16[512,2304]{1,0:T(8,128)(2,1)S(1)} custom-call(s32[10]{0:T(128)S(1)} %copy-done.57, bf16[512,2304]{1,0:T(8,128)(2,1)S(1)} %copy-done.62, bf16[288,2304]{1,0:T(8,128)(2,1)} %bitcast.11.refs_0_, bf16[288,2304]{1,0:T(8,128)(2,1)S(1)} %collective-permute-done.41.refs_1_, bf16[288,2304]{1,0:T(8,128)(2,1)S(1)} %collective-permute-done.42.refs_2_, ...), custom_call_target="tpu_custom_call" | custom-call | flops 5435817984 | bytes 15335464 | tf_op jit(solution)/shard_map/project_down/pallas_call | solution.py:53
  265.1 9.1 %assemble.7.down_ref = bf16[2304,2304]{1,0:T(8,128)(2,1)} custom-call(s32[10]{0:T(128)} %copy-done.56, bf16[288,2304]{1,0:T(8,128)(2,1)} %bitcast.11.refs_0_, bf16[288,2304]{1,0:T(8,128)(2,1)} %copy-done.1, bf16[288,2304]{1,0:T(8,128)(2,1)} %copy-done.2, bf16[144,2304]{1,0:T(8,128)(2,1)} %copy-done.12, bf16[144,2304]{1,0:T(8,128)(2,1)} %collective-permute-done.44.refs_4_, ...), custom_call_target="tpu_custom_call" | custom-call | bytes 21233664 | tf_op jit(solution)/shard_map/assemble/pallas_call | solution.py:129
  283.1 77.0 %all-reduce.7.cloned.1.call-done.mlp_ref = bf16[512,2304]{1,0:T(8,128)(2,1)} async-done(((bf16[512,2304]{1,0:T(8,128)(2,1)}), bf16[512,2304]{1,0:T(8,128)(2,1)}) %all-reduce.7.cloned.1.call-update) | async-done | bytes 2359312 | tf_op jit(solution)/shard_map/psum | solution.py:935
  360.1 8.5 %top_norms.1 = (bf16[512,2304]{1,0:T(8,128)(2,1)}, bf16[512,2304]{1,0:T(8,128)(2,1)}, f32[1,2304]{1,0:T(1,128)}) custom-call(bf16[512,2304]{1,0:T(8,128)(2,1)} %tok_ref.7, bf16[512,2304]{1,0:T(8,128)(2,1)} %all-reduce.5.cloned.1.call-done.branch_ref, bf16[512,2304]{1,0:T(8,128)(2,1)} %all-reduce.7.cloned.1.call-done.mlp_ref, bf16[512,2304]{1,0:T(8,128)(2,1)} %cot_ref.3, ...), custom_call_target="tpu_custom_call" | custom-call | bytes 14164992 | tf_op jit(solution)/shard_map/top_norms/pallas_call | solution.py:428
  368.6 11.9 %units_back.1 = (bf16[512,2304]{1,0:T(8,128)(2,1)}, bf16[512,2304]{1,0:T(8,128)(2,1)}) custom-call(bf16[512,2304]{1,0:T(8,128)(2,1)} %get-tuple-element.256.grad_ref, bf16[2304,2304]{1,0:T(8,128)(2,1)} %assemble.7.down_ref, bf16[512,2304]{1,0:T(8,128)(2,1)} %get-tuple-element.235.active_ref, bf16[512,2304]{1,0:T(8,128)(2,1)} %get-tuple-element.236.slope_ref), custom_call_target="tpu_custom_call" | custom-call | flops 5435817984 | bytes 10616832 | tf_op jit(solution)/shard_map/units_back/pallas_call | solution.py:495
  380.5 16.9 %features_back.1 = bf16[512,2304]{1,0:T(8,128)(2,1)} custom-call(bf16[512,2304]{1,0:T(8,128)(2,1)} %get-tuple-element.241.dg_ref, bf16[512,2304]{1,0:T(8,128)(2,1)} %get-tuple-element.240.du_ref, bf16[2304,2304]{1,0:T(8,128)(2,1)} %assemble.5.gate_ref, bf16[2304,2304]{1,0:T(8,128)(2,1)} %all-gather.2.cloned.1.call-done.up_ref), custom_call_target="tpu_custom_call" | custom-call | flops 10871635968 | bytes 21233664 | tf_op jit(solution)/shard_map/features_back/pallas_call | solution.py:521
  399.1 9.7 %convolution_convert_fusion = bf16[2304,2304]{0,1:T(8,128)(2,1)} fusion(bf16[512,2304]{1,0:T(8,128)(2,1)S(1)} %copy-done.63, bf16[512,2304]{1,0:T(8,128)(2,1)} %get-tuple-element.256.grad_ref), kind=kOutput, calls=%fused_computation | convolution fusion | flops 5441126400 | bytes 15335424 | tf_op jit(solution)/shard_map/dot_general | solution.py:33
  410.5 7.6 %convolution_convert_fusion.1 = bf16[2304,2304]{1,0:T(8,128)(2,1)S(1)} fusion(bf16[512,2304]{1,0:T(8,128)(2,1)S(1)} %copy-done.71, bf16[512,2304]{1,0:T(8,128)(2,1)} %get-tuple-element.241.dg_ref), kind=kOutput, calls=%fused_computation.1 | convolution fusion | flops 5441126400 | bytes 15335424 | tf_op jit(solution)/shard_map/dot_general | solution.py:33
  426.4 9.1 %collective-permute-done.50 = bf16[4,288,2304]{2,1,0:T(8,128)(2,1)} collective-permute-done((bf16[4,288,2304]{2,1,0:T(8,128)(2,1)}, bf16[4,288,2304]{2,1,0:T(8,128)(2,1)}, u32[]{:S(2)}, u32[]{:S(2)}) %collective-permute-start.50) | collective-permute-done | bytes 5308448 | tf_op jit(solution)/shard_map/ppermute | solution.py:67
  446.5 8.3 %convolution_convert_fusion.2 = bf16[2304,2304]{1,0:T(8,128)(2,1)} fusion(bf16[512,2304]{1,0:T(8,128)(2,1)S(1)} %copy-done.72, bf16[512,2304]{1,0:T(8,128)(2,1)S(1)} %copy-done.86), kind=kOutput, calls=%fused_computation.2 | convolution fusion | flops 5441126400 | bytes 15335424 | tf_op jit(solution)/shard_map/dot_general | solution.py:33
  457.3 18.1 %collective-permute-done.51 = bf16[144,2304]{1,0:T(8,128)(2,1)S(1)} collective-permute-done((bf16[144,2304]{1,0:T(8,128)(2,1)}, bf16[144,2304]{1,0:T(8,128)(2,1)S(1)}, u32[]{:S(2)}, u32[]{:S(2)}) %collective-permute-start.51) | collective-permute-done | bytes 663584 | tf_op jit(solution)/shard_map/ppermute | solution.py:67
  482.0 10.3 %all-reduce.9.cloned.1.call-done.mid_ref = bf16[512,2304]{1,0:T(8,128)(2,1)} async-done(((bf16[512,2304]{1,0:T(8,128)(2,1)}), bf16[512,2304]{1,0:T(8,128)(2,1)}) %all-reduce.9.cloned.1.call-update) | async-done | bytes 2359312 | tf_op jit(solution)/shard_map/psum | solution.py:948
  492.3 11.6 %low_norms.1 = (f32[512,2304]{1,0:T(8,128)}, bf16[512,2304]{1,0:T(8,128)(2,1)}, f32[2,2304]{1,0:T(2,128)}) custom-call(bf16[512,2304]{1,0:T(8,128)(2,1)} %tok_ref.7, bf16[512,2304]{1,0:T(8,128)(2,1)} %all-reduce.5.cloned.1.call-done.branch_ref, bf16[512,2304]{1,0:T(8,128)(2,1)} %all-reduce.9.cloned.1.call-done.mid_ref, bf16[512,2304]{1,0:T(8,128)(2,1)} %cot_ref.3, ...), custom_call_target="tpu_custom_call" | custom-call | bytes 16533504 | tf_op jit(solution)/shard_map/low_norms/pallas_call | solution.py:428
  503.9 25.2 %attend_back.1 = (bf16[512,512]{1,0:T(8,128)(2,1)}, bf16[1536,512]{1,0:T(8,128)(2,1)}, bf16[512,512]{1,0:T(8,128)(2,1)}, bf16[1536,512]{1,0:T(8,128)(2,1)}, bf16[512,512]{1,0:T(8,128)(2,1)}) custom-call(s32[16]{0:T(128)} %reshape.111.map_ref, s32[1]{0:T(128)} %bitcast.8.me_ref, bf16[512,2304]{1,0:T(8,128)(2,1)} %get-tuple-element.270.da_ref, ...), custom_call_target="tpu_custom_call" | custom-call | flops 10737418240 | bytes 14680064 | tf_op jit(solution)/shard_map/attend_back/pallas_call | solution.py:811
  539.0 6.1 collective-permute-done.57
  547.6 12.0 %collective-permute-done.60.refs_2_ = bf16[512,512]{1,0:T(8,128)(2,1)S(1)} collective-permute-done((bf16[512,512]{1,0:T(8,128)(2,1)S(1)}, bf16[512,512]{1,0:T(8,128)(2,1)S(1)}, u32[]{:S(2)}, u32[]{:S(2)}) %collective-permute-start.60) | collective-permute-done | bytes 524320 | tf_op jit(solution)/shard_map/ppermute | solution.py:67
  609.2 10.1 %collective-permute-done.62 = bf16[144,1024]{1,0:T(8,128)(2,1)S(1)} collective-permute-done((bf16[144,1024]{1,0:T(8,128)(2,1)S(1)}, bf16[144,1024]{1,0:T(8,128)(2,1)S(1)}, u32[]{:S(2)}, u32[]{:S(2)}) %collective-permute-start.62) | collective-permute-done | bytes 294944 | tf_op jit(solution)/shard_map/ppermute | solution.py:67
  627.7 5.7 collective-permute-done.68
  634.3 19.7 %collective-permute-done.63 = bf16[288,1024]{1,0:T(8,128)(2,1)S(1)} collective-permute-done((bf16[288,1024]{1,0:T(8,128)(2,1)S(1)}, bf16[288,1024]{1,0:T(8,128)(2,1)S(1)}, u32[]{:S(2)}, u32[]{:S(2)}) %collective-permute-start.63) | collective-permute-done | bytes 589856 | tf_op jit(solution)/shard_map/ppermute | solution.py:67
  656.0 22.4 %reduce-scatter.5.cloned.1.call-done = bf16[288,2304]{1,0:T(8,128)(2,1)} async-done(((bf16[2304,2304]{1,0:T(8,128)(2,1)}), bf16[288,2304]{1,0:T(8,128)(2,1)}) %reduce-scatter.5.cloned.1.call-update) | async-done | bytes 1327120 | tf_op jit(solution)/shard_map/reduce_scatter | solution.py:979
  681.4 6.1 all-reduce.11.cloned.1.call-done.sum_ref
  687.5 8.2 %end_norms.1 = f32[512,2304]{1,0:T(8,128)} custom-call(bf16[512,2304]{1,0:T(8,128)(2,1)} %tok_ref.7, bf16[512,2304]{1,0:T(8,128)(2,1)} %all-reduce.11.cloned.1.call-done.sum_ref, f32[512,2304]{1,0:T(8,128)} %get-tuple-element.279.resid_ref, f32[4,2304]{1,0:T(4,128)} %bitcast.119), custom_call_target="tpu_custom_call" | custom-call | bytes 14155776 | tf_op jit(solution)/shard_map/end_norms/pallas_call | solution.py:428
  (413 shorter events, 217.9 us)
Async XLA Ops:
  8.0 210.2 %all-reduce.5.cloned.1.call-start = ((), (), s32[]{:S(2)}) async-start(), calls=%async_computation.2 | async-start | bytes 4718592 | tf_op jit(solution)/shard_map/psum | solution.py:902
  16.4 26.5 %collective-permute-start.4 = (bf16[288,1152]{1,0:T(8,128)(2,1)S(1)}, bf16[288,1152]{1,0:T(8,128)(2,1)}, u32[]{:S(2)}, u32[]{:S(2)}) collective-permute-start(bf16[288,1152]{1,0:T(8,128)(2,1)S(1)} %pack.1.refs_0_), channel_id=1, source_target_pairs={{0,4},{4,0},{8,12},{12,8},{16,20},{20,16},{24,28},{28,24},{1,5},{5... | collective-permute-start | bytes 1990664 | tf_op jit(solution)/shard_map/ppermute | solution.py:67
  82.0 29.8 %collective-permute-start.32 = (bf16[288,2304]{1,0:T(8,128)(2,1)}, bf16[288,2304]{1,0:T(8,128)(2,1)}, u32[]{:S(2)}, u32[]{:S(2)}) collective-permute-start(bf16[288,2304]{1,0:T(8,128)(2,1)} %refs_0_), channel_id=1, source_target_pairs={{0,8},{4,12},{8,0},{12,4},{16,24},{20,28},{24,16},{28,20},{1,9},{5... | collective-permute-start | bytes 3981320 | tf_op jit(solution)/shard_map/ppermute | solution.py:67
  83.5 28.9 %collective-permute-start.33 = (bf16[288,2304]{1,0:T(8,128)(2,1)}, bf16[288,2304]{1,0:T(8,128)(2,1)}, u32[]{:S(2)}, u32[]{:S(2)}) collective-permute-start(bf16[288,2304]{1,0:T(8,128)(2,1)} %refs_0_), channel_id=1, source_target_pairs={{0,16},{4,20},{8,24},{12,28},{16,0},{20,4},{24,8},{28,12},{1,17},{... | collective-permute-start | bytes 3981320 | tf_op jit(solution)/shard_map/ppermute | solution.py:67
  112.4 105.9 %all-gather.2.cloned.1.call-start = ((), (), s32[]{:S(2)}) async-start(), calls=%async_computation.3 | async-start | bytes 11943936 | tf_op jit(solution)/shard_map/all_gather | solution.py:903
  113.0 247.1 %all-reduce.7.cloned.1.call-start = ((), (), s32[]{:S(2)}) async-start(), calls=%async_computation.4 | async-start | bytes 4718592 | tf_op jit(solution)/shard_map/psum | solution.py:935
  113.0 43.3 %collective-permute-start.36 = (bf16[288,2304]{1,0:T(8,128)(2,1)}, bf16[288,2304]{1,0:T(8,128)(2,1)}, u32[]{:S(2)}, u32[]{:S(2)}) collective-permute-start(bf16[288,2304]{1,0:T(8,128)(2,1)} %refs_0_), channel_id=1, source_target_pairs={{0,4},{4,0},{8,12},{12,8},{16,20},{20,16},{24,28},{28,24},{1,5},{5... | collective-permute-start | bytes 3981320 | tf_op jit(solution)/shard_map/ppermute | solution.py:67
  115.1 44.0 %collective-permute-start.37 = (bf16[288,2304]{1,0:T(8,128)(2,1)}, bf16[288,2304]{1,0:T(8,128)(2,1)}, u32[]{:S(2)}, u32[]{:S(2)}) collective-permute-start(bf16[288,2304]{1,0:T(8,128)(2,1)} %collective-permute-done.32.refs_1_), channel_id=1, source_target_pairs={{0,4},{4,0},{8,12},{12,8},{16,20},{20,16},{24,28},{28,24},{1,5},{5... | collective-permute-start | bytes 3981320 | tf_op jit(solution)/shard_map/ppermute | solution.py:67
  117.5 42.3 %collective-permute-start.38 = (bf16[288,2304]{1,0:T(8,128)(2,1)}, bf16[288,2304]{1,0:T(8,128)(2,1)}, u32[]{:S(2)}, u32[]{:S(2)}) collective-permute-start(bf16[288,2304]{1,0:T(8,128)(2,1)} %collective-permute-done.33.refs_2_), channel_id=1, source_target_pairs={{0,4},{4,0},{8,12},{12,8},{16,20},{20,16},{24,28},{28,24},{1,5},{5... | collective-permute-start | bytes 3981320 | tf_op jit(solution)/shard_map/ppermute | solution.py:67
  125.6 29.1 %collective-permute-start.34 = (bf16[144,2304]{1,0:T(8,128)(2,1)}, bf16[144,2304]{1,0:T(8,128)(2,1)S(1)}, u32[]{:S(2)}, u32[]{:S(2)}) collective-permute-start(bf16[144,2304]{1,0:T(8,128)(2,1)} %slice.210), channel_id=1, source_target_pairs={{0,16},{4,20},{8,24},{12,28},{16,0},{20,4},{24,8},{28,12},{1,17},{... | collective-permute-start | bytes 1990664 | tf_op jit(solution)/shard_map/ppermute | solution.py:67
  127.3 27.5 %collective-permute-start.35 = (bf16[144,2304]{1,0:T(8,128)(2,1)}, bf16[144,2304]{1,0:T(8,128)(2,1)S(1)}, u32[]{:S(2)}, u32[]{:S(2)}) collective-permute-start(bf16[144,2304]{1,0:T(8,128)(2,1)} %slice.211), channel_id=1, source_target_pairs={{0,8},{4,12},{8,0},{12,4},{16,24},{20,28},{24,16},{28,20},{1,9},{5... | collective-permute-start | bytes 1990664 | tf_op jit(solution)/shard_map/ppermute | solution.py:67
  154.8 58.4 %collective-permute-start.41 = (bf16[288,2304]{1,0:T(8,128)(2,1)}, bf16[288,2304]{1,0:T(8,128)(2,1)S(1)}, u32[]{:S(2)}, u32[]{:S(2)}) collective-permute-start(bf16[288,2304]{1,0:T(8,128)(2,1)} %bitcast.11.refs_0_), channel_id=1, source_target_pairs={{0,8},{4,12},{8,0},{12,4},{16,24},{20,28},{24,16},{28,20},{1,9},{5... | collective-permute-start | bytes 3981320 | tf_op jit(solution)/shard_map/ppermute | solution.py:67
  156.3 59.3 %collective-permute-start.42 = (bf16[288,2304]{1,0:T(8,128)(2,1)}, bf16[288,2304]{1,0:T(8,128)(2,1)S(1)}, u32[]{:S(2)}, u32[]{:S(2)}) collective-permute-start(bf16[288,2304]{1,0:T(8,128)(2,1)} %bitcast.11.refs_0_), channel_id=1, source_target_pairs={{0,16},{4,20},{8,24},{12,28},{16,0},{20,4},{24,8},{28,12},{1,17},{... | collective-permute-start | bytes 3981320 | tf_op jit(solution)/shard_map/ppermute | solution.py:67
  218.3 33.8 %collective-permute-start.45 = (bf16[288,2304]{1,0:T(8,128)(2,1)}, bf16[288,2304]{1,0:T(8,128)(2,1)}, u32[]{:S(2)}, u32[]{:S(2)}) collective-permute-start(bf16[288,2304]{1,0:T(8,128)(2,1)} %bitcast.11.refs_0_), channel_id=1, source_target_pairs={{0,4},{4,0},{8,12},{12,8},{16,20},{20,16},{24,28},{28,24},{1,5},{5... | collective-permute-start | bytes 3981320 | tf_op jit(solution)/shard_map/ppermute | solution.py:67
  218.5 33.5 %collective-permute-start.46 = (bf16[288,2304]{1,0:T(8,128)(2,1)S(1)}, bf16[288,2304]{1,0:T(8,128)(2,1)}, u32[]{:S(2)}, u32[]{:S(2)}) collective-permute-start(bf16[288,2304]{1,0:T(8,128)(2,1)S(1)} %collective-permute-done.41.refs_1_), channel_id=1, source_target_pairs={{0,4},{4,0},{8,12},{12,8},{16,20},{20,16},{24,28},{28,24},{1,5},{5... | collective-permute-start | bytes 3981320 | tf_op jit(solution)/shard_map/ppermute | solution.py:67
  218.8 33.3 %collective-permute-start.47 = (bf16[288,2304]{1,0:T(8,128)(2,1)S(1)}, bf16[288,2304]{1,0:T(8,128)(2,1)}, u32[]{:S(2)}, u32[]{:S(2)}) collective-permute-start(bf16[288,2304]{1,0:T(8,128)(2,1)S(1)} %collective-permute-done.42.refs_2_), channel_id=1, source_target_pairs={{0,4},{4,0},{8,12},{12,8},{16,20},{20,16},{24,28},{28,24},{1,5},{5... | collective-permute-start | bytes 3981320 | tf_op jit(solution)/shard_map/ppermute | solution.py:67
  233.0 19.1 %collective-permute-start.48 = (bf16[144,2304]{1,0:T(8,128)(2,1)S(1)}, bf16[144,2304]{1,0:T(8,128)(2,1)}, u32[]{:S(2)}, u32[]{:S(2)}) collective-permute-start(bf16[144,2304]{1,0:T(8,128)(2,1)S(1)} %collective-permute-done.43.refs_3_), channel_id=1, source_target_pairs={{0,4},{4,0},{8,12},{12,8},{16,20},{20,16},{24,28},{28,24},{1,5},{5... | collective-permute-start | bytes 1990664 | tf_op jit(solution)/shard_map/ppermute | solution.py:67
  233.0 19.1 %collective-permute-start.49 = (bf16[144,2304]{1,0:T(8,128)(2,1)}, bf16[144,2304]{1,0:T(8,128)(2,1)}, u32[]{:S(2)}, u32[]{:S(2)}) collective-permute-start(bf16[144,2304]{1,0:T(8,128)(2,1)} %collective-permute-done.44.refs_4_), channel_id=1, source_target_pairs={{0,4},{4,0},{8,12},{12,8},{16,20},{20,16},{24,28},{28,24},{1,5},{5... | collective-permute-start | bytes 1990664 | tf_op jit(solution)/shard_map/ppermute | solution.py:67
  264.7 227.6 %all-reduce.9.cloned.1.call-start = ((), (), s32[]{:S(2)}) async-start(), calls=%async_computation.5 | async-start | bytes 4718592 | tf_op jit(solution)/shard_map/psum | solution.py:948
  397.5 131.7 %reduce-scatter.3.cloned.1.call-start = ((), (), s32[]{:S(2)}) async-start(), calls=%async_computation.6 | async-start | bytes 11943936 | tf_op jit(solution)/shard_map/reduce_scatter | solution.py:950
  408.8 269.6 %reduce-scatter.5.cloned.1.call-start = ((), (), s32[]{:S(2)}) async-start(), calls=%async_computation.8 | async-start | bytes 11943936 | tf_op jit(solution)/shard_map/reduce_scatter | solution.py:979
  443.5 31.9 %collective-permute-start.51 = (bf16[144,2304]{1,0:T(8,128)(2,1)}, bf16[144,2304]{1,0:T(8,128)(2,1)S(1)}, u32[]{:S(2)}, u32[]{:S(2)}) collective-permute-start(bf16[144,2304]{1,0:T(8,128)(2,1)} %get-tuple-element.293), channel_id=1, source_target_pairs={{0,16},{4,20},{8,24},{12,28},{16,0},{20,4},{24,8},{28,12},{1,17},{... | collective-permute-start | bytes 1990664 | tf_op jit(solution)/shard_map/ppermute | solution.py:67
  445.0 31.6 %collective-permute-start.52 = (bf16[144,2304]{1,0:T(8,128)(2,1)S(1)}, bf16[144,2304]{1,0:T(8,128)(2,1)S(1)}, u32[]{:S(2)}, u32[]{:S(2)}) collective-permute-start(bf16[144,2304]{1,0:T(8,128)(2,1)S(1)} %get-tuple-element.292), channel_id=1, source_target_pairs={{0,8},{4,12},{8,0},{12,4},{16,24},{20,28},{24,16},{28,20},{1,9},{5... | collective-permute-start | bytes 1990664 | tf_op jit(solution)/shard_map/ppermute | solution.py:67
  479.9 49.1 %collective-permute-start.53 = (bf16[288,2304]{1,0:T(8,128)(2,1)}, bf16[288,2304]{1,0:T(8,128)(2,1)S(1)}, u32[]{:S(2)}, u32[]{:S(2)}) collective-permute-start(bf16[288,2304]{1,0:T(8,128)(2,1)} %get-tuple-element.258), channel_id=1, source_target_pairs={{0,8},{4,12},{8,0},{12,4},{16,24},{20,28},{24,16},{28,20},{1,9},{5... | collective-permute-start | bytes 3981320 | tf_op jit(solution)/shard_map/ppermute | solution.py:67
  481.4 47.7 %collective-permute-start.54 = (bf16[288,2304]{1,0:T(8,128)(2,1)}, bf16[288,2304]{1,0:T(8,128)(2,1)}, u32[]{:S(2)}, u32[]{:S(2)}) collective-permute-start(bf16[288,2304]{1,0:T(8,128)(2,1)} %get-tuple-element.259), channel_id=1, source_target_pairs={{0,16},{4,20},{8,24},{12,28},{16,0},{20,4},{24,8},{28,12},{1,17},{... | collective-permute-start | bytes 3981320 | tf_op jit(solution)/shard_map/ppermute | solution.py:67
  575.2 23.2 %collective-permute-start.61 = (bf16[4,288,1024]{2,1,0:T(8,128)(2,1)}, bf16[4,288,1024]{2,1,0:T(8,128)(2,1)}, u32[]{:S(2)}, u32[]{:S(2)}) collective-permute-start(bf16[4,288,1024]{2,1,0:T(8,128)(2,1)} %dynamic-slice_bitcast_fusion.1), channel_id=1, source_target_pairs={{0,4},{4,0},{8,12},{12,8},{16,20},{20,16},{24,28},{28,24},{1,5},{5... | collective-permute-start | bytes 7077896 | tf_op jit(solution)/shard_map/ppermute | solution.py:67
  578.4 109.1 %all-reduce.11.cloned.1.call-start = ((), (), s32[]{:S(2)}) async-start(), calls=%async_computation.7 | async-start | bytes 4718592 | tf_op jit(solution)/shard_map/psum | solution.py:978
  594.9 32.2 %collective-permute-start.75 = (f32[1,4,288]{2,1,0:T(4,128)S(1)}, f32[1,4,288]{2,1,0:T(4,128)S(1)}, u32[]{:S(2)}, u32[]{:S(2)}) collective-permute-start(f32[1,4,288]{2,1,0:T(4,128)S(1)} %slice_select_fusion.2), channel_id=1, source_target_pairs={{0,4},{4,0},{8,12},{12,8},{16,20},{20,16},{24,28},{28,24},{1,5},{5... | collective-permute-start | bytes 13832 | tf_op jit(solution)/shard_map/ppermute | solution.py:67
  608.2 25.2 %collective-permute-start.68 = (bf16[288,512]{1,0:T(8,128)(2,1)S(1)}, bf16[288,512]{1,0:T(8,128)(2,1)S(1)}, u32[]{:S(2)}, u32[]{:S(2)}) collective-permute-start(bf16[288,512]{1,0:T(8,128)(2,1)S(1)} %pad_maximum_fusion.6), channel_id=1, source_target_pairs={{0,8},{4,12},{8,0},{12,4},{16,24},{20,28},{24,16},{28,20},{1,9},{5... | collective-permute-start | bytes 884744 | tf_op jit(solution)/shard_map/ppermute | solution.py:67
  608.5 24.9 %collective-permute-start.70 = (bf16[288,512]{1,0:T(8,128)(2,1)S(1)}, bf16[288,512]{1,0:T(8,128)(2,1)S(1)}, u32[]{:S(2)}, u32[]{:S(2)}) collective-permute-start(bf16[288,512]{1,0:T(8,128)(2,1)S(1)} %pad_maximum_fusion.7), channel_id=1, source_target_pairs={{0,16},{4,20},{8,24},{12,28},{16,0},{20,4},{24,8},{28,12},{1,17},{... | collective-permute-start | bytes 884744 | tf_op jit(solution)/shard_map/ppermute | solution.py:67
  621.0 33.0 %collective-permute-start.63 = (bf16[288,1024]{1,0:T(8,128)(2,1)S(1)}, bf16[288,1024]{1,0:T(8,128)(2,1)S(1)}, u32[]{:S(2)}, u32[]{:S(2)}) collective-permute-start(bf16[288,1024]{1,0:T(8,128)(2,1)S(1)} %pad_maximum_fusion.2), channel_id=1, source_target_pairs={{0,8},{4,12},{8,0},{12,4},{16,24},{20,28},{24,16},{28,20},{1,9},{5... | collective-permute-start | bytes 1769480 | tf_op jit(solution)/shard_map/ppermute | solution.py:67
  621.3 32.7 %collective-permute-start.65 = (bf16[288,1024]{1,0:T(8,128)(2,1)S(1)}, bf16[288,1024]{1,0:T(8,128)(2,1)S(1)}, u32[]{:S(2)}, u32[]{:S(2)}) collective-permute-start(bf16[288,1024]{1,0:T(8,128)(2,1)S(1)} %pad_maximum_fusion.3), channel_id=1, source_target_pairs={{0,16},{4,20},{8,24},{12,28},{16,0},{20,4},{24,8},{28,12},{1,17},{... | collective-permute-start | bytes 1769480 | tf_op jit(solution)/shard_map/ppermute | solution.py:67
  (138 other events, 1290.9 us)
Sparse Core Ops, SparseCore 0:
  112.5 95.9 all-reduce.4
  264.8 95.2 all-reduce.6
  397.6 94.6 all-reduce.8
  591.9 95.6 all-reduce.10
Sparse Core Ops, SparseCore 1:
  114.8 103.5 all-gather.1
  408.9 109.6 reduce-scatter.2
  566.8 111.6 reduce-scatter.4

commit v5 on v4

--- a/solution.py
+++ b/solution.py
@@ -147,18 +147,26 @@
     return own, by_x, by_y
 
 
-def scatter_start(whole):
+def scatter_chips(whole):
     if not paired():
-        return (lax.psum_scatter(whole, "ctx", scatter_dimension=0, tiled=True),)
-    me = lax.axis_index("ctx")
-    chip, core = me // 2, me % 2
-    rows = whole.shape[0] // 8
-    blocks = whole.reshape(4, 2, rows, whole.shape[1])
+        return lax.psum_scatter(whole, "ctx", scatter_dimension=0, tiled=True)
+    core = lax.axis_index("ctx") % 2
+    blocks = whole.reshape(4, 2, whole.shape[0] // 8, whole.shape[1])
     theirs = lax.dynamic_index_in_dim(blocks, 1 - core, 1, keepdims=False)
     mine = lax.dynamic_index_in_dim(blocks, core, 1, keepdims=False)
-    mine = mine + swap(theirs, 1)
-    pick = lambda bits: lax.dynamic_index_in_dim(mine, chip ^ bits, 0, keepdims=False)
+    return mine + swap(theirs, 1)
+
+
+def scatter_blocks(chips):
+    if not paired():
+        return (chips,)
+    chip = lax.axis_index("ctx") // 2
+    pick = lambda bits: lax.dynamic_index_in_dim(chips, chip ^ bits, 0, keepdims=False)
     return scatter_corner(pick(0), pick(1), pick(2), pick(3))
+
+
+def scatter_start(whole):
+    return scatter_blocks(scatter_chips(whole))
 
 
 def scatter_finish(blocks):
@@ -883,8 +891,11 @@
         kv_local, out_near = lax.optimization_barrier((kv_local, out_near))
         kv_near = nearby_halves(*kv_local)
         kv_pieces = gather_halves(*kv_local, kv_near)
-        out_pieces = gather_pieces(tie(out_shard, *kv_near), out_near)
-        late = (*kv_pieces[2:8], *out_pieces[3:5])
+        half = out_shard.shape[0] // 2
+        out_far = (swap(out_near[0][:half], 4), swap(out_near[1][half:], 2))
+        out_mine = tie_all((out_shard, *out_near, *out_far), *kv_pieces[6:8])
+        out_pieces = out_mine + tuple(swap(part, 1) for part in out_mine)
+        late = (*kv_pieces[2:8], *out_far)
     else:
         kv_pieces = (lax.all_gather(jnp.concatenate(kv_local), "ctx", axis=0, tiled=True),)
         late = kv_pieces
@@ -953,7 +964,8 @@
     up_grad = matmul(normed_mid.T, up_t).astype(jnp.bfloat16)
     up_grad, gate_blocks = lax.optimization_barrier((up_grad, gate_blocks))
     gate_terms = scatter_finish(gate_blocks)
-    mid_sum, up_grad = lax.optimization_barrier((mid_sum, up_grad))
+    up_chips = scatter_chips(up_grad)
+    mid_sum, up_chips = lax.optimization_barrier((mid_sum, up_chips))
     resid_grad, branch_low, gain_mid = by_rows(
         low_kernel, (tokens, branch, mid_sum, cotangent), gains, (jnp.float32, jnp.bfloat16), 2,
         "low_norms",
@@ -972,11 +984,11 @@
     else:
         kv_sums = (lax.psum_scatter(kv_terms[0], "ctx", scatter_dimension=0, tiled=True),)
     qkv_low, in_part = join(cosine, sine, query_low, full_qkv, kv_sums)
-    in_part, qkv_low, branch_t, up_grad = lax.optimization_barrier(
-        (in_part, qkv_low, branch_low, up_grad)
+    in_part, qkv_low, branch_t, up_chips = lax.optimization_barrier(
+        (in_part, qkv_low, branch_low, up_chips)
     )
     in_sum = lax.psum(in_part, "tp")
-    up_shard = lax.psum_scatter(up_grad, "ctx", scatter_dimension=0, tiled=True)
+    up_shard = add_terms(scatter_finish(scatter_blocks(up_chips)))
     gain_one = jnp.sum(in_part.astype(jnp.float32) * (inputs * in_scale), axis=0)
     gain_one = sum_small_tp(gain_one)
     gains_shard = scatter_gains(jnp.concatenate([gain_one[None], gain_mid[1:], gain_mid[:1], gain_four]))
@@ -990,11 +1002,10 @@
         qkv_shard[:, q_width + HD :],
         out_grad_t.T,
         gate_shard,
-        up_shard.astype(jnp.float32),
+        up_shard,
         down_shard.astype(jnp.float32),
         gains_shard,
     )
-    in_sum, shards = lax.optimization_barrier((in_sum, shards))
     input_grad = by_rows(
         end_kernel, (tokens, in_sum, resid_grad), gains, (jnp.float32,), 0, "end_norms"
     )

time: 713 us -> 697 us (0.978)
  waiting for transfers between devices: 334 us -> 305 us
  starting transfers between devices: 52.2 us -> 63.8 us
  other arithmetic: 35.8 us -> 44.8 us
    ppermute x74 -> x79, waiting for transfers between devices: 215 us -> 184 us  [swap(): return lax.ppermute(value, 'ctx', pairs)]
    reduce_scatter x1 -> x0, waiting for transfers between devices: 22.4 us -> none  [body(): up_shard = lax.psum_scatter(up_grad, 'ctx', scatter_dimension=0, tiled=True)]
    psum x1, waiting for transfers between devices: 10.3 us -> 25.5 us  [body(): mid_sum = lax.psum(mid_part, 'tp')]
    ppermute x74 -> x79, starting transfers between devices: 49.2 us -> 61.1 us  [swap(): return lax.ppermute(value, 'ctx', pairs)]
    unnamed x178 -> x186, local copies, waits for them, and re-layouts: 37 us -> 25.9 us
  transfers between devices with their start and end apart: 83 -> 87, of which waited for: 43 -> 40; matrix products, arithmetic and copies ran while one was open for 13% -> 14% of each run, Pallas kernels for 16% -> 18%
where the time goes in v5:
time: 697 us; the launch traced here: 688 us
  waiting for transfers between devices  305 us (44%)
  Pallas kernels  175 us (25%)
  starting transfers between devices  63.8 us (9%)
  local copies, waits for them, and re-layouts  53.2 us (8%)
  other arithmetic  44.8 us (6%)
  matrix products  30.6 us (4%)
  between operations  16.8 us (2%)
    ppermute x79, waiting for transfers between devices, swap(): return lax.ppermute(value, 'ctx', pairs)  184 us
    psum x1, waiting for transfers between devices, body(): mlp_out = lax.psum(mlp_part, 'tp')  77.2 us
    ppermute x79, starting transfers between devices, swap(): return lax.ppermute(value, 'ctx', pairs)  61.1 us
    pallas_call x4, Pallas kernels, by_rows(): pl.pallas_call(kernel, out_shape=tuple(shapes), grid=(rows // block,), in...  35.3 us
    dot_general x5, matrix products, matmul(): return jnp.dot(left, right, preferred_element_type=jnp.float32)  30.6 us
    pallas_call x4, Pallas kernels, assemble(): pl.pallas_call(assemble_kernel, out_shape=jax.ShapeDtypeStruct((8 * rows,...  27.4 us
    unnamed x186, local copies, waits for them, and re-layouts  25.9 us
    psum x1, waiting for transfers between devices, body(): mid_sum = lax.psum(mid_part, 'tp')  25.5 us
  transfers between devices with their start and end apart: 87, of which 40 were waited for; matrix products, arithmetic and copies ran while one was open for 14% of the time, Pallas kernels for 18%

profile of v5, /device:TPU:0, one launch (start us, length us, event | category | flops | bytes accessed | tf_op | source)
XLA Modules:
  0.0 688.5 jit_solution(12078124231981390625)
XLA Ops:
  18.7 11.2 %collective-permute-done.refs_1_ = bf16[288,1152]{1,0:T(8,128)(2,1)S(1)} collective-permute-done((bf16[288,1152]{1,0:T(8,128)(2,1)S(1)}, bf16[288,1152]{1,0:T(8,128)(2,1)S(1)}, u32[]{:S(2)}, u32[]{:S(2)}) %collective-permute-start) | collective-permute-done | bytes 663584 | tf_op jit(solution)/shard_map/ppermute | solution.py:67
  51.6 5.2 project.1
  72.1 8.1 %collective-permute-done.26.refs_4_ = bf16[144,512]{1,0:T(8,128)(2,1)S(1)} collective-permute-done((bf16[144,512]{1,0:T(8,128)(2,1)S(1)}, bf16[144,512]{1,0:T(8,128)(2,1)S(1)}, u32[]{:S(2)}, u32[]{:S(2)}) %collective-permute-start.26) | collective-permute-done | bytes 147488 | tf_op jit(solution)/shard_map/ppermute | solution.py:67
  90.0 14.3 %attend.1 = (f32[512,512]{1,0:T(8,128)}, bf16[512,512]{1,0:T(8,128)(2,1)}, f32[512,256]{1,0:T(8,128)}) custom-call(s32[16]{0:T(128)} %reshape.122.map_ref, s32[1]{0:T(128)} %bitcast.8.me_ref, bf16[512,512]{1,0:T(8,128)(2,1)} %copy-done.62, bf16[256,512]{1,0:T(8,128)(2,1)} %copy-done.21, bf16[256,512]{1,0:T(8,128)(2,1)} %copy-done.23, ...), custom_call_target="tpu_custom_call" | custom-call | flops 4294967296 | bytes 10485760 | tf_op jit(solution)/shard_map/attend/pallas_call | solution.py:700
  117.8 5.7 assemble.4.full_ref
  131.5 24.3 %collective-permute-done.34.refs_3_ = bf16[144,2304]{1,0:T(8,128)(2,1)S(1)} collective-permute-done((bf16[144,2304]{1,0:T(8,128)(2,1)}, bf16[144,2304]{1,0:T(8,128)(2,1)S(1)}, u32[]{:S(2)}, u32[]{:S(2)}) %collective-permute-start.34) | collective-permute-done | bytes 663584 | tf_op jit(solution)/shard_map/ppermute | solution.py:67
  161.0 9.2 %assemble.5.gate_ref = bf16[2304,2304]{1,0:T(8,128)(2,1)} custom-call(s32[10]{0:T(128)} %copy-done.57, bf16[288,2304]{1,0:T(8,128)(2,1)} %refs_0_, bf16[288,2304]{1,0:T(8,128)(2,1)} %collective-permute-done.32.refs_1_, bf16[288,2304]{1,0:T(8,128)(2,1)} %collective-permute-done.33.refs_2_, bf16[144,2304]{1,0:T(8,128)(2,1)} %copy-done.75, ...), custom_call_target="tpu_custom_call" | custom-call | bytes 21233664 | tf_op jit(solution)/shard_map/assemble/pallas_call | solution.py:129
  170.2 44.1 %collective-permute-done.41.refs_1_ = bf16[288,2304]{1,0:T(8,128)(2,1)S(1)} collective-permute-done((bf16[288,2304]{1,0:T(8,128)(2,1)}, bf16[288,2304]{1,0:T(8,128)(2,1)S(1)}, u32[]{:S(2)}, u32[]{:S(2)}) %collective-permute-start.41) | collective-permute-done | bytes 1327136 | tf_op jit(solution)/shard_map/ppermute | solution.py:67
  220.1 6.8 mid_norms.1.in_ref
  226.9 5.6 collective-permute-done.43.refs_3_
  234.6 18.6 %units.1 = (bf16[512,2304]{1,0:T(8,128)(2,1)}, bf16[512,2304]{1,0:T(8,128)(2,1)}, bf16[512,2304]{1,0:T(8,128)(2,1)}) custom-call(bf16[512,2304]{1,0:T(8,128)(2,1)} %mid_norms.1.in_ref, bf16[2304,2304]{1,0:T(8,128)(2,1)} %assemble.5.gate_ref, bf16[2304,2304]{1,0:T(8,128)(2,1)} %all-gather.2.cloned.1.call-done.up_ref), custom_call_target="tpu_custom_call" | custom-call | flops 10871635968 | bytes 21233664 | tf_op jit(solution)/shard_map/units/pallas_call | solution.py:475
  254.9 9.4 %project_down.1 = bf16[512,2304]{1,0:T(8,128)(2,1)S(1)} custom-call(s32[10]{0:T(128)S(1)} %copy-done.58, bf16[512,2304]{1,0:T(8,128)(2,1)S(1)} %copy-done.63, bf16[288,2304]{1,0:T(8,128)(2,1)} %bitcast.11.refs_0_, bf16[288,2304]{1,0:T(8,128)(2,1)S(1)} %collective-permute-done.41.refs_1_, bf16[288,2304]{1,0:T(8,128)(2,1)S(1)} %collective-permute-done.42.refs_2_, ...), custom_call_target="tpu_custom_call" | custom-call | flops 5435817984 | bytes 15335464 | tf_op jit(solution)/shard_map/project_down/pallas_call | solution.py:53
  266.0 9.1 %assemble.7.down_ref = bf16[2304,2304]{1,0:T(8,128)(2,1)} custom-call(s32[10]{0:T(128)} %copy-done.57, bf16[288,2304]{1,0:T(8,128)(2,1)} %bitcast.11.refs_0_, bf16[288,2304]{1,0:T(8,128)(2,1)} %copy-done, bf16[288,2304]{1,0:T(8,128)(2,1)} %copy-done.1, bf16[144,2304]{1,0:T(8,128)(2,1)} %copy-done.11, bf16[144,2304]{1,0:T(8,128)(2,1)} %collective-permute-done.44.refs_4_, ...), custom_call_target="tpu_custom_call" | custom-call | bytes 21233664 | tf_op jit(solution)/shard_map/assemble/pallas_call | solution.py:129
  284.0 77.2 %all-reduce.7.cloned.1.call-done.mlp_ref = bf16[512,2304]{1,0:T(8,128)(2,1)} async-done(((bf16[512,2304]{1,0:T(8,128)(2,1)}), bf16[512,2304]{1,0:T(8,128)(2,1)}) %all-reduce.7.cloned.1.call-update) | async-done | bytes 2359312 | tf_op jit(solution)/shard_map/psum | solution.py:946
  361.2 8.5 %top_norms.1 = (bf16[512,2304]{1,0:T(8,128)(2,1)}, bf16[512,2304]{1,0:T(8,128)(2,1)}, f32[1,2304]{1,0:T(1,128)}) custom-call(bf16[512,2304]{1,0:T(8,128)(2,1)} %tok_ref.7, bf16[512,2304]{1,0:T(8,128)(2,1)} %all-reduce.5.cloned.1.call-done.branch_ref, bf16[512,2304]{1,0:T(8,128)(2,1)} %all-reduce.7.cloned.1.call-done.mlp_ref, bf16[512,2304]{1,0:T(8,128)(2,1)} %cot_ref.3, ...), custom_call_target="tpu_custom_call" | custom-call | bytes 14164992 | tf_op jit(solution)/shard_map/top_norms/pallas_call | solution.py:436
  369.8 11.9 %units_back.1 = (bf16[512,2304]{1,0:T(8,128)(2,1)}, bf16[512,2304]{1,0:T(8,128)(2,1)}) custom-call(bf16[512,2304]{1,0:T(8,128)(2,1)} %get-tuple-element.255.grad_ref, bf16[2304,2304]{1,0:T(8,128)(2,1)} %assemble.7.down_ref, bf16[512,2304]{1,0:T(8,128)(2,1)} %get-tuple-element.234.active_ref, bf16[512,2304]{1,0:T(8,128)(2,1)} %get-tuple-element.235.slope_ref), custom_call_target="tpu_custom_call" | custom-call | flops 5435817984 | bytes 10616832 | tf_op jit(solution)/shard_map/units_back/pallas_call | solution.py:503
  381.7 16.9 %features_back.1 = bf16[512,2304]{1,0:T(8,128)(2,1)} custom-call(bf16[512,2304]{1,0:T(8,128)(2,1)} %get-tuple-element.240.dg_ref, bf16[512,2304]{1,0:T(8,128)(2,1)} %get-tuple-element.239.du_ref, bf16[2304,2304]{1,0:T(8,128)(2,1)} %assemble.5.gate_ref, bf16[2304,2304]{1,0:T(8,128)(2,1)} %all-gather.2.cloned.1.call-done.up_ref), custom_call_target="tpu_custom_call" | custom-call | flops 10871635968 | bytes 21233664 | tf_op jit(solution)/shard_map/features_back/pallas_call | solution.py:529
  400.3 7.6 %convolution_convert_fusion.1 = bf16[2304,2304]{1,0:T(8,128)(2,1)S(1)} fusion(bf16[512,2304]{1,0:T(8,128)(2,1)S(1)} %copy-done.69, bf16[512,2304]{1,0:T(8,128)(2,1)} %get-tuple-element.240.dg_ref), kind=kOutput, calls=%fused_computation.1 | convolution fusion | flops 5441126400 | bytes 15335424 | tf_op jit(solution)/shard_map/dot_general | solution.py:33
  414.8 8.4 %convolution_convert_fusion = bf16[2304,2304]{0,1:T(8,128)(2,1)} fusion(bf16[512,2304]{1,0:T(8,128)(2,1)S(1)} %copy-done.64, bf16[512,2304]{1,0:T(8,128)(2,1)S(1)} %copy-done.83), kind=kOutput, calls=%fused_computation | convolution fusion | flops 5441126400 | bytes 15335424 | tf_op jit(solution)/shard_map/dot_general | solution.py:33
  423.9 4.8 bitcast_add_fusion.1
  431.8 8.5 %convolution_convert_fusion.2 = bf16[2304,2304]{1,0:T(8,128)(2,1)} fusion(bf16[512,2304]{1,0:T(8,128)(2,1)S(1)} %copy-done.69, bf16[512,2304]{1,0:T(8,128)(2,1)S(1)} %copy-done.85), kind=kOutput, calls=%fused_computation.2 | convolution fusion | flops 5441126400 | bytes 15335424 | tf_op jit(solution)/shard_map/dot_general | solution.py:33
  440.4 5.4 collective-permute-done.51
  456.0 6.6 collective-permute-done.53
  462.5 5.4 bitcast_add_fusion
  467.9 25.5 %all-reduce.9.cloned.1.call-done.mid_ref = bf16[512,2304]{1,0:T(8,128)(2,1)} async-done(((bf16[512,2304]{1,0:T(8,128)(2,1)}), bf16[512,2304]{1,0:T(8,128)(2,1)}) %all-reduce.9.cloned.1.call-update) | async-done | bytes 2359312 | tf_op jit(solution)/shard_map/psum | solution.py:959
  493.4 11.7 %low_norms.1 = (f32[512,2304]{1,0:T(8,128)}, bf16[512,2304]{1,0:T(8,128)(2,1)}, f32[2,2304]{1,0:T(2,128)}) custom-call(bf16[512,2304]{1,0:T(8,128)(2,1)} %tok_ref.7, bf16[512,2304]{1,0:T(8,128)(2,1)} %all-reduce.5.cloned.1.call-done.branch_ref, bf16[512,2304]{1,0:T(8,128)(2,1)} %all-reduce.9.cloned.1.call-done.mid_ref, bf16[512,2304]{1,0:T(8,128)(2,1)} %cot_ref.3, ...), custom_call_target="tpu_custom_call" | custom-call | bytes 16533504 | tf_op jit(solution)/shard_map/low_norms/pallas_call | solution.py:436
  505.2 25.4 %attend_back.1 = (bf16[512,512]{1,0:T(8,128)(2,1)}, bf16[1536,512]{1,0:T(8,128)(2,1)}, bf16[512,512]{1,0:T(8,128)(2,1)}, bf16[1536,512]{1,0:T(8,128)(2,1)}, bf16[512,512]{1,0:T(8,128)(2,1)}) custom-call(s32[16]{0:T(128)} %reshape.122.map_ref, s32[1]{0:T(128)} %bitcast.8.me_ref, bf16[512,2304]{1,0:T(8,128)(2,1)} %get-tuple-element.270.da_ref, ...), custom_call_target="tpu_custom_call" | custom-call | flops 10737418240 | bytes 14680064 | tf_op jit(solution)/shard_map/attend_back/pallas_call | solution.py:819
  538.7 4.8 collective-permute-start.60
  557.4 7.2 %collective-permute-done.61.refs_2_ = bf16[512,512]{1,0:T(8,128)(2,1)S(1)} collective-permute-done((bf16[512,512]{1,0:T(8,128)(2,1)S(1)}, bf16[512,512]{1,0:T(8,128)(2,1)S(1)}, u32[]{:S(2)}, u32[]{:S(2)}) %collective-permute-start.61) | collective-permute-done | bytes 524320 | tf_op jit(solution)/shard_map/ppermute | solution.py:67
  609.6 25.4 %collective-permute-done.70 = bf16[144,512]{1,0:T(8,128)(2,1)S(1)} collective-permute-done((bf16[144,512]{1,0:T(8,128)(2,1)S(1)}, bf16[144,512]{1,0:T(8,128)(2,1)S(1)}, u32[]{:S(2)}, u32[]{:S(2)}) %collective-permute-start.70) | collective-permute-done | bytes 147488 | tf_op jit(solution)/shard_map/ppermute | solution.py:67
  657.0 12.7 %all-reduce.11.cloned.1.call-done.sum_ref = bf16[512,2304]{1,0:T(8,128)(2,1)} async-done(((bf16[512,2304]{1,0:T(8,128)(2,1)}), bf16[512,2304]{1,0:T(8,128)(2,1)}) %all-reduce.11.cloned.1.call-update) | async-done | bytes 2359312 | tf_op jit(solution)/shard_map/psum | solution.py:990
  669.6 8.3 %end_norms.1 = f32[512,2304]{1,0:T(8,128)} custom-call(bf16[512,2304]{1,0:T(8,128)(2,1)} %tok_ref.7, bf16[512,2304]{1,0:T(8,128)(2,1)} %all-reduce.11.cloned.1.call-done.sum_ref, f32[512,2304]{1,0:T(8,128)} %get-tuple-element.267.resid_ref, f32[4,2304]{1,0:T(4,128)} %bitcast.149), custom_call_target="tpu_custom_call" | custom-call | bytes 14155776 | tf_op jit(solution)/shard_map/end_norms/pallas_call | solution.py:436
  (436 shorter events, 217.7 us)
Async XLA Ops:
  8.0 211.3 %all-reduce.5.cloned.1.call-start = ((), (), s32[]{:S(2)}) async-start(), calls=%async_computation.1 | async-start | bytes 4718592 | tf_op jit(solution)/shard_map/psum | solution.py:913
  16.4 26.5 %collective-permute-start.4 = (bf16[288,1152]{1,0:T(8,128)(2,1)S(1)}, bf16[288,1152]{1,0:T(8,128)(2,1)}, u32[]{:S(2)}, u32[]{:S(2)}) collective-permute-start(bf16[288,1152]{1,0:T(8,128)(2,1)S(1)} %pack.1.refs_0_), channel_id=1, source_target_pairs={{0,4},{4,0},{8,12},{12,8},{16,20},{20,16},{24,28},{28,24},{1,5},{5... | collective-permute-start | bytes 1990664 | tf_op jit(solution)/shard_map/ppermute | solution.py:67
  80.6 31.7 %collective-permute-start.32 = (bf16[288,2304]{1,0:T(8,128)(2,1)}, bf16[288,2304]{1,0:T(8,128)(2,1)}, u32[]{:S(2)}, u32[]{:S(2)}) collective-permute-start(bf16[288,2304]{1,0:T(8,128)(2,1)} %refs_0_), channel_id=1, source_target_pairs={{0,8},{4,12},{8,0},{12,4},{16,24},{20,28},{24,16},{28,20},{1,9},{5... | collective-permute-start | bytes 3981320 | tf_op jit(solution)/shard_map/ppermute | solution.py:67
  82.1 30.5 %collective-permute-start.33 = (bf16[288,2304]{1,0:T(8,128)(2,1)}, bf16[288,2304]{1,0:T(8,128)(2,1)}, u32[]{:S(2)}, u32[]{:S(2)}) collective-permute-start(bf16[288,2304]{1,0:T(8,128)(2,1)} %refs_0_), channel_id=1, source_target_pairs={{0,16},{4,20},{8,24},{12,28},{16,0},{20,4},{24,8},{28,12},{1,17},{... | collective-permute-start | bytes 3981320 | tf_op jit(solution)/shard_map/ppermute | solution.py:67
  112.6 106.8 %all-gather.2.cloned.1.call-start = ((), (), s32[]{:S(2)}) async-start(), calls=%async_computation.2 | async-start | bytes 11943936 | tf_op jit(solution)/shard_map/all_gather | solution.py:914
  113.2 248.1 %all-reduce.7.cloned.1.call-start = ((), (), s32[]{:S(2)}) async-start(), calls=%async_computation.3 | async-start | bytes 4718592 | tf_op jit(solution)/shard_map/psum | solution.py:946
  113.2 44.2 %collective-permute-start.36 = (bf16[288,2304]{1,0:T(8,128)(2,1)}, bf16[288,2304]{1,0:T(8,128)(2,1)}, u32[]{:S(2)}, u32[]{:S(2)}) collective-permute-start(bf16[288,2304]{1,0:T(8,128)(2,1)} %refs_0_), channel_id=1, source_target_pairs={{0,4},{4,0},{8,12},{12,8},{16,20},{20,16},{24,28},{28,24},{1,5},{5... | collective-permute-start | bytes 3981320 | tf_op jit(solution)/shard_map/ppermute | solution.py:67
  115.3 44.8 %collective-permute-start.37 = (bf16[288,2304]{1,0:T(8,128)(2,1)}, bf16[288,2304]{1,0:T(8,128)(2,1)}, u32[]{:S(2)}, u32[]{:S(2)}) collective-permute-start(bf16[288,2304]{1,0:T(8,128)(2,1)} %collective-permute-done.32.refs_1_), channel_id=1, source_target_pairs={{0,4},{4,0},{8,12},{12,8},{16,20},{20,16},{24,28},{28,24},{1,5},{5... | collective-permute-start | bytes 3981320 | tf_op jit(solution)/shard_map/ppermute | solution.py:67
  117.7 43.2 %collective-permute-start.38 = (bf16[288,2304]{1,0:T(8,128)(2,1)}, bf16[288,2304]{1,0:T(8,128)(2,1)}, u32[]{:S(2)}, u32[]{:S(2)}) collective-permute-start(bf16[288,2304]{1,0:T(8,128)(2,1)} %collective-permute-done.33.refs_2_), channel_id=1, source_target_pairs={{0,4},{4,0},{8,12},{12,8},{16,20},{20,16},{24,28},{28,24},{1,5},{5... | collective-permute-start | bytes 3981320 | tf_op jit(solution)/shard_map/ppermute | solution.py:67
  125.8 30.0 %collective-permute-start.34 = (bf16[144,2304]{1,0:T(8,128)(2,1)}, bf16[144,2304]{1,0:T(8,128)(2,1)S(1)}, u32[]{:S(2)}, u32[]{:S(2)}) collective-permute-start(bf16[144,2304]{1,0:T(8,128)(2,1)} %slice.246), channel_id=1, source_target_pairs={{0,16},{4,20},{8,24},{12,28},{16,0},{20,4},{24,8},{28,12},{1,17},{... | collective-permute-start | bytes 1990664 | tf_op jit(solution)/shard_map/ppermute | solution.py:67
  127.2 28.7 %collective-permute-start.35 = (bf16[144,2304]{1,0:T(8,128)(2,1)}, bf16[144,2304]{1,0:T(8,128)(2,1)S(1)}, u32[]{:S(2)}, u32[]{:S(2)}) collective-permute-start(bf16[144,2304]{1,0:T(8,128)(2,1)} %slice.247), channel_id=1, source_target_pairs={{0,8},{4,12},{8,0},{12,4},{16,24},{20,28},{24,16},{28,20},{1,9},{5... | collective-permute-start | bytes 1990664 | tf_op jit(solution)/shard_map/ppermute | solution.py:67
  155.9 58.4 %collective-permute-start.41 = (bf16[288,2304]{1,0:T(8,128)(2,1)}, bf16[288,2304]{1,0:T(8,128)(2,1)S(1)}, u32[]{:S(2)}, u32[]{:S(2)}) collective-permute-start(bf16[288,2304]{1,0:T(8,128)(2,1)} %bitcast.11.refs_0_), channel_id=1, source_target_pairs={{0,8},{4,12},{8,0},{12,4},{16,24},{20,28},{24,16},{28,20},{1,9},{5... | collective-permute-start | bytes 3981320 | tf_op jit(solution)/shard_map/ppermute | solution.py:67
  157.4 59.3 %collective-permute-start.42 = (bf16[288,2304]{1,0:T(8,128)(2,1)}, bf16[288,2304]{1,0:T(8,128)(2,1)S(1)}, u32[]{:S(2)}, u32[]{:S(2)}) collective-permute-start(bf16[288,2304]{1,0:T(8,128)(2,1)} %bitcast.11.refs_0_), channel_id=1, source_target_pairs={{0,16},{4,20},{8,24},{12,28},{16,0},{20,4},{24,8},{28,12},{1,17},{... | collective-permute-start | bytes 3981320 | tf_op jit(solution)/shard_map/ppermute | solution.py:67
  219.4 33.8 %collective-permute-start.45 = (bf16[288,2304]{1,0:T(8,128)(2,1)}, bf16[288,2304]{1,0:T(8,128)(2,1)}, u32[]{:S(2)}, u32[]{:S(2)}) collective-permute-start(bf16[288,2304]{1,0:T(8,128)(2,1)} %bitcast.11.refs_0_), channel_id=1, source_target_pairs={{0,4},{4,0},{8,12},{12,8},{16,20},{20,16},{24,28},{28,24},{1,5},{5... | collective-permute-start | bytes 3981320 | tf_op jit(solution)/shard_map/ppermute | solution.py:67
  219.6 33.6 %collective-permute-start.46 = (bf16[288,2304]{1,0:T(8,128)(2,1)S(1)}, bf16[288,2304]{1,0:T(8,128)(2,1)}, u32[]{:S(2)}, u32[]{:S(2)}) collective-permute-start(bf16[288,2304]{1,0:T(8,128)(2,1)S(1)} %collective-permute-done.41.refs_1_), channel_id=1, source_target_pairs={{0,4},{4,0},{8,12},{12,8},{16,20},{20,16},{24,28},{28,24},{1,5},{5... | collective-permute-start | bytes 3981320 | tf_op jit(solution)/shard_map/ppermute | solution.py:67
  219.9 33.3 %collective-permute-start.47 = (bf16[288,2304]{1,0:T(8,128)(2,1)S(1)}, bf16[288,2304]{1,0:T(8,128)(2,1)}, u32[]{:S(2)}, u32[]{:S(2)}) collective-permute-start(bf16[288,2304]{1,0:T(8,128)(2,1)S(1)} %collective-permute-done.42.refs_2_), channel_id=1, source_target_pairs={{0,4},{4,0},{8,12},{12,8},{16,20},{20,16},{24,28},{28,24},{1,5},{5... | collective-permute-start | bytes 3981320 | tf_op jit(solution)/shard_map/ppermute | solution.py:67
  234.1 19.1 %collective-permute-start.49 = (bf16[144,2304]{1,0:T(8,128)(2,1)}, bf16[144,2304]{1,0:T(8,128)(2,1)}, u32[]{:S(2)}, u32[]{:S(2)}) collective-permute-start(bf16[144,2304]{1,0:T(8,128)(2,1)} %collective-permute-done.44.refs_4_), channel_id=1, source_target_pairs={{0,4},{4,0},{8,12},{12,8},{16,20},{20,16},{24,28},{28,24},{1,5},{5... | collective-permute-start | bytes 1990664 | tf_op jit(solution)/shard_map/ppermute | solution.py:67
  265.8 227.7 %all-reduce.9.cloned.1.call-start = ((), (), s32[]{:S(2)}) async-start(), calls=%async_computation.4 | async-start | bytes 4718592 | tf_op jit(solution)/shard_map/psum | solution.py:959
  398.6 132.7 %reduce-scatter.2.cloned.1.call-start = ((), (), s32[]{:S(2)}) async-start(), calls=%async_computation.5 | async-start | bytes 11943936 | tf_op jit(solution)/shard_map/reduce_scatter | solution.py:961
  453.7 77.0 %collective-permute-start.54 = (bf16[288,2304]{1,0:T(8,128)(2,1)}, bf16[288,2304]{1,0:T(8,128)(2,1)S(1)}, u32[]{:S(2)}, u32[]{:S(2)}) collective-permute-start(bf16[288,2304]{1,0:T(8,128)(2,1)} %get-tuple-element.257), channel_id=1, source_target_pairs={{0,8},{4,12},{8,0},{12,4},{16,24},{20,28},{24,16},{28,20},{1,9},{5... | collective-permute-start | bytes 3981320 | tf_op jit(solution)/shard_map/ppermute | solution.py:67
  455.4 75.3 %collective-permute-start.55 = (bf16[288,2304]{1,0:T(8,128)(2,1)}, bf16[288,2304]{1,0:T(8,128)(2,1)}, u32[]{:S(2)}, u32[]{:S(2)}) collective-permute-start(bf16[288,2304]{1,0:T(8,128)(2,1)} %get-tuple-element.258), channel_id=1, source_target_pairs={{0,16},{4,20},{8,24},{12,28},{16,0},{20,4},{24,8},{28,12},{1,17},{... | collective-permute-start | bytes 3981320 | tf_op jit(solution)/shard_map/ppermute | solution.py:67
  572.9 96.8 %all-reduce.11.cloned.1.call-start = ((), (), s32[]{:S(2)}) async-start(), calls=%async_computation.6 | async-start | bytes 4718592 | tf_op jit(solution)/shard_map/psum | solution.py:990
  576.5 21.5 %collective-permute-start.72 = (bf16[144,2304]{1,0:T(8,128)(2,1)}, bf16[144,2304]{1,0:T(8,128)(2,1)}, u32[]{:S(2)}, u32[]{:S(2)}) collective-permute-start(bf16[144,2304]{1,0:T(8,128)(2,1)} %get-tuple-element.281), channel_id=1, source_target_pairs={{0,16},{4,20},{8,24},{12,28},{16,0},{20,4},{24,8},{28,12},{1,17},{... | collective-permute-start | bytes 1990664 | tf_op jit(solution)/shard_map/ppermute | solution.py:67
  576.9 21.2 %collective-permute-start.74 = (bf16[144,2304]{1,0:T(8,128)(2,1)}, bf16[144,2304]{1,0:T(8,128)(2,1)}, u32[]{:S(2)}, u32[]{:S(2)}) collective-permute-start(bf16[144,2304]{1,0:T(8,128)(2,1)} %get-tuple-element.283), channel_id=1, source_target_pairs={{0,8},{4,12},{8,0},{12,4},{16,24},{20,28},{24,16},{28,20},{1,9},{5... | collective-permute-start | bytes 1990664 | tf_op jit(solution)/shard_map/ppermute | solution.py:67
  581.3 20.6 %collective-permute-start.67 = (bf16[4,288,512]{2,1,0:T(8,128)(2,1)S(1)}, bf16[4,288,512]{2,1,0:T(8,128)(2,1)}, u32[]{:S(2)}, u32[]{:S(2)}) collective-permute-start(bf16[4,288,512]{2,1,0:T(8,128)(2,1)S(1)} %dynamic-slice_bitcast_fusion.4), channel_id=1, source_target_pairs={{0,4},{4,0},{8,12},{12,8},{16,20},{20,16},{24,28},{28,24},{1,5},{5... | collective-permute-start | bytes 3538952 | tf_op jit(solution)/shard_map/ppermute | solution.py:67
  595.9 40.7 %collective-permute-start.62 = (bf16[4,288,1024]{2,1,0:T(8,128)(2,1)S(1)}, bf16[4,288,1024]{2,1,0:T(8,128)(2,1)S(1)}, u32[]{:S(2)}, u32[]{:S(2)}) collective-permute-start(bf16[4,288,1024]{2,1,0:T(8,128)(2,1)S(1)} %dynamic-slice_bitcast_fusion.2), channel_id=1, source_target_pairs={{0,4},{4,0},{8,12},{12,8},{16,20},{20,16},{24,28},{28,24},{1,5},{5... | collective-permute-start | bytes 7077896 | tf_op jit(solution)/shard_map/ppermute | solution.py:67
  598.0 39.4 %collective-permute-start.80 = (f32[1,4,288]{2,1,0:T(4,128)S(1)}, f32[1,4,288]{2,1,0:T(4,128)S(1)}, u32[]{:S(2)}, u32[]{:S(2)}) collective-permute-start(f32[1,4,288]{2,1,0:T(4,128)S(1)} %slice_select_fusion.2), channel_id=1, source_target_pairs={{0,4},{4,0},{8,12},{12,8},{16,20},{20,16},{24,28},{28,24},{1,5},{5... | collective-permute-start | bytes 13832 | tf_op jit(solution)/shard_map/ppermute | solution.py:67
  600.3 53.4 %collective-permute-start.73 = (bf16[288,2304]{1,0:T(8,128)(2,1)S(1)}, bf16[288,2304]{1,0:T(8,128)(2,1)S(1)}, u32[]{:S(2)}, u32[]{:S(2)}) collective-permute-start(bf16[288,2304]{1,0:T(8,128)(2,1)S(1)} %pad_maximum_fusion.2), channel_id=1, source_target_pairs={{0,8},{4,12},{8,0},{12,4},{16,24},{20,28},{24,16},{28,20},{1,9},{5... | collective-permute-start | bytes 3981320 | tf_op jit(solution)/shard_map/ppermute | solution.py:67
  603.8 31.2 %collective-permute-start.70 = (bf16[144,512]{1,0:T(8,128)(2,1)S(1)}, bf16[144,512]{1,0:T(8,128)(2,1)S(1)}, u32[]{:S(2)}, u32[]{:S(2)}) collective-permute-start(bf16[144,512]{1,0:T(8,128)(2,1)S(1)} %get-tuple-element.305), channel_id=1, source_target_pairs={{0,8},{4,12},{8,0},{12,4},{16,24},{20,28},{24,16},{28,20},{1,9},{5... | collective-permute-start | bytes 442376 | tf_op jit(solution)/shard_map/ppermute | solution.py:67
  609.3 44.4 %collective-permute-start.75 = (bf16[288,2304]{1,0:T(8,128)(2,1)S(1)}, bf16[288,2304]{1,0:T(8,128)(2,1)S(1)}, u32[]{:S(2)}, u32[]{:S(2)}) collective-permute-start(bf16[288,2304]{1,0:T(8,128)(2,1)S(1)} %pad_maximum_fusion.3), channel_id=1, source_target_pairs={{0,16},{4,20},{8,24},{12,28},{16,0},{20,4},{24,8},{28,12},{1,17},{... | collective-permute-start | bytes 3981320 | tf_op jit(solution)/shard_map/ppermute | solution.py:67
  652.6 25.3 %collective-permute-start.64 = (bf16[288,1024]{1,0:T(8,128)(2,1)S(1)}, bf16[288,1024]{1,0:T(8,128)(2,1)}, u32[]{:S(2)}, u32[]{:S(2)}) collective-permute-start(bf16[288,1024]{1,0:T(8,128)(2,1)S(1)} %pad_maximum_fusion.4), channel_id=1, source_target_pairs={{0,8},{4,12},{8,0},{12,4},{16,24},{20,28},{24,16},{28,20},{1,9},{5... | collective-permute-start | bytes 1769480 | tf_op jit(solution)/shard_map/ppermute | solution.py:67
  653.3 24.6 %collective-permute-start.66 = (bf16[288,1024]{1,0:T(8,128)(2,1)S(1)}, bf16[288,1024]{1,0:T(8,128)(2,1)}, u32[]{:S(2)}, u32[]{:S(2)}) collective-permute-start(bf16[288,1024]{1,0:T(8,128)(2,1)S(1)} %pad_maximum_fusion.5), channel_id=1, source_target_pairs={{0,16},{4,20},{8,24},{12,28},{16,0},{20,4},{24,8},{28,12},{1,17},{... | collective-permute-start | bytes 1769480 | tf_op jit(solution)/shard_map/ppermute | solution.py:67
  (146 other events, 1389.4 us)
Sparse Core Ops, SparseCore 0:
  112.7 96.7 all-reduce.4
  265.9 95.2 all-reduce.6
  398.8 94.6 all-reduce.8
  576.3 93.2 all-reduce.10
Sparse Core Ops, SparseCore 1:
  114.9 104.3 all-gather.1
  423.4 107.9 reduce-scatter.1

commit v6 on v5

--- a/solution.py
+++ b/solution.py
@@ -344,7 +344,7 @@
         step(pl.ds(pl.multiple_of(index * GROUP, GROUP), GROUP))
         return carry
 
-    lax.fori_loop(0, count // GROUP, run, 0, unroll=2)
+    lax.fori_loop(0, count // GROUP, run, 0, unroll=8)
 
 
 def mid_kernel(tok_ref, branch_ref, gains_ref, out_ref):
@@ -452,8 +452,8 @@
 
 
 def units_kernel(in_ref, gate_ref, up_ref, hidden_ref, active_ref, slope_ref):
-    for n in range(0, UNITS, STEP):
-        at = slice(n, n + STEP)
+    for n in range(0, UNITS, UNITS):
+        at = slice(n, n + UNITS)
         gate = matmul(in_ref[...], gate_ref[:, at])
         up = matmul(in_ref[...], up_ref[:, at])
         root = (2.0 / jnp.pi) ** 0.5
@@ -575,11 +575,16 @@
         own = map_ref[me * q_blocks + b]
         count = block_list(lookup, key_blocks, own, seq_blocks, reach, list_ref)
 
-        def pair(step, carry):
-            tile(b, (list_ref[2 * step], list_ref[2 * step + 1]), None)
+        def four(step, carry):
+            tile(b, tuple(list_ref[4 * step + k] for k in range(4)), None)
             return carry
 
-        lax.fori_loop(0, count // 2, pair, 0)
+        lax.fori_loop(0, count // 4, four, 0)
+
+        @pl.when(count % 4 >= 2)
+        def _():
+            first = (count // 4) * 4
+            tile(b, (list_ref[first], list_ref[first + 1]), None)
 
         @pl.when(count % 2 == 1)
         def _():
@@ -642,6 +647,22 @@
     def tile(b, slots, mask):
         rows = [pl.ds(pl.multiple_of(slot * blk, blk), blk) for slot in slots]
         cols = slice(b * blk, (b + 1) * blk)
+        if mask is None:
+            query = jnp.concatenate([q_ref[cols, h * HD : (h + 1) * HD] for h in range(heads)], axis=0)
+            part, held = None, []
+            for row in rows:
+                capped = jnp.tanh(matmul_nt(query, kv_ref[row, :HD]) * (1.0 / soft_cap))
+                weights = jnp.exp2(capped * (soft_cap * LOG2E))
+                for piece in range(0, blk, 128):
+                    term = weights[:, piece : piece + 128]
+                    part = term if part is None else part + term
+                held.append(weights.astype(jnp.bfloat16))
+            values = jnp.concatenate([kv_ref[row, HD:] for row in rows], axis=0)
+            result = matmul(jnp.concatenate(held, axis=1), values)
+            for h in range(heads):
+                sum_ref[cols, h * 128 : (h + 1) * 128] += part[h * blk : (h + 1) * blk]
+                acc_ref[cols, h * HD : (h + 1) * HD] += result[h * blk : (h + 1) * blk]
+            return
         for h in range(heads):
             query = q_ref[cols, h * HD : (h + 1) * HD]
             part = result = None
@@ -749,29 +770,30 @@
     def tile(b, slots, mask):
         rows = [pl.ds(pl.multiple_of(slot * blk, blk), blk) for slot in slots]
         cols = slice(b * blk, (b + 1) * blk)
-        dk_parts, dv_parts = [None] * len(rows), [None] * len(rows)
-        dq_parts = [None] * heads
+        keys = jnp.concatenate([kv_ref[row, :HD] for row in rows], axis=0)
+        vals = jnp.concatenate([kv_ref[row, HD:] for row in rows], axis=0)
+        turned = jnp.concatenate([kt_ref[:, row] for row in rows], axis=1)
+        dk_part = dv_part = None
+        dq_parts = []
         add = lambda total, term: term if total is None else total + term
         for h in range(heads):
             query = q_ref[cols, h * HD : (h + 1) * HD]
             out_grad = do_ref[cols, h * HD : (h + 1) * HD]
-            log_total = stat_ref[h : h + 1, cols]
+            tangent = jnp.tanh(matmul_nt(keys, query) * (1.0 / soft_cap))
+            probs = jnp.exp2(tangent * (soft_cap * LOG2E) - stat_ref[h : h + 1, cols])
+            if mask is not None:
+                probs = jnp.where(mask, probs, 0.0)
+            prob_grad = matmul_nt(vals, out_grad)
             delta = stat_ref[heads + h : heads + h + 1, cols]
-            for k, row in enumerate(rows):
-                tangent = jnp.tanh(matmul_nt(kv_ref[row, :HD], query) * (1.0 / soft_cap))
-                probs = jnp.exp2(tangent * (soft_cap * LOG2E) - log_total)
-                if mask is not None:
-                    probs = jnp.where(mask, probs, 0.0)
-                prob_grad = matmul_nt(kv_ref[row, HD:], out_grad)
-                score = (probs * (prob_grad - delta) * (1.0 - tangent * tangent)).astype(jnp.bfloat16)
-                dk_parts[k] = add(dk_parts[k], matmul(score, query))
-                dv_parts[k] = add(dv_parts[k], matmul(probs.astype(jnp.bfloat16), out_grad))
-                dq_parts[h] = add(dq_parts[h], matmul(kt_ref[:, row], score))
+            score = (probs * (prob_grad - delta) * (1.0 - tangent * tangent)).astype(jnp.bfloat16)
+            dk_part = add(dk_part, matmul(score, query))
+            dv_part = add(dv_part, matmul(probs.astype(jnp.bfloat16), out_grad))
+            dq_parts.append(matmul(turned, score))
         for h in range(heads):
             dqt_ref[h * HD : (h + 1) * HD, cols] += dq_parts[h]
         for k, row in enumerate(rows):
-            dk_ref[row, :] += dk_parts[k]
-            dv_ref[row, :] += dv_parts[k]
+            dk_ref[row, :] += dk_part[k * blk : (k + 1) * blk]
+            dv_ref[row, :] += dv_part[k * blk : (k + 1) * blk]
 
     visit_blocks(
         map_ref, me_ref[0], chunk, q_blocks, key_blocks, seq_blocks, reach, swapped, list_ref,

time: 697 us -> 693 us (level)
  Pallas kernels: 175 us -> 162 us
  waiting for transfers between devices: 305 us -> 313 us
  transfers between devices with their start and end apart: 87 -> 87, of which waited for: 40 -> 41; matrix products, arithmetic and copies ran while one was open for 14% -> 14% of each run, Pallas kernels for 18% -> 16%
where the time goes in v6:
time: 693 us; the launch traced here: 683 us
  waiting for transfers between devices  313 us (45%)
  Pallas kernels  162 us (23%)
  starting transfers between devices  62.5 us (9%)
  local copies, waits for them, and re-layouts  53.2 us (8%)
  other arithmetic  44.8 us (6%)
  matrix products  30.5 us (4%)
  between operations  16.8 us (2%)
    ppermute x79, waiting for transfers between devices, swap(): return lax.ppermute(value, 'ctx', pairs)  187 us
    psum x1, waiting for transfers between devices, body(): mlp_out = lax.psum(mlp_part, 'tp')  77.2 us
    ppermute x79, starting transfers between devices, swap(): return lax.ppermute(value, 'ctx', pairs)  57.9 us
    dot_general x5, matrix products, matmul(): return jnp.dot(left, right, preferred_element_type=jnp.float32)  30.5 us
    pallas_call x4, Pallas kernels, by_rows(): pl.pallas_call(kernel, out_shape=tuple(shapes), grid=(rows // block,), in...  30.3 us
    pallas_call x4, Pallas kernels, assemble(): pl.pallas_call(assemble_kernel, out_shape=jax.ShapeDtypeStruct((8 * rows,...  27.4 us
    unnamed x186, local copies, waits for them, and re-layouts  25.9 us
    psum x1, waiting for transfers between devices, body(): mid_sum = lax.psum(mid_part, 'tp')  25.5 us
  transfers between devices with their start and end apart: 87, of which 41 were waited for; matrix products, arithmetic and copies ran while one was open for 14% of the time, Pallas kernels for 16%

profile of v6, /device:TPU:0, one launch (start us, length us, event | category | flops | bytes accessed | tf_op | source)
XLA Modules:
  0.0 683.1 jit_solution(813364503202643056)
XLA Ops:
  18.7 11.2 %collective-permute-done.refs_1_ = bf16[288,1152]{1,0:T(8,128)(2,1)S(1)} collective-permute-done((bf16[288,1152]{1,0:T(8,128)(2,1)S(1)}, bf16[288,1152]{1,0:T(8,128)(2,1)S(1)}, u32[]{:S(2)}, u32[]{:S(2)}) %collective-permute-start) | collective-permute-done | bytes 663584 | tf_op jit(solution)/shard_map/ppermute | solution.py:67
  51.6 5.2 project.1
  72.1 8.1 %collective-permute-done.26.refs_4_ = bf16[144,512]{1,0:T(8,128)(2,1)S(1)} collective-permute-done((bf16[144,512]{1,0:T(8,128)(2,1)S(1)}, bf16[144,512]{1,0:T(8,128)(2,1)S(1)}, u32[]{:S(2)}, u32[]{:S(2)}) %collective-permute-start.26) | collective-permute-done | bytes 147488 | tf_op jit(solution)/shard_map/ppermute | solution.py:67
  90.0 12.1 %attend.1 = (f32[512,512]{1,0:T(8,128)}, bf16[512,512]{1,0:T(8,128)(2,1)}, f32[512,256]{1,0:T(8,128)}) custom-call(s32[16]{0:T(128)} %reshape.122.map_ref, s32[1]{0:T(128)} %bitcast.8.me_ref, bf16[512,512]{1,0:T(8,128)(2,1)} %copy-done.62, bf16[256,512]{1,0:T(8,128)(2,1)} %copy-done.21, bf16[256,512]{1,0:T(8,128)(2,1)} %copy-done.23, ...), custom_call_target="tpu_custom_call" | custom-call | flops 4294967296 | bytes 10485760 | tf_op jit(solution)/shard_map/attend/pallas_call | solution.py:721
  117.8 5.7 assemble.4.full_ref
  131.5 24.3 %collective-permute-done.34.refs_3_ = bf16[144,2304]{1,0:T(8,128)(2,1)S(1)} collective-permute-done((bf16[144,2304]{1,0:T(8,128)(2,1)}, bf16[144,2304]{1,0:T(8,128)(2,1)S(1)}, u32[]{:S(2)}, u32[]{:S(2)}) %collective-permute-start.34) | collective-permute-done | bytes 663584 | tf_op jit(solution)/shard_map/ppermute | solution.py:67
  161.0 9.2 %assemble.5.gate_ref = bf16[2304,2304]{1,0:T(8,128)(2,1)} custom-call(s32[10]{0:T(128)} %copy-done.57, bf16[288,2304]{1,0:T(8,128)(2,1)} %refs_0_, bf16[288,2304]{1,0:T(8,128)(2,1)} %collective-permute-done.32.refs_1_, bf16[288,2304]{1,0:T(8,128)(2,1)} %collective-permute-done.33.refs_2_, bf16[144,2304]{1,0:T(8,128)(2,1)} %copy-done.75, ...), custom_call_target="tpu_custom_call" | custom-call | bytes 21233664 | tf_op jit(solution)/shard_map/assemble/pallas_call | solution.py:129
  170.2 44.1 %collective-permute-done.41.refs_1_ = bf16[288,2304]{1,0:T(8,128)(2,1)S(1)} collective-permute-done((bf16[288,2304]{1,0:T(8,128)(2,1)}, bf16[288,2304]{1,0:T(8,128)(2,1)S(1)}, u32[]{:S(2)}, u32[]{:S(2)}) %collective-permute-start.41) | collective-permute-done | bytes 1327136 | tf_op jit(solution)/shard_map/ppermute | solution.py:67
  220.1 5.2 mid_norms.1.in_ref
  225.3 7.3 %collective-permute-done.43.refs_3_ = bf16[144,2304]{1,0:T(8,128)(2,1)S(1)} collective-permute-done((bf16[144,2304]{1,0:T(8,128)(2,1)}, bf16[144,2304]{1,0:T(8,128)(2,1)S(1)}, u32[]{:S(2)}, u32[]{:S(2)}) %collective-permute-start.43) | collective-permute-done | bytes 663584 | tf_op jit(solution)/shard_map/ppermute | solution.py:67
  234.6 16.6 %units.1 = (bf16[512,2304]{1,0:T(8,128)(2,1)}, bf16[512,2304]{1,0:T(8,128)(2,1)}, bf16[512,2304]{1,0:T(8,128)(2,1)}) custom-call(bf16[512,2304]{1,0:T(8,128)(2,1)} %mid_norms.1.in_ref, bf16[2304,2304]{1,0:T(8,128)(2,1)} %assemble.5.gate_ref, bf16[2304,2304]{1,0:T(8,128)(2,1)} %all-gather.2.cloned.1.call-done.up_ref), custom_call_target="tpu_custom_call" | custom-call | flops 10871635968 | bytes 21233664 | tf_op jit(solution)/shard_map/units/pallas_call | solution.py:475
  252.9 9.4 %project_down.1 = bf16[512,2304]{1,0:T(8,128)(2,1)S(1)} custom-call(s32[10]{0:T(128)S(1)} %copy-done.58, bf16[512,2304]{1,0:T(8,128)(2,1)S(1)} %copy-done.63, bf16[288,2304]{1,0:T(8,128)(2,1)} %bitcast.11.refs_0_, bf16[288,2304]{1,0:T(8,128)(2,1)S(1)} %collective-permute-done.41.refs_1_, bf16[288,2304]{1,0:T(8,128)(2,1)S(1)} %collective-permute-done.42.refs_2_, ...), custom_call_target="tpu_custom_call" | custom-call | flops 5435817984 | bytes 15335464 | tf_op jit(solution)/shard_map/project_down/pallas_call | solution.py:53
  264.0 9.1 %assemble.7.down_ref = bf16[2304,2304]{1,0:T(8,128)(2,1)} custom-call(s32[10]{0:T(128)} %copy-done.57, bf16[288,2304]{1,0:T(8,128)(2,1)} %bitcast.11.refs_0_, bf16[288,2304]{1,0:T(8,128)(2,1)} %copy-done, bf16[288,2304]{1,0:T(8,128)(2,1)} %copy-done.1, bf16[144,2304]{1,0:T(8,128)(2,1)} %copy-done.11, bf16[144,2304]{1,0:T(8,128)(2,1)} %collective-permute-done.44.refs_4_, ...), custom_call_target="tpu_custom_call" | custom-call | bytes 21233664 | tf_op jit(solution)/shard_map/assemble/pallas_call | solution.py:129
  282.0 77.2 %all-reduce.7.cloned.1.call-done.mlp_ref = bf16[512,2304]{1,0:T(8,128)(2,1)} async-done(((bf16[512,2304]{1,0:T(8,128)(2,1)}), bf16[512,2304]{1,0:T(8,128)(2,1)}) %all-reduce.7.cloned.1.call-update) | async-done | bytes 2359312 | tf_op jit(solution)/shard_map/psum | solution.py:968
  359.2 8.3 %top_norms.1 = (bf16[512,2304]{1,0:T(8,128)(2,1)}, bf16[512,2304]{1,0:T(8,128)(2,1)}, f32[1,2304]{1,0:T(1,128)}) custom-call(bf16[512,2304]{1,0:T(8,128)(2,1)} %tok_ref.7, bf16[512,2304]{1,0:T(8,128)(2,1)} %all-reduce.5.cloned.1.call-done.branch_ref, bf16[512,2304]{1,0:T(8,128)(2,1)} %all-reduce.7.cloned.1.call-done.mlp_ref, bf16[512,2304]{1,0:T(8,128)(2,1)} %cot_ref.3, ...), custom_call_target="tpu_custom_call" | custom-call | bytes 14164992 | tf_op jit(solution)/shard_map/top_norms/pallas_call | solution.py:436
  367.5 11.9 %units_back.1 = (bf16[512,2304]{1,0:T(8,128)(2,1)}, bf16[512,2304]{1,0:T(8,128)(2,1)}) custom-call(bf16[512,2304]{1,0:T(8,128)(2,1)} %get-tuple-element.255.grad_ref, bf16[2304,2304]{1,0:T(8,128)(2,1)} %assemble.7.down_ref, bf16[512,2304]{1,0:T(8,128)(2,1)} %get-tuple-element.234.active_ref, bf16[512,2304]{1,0:T(8,128)(2,1)} %get-tuple-element.235.slope_ref), custom_call_target="tpu_custom_call" | custom-call | flops 5435817984 | bytes 10616832 | tf_op jit(solution)/shard_map/units_back/pallas_call | solution.py:503
  379.4 16.9 %features_back.1 = bf16[512,2304]{1,0:T(8,128)(2,1)} custom-call(bf16[512,2304]{1,0:T(8,128)(2,1)} %get-tuple-element.240.dg_ref, bf16[512,2304]{1,0:T(8,128)(2,1)} %get-tuple-element.239.du_ref, bf16[2304,2304]{1,0:T(8,128)(2,1)} %assemble.5.gate_ref, bf16[2304,2304]{1,0:T(8,128)(2,1)} %all-gather.2.cloned.1.call-done.up_ref), custom_call_target="tpu_custom_call" | custom-call | flops 10871635968 | bytes 21233664 | tf_op jit(solution)/shard_map/features_back/pallas_call | solution.py:529
  398.0 7.6 %convolution_convert_fusion.1 = bf16[2304,2304]{1,0:T(8,128)(2,1)S(1)} fusion(bf16[512,2304]{1,0:T(8,128)(2,1)S(1)} %copy-done.69, bf16[512,2304]{1,0:T(8,128)(2,1)} %get-tuple-element.240.dg_ref), kind=kOutput, calls=%fused_computation.1 | convolution fusion | flops 5441126400 | bytes 15335424 | tf_op jit(solution)/shard_map/dot_general | solution.py:33
  412.5 8.4 %convolution_convert_fusion = bf16[2304,2304]{0,1:T(8,128)(2,1)} fusion(bf16[512,2304]{1,0:T(8,128)(2,1)S(1)} %copy-done.64, bf16[512,2304]{1,0:T(8,128)(2,1)S(1)} %copy-done.83), kind=kOutput, calls=%fused_computation | convolution fusion | flops 5441126400 | bytes 15335424 | tf_op jit(solution)/shard_map/dot_general | solution.py:33
  429.5 8.5 %convolution_convert_fusion.2 = bf16[2304,2304]{1,0:T(8,128)(2,1)} fusion(bf16[512,2304]{1,0:T(8,128)(2,1)S(1)} %copy-done.69, bf16[512,2304]{1,0:T(8,128)(2,1)S(1)} %copy-done.85), kind=kOutput, calls=%fused_computation.2 | convolution fusion | flops 5441126400 | bytes 15335424 | tf_op jit(solution)/shard_map/dot_general | solution.py:33
  438.1 5.4 collective-permute-done.51
  453.7 6.6 collective-permute-done.53
  460.2 5.4 bitcast_add_fusion
  465.6 25.5 %all-reduce.9.cloned.1.call-done.mid_ref = bf16[512,2304]{1,0:T(8,128)(2,1)} async-done(((bf16[512,2304]{1,0:T(8,128)(2,1)}), bf16[512,2304]{1,0:T(8,128)(2,1)}) %all-reduce.9.cloned.1.call-update) | async-done | bytes 2359312 | tf_op jit(solution)/shard_map/psum | solution.py:981
  491.1 9.6 %low_norms.1 = (f32[512,2304]{1,0:T(8,128)}, bf16[512,2304]{1,0:T(8,128)(2,1)}, f32[2,2304]{1,0:T(2,128)}) custom-call(bf16[512,2304]{1,0:T(8,128)(2,1)} %tok_ref.7, bf16[512,2304]{1,0:T(8,128)(2,1)} %all-reduce.5.cloned.1.call-done.branch_ref, bf16[512,2304]{1,0:T(8,128)(2,1)} %all-reduce.9.cloned.1.call-done.mid_ref, bf16[512,2304]{1,0:T(8,128)(2,1)} %cot_ref.3, ...), custom_call_target="tpu_custom_call" | custom-call | bytes 16533504 | tf_op jit(solution)/shard_map/low_norms/pallas_call | solution.py:436
  500.7 22.4 %attend_back.1 = (bf16[512,512]{1,0:T(8,128)(2,1)}, bf16[1536,512]{1,0:T(8,128)(2,1)}, bf16[512,512]{1,0:T(8,128)(2,1)}, bf16[1536,512]{1,0:T(8,128)(2,1)}, bf16[512,512]{1,0:T(8,128)(2,1)}) custom-call(s32[16]{0:T(128)} %reshape.122.map_ref, s32[1]{0:T(128)} %bitcast.8.me_ref, bf16[512,2304]{1,0:T(8,128)(2,1)} %get-tuple-element.270.da_ref, ...), custom_call_target="tpu_custom_call" | custom-call | flops 10737418240 | bytes 14680064 | tf_op jit(solution)/shard_map/attend_back/pallas_call | solution.py:841
  523.1 5.9 reduce-scatter.2.cloned.1.call-done
  550.6 7.6 %collective-permute-done.61.refs_2_ = bf16[512,512]{1,0:T(8,128)(2,1)S(1)} collective-permute-done((bf16[512,512]{1,0:T(8,128)(2,1)S(1)}, bf16[512,512]{1,0:T(8,128)(2,1)S(1)}, u32[]{:S(2)}, u32[]{:S(2)}) %collective-permute-start.61) | collective-permute-done | bytes 524320 | tf_op jit(solution)/shard_map/ppermute | solution.py:67
  604.2 24.8 %collective-permute-done.70 = bf16[144,512]{1,0:T(8,128)(2,1)S(1)} collective-permute-done((bf16[144,512]{1,0:T(8,128)(2,1)S(1)}, bf16[144,512]{1,0:T(8,128)(2,1)S(1)}, u32[]{:S(2)}, u32[]{:S(2)}) %collective-permute-start.70) | collective-permute-done | bytes 147488 | tf_op jit(solution)/shard_map/ppermute | solution.py:67
  632.3 5.4 collective-permute-done.69
  652.6 12.6 %all-reduce.11.cloned.1.call-done.sum_ref = bf16[512,2304]{1,0:T(8,128)(2,1)} async-done(((bf16[512,2304]{1,0:T(8,128)(2,1)}), bf16[512,2304]{1,0:T(8,128)(2,1)}) %all-reduce.11.cloned.1.call-update) | async-done | bytes 2359312 | tf_op jit(solution)/shard_map/psum | solution.py:1012
  665.2 7.2 %end_norms.1 = f32[512,2304]{1,0:T(8,128)} custom-call(bf16[512,2304]{1,0:T(8,128)(2,1)} %tok_ref.7, bf16[512,2304]{1,0:T(8,128)(2,1)} %all-reduce.11.cloned.1.call-done.sum_ref, f32[512,2304]{1,0:T(8,128)} %get-tuple-element.267.resid_ref, f32[4,2304]{1,0:T(4,128)} %bitcast.149), custom_call_target="tpu_custom_call" | custom-call | bytes 14155776 | tf_op jit(solution)/shard_map/end_norms/pallas_call | solution.py:436
  (436 shorter events, 221.5 us)
Async XLA Ops:
  8.0 211.3 %all-reduce.5.cloned.1.call-start = ((), (), s32[]{:S(2)}) async-start(), calls=%async_computation.1 | async-start | bytes 4718592 | tf_op jit(solution)/shard_map/psum | solution.py:935
  14.9 18.3 %collective-permute-start.1 = (bf16[288,1152]{1,0:T(8,128)(2,1)S(1)}, bf16[288,1152]{1,0:T(8,128)(2,1)}, u32[]{:S(2)}, u32[]{:S(2)}) collective-permute-start(bf16[288,1152]{1,0:T(8,128)(2,1)S(1)} %pack.1.refs_0_), channel_id=1, source_target_pairs={{0,16},{4,20},{8,24},{12,28},{16,0},{20,4},{24,8},{28,12},{1,17},{... | collective-permute-start | bytes 1990664 | tf_op jit(solution)/shard_map/ppermute | solution.py:67
  16.4 26.5 %collective-permute-start.4 = (bf16[288,1152]{1,0:T(8,128)(2,1)S(1)}, bf16[288,1152]{1,0:T(8,128)(2,1)}, u32[]{:S(2)}, u32[]{:S(2)}) collective-permute-start(bf16[288,1152]{1,0:T(8,128)(2,1)S(1)} %pack.1.refs_0_), channel_id=1, source_target_pairs={{0,4},{4,0},{8,12},{12,8},{16,20},{20,16},{24,28},{28,24},{1,5},{5... | collective-permute-start | bytes 1990664 | tf_op jit(solution)/shard_map/ppermute | solution.py:67
  61.3 18.9 %collective-permute-start.12 = (bf16[256,512]{1,0:T(8,128)(2,1)S(1)}, bf16[256,512]{1,0:T(8,128)(2,1)S(1)}, u32[]{:S(2)}, u32[]{:S(2)}) collective-permute-start(bf16[256,512]{1,0:T(8,128)(2,1)S(1)} %get-tuple-element.203.refs_1_), channel_id=1, source_target_pairs={{0,8},{4,12},{8,0},{12,4},{16,24},{20,28},{24,16},{28,20},{1,9},{5... | collective-permute-start | bytes 786440 | tf_op jit(solution)/shard_map/ppermute | solution.py:67
  80.6 31.7 %collective-permute-start.32 = (bf16[288,2304]{1,0:T(8,128)(2,1)}, bf16[288,2304]{1,0:T(8,128)(2,1)}, u32[]{:S(2)}, u32[]{:S(2)}) collective-permute-start(bf16[288,2304]{1,0:T(8,128)(2,1)} %refs_0_), channel_id=1, source_target_pairs={{0,8},{4,12},{8,0},{12,4},{16,24},{20,28},{24,16},{28,20},{1,9},{5... | collective-permute-start | bytes 3981320 | tf_op jit(solution)/shard_map/ppermute | solution.py:67
  82.1 30.5 %collective-permute-start.33 = (bf16[288,2304]{1,0:T(8,128)(2,1)}, bf16[288,2304]{1,0:T(8,128)(2,1)}, u32[]{:S(2)}, u32[]{:S(2)}) collective-permute-start(bf16[288,2304]{1,0:T(8,128)(2,1)} %refs_0_), channel_id=1, source_target_pairs={{0,16},{4,20},{8,24},{12,28},{16,0},{20,4},{24,8},{28,12},{1,17},{... | collective-permute-start | bytes 3981320 | tf_op jit(solution)/shard_map/ppermute | solution.py:67
  112.6 106.8 %all-gather.2.cloned.1.call-start = ((), (), s32[]{:S(2)}) async-start(), calls=%async_computation.2 | async-start | bytes 11943936 | tf_op jit(solution)/shard_map/all_gather | solution.py:936
  113.2 246.0 %all-reduce.7.cloned.1.call-start = ((), (), s32[]{:S(2)}) async-start(), calls=%async_computation.3 | async-start | bytes 4718592 | tf_op jit(solution)/shard_map/psum | solution.py:968
  113.2 44.2 %collective-permute-start.36 = (bf16[288,2304]{1,0:T(8,128)(2,1)}, bf16[288,2304]{1,0:T(8,128)(2,1)}, u32[]{:S(2)}, u32[]{:S(2)}) collective-permute-start(bf16[288,2304]{1,0:T(8,128)(2,1)} %refs_0_), channel_id=1, source_target_pairs={{0,4},{4,0},{8,12},{12,8},{16,20},{20,16},{24,28},{28,24},{1,5},{5... | collective-permute-start | bytes 3981320 | tf_op jit(solution)/shard_map/ppermute | solution.py:67
  115.3 44.8 %collective-permute-start.37 = (bf16[288,2304]{1,0:T(8,128)(2,1)}, bf16[288,2304]{1,0:T(8,128)(2,1)}, u32[]{:S(2)}, u32[]{:S(2)}) collective-permute-start(bf16[288,2304]{1,0:T(8,128)(2,1)} %collective-permute-done.32.refs_1_), channel_id=1, source_target_pairs={{0,4},{4,0},{8,12},{12,8},{16,20},{20,16},{24,28},{28,24},{1,5},{5... | collective-permute-start | bytes 3981320 | tf_op jit(solution)/shard_map/ppermute | solution.py:67
  117.7 43.2 %collective-permute-start.38 = (bf16[288,2304]{1,0:T(8,128)(2,1)}, bf16[288,2304]{1,0:T(8,128)(2,1)}, u32[]{:S(2)}, u32[]{:S(2)}) collective-permute-start(bf16[288,2304]{1,0:T(8,128)(2,1)} %collective-permute-done.33.refs_2_), channel_id=1, source_target_pairs={{0,4},{4,0},{8,12},{12,8},{16,20},{20,16},{24,28},{28,24},{1,5},{5... | collective-permute-start | bytes 3981320 | tf_op jit(solution)/shard_map/ppermute | solution.py:67
  125.8 30.0 %collective-permute-start.34 = (bf16[144,2304]{1,0:T(8,128)(2,1)}, bf16[144,2304]{1,0:T(8,128)(2,1)S(1)}, u32[]{:S(2)}, u32[]{:S(2)}) collective-permute-start(bf16[144,2304]{1,0:T(8,128)(2,1)} %slice.246), channel_id=1, source_target_pairs={{0,16},{4,20},{8,24},{12,28},{16,0},{20,4},{24,8},{28,12},{1,17},{... | collective-permute-start | bytes 1990664 | tf_op jit(solution)/shard_map/ppermute | solution.py:67
  127.2 28.7 %collective-permute-start.35 = (bf16[144,2304]{1,0:T(8,128)(2,1)}, bf16[144,2304]{1,0:T(8,128)(2,1)S(1)}, u32[]{:S(2)}, u32[]{:S(2)}) collective-permute-start(bf16[144,2304]{1,0:T(8,128)(2,1)} %slice.247), channel_id=1, source_target_pairs={{0,8},{4,12},{8,0},{12,4},{16,24},{20,28},{24,16},{28,20},{1,9},{5... | collective-permute-start | bytes 1990664 | tf_op jit(solution)/shard_map/ppermute | solution.py:67
  155.9 58.4 %collective-permute-start.41 = (bf16[288,2304]{1,0:T(8,128)(2,1)}, bf16[288,2304]{1,0:T(8,128)(2,1)S(1)}, u32[]{:S(2)}, u32[]{:S(2)}) collective-permute-start(bf16[288,2304]{1,0:T(8,128)(2,1)} %bitcast.11.refs_0_), channel_id=1, source_target_pairs={{0,8},{4,12},{8,0},{12,4},{16,24},{20,28},{24,16},{28,20},{1,9},{5... | collective-permute-start | bytes 3981320 | tf_op jit(solution)/shard_map/ppermute | solution.py:67
  157.4 59.3 %collective-permute-start.42 = (bf16[288,2304]{1,0:T(8,128)(2,1)}, bf16[288,2304]{1,0:T(8,128)(2,1)S(1)}, u32[]{:S(2)}, u32[]{:S(2)}) collective-permute-start(bf16[288,2304]{1,0:T(8,128)(2,1)} %bitcast.11.refs_0_), channel_id=1, source_target_pairs={{0,16},{4,20},{8,24},{12,28},{16,0},{20,4},{24,8},{28,12},{1,17},{... | collective-permute-start | bytes 3981320 | tf_op jit(solution)/shard_map/ppermute | solution.py:67
  219.4 31.8 %collective-permute-start.45 = (bf16[288,2304]{1,0:T(8,128)(2,1)}, bf16[288,2304]{1,0:T(8,128)(2,1)}, u32[]{:S(2)}, u32[]{:S(2)}) collective-permute-start(bf16[288,2304]{1,0:T(8,128)(2,1)} %bitcast.11.refs_0_), channel_id=1, source_target_pairs={{0,4},{4,0},{8,12},{12,8},{16,20},{20,16},{24,28},{28,24},{1,5},{5... | collective-permute-start | bytes 3981320 | tf_op jit(solution)/shard_map/ppermute | solution.py:67
  219.6 31.5 %collective-permute-start.46 = (bf16[288,2304]{1,0:T(8,128)(2,1)S(1)}, bf16[288,2304]{1,0:T(8,128)(2,1)}, u32[]{:S(2)}, u32[]{:S(2)}) collective-permute-start(bf16[288,2304]{1,0:T(8,128)(2,1)S(1)} %collective-permute-done.41.refs_1_), channel_id=1, source_target_pairs={{0,4},{4,0},{8,12},{12,8},{16,20},{20,16},{24,28},{28,24},{1,5},{5... | collective-permute-start | bytes 3981320 | tf_op jit(solution)/shard_map/ppermute | solution.py:67
  219.9 31.3 %collective-permute-start.47 = (bf16[288,2304]{1,0:T(8,128)(2,1)S(1)}, bf16[288,2304]{1,0:T(8,128)(2,1)}, u32[]{:S(2)}, u32[]{:S(2)}) collective-permute-start(bf16[288,2304]{1,0:T(8,128)(2,1)S(1)} %collective-permute-done.42.refs_2_), channel_id=1, source_target_pairs={{0,4},{4,0},{8,12},{12,8},{16,20},{20,16},{24,28},{28,24},{1,5},{5... | collective-permute-start | bytes 3981320 | tf_op jit(solution)/shard_map/ppermute | solution.py:67
  263.7 227.4 %all-reduce.9.cloned.1.call-start = ((), (), s32[]{:S(2)}) async-start(), calls=%async_computation.4 | async-start | bytes 4718592 | tf_op jit(solution)/shard_map/psum | solution.py:981
  396.3 132.7 %reduce-scatter.2.cloned.1.call-start = ((), (), s32[]{:S(2)}) async-start(), calls=%async_computation.5 | async-start | bytes 11943936 | tf_op jit(solution)/shard_map/reduce_scatter | solution.py:983
  451.4 71.8 %collective-permute-start.54 = (bf16[288,2304]{1,0:T(8,128)(2,1)}, bf16[288,2304]{1,0:T(8,128)(2,1)S(1)}, u32[]{:S(2)}, u32[]{:S(2)}) collective-permute-start(bf16[288,2304]{1,0:T(8,128)(2,1)} %get-tuple-element.257), channel_id=1, source_target_pairs={{0,8},{4,12},{8,0},{12,4},{16,24},{20,28},{24,16},{28,20},{1,9},{5... | collective-permute-start | bytes 3981320 | tf_op jit(solution)/shard_map/ppermute | solution.py:67
  453.1 70.1 %collective-permute-start.55 = (bf16[288,2304]{1,0:T(8,128)(2,1)}, bf16[288,2304]{1,0:T(8,128)(2,1)}, u32[]{:S(2)}, u32[]{:S(2)}) collective-permute-start(bf16[288,2304]{1,0:T(8,128)(2,1)} %get-tuple-element.258), channel_id=1, source_target_pairs={{0,16},{4,20},{8,24},{12,28},{16,0},{20,4},{24,8},{28,12},{1,17},{... | collective-permute-start | bytes 3981320 | tf_op jit(solution)/shard_map/ppermute | solution.py:67
  566.0 99.2 %all-reduce.11.cloned.1.call-start = ((), (), s32[]{:S(2)}) async-start(), calls=%async_computation.6 | async-start | bytes 4718592 | tf_op jit(solution)/shard_map/psum | solution.py:1012
  570.9 21.3 %collective-permute-start.72 = (bf16[144,2304]{1,0:T(8,128)(2,1)}, bf16[144,2304]{1,0:T(8,128)(2,1)}, u32[]{:S(2)}, u32[]{:S(2)}) collective-permute-start(bf16[144,2304]{1,0:T(8,128)(2,1)} %get-tuple-element.281), channel_id=1, source_target_pairs={{0,16},{4,20},{8,24},{12,28},{16,0},{20,4},{24,8},{28,12},{1,17},{... | collective-permute-start | bytes 1990664 | tf_op jit(solution)/shard_map/ppermute | solution.py:67
  571.6 20.5 %collective-permute-start.74 = (bf16[144,2304]{1,0:T(8,128)(2,1)}, bf16[144,2304]{1,0:T(8,128)(2,1)}, u32[]{:S(2)}, u32[]{:S(2)}) collective-permute-start(bf16[144,2304]{1,0:T(8,128)(2,1)} %get-tuple-element.283), channel_id=1, source_target_pairs={{0,8},{4,12},{8,0},{12,4},{16,24},{20,28},{24,16},{28,20},{1,9},{5... | collective-permute-start | bytes 1990664 | tf_op jit(solution)/shard_map/ppermute | solution.py:67
  589.1 40.7 %collective-permute-start.62 = (bf16[4,288,1024]{2,1,0:T(8,128)(2,1)S(1)}, bf16[4,288,1024]{2,1,0:T(8,128)(2,1)S(1)}, u32[]{:S(2)}, u32[]{:S(2)}) collective-permute-start(bf16[4,288,1024]{2,1,0:T(8,128)(2,1)S(1)} %dynamic-slice_bitcast_fusion.2), channel_id=1, source_target_pairs={{0,4},{4,0},{8,12},{12,8},{16,20},{20,16},{24,28},{28,24},{1,5},{5... | collective-permute-start | bytes 7077896 | tf_op jit(solution)/shard_map/ppermute | solution.py:67
  592.1 39.9 %collective-permute-start.80 = (f32[1,4,288]{2,1,0:T(4,128)S(1)}, f32[1,4,288]{2,1,0:T(4,128)S(1)}, u32[]{:S(2)}, u32[]{:S(2)}) collective-permute-start(f32[1,4,288]{2,1,0:T(4,128)S(1)} %slice_select_fusion.2), channel_id=1, source_target_pairs={{0,4},{4,0},{8,12},{12,8},{16,20},{20,16},{24,28},{28,24},{1,5},{5... | collective-permute-start | bytes 13832 | tf_op jit(solution)/shard_map/ppermute | solution.py:67
  594.5 54.9 %collective-permute-start.73 = (bf16[288,2304]{1,0:T(8,128)(2,1)S(1)}, bf16[288,2304]{1,0:T(8,128)(2,1)S(1)}, u32[]{:S(2)}, u32[]{:S(2)}) collective-permute-start(bf16[288,2304]{1,0:T(8,128)(2,1)S(1)} %pad_maximum_fusion.2), channel_id=1, source_target_pairs={{0,8},{4,12},{8,0},{12,4},{16,24},{20,28},{24,16},{28,20},{1,9},{5... | collective-permute-start | bytes 3981320 | tf_op jit(solution)/shard_map/ppermute | solution.py:67
  598.2 30.9 %collective-permute-start.70 = (bf16[144,512]{1,0:T(8,128)(2,1)S(1)}, bf16[144,512]{1,0:T(8,128)(2,1)S(1)}, u32[]{:S(2)}, u32[]{:S(2)}) collective-permute-start(bf16[144,512]{1,0:T(8,128)(2,1)S(1)} %get-tuple-element.305), channel_id=1, source_target_pairs={{0,8},{4,12},{8,0},{12,4},{16,24},{20,28},{24,16},{28,20},{1,9},{5... | collective-permute-start | bytes 442376 | tf_op jit(solution)/shard_map/ppermute | solution.py:67
  602.5 46.9 %collective-permute-start.75 = (bf16[288,2304]{1,0:T(8,128)(2,1)S(1)}, bf16[288,2304]{1,0:T(8,128)(2,1)S(1)}, u32[]{:S(2)}, u32[]{:S(2)}) collective-permute-start(bf16[288,2304]{1,0:T(8,128)(2,1)S(1)} %pad_maximum_fusion.3), channel_id=1, source_target_pairs={{0,16},{4,20},{8,24},{12,28},{16,0},{20,4},{24,8},{28,12},{1,17},{... | collective-permute-start | bytes 3981320 | tf_op jit(solution)/shard_map/ppermute | solution.py:67
  646.0 26.5 %collective-permute-start.64 = (bf16[288,1024]{1,0:T(8,128)(2,1)S(1)}, bf16[288,1024]{1,0:T(8,128)(2,1)}, u32[]{:S(2)}, u32[]{:S(2)}) collective-permute-start(bf16[288,1024]{1,0:T(8,128)(2,1)S(1)} %pad_maximum_fusion.4), channel_id=1, source_target_pairs={{0,8},{4,12},{8,0},{12,4},{16,24},{20,28},{24,16},{28,20},{1,9},{5... | collective-permute-start | bytes 1769480 | tf_op jit(solution)/shard_map/ppermute | solution.py:67
  647.8 24.7 %collective-permute-start.66 = (bf16[288,1024]{1,0:T(8,128)(2,1)S(1)}, bf16[288,1024]{1,0:T(8,128)(2,1)}, u32[]{:S(2)}, u32[]{:S(2)}) collective-permute-start(bf16[288,1024]{1,0:T(8,128)(2,1)S(1)} %pad_maximum_fusion.5), channel_id=1, source_target_pairs={{0,16},{4,20},{8,24},{12,28},{16,0},{20,4},{24,8},{28,12},{1,17},{... | collective-permute-start | bytes 1769480 | tf_op jit(solution)/shard_map/ppermute | solution.py:67
  (146 other events, 1348.3 us)
Sparse Core Ops, SparseCore 0:
  112.7 96.7 all-reduce.4
  263.9 95.2 all-reduce.6
  396.4 94.6 all-reduce.8
  569.5 95.7 all-reduce.10
Sparse Core Ops, SparseCore 1:
  114.9 104.3 all-gather.1
  421.0 107.9 reduce-scatter.1

commit v7 on v6

--- a/solution.py
+++ b/solution.py
@@ -290,8 +290,8 @@
     )
 
 
-def join_kernel(cos_ref, sin_ref, query_ref, full_ref, *refs):
-    *terms, low_ref, part_ref = refs
+def join_kernel(cos_ref, sin_ref, query_ref, full_ref, unit_ref, *refs):
+    *terms, low_ref, part_ref, gain_ref = refs
     total = terms[0][...].astype(jnp.float32)
     for term in terms[1:]:
         total = total + term[...].astype(jnp.float32)
@@ -305,14 +305,17 @@
     for n in range(0, part_ref.shape[1], 256):
         part = matmul_nt(low_ref[...], full_ref[n : n + 256, : low_ref.shape[1]])
         part_ref[:, n : n + 256] = part.astype(jnp.bfloat16)
-
-
-def join(cosine, sine, query_low, full_qkv, terms):
+        unit = unit_ref[:, n : n + 256].astype(jnp.float32)
+        gain_ref[:, n : n + 256] = jnp.sum(part * unit, axis=0, keepdims=True)
+
+
+def join(cosine, sine, query_low, full_qkv, unit_in, terms):
     rows = query_low.shape[0]
     depth, width = full_qkv.shape[0], query_low.shape[1] + 2 * HD
     low = lambda n: jax.ShapeDtypeStruct((rows, n), jnp.bfloat16)
     return call(
-        join_kernel, (low(width), low(depth)), (cosine, sine, query_low, full_qkv, *terms), "join",
+        join_kernel, (low(width), low(depth), jax.ShapeDtypeStruct((1, depth), jnp.float32)),
+        (cosine, sine, query_low, full_qkv, unit_in, *terms), "join",
         flops=2 * rows * depth * width,
     )
 
@@ -953,11 +956,11 @@
         (branch, full_gate, full_up, *down_pieces[:3])
     )
     normed_mid = by_rows(mid_kernel, (tokens, branch), gains, (jnp.bfloat16,), 0, "mid_norms")
+    hidden, active, slope = units(normed_mid, full_gate, full_up)
     if pairs:
-        normed_mid, *far = lax.optimization_barrier((normed_mid, *down_pieces[3:5]))
+        hidden, *far = lax.optimization_barrier((hidden, *down_pieces[3:5]))
         mine = (*near, *far)
         down_pieces = (*mine, *(swap(part, 1) for part in mine))
-    hidden, active, slope = units(normed_mid, full_gate, full_up)
     mlp_part = out_project(hidden, down_pieces, depth, "project_down")
     mlp_part, out_pieces, kv_pieces, down_pieces = lax.optimization_barrier(
         (mlp_part, out_pieces, kv_pieces, down_pieces)
@@ -997,7 +1000,6 @@
         cosine, sine, block_rows, seq_blocks, pairs,
     )
     *kv_terms, down_shard, gate_terms = lax.optimization_barrier((*kv_terms, down_shard, gate_terms))
-    gate_shard = add_terms(gate_terms)
     if pairs:
         far = kv_terms[1] + swap(kv_terms[3], 1)
         near = kv_terms[0] + swap(kv_terms[2], 1)
@@ -1005,15 +1007,14 @@
         kv_sums = scatter_finish(scatter_corner(*blocks, far))
     else:
         kv_sums = (lax.psum_scatter(kv_terms[0], "ctx", scatter_dimension=0, tiled=True),)
-    qkv_low, in_part = join(cosine, sine, query_low, full_qkv, kv_sums)
-    in_part, qkv_low, branch_t, up_chips = lax.optimization_barrier(
-        (in_part, qkv_low, branch_low, up_chips)
+    qkv_low, in_part, gain_one = join(cosine, sine, query_low, full_qkv, unit_in, kv_sums)
+    in_part, qkv_low, branch_t, up_chips, gate_terms, down_shard = lax.optimization_barrier(
+        (in_part, qkv_low, branch_low, up_chips, gate_terms, down_shard)
     )
     in_sum = lax.psum(in_part, "tp")
     up_shard = add_terms(scatter_finish(scatter_blocks(up_chips)))
-    gain_one = jnp.sum(in_part.astype(jnp.float32) * (inputs * in_scale), axis=0)
     gain_one = sum_small_tp(gain_one)
-    gains_shard = scatter_gains(jnp.concatenate([gain_one[None], gain_mid[1:], gain_mid[:1], gain_four]))
+    gains_shard = scatter_gains(jnp.concatenate([gain_one, gain_mid[1:], gain_mid[:1], gain_four]))
     qkv_grad = matmul(normed_in.T, qkv_low).astype(jnp.bfloat16)
     qkv_shard = add_terms(scatter_finish(scatter_start(qkv_grad)))
     out_weight_grad = matmul(branch_t.T, attn_flat).astype(jnp.bfloat16)
@@ -1023,7 +1024,7 @@
         qkv_shard[:, q_width : q_width + HD],
         qkv_shard[:, q_width + HD :],
         out_grad_t.T,
-        gate_shard,
+        add_terms(gate_terms),
         up_shard,
         down_shard.astype(jnp.float32),
         gains_shard,

time: 693 us -> 706 us (1.019)
  local copies, waits for them, and re-layouts: 53.2 us -> 72.3 us
    unnamed x186 -> x196, local copies, waits for them, and re-layouts: 25.9 us -> 43.8 us
    psum x1, waiting for transfers between devices: 12.6 us -> 26.3 us  [body(): in_sum = lax.psum(in_part, 'tp')]
    ppermute x79, waiting for transfers between devices: 187 us -> 179 us  [swap(): return lax.ppermute(value, 'ctx', pairs)]
  transfers between devices with their start and end apart: 87 -> 87, of which waited for: 41 -> 39; matrix products, arithmetic and copies ran while one was open for 14% -> 15% of each run, Pallas kernels for 16% -> 16%
where the time goes in v7:
time: 706 us; the launch traced here: 696 us
  waiting for transfers between devices  310 us (44%)
  Pallas kernels  161 us (23%)
  local copies, waits for them, and re-layouts  72.3 us (10%)
  starting transfers between devices  61.1 us (9%)
  other arithmetic  44.5 us (6%)
  matrix products  30.8 us (4%)
  between operations  16.6 us (2%)
    ppermute x79, waiting for transfers between devices, swap(): return lax.ppermute(value, 'ctx', pairs)  179 us
    psum x1, waiting for transfers between devices, body(): mlp_out = lax.psum(mlp_part, 'tp')  72 us
    ppermute x79, starting transfers between devices, swap(): return lax.ppermute(value, 'ctx', pairs)  56.5 us
    unnamed x196, local copies, waits for them, and re-layouts  43.8 us
    dot_general x5, matrix products, matmul(): return jnp.dot(left, right, preferred_element_type=jnp.float32)  30.8 us
    pallas_call x4, Pallas kernels, by_rows(): pl.pallas_call(kernel, out_shape=tuple(shapes), grid=(rows // block,), in...  30 us
    pallas_call x4, Pallas kernels, assemble(): pl.pallas_call(assemble_kernel, out_shape=jax.ShapeDtypeStruct((8 * rows,...  27.3 us
    psum x1, waiting for transfers between devices, body(): mid_sum = lax.psum(mid_part, 'tp')  27 us
  transfers between devices with their start and end apart: 87, of which 39 were waited for; matrix products, arithmetic and copies ran while one was open for 15% of the time, Pallas kernels for 16%

profile of v7, /device:TPU:0, one launch (start us, length us, event | category | flops | bytes accessed | tf_op | source)
XLA Modules:
  0.0 696.0 jit_solution(17975227872109807318)
XLA Ops:
  18.7 11.2 %collective-permute-done.refs_1_ = bf16[288,1152]{1,0:T(8,128)(2,1)S(1)} collective-permute-done((bf16[288,1152]{1,0:T(8,128)(2,1)S(1)}, bf16[288,1152]{1,0:T(8,128)(2,1)S(1)}, u32[]{:S(2)}, u32[]{:S(2)}) %collective-permute-start) | collective-permute-done | bytes 663584 | tf_op jit(solution)/shard_map/ppermute | solution.py:67
  51.5 5.1 project.1
  71.9 8.1 %collective-permute-done.26.refs_4_ = bf16[144,512]{1,0:T(8,128)(2,1)S(1)} collective-permute-done((bf16[144,512]{1,0:T(8,128)(2,1)S(1)}, bf16[144,512]{1,0:T(8,128)(2,1)S(1)}, u32[]{:S(2)}, u32[]{:S(2)}) %collective-permute-start.26) | collective-permute-done | bytes 147488 | tf_op jit(solution)/shard_map/ppermute | solution.py:67
  91.2 11.9 %attend.1 = (f32[512,512]{1,0:T(8,128)}, bf16[512,512]{1,0:T(8,128)(2,1)}, f32[512,256]{1,0:T(8,128)}) custom-call(s32[16]{0:T(128)} %reshape.119.map_ref, s32[1]{0:T(128)} %bitcast.8.me_ref, bf16[512,512]{1,0:T(8,128)(2,1)} %copy-done.64, bf16[256,512]{1,0:T(8,128)(2,1)} %copy-done.31, bf16[256,512]{1,0:T(8,128)(2,1)} %copy-done.33, ...), custom_call_target="tpu_custom_call" | custom-call | flops 4294967296 | bytes 10485760 | tf_op jit(solution)/shard_map/attend/pallas_call | solution.py:724
  118.7 5.7 assemble.4.full_ref
  132.9 22.7 %collective-permute-done.34.refs_3_ = bf16[144,2304]{1,0:T(8,128)(2,1)S(1)} collective-permute-done((bf16[144,2304]{1,0:T(8,128)(2,1)}, bf16[144,2304]{1,0:T(8,128)(2,1)S(1)}, u32[]{:S(2)}, u32[]{:S(2)}) %collective-permute-start.34) | collective-permute-done | bytes 663584 | tf_op jit(solution)/shard_map/ppermute | solution.py:67
  162.5 9.1 %assemble.5.gate_ref = bf16[2304,2304]{1,0:T(8,128)(2,1)} custom-call(s32[10]{0:T(128)} %copy-done.59, bf16[288,2304]{1,0:T(8,128)(2,1)} %refs_0_, bf16[288,2304]{1,0:T(8,128)(2,1)} %collective-permute-done.32.refs_1_, bf16[288,2304]{1,0:T(8,128)(2,1)} %collective-permute-done.33.refs_2_, bf16[144,2304]{1,0:T(8,128)(2,1)} %copy-done.76, ...), custom_call_target="tpu_custom_call" | custom-call | bytes 21233664 | tf_op jit(solution)/shard_map/assemble/pallas_call | solution.py:129
  171.6 43.4 %collective-permute-done.41.refs_1_ = bf16[288,2304]{1,0:T(8,128)(2,1)S(1)} collective-permute-done((bf16[288,2304]{1,0:T(8,128)(2,1)}, bf16[288,2304]{1,0:T(8,128)(2,1)S(1)}, u32[]{:S(2)}, u32[]{:S(2)}) %collective-permute-start.41) | collective-permute-done | bytes 1327136 | tf_op jit(solution)/shard_map/ppermute | solution.py:67
  221.9 5.2 mid_norms.1.in_ref
  227.0 16.7 %units.1 = (bf16[512,2304]{1,0:T(8,128)(2,1)}, bf16[512,2304]{1,0:T(8,128)(2,1)}, bf16[512,2304]{1,0:T(8,128)(2,1)}) custom-call(bf16[512,2304]{1,0:T(8,128)(2,1)} %mid_norms.1.in_ref, bf16[2304,2304]{1,0:T(8,128)(2,1)} %assemble.5.gate_ref, bf16[2304,2304]{1,0:T(8,128)(2,1)} %all-gather.2.cloned.1.call-done.up_ref), custom_call_target="tpu_custom_call" | custom-call | flops 10871635968 | bytes 21233664 | tf_op jit(solution)/shard_map/units/pallas_call | solution.py:478
  249.0 9.7 %project_down.1 = bf16[512,2304]{1,0:T(8,128)(2,1)S(1)} custom-call(s32[10]{0:T(128)S(1)} %copy-done.61, bf16[512,2304]{1,0:T(8,128)(2,1)S(1)} %copy-done.65, bf16[288,2304]{1,0:T(8,128)(2,1)} %bitcast.11.refs_0_, bf16[288,2304]{1,0:T(8,128)(2,1)S(1)} %copy-done.3, bf16[288,2304]{1,0:T(8,128)(2,1)} %collective-permute-done.42.refs_2_, ...), custom_call_target="tpu_custom_call" | custom-call | flops 5435817984 | bytes 15335464 | tf_op jit(solution)/shard_map/project_down/pallas_call | solution.py:53
  262.0 9.2 %assemble.7.down_ref = bf16[2304,2304]{1,0:T(8,128)(2,1)} custom-call(s32[10]{0:T(128)} %copy-done.59, bf16[288,2304]{1,0:T(8,128)(2,1)} %bitcast.11.refs_0_, bf16[288,2304]{1,0:T(8,128)(2,1)} %copy-done.2, bf16[288,2304]{1,0:T(8,128)(2,1)} %collective-permute-done.42.refs_2_, bf16[144,2304]{1,0:T(8,128)(2,1)} %collective-permute-done.43.refs_3_, ...), custom_call_target="tpu_custom_call" | custom-call | bytes 21233664 | tf_op jit(solution)/shard_map/assemble/pallas_call | solution.py:129
  286.7 72.0 %all-reduce.7.cloned.1.call-done.mlp_ref = bf16[512,2304]{1,0:T(8,128)(2,1)} async-done(((bf16[512,2304]{1,0:T(8,128)(2,1)}), bf16[512,2304]{1,0:T(8,128)(2,1)}) %all-reduce.7.cloned.1.call-update) | async-done | bytes 2359312 | tf_op jit(solution)/shard_map/psum | solution.py:971
  358.7 8.2 %top_norms.1 = (bf16[512,2304]{1,0:T(8,128)(2,1)}, bf16[512,2304]{1,0:T(8,128)(2,1)}, f32[1,2304]{1,0:T(1,128)}) custom-call(bf16[512,2304]{1,0:T(8,128)(2,1)} %tok_ref.7, bf16[512,2304]{1,0:T(8,128)(2,1)} %all-reduce.5.cloned.1.call-done.branch_ref, bf16[512,2304]{1,0:T(8,128)(2,1)} %all-reduce.7.cloned.1.call-done.mlp_ref, bf16[512,2304]{1,0:T(8,128)(2,1)} %cot_ref.3, ...), custom_call_target="tpu_custom_call" | custom-call | bytes 14164992 | tf_op jit(solution)/shard_map/top_norms/pallas_call | solution.py:439
  366.9 12.0 %units_back.1 = (bf16[512,2304]{1,0:T(8,128)(2,1)}, bf16[512,2304]{1,0:T(8,128)(2,1)}) custom-call(bf16[512,2304]{1,0:T(8,128)(2,1)} %get-tuple-element.260.grad_ref, bf16[2304,2304]{1,0:T(8,128)(2,1)} %assemble.7.down_ref, bf16[512,2304]{1,0:T(8,128)(2,1)} %get-tuple-element.239.active_ref, bf16[512,2304]{1,0:T(8,128)(2,1)} %get-tuple-element.240.slope_ref), custom_call_target="tpu_custom_call" | custom-call | flops 5435817984 | bytes 10616832 | tf_op jit(solution)/shard_map/units_back/pallas_call | solution.py:506
  378.9 16.9 %features_back.1 = bf16[512,2304]{1,0:T(8,128)(2,1)} custom-call(bf16[512,2304]{1,0:T(8,128)(2,1)} %get-tuple-element.245.dg_ref, bf16[512,2304]{1,0:T(8,128)(2,1)} %get-tuple-element.244.du_ref, bf16[2304,2304]{1,0:T(8,128)(2,1)} %assemble.5.gate_ref, bf16[2304,2304]{1,0:T(8,128)(2,1)} %all-gather.2.cloned.1.call-done.up_ref), custom_call_target="tpu_custom_call" | custom-call | flops 10871635968 | bytes 21233664 | tf_op jit(solution)/shard_map/features_back/pallas_call | solution.py:532
  395.9 8.0 %convolution_convert_fusion.1 = bf16[2304,2304]{1,0:T(8,128)(2,1)S(1)} fusion(bf16[512,2304]{1,0:T(8,128)(2,1)} %mid_norms.1.in_ref, bf16[512,2304]{1,0:T(8,128)(2,1)} %get-tuple-element.245.dg_ref), kind=kOutput, calls=%fused_computation.1 | convolution fusion | flops 5441126400 | bytes 15335424 | tf_op jit(solution)/shard_map/dot_general | solution.py:33
  410.8 8.5 %convolution_convert_fusion = bf16[2304,2304]{0,1:T(8,128)(2,1)} fusion(bf16[512,2304]{1,0:T(8,128)(2,1)S(1)} %copy-done.66, bf16[512,2304]{1,0:T(8,128)(2,1)S(1)} %copy-done.86), kind=kOutput, calls=%fused_computation | convolution fusion | flops 5441126400 | bytes 15335424 | tf_op jit(solution)/shard_map/dot_general | solution.py:33
  419.9 4.8 bitcast_add_fusion.1
  427.8 8.5 %convolution_convert_fusion.2 = bf16[2304,2304]{1,0:T(8,128)(2,1)} fusion(bf16[512,2304]{1,0:T(8,128)(2,1)S(1)} %copy-done.71, bf16[512,2304]{1,0:T(8,128)(2,1)S(1)} %copy-done.88), kind=kOutput, calls=%fused_computation.2 | convolution fusion | flops 5441126400 | bytes 15335424 | tf_op jit(solution)/shard_map/dot_general | solution.py:33
  451.8 6.5 collective-permute-done.53
  458.3 5.4 bitcast_add_fusion
  463.7 27.0 %all-reduce.9.cloned.1.call-done.mid_ref = bf16[512,2304]{1,0:T(8,128)(2,1)} async-done(((bf16[512,2304]{1,0:T(8,128)(2,1)}), bf16[512,2304]{1,0:T(8,128)(2,1)}) %all-reduce.9.cloned.1.call-update) | async-done | bytes 2359312 | tf_op jit(solution)/shard_map/psum | solution.py:984
  490.7 9.4 %low_norms.1 = (f32[512,2304]{1,0:T(8,128)}, bf16[512,2304]{1,0:T(8,128)(2,1)}, f32[2,2304]{1,0:T(2,128)}) custom-call(bf16[512,2304]{1,0:T(8,128)(2,1)} %tok_ref.7, bf16[512,2304]{1,0:T(8,128)(2,1)} %all-reduce.5.cloned.1.call-done.branch_ref, bf16[512,2304]{1,0:T(8,128)(2,1)} %all-reduce.9.cloned.1.call-done.mid_ref, bf16[512,2304]{1,0:T(8,128)(2,1)} %cot_ref.3, ...), custom_call_target="tpu_custom_call" | custom-call | bytes 16533504 | tf_op jit(solution)/shard_map/low_norms/pallas_call | solution.py:439
  500.1 22.3 %attend_back.1 = (bf16[512,512]{1,0:T(8,128)(2,1)}, bf16[1536,512]{1,0:T(8,128)(2,1)}, bf16[512,512]{1,0:T(8,128)(2,1)}, bf16[1536,512]{1,0:T(8,128)(2,1)}, bf16[512,512]{1,0:T(8,128)(2,1)}) custom-call(s32[16]{0:T(128)} %reshape.119.map_ref, s32[1]{0:T(128)} %bitcast.8.me_ref, bf16[512,2304]{1,0:T(8,128)(2,1)} %get-tuple-element.279.da_ref, ...), custom_call_target="tpu_custom_call" | custom-call | flops 10737418240 | bytes 14680064 | tf_op jit(solution)/shard_map/attend_back/pallas_call | solution.py:844
  522.4 5.0 reduce-scatter.2.cloned.1.call-done
  544.7 10.9 %collective-permute-done.61.refs_2_ = bf16[512,512]{1,0:T(8,128)(2,1)S(1)} collective-permute-done((bf16[512,512]{1,0:T(8,128)(2,1)S(1)}, bf16[512,512]{1,0:T(8,128)(2,1)S(1)}, u32[]{:S(2)}, u32[]{:S(2)}) %collective-permute-start.61) | collective-permute-done | bytes 524320 | tf_op jit(solution)/shard_map/ppermute | solution.py:67
  586.2 4.7 convert_add_fusion.1
  604.0 25.2 %collective-permute-done.70 = bf16[144,512]{1,0:T(8,128)(2,1)S(1)} collective-permute-done((bf16[144,512]{1,0:T(8,128)(2,1)S(1)}, bf16[144,512]{1,0:T(8,128)(2,1)S(1)}, u32[]{:S(2)}, u32[]{:S(2)}) %collective-permute-start.70) | collective-permute-done | bytes 147488 | tf_op jit(solution)/shard_map/ppermute | solution.py:67
  641.2 4.5 collective-permute-done.63
  652.0 26.3 %all-reduce.11.cloned.1.call-done.sum_ref = bf16[512,2304]{1,0:T(8,128)(2,1)} async-done(((bf16[512,2304]{1,0:T(8,128)(2,1)}), bf16[512,2304]{1,0:T(8,128)(2,1)}) %all-reduce.11.cloned.1.call-update) | async-done | bytes 2359312 | tf_op jit(solution)/shard_map/psum | solution.py:1014
  678.3 7.2 %end_norms.1 = f32[512,2304]{1,0:T(8,128)} custom-call(bf16[512,2304]{1,0:T(8,128)(2,1)} %tok_ref.7, bf16[512,2304]{1,0:T(8,128)(2,1)} %all-reduce.11.cloned.1.call-done.sum_ref, f32[512,2304]{1,0:T(8,128)} %get-tuple-element.276.resid_ref, f32[4,2304]{1,0:T(4,128)} %bitcast.152), custom_call_target="tpu_custom_call" | custom-call | bytes 14155776 | tf_op jit(solution)/shard_map/end_norms/pallas_call | solution.py:439
  (443 shorter events, 228.4 us)
Async XLA Ops:
  8.0 213.3 %all-reduce.5.cloned.1.call-start = ((), (), s32[]{:S(2)}) async-start(), calls=%async_computation.1 | async-start | bytes 4718592 | tf_op jit(solution)/shard_map/psum | solution.py:938
  16.4 26.4 %collective-permute-start.4 = (bf16[288,1152]{1,0:T(8,128)(2,1)S(1)}, bf16[288,1152]{1,0:T(8,128)(2,1)}, u32[]{:S(2)}, u32[]{:S(2)}) collective-permute-start(bf16[288,1152]{1,0:T(8,128)(2,1)S(1)} %pack.1.refs_0_), channel_id=1, source_target_pairs={{0,4},{4,0},{8,12},{12,8},{16,20},{20,16},{24,28},{28,24},{1,5},{5... | collective-permute-start | bytes 1990664 | tf_op jit(solution)/shard_map/ppermute | solution.py:67
  80.4 31.6 %collective-permute-start.32 = (bf16[288,2304]{1,0:T(8,128)(2,1)}, bf16[288,2304]{1,0:T(8,128)(2,1)}, u32[]{:S(2)}, u32[]{:S(2)}) collective-permute-start(bf16[288,2304]{1,0:T(8,128)(2,1)} %refs_0_), channel_id=1, source_target_pairs={{0,8},{4,12},{8,0},{12,4},{16,24},{20,28},{24,16},{28,20},{1,9},{5... | collective-permute-start | bytes 3981320 | tf_op jit(solution)/shard_map/ppermute | solution.py:67
  81.8 30.6 %collective-permute-start.33 = (bf16[288,2304]{1,0:T(8,128)(2,1)}, bf16[288,2304]{1,0:T(8,128)(2,1)}, u32[]{:S(2)}, u32[]{:S(2)}) collective-permute-start(bf16[288,2304]{1,0:T(8,128)(2,1)} %refs_0_), channel_id=1, source_target_pairs={{0,16},{4,20},{8,24},{12,28},{16,0},{20,4},{24,8},{28,12},{1,17},{... | collective-permute-start | bytes 3981320 | tf_op jit(solution)/shard_map/ppermute | solution.py:67
  112.4 109.0 %all-gather.2.cloned.1.call-start = ((), (), s32[]{:S(2)}) async-start(), calls=%async_computation.2 | async-start | bytes 11943936 | tf_op jit(solution)/shard_map/all_gather | solution.py:939
  113.0 245.7 %all-reduce.7.cloned.1.call-start = ((), (), s32[]{:S(2)}) async-start(), calls=%async_computation.3 | async-start | bytes 4718592 | tf_op jit(solution)/shard_map/psum | solution.py:971
  113.0 44.9 %collective-permute-start.36 = (bf16[288,2304]{1,0:T(8,128)(2,1)}, bf16[288,2304]{1,0:T(8,128)(2,1)}, u32[]{:S(2)}, u32[]{:S(2)}) collective-permute-start(bf16[288,2304]{1,0:T(8,128)(2,1)} %refs_0_), channel_id=1, source_target_pairs={{0,4},{4,0},{8,12},{12,8},{16,20},{20,16},{24,28},{28,24},{1,5},{5... | collective-permute-start | bytes 3981320 | tf_op jit(solution)/shard_map/ppermute | solution.py:67
  116.2 45.4 %collective-permute-start.37 = (bf16[288,2304]{1,0:T(8,128)(2,1)}, bf16[288,2304]{1,0:T(8,128)(2,1)}, u32[]{:S(2)}, u32[]{:S(2)}) collective-permute-start(bf16[288,2304]{1,0:T(8,128)(2,1)} %collective-permute-done.32.refs_1_), channel_id=1, source_target_pairs={{0,4},{4,0},{8,12},{12,8},{16,20},{20,16},{24,28},{28,24},{1,5},{5... | collective-permute-start | bytes 3981320 | tf_op jit(solution)/shard_map/ppermute | solution.py:67
  118.2 44.3 %collective-permute-start.38 = (bf16[288,2304]{1,0:T(8,128)(2,1)}, bf16[288,2304]{1,0:T(8,128)(2,1)}, u32[]{:S(2)}, u32[]{:S(2)}) collective-permute-start(bf16[288,2304]{1,0:T(8,128)(2,1)} %collective-permute-done.33.refs_2_), channel_id=1, source_target_pairs={{0,4},{4,0},{8,12},{12,8},{16,20},{20,16},{24,28},{28,24},{1,5},{5... | collective-permute-start | bytes 3981320 | tf_op jit(solution)/shard_map/ppermute | solution.py:67
  126.5 29.1 %collective-permute-start.34 = (bf16[144,2304]{1,0:T(8,128)(2,1)}, bf16[144,2304]{1,0:T(8,128)(2,1)S(1)}, u32[]{:S(2)}, u32[]{:S(2)}) collective-permute-start(bf16[144,2304]{1,0:T(8,128)(2,1)} %slice.246), channel_id=1, source_target_pairs={{0,16},{4,20},{8,24},{12,28},{16,0},{20,4},{24,8},{28,12},{1,17},{... | collective-permute-start | bytes 1990664 | tf_op jit(solution)/shard_map/ppermute | solution.py:67
  126.8 28.8 %collective-permute-start.35 = (bf16[144,2304]{1,0:T(8,128)(2,1)}, bf16[144,2304]{1,0:T(8,128)(2,1)S(1)}, u32[]{:S(2)}, u32[]{:S(2)}) collective-permute-start(bf16[144,2304]{1,0:T(8,128)(2,1)} %slice.247), channel_id=1, source_target_pairs={{0,8},{4,12},{8,0},{12,4},{16,24},{20,28},{24,16},{28,20},{1,9},{5... | collective-permute-start | bytes 1990664 | tf_op jit(solution)/shard_map/ppermute | solution.py:67
  156.5 58.6 %collective-permute-start.41 = (bf16[288,2304]{1,0:T(8,128)(2,1)}, bf16[288,2304]{1,0:T(8,128)(2,1)S(1)}, u32[]{:S(2)}, u32[]{:S(2)}) collective-permute-start(bf16[288,2304]{1,0:T(8,128)(2,1)} %bitcast.11.refs_0_), channel_id=1, source_target_pairs={{0,8},{4,12},{8,0},{12,4},{16,24},{20,28},{24,16},{28,20},{1,9},{5... | collective-permute-start | bytes 3981320 | tf_op jit(solution)/shard_map/ppermute | solution.py:67
  157.9 59.5 %collective-permute-start.42 = (bf16[288,2304]{1,0:T(8,128)(2,1)}, bf16[288,2304]{1,0:T(8,128)(2,1)}, u32[]{:S(2)}, u32[]{:S(2)}) collective-permute-start(bf16[288,2304]{1,0:T(8,128)(2,1)} %bitcast.11.refs_0_), channel_id=1, source_target_pairs={{0,16},{4,20},{8,24},{12,28},{16,0},{20,4},{24,8},{28,12},{1,17},{... | collective-permute-start | bytes 3981320 | tf_op jit(solution)/shard_map/ppermute | solution.py:67
  218.4 25.4 %collective-permute-start.43 = (bf16[144,2304]{1,0:T(8,128)(2,1)}, bf16[144,2304]{1,0:T(8,128)(2,1)}, u32[]{:S(2)}, u32[]{:S(2)}) collective-permute-start(bf16[144,2304]{1,0:T(8,128)(2,1)} %slice.248), channel_id=1, source_target_pairs={{0,16},{4,20},{8,24},{12,28},{16,0},{20,4},{24,8},{28,12},{1,17},{... | collective-permute-start | bytes 1990664 | tf_op jit(solution)/shard_map/ppermute | solution.py:67
  221.4 25.9 %collective-permute-start.45 = (bf16[288,2304]{1,0:T(8,128)(2,1)}, bf16[288,2304]{1,0:T(8,128)(2,1)}, u32[]{:S(2)}, u32[]{:S(2)}) collective-permute-start(bf16[288,2304]{1,0:T(8,128)(2,1)} %bitcast.11.refs_0_), channel_id=1, source_target_pairs={{0,4},{4,0},{8,12},{12,8},{16,20},{20,16},{24,28},{28,24},{1,5},{5... | collective-permute-start | bytes 3981320 | tf_op jit(solution)/shard_map/ppermute | solution.py:67
  221.4 25.9 %collective-permute-start.46 = (bf16[288,2304]{1,0:T(8,128)(2,1)}, bf16[288,2304]{1,0:T(8,128)(2,1)}, u32[]{:S(2)}, u32[]{:S(2)}) collective-permute-start(bf16[288,2304]{1,0:T(8,128)(2,1)} %copy-done.2), channel_id=1, source_target_pairs={{0,4},{4,0},{8,12},{12,8},{16,20},{20,16},{24,28},{28,24},{1,5},{5... | collective-permute-start | bytes 3981320 | tf_op jit(solution)/shard_map/ppermute | solution.py:67
  221.9 25.4 %collective-permute-start.47 = (bf16[288,2304]{1,0:T(8,128)(2,1)}, bf16[288,2304]{1,0:T(8,128)(2,1)}, u32[]{:S(2)}, u32[]{:S(2)}) collective-permute-start(bf16[288,2304]{1,0:T(8,128)(2,1)} %collective-permute-done.42.refs_2_), channel_id=1, source_target_pairs={{0,4},{4,0},{8,12},{12,8},{16,20},{20,16},{24,28},{28,24},{1,5},{5... | collective-permute-start | bytes 3981320 | tf_op jit(solution)/shard_map/ppermute | solution.py:67
  261.8 228.9 %all-reduce.9.cloned.1.call-start = ((), (), s32[]{:S(2)}) async-start(), calls=%async_computation.4 | async-start | bytes 4718592 | tf_op jit(solution)/shard_map/psum | solution.py:984
  395.9 131.5 %reduce-scatter.2.cloned.1.call-start = ((), (), s32[]{:S(2)}) async-start(), calls=%async_computation.5 | async-start | bytes 11943936 | tf_op jit(solution)/shard_map/reduce_scatter | solution.py:986
  419.3 259.0 %all-reduce.11.cloned.1.call-start = ((), (), s32[]{:S(2)}) async-start(), calls=%async_computation.6 | async-start | bytes 4718592 | tf_op jit(solution)/shard_map/psum | solution.py:1014
  449.4 72.9 %collective-permute-start.54 = (bf16[288,2304]{1,0:T(8,128)(2,1)}, bf16[288,2304]{1,0:T(8,128)(2,1)}, u32[]{:S(2)}, u32[]{:S(2)}) collective-permute-start(bf16[288,2304]{1,0:T(8,128)(2,1)} %get-tuple-element.262), channel_id=1, source_target_pairs={{0,8},{4,12},{8,0},{12,4},{16,24},{20,28},{24,16},{28,20},{1,9},{5... | collective-permute-start | bytes 3981320 | tf_op jit(solution)/shard_map/ppermute | solution.py:67
  451.1 71.2 %collective-permute-start.55 = (bf16[288,2304]{1,0:T(8,128)(2,1)}, bf16[288,2304]{1,0:T(8,128)(2,1)}, u32[]{:S(2)}, u32[]{:S(2)}) collective-permute-start(bf16[288,2304]{1,0:T(8,128)(2,1)} %get-tuple-element.263), channel_id=1, source_target_pairs={{0,16},{4,20},{8,24},{12,28},{16,0},{20,4},{24,8},{28,12},{1,17},{... | collective-permute-start | bytes 3981320 | tf_op jit(solution)/shard_map/ppermute | solution.py:67
  567.4 25.3 %collective-permute-start.72 = (bf16[144,2304]{1,0:T(8,128)(2,1)}, bf16[144,2304]{1,0:T(8,128)(2,1)}, u32[]{:S(2)}, u32[]{:S(2)}) collective-permute-start(bf16[144,2304]{1,0:T(8,128)(2,1)} %get-tuple-element.289), channel_id=1, source_target_pairs={{0,16},{4,20},{8,24},{12,28},{16,0},{20,4},{24,8},{28,12},{1,17},{... | collective-permute-start | bytes 1990664 | tf_op jit(solution)/shard_map/ppermute | solution.py:67
  568.8 23.9 %collective-permute-start.74 = (bf16[144,2304]{1,0:T(8,128)(2,1)}, bf16[144,2304]{1,0:T(8,128)(2,1)}, u32[]{:S(2)}, u32[]{:S(2)}) collective-permute-start(bf16[144,2304]{1,0:T(8,128)(2,1)} %get-tuple-element.291), channel_id=1, source_target_pairs={{0,8},{4,12},{8,0},{12,4},{16,24},{20,28},{24,16},{28,20},{1,9},{5... | collective-permute-start | bytes 1990664 | tf_op jit(solution)/shard_map/ppermute | solution.py:67
  572.1 23.0 %collective-permute-start.67 = (bf16[4,288,512]{2,1,0:T(8,128)(2,1)}, bf16[4,288,512]{2,1,0:T(8,128)(2,1)}, u32[]{:S(2)}, u32[]{:S(2)}) collective-permute-start(bf16[4,288,512]{2,1,0:T(8,128)(2,1)} %dynamic-slice_bitcast_fusion.4), channel_id=1, source_target_pairs={{0,4},{4,0},{8,12},{12,8},{16,20},{20,16},{24,28},{28,24},{1,5},{5... | collective-permute-start | bytes 3538952 | tf_op jit(solution)/shard_map/ppermute | solution.py:67
  584.5 45.3 %collective-permute-start.62 = (bf16[4,288,1024]{2,1,0:T(8,128)(2,1)}, bf16[4,288,1024]{2,1,0:T(8,128)(2,1)}, u32[]{:S(2)}, u32[]{:S(2)}) collective-permute-start(bf16[4,288,1024]{2,1,0:T(8,128)(2,1)} %dynamic-slice_bitcast_fusion.2), channel_id=1, source_target_pairs={{0,4},{4,0},{8,12},{12,8},{16,20},{20,16},{24,28},{28,24},{1,5},{5... | collective-permute-start | bytes 7077896 | tf_op jit(solution)/shard_map/ppermute | solution.py:67
  592.6 40.6 %collective-permute-start.80 = (f32[1,4,288]{2,1,0:T(4,128)S(1)}, f32[1,4,288]{2,1,0:T(4,128)S(1)}, u32[]{:S(2)}, u32[]{:S(2)}) collective-permute-start(f32[1,4,288]{2,1,0:T(4,128)S(1)} %slice_select_fusion.2), channel_id=1, source_target_pairs={{0,4},{4,0},{8,12},{12,8},{16,20},{20,16},{24,28},{28,24},{1,5},{5... | collective-permute-start | bytes 13832 | tf_op jit(solution)/shard_map/ppermute | solution.py:67
  594.7 55.4 %collective-permute-start.73 = (bf16[288,2304]{1,0:T(8,128)(2,1)S(1)}, bf16[288,2304]{1,0:T(8,128)(2,1)S(1)}, u32[]{:S(2)}, u32[]{:S(2)}) collective-permute-start(bf16[288,2304]{1,0:T(8,128)(2,1)S(1)} %pad_maximum_fusion.2), channel_id=1, source_target_pairs={{0,8},{4,12},{8,0},{12,4},{16,24},{20,28},{24,16},{28,20},{1,9},{5... | collective-permute-start | bytes 3981320 | tf_op jit(solution)/shard_map/ppermute | solution.py:67
  597.9 31.3 %collective-permute-start.70 = (bf16[144,512]{1,0:T(8,128)(2,1)S(1)}, bf16[144,512]{1,0:T(8,128)(2,1)S(1)}, u32[]{:S(2)}, u32[]{:S(2)}) collective-permute-start(bf16[144,512]{1,0:T(8,128)(2,1)S(1)} %get-tuple-element.313), channel_id=1, source_target_pairs={{0,8},{4,12},{8,0},{12,4},{16,24},{20,28},{24,16},{28,20},{1,9},{5... | collective-permute-start | bytes 442376 | tf_op jit(solution)/shard_map/ppermute | solution.py:67
  602.6 47.4 %collective-permute-start.75 = (bf16[288,2304]{1,0:T(8,128)(2,1)S(1)}, bf16[288,2304]{1,0:T(8,128)(2,1)S(1)}, u32[]{:S(2)}, u32[]{:S(2)}) collective-permute-start(bf16[288,2304]{1,0:T(8,128)(2,1)S(1)} %pad_maximum_fusion.3), channel_id=1, source_target_pairs={{0,16},{4,20},{8,24},{12,28},{16,0},{20,4},{24,8},{28,12},{1,17},{... | collective-permute-start | bytes 3981320 | tf_op jit(solution)/shard_map/ppermute | solution.py:67
  646.8 38.7 %collective-permute-start.64 = (bf16[288,1024]{1,0:T(8,128)(2,1)}, bf16[288,1024]{1,0:T(8,128)(2,1)}, u32[]{:S(2)}, u32[]{:S(2)}) collective-permute-start(bf16[288,1024]{1,0:T(8,128)(2,1)} %pad_maximum_fusion.4), channel_id=1, source_target_pairs={{0,8},{4,12},{8,0},{12,4},{16,24},{20,28},{24,16},{28,20},{1,9},{5... | collective-permute-start | bytes 1769480 | tf_op jit(solution)/shard_map/ppermute | solution.py:67
  649.0 36.4 %collective-permute-start.66 = (bf16[288,1024]{1,0:T(8,128)(2,1)}, bf16[288,1024]{1,0:T(8,128)(2,1)}, u32[]{:S(2)}, u32[]{:S(2)}) collective-permute-start(bf16[288,1024]{1,0:T(8,128)(2,1)} %pad_maximum_fusion.5), channel_id=1, source_target_pairs={{0,16},{4,20},{8,24},{12,28},{16,0},{20,4},{24,8},{28,12},{1,17},{... | collective-permute-start | bytes 1769480 | tf_op jit(solution)/shard_map/ppermute | solution.py:67
  (151 other events, 1216.4 us)
Sparse Core Ops, SparseCore 0:
  112.5 96.7 all-reduce.4
  261.9 96.7 all-reduce.6
  396.0 94.6 all-reduce.8
  584.7 93.5 all-reduce.10
Sparse Core Ops, SparseCore 1:
  114.7 104.7 all-gather.1
  419.3 107.9 reduce-scatter.1
